TPU v7x, 32 devices: a whole 2x2x4 slice. The times are simulated.
32 devices in a mesh: ctx: 4 (over z), tp: 8 (over y, x, core).
Axes of the slice: x: 2, y: 2, z: 4, core: 2. Of those that a mesh axis runs over, the one named last changes fastest.
Arguments:
- byte_embeds: bfloat16 [6144, 1024], P(('ctx', 'tp')), may hold values from -6 to 6
- local_embeds: bfloat16 [6144, 1024], P(('ctx', 'tp')), may hold values from -6 to 6
- global_qkv: bfloat16 [3, 8192, 4096], P(None, None, 'tp'), may hold values from -0.0625 to 0.0625
- global_out: bfloat16 [4096, 8192], P('tp'), may hold values from -1.5 to 1.5
- local_qkv: bfloat16 [1, 1024, 3072], replicated, may hold values from -0.1875 to 0.1875
- local_out: bfloat16 [1, 1024, 1024], replicated, may hold values from -0.1875 to 0.1875
- cotangent: bfloat16 [6144, 1024], P(('ctx', 'tp')), may hold values from -6 to 6
Outputs:
- hidden: bfloat16 [6144, 1024], P(('ctx', 'tp'))
- grad_qkv: float32 [1, 1024, 3072], P(None, ('ctx', 'tp'))
- grad_out: float32 [1, 1024, 1024], P(None, ('ctx', 'tp'))
All inputs are finite; a program needn't handle non-finite values.
Results may differ from a plain program's by a relative error of at most 0.028.
Values may be sent and summed in bfloat16 or wider, within the bound.
No kernel may reach another device: no remote copies, remote signals or barrier semaphores. Data moves between devices by JAX's collectives and lax.ppermute only.
A program may use at most 128 MiB of HBM per device.

v0:
```python
import math

import jax
import jax.numpy as jnp
from jax import lax
from jax.sharding import PartitionSpec as P

PATCH = 8
HEAD_DIM = 128
LOCAL_HEADS = 8
LOCAL_HEAD_DIM = 128


def from_behind(value, axis, steps):
    count = lax.axis_size(axis)
    initial, last = (max(0, -steps), min(count, count - steps))
    return lax.ppermute(value, axis, [(source, source + steps) for source in range(initial, last)])


def rms_norm(values):
    return values * lax.rsqrt(jnp.mean(values * values, axis=-1, keepdims=True) + 1e-06)


def local_core(qkv_rows):
    total = qkv_rows.shape[0]
    groups = total // PATCH
    width = qkv_rows.shape[1] // 3
    parts = qkv_rows.reshape(groups, PATCH, 3, LOCAL_HEADS, LOCAL_HEAD_DIM)
    queries = rms_norm(parts[:, :, 0])
    keys_all = rms_norm(parts[:, :, 1])
    values = parts[:, :, 2]
    scores = jnp.einsum("npha,nqha->nhpq", queries, keys_all) / math.sqrt(LOCAL_HEAD_DIM)
    causal = jnp.arange(PATCH)[:, None] >= jnp.arange(PATCH)[None, :]
    weights = jnp.where(causal[None, None], jnp.exp(scores), 0.0)
    numerator = jnp.einsum("nhpq,nqha->npha", weights, values)
    denominator = jnp.sum(weights, axis=-1).transpose(0, 2, 1)[..., None]
    return (numerator / denominator).reshape(total, width)


def local_pass(state, local_qkv, local_out, cotangent):
    layer = 0
    normed = rms_norm(state).astype(jnp.bfloat16)
    qkv_rows = jnp.dot(normed, local_qkv[layer], preferred_element_type=jnp.float32)
    core, core_back = jax.vjp(local_core, qkv_rows)
    attended = core.astype(jnp.bfloat16)
    saved = [(state, normed, core_back, attended)]
    state = state + jnp.dot(attended, local_out[layer], preferred_element_type=jnp.float32)
    hidden = state.astype(jnp.bfloat16)
    grad_state = cotangent.astype(jnp.float32)
    layer = 0
    before, normed, core_back, attended = saved[layer]
    grad_round = grad_state.astype(jnp.bfloat16)
    grads_out = [jnp.dot(attended.T, grad_round, preferred_element_type=jnp.float32)]
    grad_core = jnp.dot(grad_round, local_out[layer].T, preferred_element_type=jnp.float32)
    grad_rows = core_back(grad_core)[0].astype(jnp.bfloat16)
    grads_qkv = [jnp.dot(normed.T, grad_rows, preferred_element_type=jnp.float32)]
    return (hidden, jnp.stack(grads_qkv[::-1]), jnp.stack(grads_out[::-1]))


def per_device(byte_embeds, local_embeds, global_qkv, global_out, local_qkv, local_out, cotangent):
    byte_count = byte_embeds.shape[0]
    patch_count = byte_count // PATCH
    full_width = PATCH * byte_embeds.shape[1]
    patch_in = byte_embeds.reshape(patch_count, full_width).astype(jnp.float32)
    normed = rms_norm(patch_in).astype(jnp.bfloat16)
    projected = jnp.einsum(
        "nd,cdh->nch",
        lax.all_gather(normed, "tp", axis=0, tiled=True),
        global_qkv,
        preferred_element_type=jnp.float32,
    )
    shard_rows = projected.shape[0]
    head_width = global_qkv.shape[2]
    head_count = head_width // HEAD_DIM
    queries = rms_norm(projected[:, 0].reshape(shard_rows, head_count, HEAD_DIM)).astype(
        jnp.bfloat16
    )
    keys_mine = rms_norm(projected[:, 1].reshape(shard_rows, head_count, HEAD_DIM)).astype(
        jnp.bfloat16
    )
    values_mine = projected[:, 2].reshape(shard_rows, head_count, HEAD_DIM).astype(jnp.bfloat16)
    query_pos = lax.axis_index("ctx") * shard_rows + jnp.arange(shard_rows, dtype=jnp.int32)
    key_piece = lax.all_gather(keys_mine, "ctx", axis=0, tiled=True)
    value_piece = lax.all_gather(values_mine, "ctx", axis=0, tiled=True)
    key_count = key_piece.shape[0]
    scores = jnp.einsum(
        "rha,kha->rhk", queries, key_piece, preferred_element_type=jnp.float32
    ) / math.sqrt(HEAD_DIM)
    key_pos = jnp.arange(key_count, dtype=jnp.int32)
    allowed = key_pos[None, None, :] <= query_pos[:, None, None]
    expo = jnp.where(allowed, jnp.exp(scores), 0.0)
    numerator = jnp.einsum(
        "rhk,kha->rha", expo.astype(jnp.bfloat16), value_piece, preferred_element_type=jnp.float32
    )
    denominator = jnp.sum(expo, axis=-1)
    numerator, denominator = (numerator, denominator)
    attended = (
        (numerator / denominator[..., None]).reshape(shard_rows, head_width).astype(jnp.bfloat16)
    )
    patch_out = lax.psum_scatter(
        jnp.dot(attended, global_out, preferred_element_type=jnp.float32).astype(jnp.bfloat16),
        "tp",
        scatter_dimension=0,
        tiled=True,
    )
    earlier_row = from_behind(patch_out[-1:], ("ctx", "tp"), 1)
    patch_out = jnp.concatenate([earlier_row, patch_out[:-1]], axis=0)
    context = patch_out.reshape(byte_count, byte_embeds.shape[1])
    state = local_embeds.astype(jnp.float32) + context.astype(jnp.float32)
    hidden, grad_qkv, grad_out = local_pass(state, local_qkv, local_out, cotangent)
    grad_qkv, grad_out = (
        lax.psum_scatter(
            grad_qkv.astype(jnp.bfloat16), "ctx", scatter_dimension=1, tiled=True
        ).astype(jnp.float32),
        lax.psum_scatter(
            grad_out.astype(jnp.bfloat16), "ctx", scatter_dimension=1, tiled=True
        ).astype(jnp.float32),
    )
    grad_qkv, grad_out = (
        lax.psum_scatter(
            grad_qkv.astype(jnp.bfloat16), "tp", scatter_dimension=1, tiled=True
        ).astype(jnp.float32),
        lax.psum_scatter(
            grad_out.astype(jnp.bfloat16), "tp", scatter_dimension=1, tiled=True
        ).astype(jnp.float32),
    )
    return (hidden, grad_qkv, grad_out)


def solution(mesh):
    in_specs = (
        P(("ctx", "tp"), None),
        P(("ctx", "tp"), None),
        P(None, None, "tp"),
        P("tp", None),
        P(),
        P(),
        P(("ctx", "tp"), None),
    )
    out_specs = (P(("ctx", "tp"), None), P(None, ("ctx", "tp"), None), P(None, ("ctx", "tp"), None))
    return jax.shard_map(
        per_device, mesh=mesh, in_specs=in_specs, out_specs=out_specs, check_vma=False
    )
```

profile of v0, /device:TPU:0, one launch (start us, length us, event | category | flops | bytes accessed | tf_op | source)
XLA Modules:
  0.0 423.3 jit_solution(15383733583211355774)
XLA Ops:
  7.2 1.3 reshape.141
  8.5 1.2 multiply_reduce_fusion.6
  9.9 0.9 multiply_convert_fusion.1
  10.9 0.8 iota_compare_fusion
  11.7 34.3 %all-gather.2.cloned.1.call-done = bf16[192,8192]{1,0:T(8,128)(2,1)} async-done(((bf16[24,8192]{1,0:T(8,128)(2,1)}), bf16[192,8192]{1,0:T(8,128)(2,1)}) %all-gather.2.cloned.1.call-update) | async-done | bytes 3145744 | tf_op jit(solution)/shard_map/all_gather | solution.py:68
  46.0 11.7 %fusion = f32[192,3,512]{2,0,1:T(8,128)S(1)} fusion(bf16[3,8192,512]{2,1,0:T(8,128)(2,1)} %param.9, bf16[192,8192]{1,0:T(8,128)(2,1)} %all-gather.2.cloned.1.call-done), kind=kOutput, calls=%fused_computation.2 | convolution fusion | flops 4831838208 | bytes 29491200 | tf_op jit(solution)/shard_map/nd,cdh->nch/dot_general | solution.py:66
  57.9 0.3 multiply_reduce_fusion.7
  58.2 0.9 multiply_convert_fusion.2
  59.3 0.3 multiply_reduce_fusion.8
  59.6 0.2 fusion.41
  59.8 19.5 %all_gather.11 = bf16[768,4,128]{2,0,1:T(8,128)(2,1)S(1)} all-gather(bf16[192,4,128]{2,0,1:T(8,128)(2,1)S(1)} %fusion.41), channel_id=1, replica_groups=mesh['ctx'=4,'tp'=8] {'ctx'}, dimensions={0}, use_global_device_ids=true | all-gather | bytes 983040 | tf_op jit(solution)/shard_map/all_gather | solution.py:83
  79.5 18.2 %all_gather.10 = bf16[768,4,128]{2,0,1:T(8,128)(2,1)S(1)} all-gather(bf16[192,4,128]{2,0,1:T(8,128)(2,1)S(1)} %copy.39), channel_id=1, replica_groups=mesh['ctx'=4,'tp'=8] {'ctx'}, dimensions={0}, use_global_device_ids=true | all-gather | bytes 983040 | tf_op jit(solution)/shard_map/all_gather | solution.py:84
  97.7 1.8 fusion.4
  99.5 0.6 fusion.24
  100.1 7.0 %convolution_convert_fusion = bf16[192,8192]{1,0:T(8,128)(2,1)} fusion(bf16[512,8192]{1,0:T(8,128)(2,1)} %param.10, bf16[4,24,8,128]{3,2,1,0:T(8,128)(2,1)S(1)} %fusion.24), kind=kOutput, calls=%fused_computation | convolution fusion | flops 1612185600 | bytes 11730944 | tf_op jit(solution)/shard_map/dot_general | solution.py:101
  107.2 0.9 copy-done.14
  108.1 1.8 fusion.35
  109.8 42.1 %reduce-scatter.6.cloned.1.call-done = bf16[24,8192]{1,0:T(8,128)(2,1)} async-done(((bf16[192,8192]{1,0:T(8,128)(2,1)}), bf16[24,8192]{1,0:T(8,128)(2,1)}) %reduce-scatter.6.cloned.1.call-update) | async-done | bytes 393232 | tf_op jit(solution)/shard_map/reduce_scatter | solution.py:100
  151.9 0.9 slice.36
  152.9 1.9 collective-permute-start
  154.8 8.7 %copy.57 = bf16[3072,1024]{1,0:T(8,128)(2,1)} copy(bf16[3072,1024]{0,1:T(8,128)(2,1)} %bitcast.151) | data formatting | bytes 12582912 | tf_op jit(solution)/shard_map/dot_general | solution.py:43
  163.6 1.0 maximum_convert_fusion
  164.6 1.3 reshape.142
  165.8 0.2 multiply_reduce_fusion.5
  166.2 4.4 %fusion.37 = f32[24,8,3,8,128]{4,1,3,2,0:T(8,128)S(1)} fusion(bf16[3,8,128,1024,1]{3,2,1,0,4:T(8,128)(2,1)} %bitcast.152, bf16[192,1024]{1,0:T(8,128)(2,1)S(1)} %multiply_convert_fusion), kind=kOutput, calls=%fused_computation.61 | convolution fusion | flops 1207959552 | bytes 9043968 | tf_op jit(solution)/shard_map/dot_general | solution.py:43
  170.7 0.5 multiply_reduce_fusion.4
  171.2 0.6 copy-done.6
  171.8 0.6 select_reduce_fusion
  172.5 1.3 multiply_reduce_fusion.2
  173.9 0.9 copy-done.10
  174.8 2.6 convert_bitcast_fusion.1
  177.5 1.1 negate_bitcast_fusion
  178.5 2.1 fusion.11
  180.7 0.6 convolution_bitcast_fusion
  181.3 0.9 multiply_reduce_fusion.1
  182.3 0.4 convolution_bitcast_fusion.2
  182.8 1.0 fusion.27
  183.8 0.2 add_convert_fusion
  184.1 1.2 copy.51
  185.3 3.0 convert_element_type.105
  188.3 5.9 %convert_bitcast_fusion = bf16[1,1024,3072]{2,1,0:T(8,128)(2,1)} fusion(bf16[192,1024]{1,0:T(8,128)(2,1)} %copy-done.16, bf16[192,3072]{1,0:T(8,128)(2,1)} %convert_element_type.105), kind=kOutput, calls=%fused_computation.1 | convolution fusion | flops 1211105280 | bytes 7864320 | tf_op jit(solution)/shard_map/dot_general | solution.py:56
  194.3 28.5 %reduce-scatter.12.cloned.1.call-done = bf16[1,256,1024]{2,1,0:T(8,128)(2,1)} async-done(((bf16[1,1024,1024]{2,1,0:T(8,128)(2,1)}), bf16[1,256,1024]{2,1,0:T(8,128)(2,1)}) %reduce-scatter.12.cloned.1.call-update) | async-done | bytes 524304 | tf_op jit(solution)/shard_map/reduce_scatter | solution.py:115
  222.8 112.3 %reduce-scatter.8.cloned.1.call-done = bf16[1,256,3072]{2,1,0:T(8,128)(2,1)} async-done(((bf16[1,1024,3072]{2,1,0:T(8,128)(2,1)}), bf16[1,256,3072]{2,1,0:T(8,128)(2,1)}) %reduce-scatter.8.cloned.1.call-update) | async-done | bytes 1572880 | tf_op jit(solution)/shard_map/reduce_scatter | solution.py:112
  335.1 2.5 fusion.13
  337.6 35.0 %reduce-scatter.14.cloned.1.call-done = bf16[1,32,1024]{2,1,0:T(8,128)(2,1)} async-done(((bf16[1,256,1024]{2,1,0:T(8,128)(2,1)}), bf16[1,32,1024]{2,1,0:T(8,128)(2,1)}) %reduce-scatter.14.cloned.1.call-update) | async-done | bytes 65552 | tf_op jit(solution)/shard_map/reduce_scatter | solution.py:123
  372.7 1.5 convert_element_type.111
  374.2 40.5 %reduce-scatter.10.cloned.1.call-done = bf16[1,32,3072]{2,1,0:T(8,128)(2,1)} async-done(((bf16[1,256,3072]{2,1,0:T(8,128)(2,1)}), bf16[1,32,3072]{2,1,0:T(8,128)(2,1)}) %reduce-scatter.10.cloned.1.call-update) | async-done | bytes 196624 | tf_op jit(solution)/shard_map/reduce_scatter | solution.py:120
  414.7 1.7 convert_element_type.108
  (72 shorter events, 1.5 us)
Async XLA Ops:
  7.2 100.0 %copy-start = (bf16[1,1024,1024]{2,1,0:T(8,128)(2,1)S(1)}, bf16[1,1024,1024]{2,1,0:T(8,128)(2,1)}, u32[]{:S(2)}) copy-start(bf16[1,1024,1024]{2,1,0:T(8,128)(2,1)} %param.12) | copy-start | bytes 6291460
  7.2 38.8 %all-gather.2.cloned.1.call-start = ((), (), s32[]{:S(2)}) async-start(), calls=%async_computation.5 | async-start | bytes 3538944 | tf_op jit(solution)/shard_map/all_gather | solution.py:68
  10.8 141.1 %reduce-scatter.6.cloned.1.call-start = ((), (), s32[]{:S(2)}) async-start(), calls=%async_computation.6 | async-start | bytes 3538944 | tf_op jit(solution)/shard_map/reduce_scatter | solution.py:100
  79.5 20.1 %copy-start.17 = (pred[192,768]{1,0:T(8,128)(4,1)S(1)}, pred[192,768]{1,0:T(8,128)(4,1)}, u32[]{:S(2)}) copy-start(pred[192,768]{1,0:T(8,128)(4,1)} %iota_compare_fusion) | copy-start | bytes 442372
  107.1 1.0 copy-start.14
  107.1 115.6 %reduce-scatter.12.cloned.1.call-start = ((), (), s32[]{:S(2)}) async-start(), calls=%async_computation.9 | async-start | bytes 2621440 | tf_op jit(solution)/shard_map/reduce_scatter | solution.py:115
  152.9 10.7 %collective-permute-start = (bf16[1,8192]{1,0:T(2,128)(2,1)S(1)}, bf16[1,8192]{1,0:T(2,128)(2,1)S(1)}, u32[]{:S(2)}, u32[]{:S(2)}) collective-permute-start(bf16[1,8192]{1,0:T(2,128)(2,1)S(1)} %slice.36), channel_id=1, source_target_pairs={{0,1},{1,2},{2,3},{3,4},{4,5},{5,6},{6,7},{7,8},{8,9},{9,10},{10,1... | collective-permute-start | bytes 49160 | tf_op jit(solution)/shard_map/ppermute | solution.py:17
  154.8 8.7 %copy-start.13 = (bf16[24,8192]{1,0:T(8,128)(2,1)S(1)}, bf16[24,8192]{1,0:T(8,128)(2,1)}, u32[]{:S(2)}) copy-start(bf16[24,8192]{1,0:T(8,128)(2,1)} %reduce-scatter.6.cloned.1.call-done) | copy-start | bytes 1179652
  163.5 2.3 copy-start.5
  166.2 4.4 %copy-start.16 = (bf16[192,1024]{1,0:T(8,128)(2,1)}, bf16[192,1024]{1,0:T(8,128)(2,1)S(1)}, u32[]{:S(2)}) copy-start(bf16[192,1024]{1,0:T(8,128)(2,1)S(1)} %multiply_convert_fusion) | copy-start | bytes 1179652
  170.6 1.9 copy-start.1
  170.6 1.9 copy-start.3
  171.1 0.6 copy-start.6
  171.1 0.7 copy-start.8
  172.5 1.4 copy-start.11
  172.5 1.4 copy-start.18
  172.5 2.3 copy-start.15
  173.9 0.9 copy-start.10
  177.4 157.7 %reduce-scatter.8.cloned.1.call-start = ((), (), s32[]{:S(2)}) async-start(), calls=%async_computation.7 | async-start | bytes 7864320 | tf_op jit(solution)/shard_map/reduce_scatter | solution.py:112
  177.5 3.2 copy-start.2
  180.6 1.6 copy-start.7
  180.7 1.6 copy-start.9
  180.7 1.6 copy-start.4
  180.7 1.6 copy-start.12
  180.7 1.6 copy-start.19
  194.2 140.9 %copy-start.20 = (f32[24,8,8]{2,1,0:T(8,128)S(1)}, f32[24,8,8]{2,1,0:T(8,128)}, u32[]{:S(2)}) copy-start(f32[24,8,8]{2,1,0:T(8,128)} %copy-done.18) | copy-start | bytes 18436
  194.2 178.5 %reduce-scatter.14.cloned.1.call-start = ((), (), s32[]{:S(2)}) async-start(), calls=%async_computation.10 | async-start | bytes 589824 | tf_op jit(solution)/shard_map/reduce_scatter | solution.py:123
  222.8 192.0 %reduce-scatter.10.cloned.1.call-start = ((), (), s32[]{:S(2)}) async-start(), calls=%async_computation.8 | async-start | bytes 1769472 | tf_op jit(solution)/shard_map/reduce_scatter | solution.py:120
Sparse Core Ops, SparseCore 0:
  10.9 35.0 all-gather.1
  107.2 44.6 reduce-scatter.5
  177.5 45.1 reduce-scatter.11
  224.9 110.1 reduce-scatter.7
  338.0 34.6 reduce-scatter.13
  376.2 38.4 reduce-scatter.9
where the time goes:
time: 424 us; the launch traced here: 423 us
  waiting for transfers between devices  293 us (69%)
  matrix products  44.3 us (10%)
  blocking collectives  37.7 us (9%)
  local copies, waits for them, and re-layouts  19.6 us (5%)
  between operations  14.6 us (3%)
  other arithmetic  12.1 us (3%)
    reduce_scatter x1, waiting for transfers between devices, per_device(): lax.psum_scatter(grad_qkv.astype(jnp.bfloat16), 'ctx', scatter_dimension=...  112 us
    reduce_scatter x1, waiting for transfers between devices, per_device(): lax.psum_scatter(jnp.dot(attended, global_out, preferred_element_type=jnp...  42.1 us
    reduce_scatter x1, waiting for transfers between devices, per_device(): lax.psum_scatter(grad_qkv.astype(jnp.bfloat16), 'tp', scatter_dimension=1...  40.5 us
    reduce_scatter x1, waiting for transfers between devices, per_device(): lax.psum_scatter(grad_out.astype(jnp.bfloat16), 'tp', scatter_dimension=1...  35 us
    all_gather x1, waiting for transfers between devices, per_device(): lax.all_gather(normed, 'tp', axis=0, tiled=True)  34.3 us
    reduce_scatter x1, waiting for transfers between devices, per_device(): lax.psum_scatter(grad_out.astype(jnp.bfloat16), 'ctx', scatter_dimension=...  28.5 us
    all_gather x1, blocking collectives, per_device(): key_piece = lax.all_gather(keys_mine, 'ctx', axis=0, tiled=True)  19.5 us
    all_gather x1, blocking collectives, per_device(): value_piece = lax.all_gather(values_mine, 'ctx', axis=0, tiled=True)  18.2 us
  transfers between devices with their start and end apart: 7, of which 6 were waited for; matrix products, arithmetic and copies ran while one was open for 8% of the time, Pallas kernels for 0%

commit v1 on v0

v1 whole, which is shorter than its diff:
```python
import functools
import math

import jax
import jax.numpy as jnp
from jax import lax
from jax.experimental import pallas as pl
from jax.experimental.pallas import tpu as pltpu
from jax.sharding import PartitionSpec as P

PATCH = 8
HEAD_DIM = 128
LOCAL_HEADS = 8
LOCAL_HEAD_DIM = 128
EPS = 1e-06
F32 = jnp.float32
BF16 = jnp.bfloat16
MIB = 1 << 20
LANES = 128


def params(mib):
    return pltpu.CompilerParams(vmem_limit_bytes=mib * MIB)


def call(body, outs, scratch=(), mib=32):
    return pl.pallas_call(
        body,
        out_shape=[jax.ShapeDtypeStruct(shape, dtype) for shape, dtype in outs],
        scratch_shapes=list(scratch),
        compiler_params=params(mib),
    )


def dot(a, b, dims=((1,), (0,))):
    return lax.dot_general(a, b, (dims, ((), ())), preferred_element_type=F32)


def swap(value, bits):
    count = lax.axis_size("tp")
    return lax.ppermute(value, "tp", [(source, source ^ bits) for source in range(count)])


def block_order(size):
    return list(range(0, size, 2)) + list(range(1, size, 2))


def gather(value, size):
    even = [value] + [swap(value, bits) for bits in range(2, size, 2)]
    return even + [swap(piece, 1) for piece in even]


def patch_norm_body(x_ref, low_ref, high_ref, wide):
    patches = low_ref.shape[0]
    width = x_ref.shape[1]
    total = jnp.zeros((patches, LANES), F32)
    for c in range(width // LANES):
        wide[c] = x_ref[:, c * LANES : (c + 1) * LANES].astype(F32)
    for c in range(width // LANES):
        for b in range(PATCH):
            part = wide[c, pl.ds(b, patches, stride=PATCH), :]
            total += part * part
    scale = lax.rsqrt(jnp.sum(total, axis=-1, keepdims=True) / (PATCH * width) + EPS)
    half = PATCH // 2
    for b in range(PATCH):
        out_ref = low_ref if b < half else high_ref
        for c in range(width // LANES):
            part = wide[c, pl.ds(b, patches, stride=PATCH), :]
            at = (b % half) * width + c * LANES
            out_ref[:, at : at + LANES] = (part * scale).astype(BF16)


def patch_norm(byte_embeds):
    rows, width = byte_embeds.shape
    half = (rows // PATCH, PATCH * width // 2)
    return call(
        patch_norm_body,
        [(half, BF16), (half, BF16)],
        [pltpu.VMEM((width // LANES, rows, LANES), F32)],
    )(byte_embeds)


def project_low_body(x_ref, w_ref, out_ref, total):
    step = pl.program_id(1)
    depth = w_ref.shape[1]
    x = x_ref[:, pl.ds(pl.multiple_of(step * depth, depth), depth)]

    @pl.when(step == 0)
    def _():
        total[...] = dot(x, w_ref[0])

    @pl.when(step > 0)
    def _():
        total[...] += dot(x, w_ref[0])

    @pl.when(step == pl.num_programs(1) - 1)
    def _():
        out_ref[0] = total[...]


def project_high_body(x_ref, low_ref, w_ref, out_ref, total):
    which, step = pl.program_id(0), pl.program_id(1)
    depth = w_ref.shape[1]
    x = x_ref[:, pl.ds(pl.multiple_of(step * depth, depth), depth)]

    @pl.when(step == 0)
    def _():
        total[...] = low_ref[0] + dot(x, w_ref[0])

    @pl.when(step > 0)
    def _():
        total[...] += dot(x, w_ref[0])

    last = step == pl.num_programs(1) - 1

    @pl.when(last & (which < 2))
    def _():
        for h in range(total.shape[1] // HEAD_DIM):
            part = total[:, h * HEAD_DIM : (h + 1) * HEAD_DIM]
            mean = jnp.mean(part * part, axis=-1, keepdims=True)
            out_ref[0, :, h * HEAD_DIM : (h + 1) * HEAD_DIM] = (part * lax.rsqrt(mean + EPS)).astype(
                BF16
            )

    @pl.when(last & (which == 2))
    def _():
        out_ref[0] = total[...].astype(BF16)


def project(x, weights, low=None):
    rows, half = x.shape
    kinds, _, width = weights.shape
    depth = min(half, 1024)
    steps = half // depth
    offset = 0 if low is None else steps
    x_spec = pl.BlockSpec((rows, half), lambda c, k: (0, 0))
    w_spec = pl.BlockSpec((1, depth, width), lambda c, k: (c, k + offset, 0))
    out_spec = pl.BlockSpec((1, rows, width), lambda c, k: (c, 0, 0))
    first = low is None
    return pl.pallas_call(
        project_low_body if first else project_high_body,
        grid=(kinds, steps),
        in_specs=[x_spec, w_spec] if first else [x_spec, out_spec, w_spec],
        out_specs=out_spec,
        out_shape=jax.ShapeDtypeStruct((kinds, rows, width), F32 if first else BF16),
        scratch_shapes=[pltpu.VMEM((rows, width), F32)],
        compiler_params=params(24),
        cost_estimate=pl.CostEstimate(
            flops=2 * rows * half * kinds * width,
            bytes_accessed=2 * half * kinds * width,
            transcendentals=0,
        ),
    )(*((x, weights) if first else (x, low, weights)))


def attend_body(mask_ref, qkv_ref, k_ref, v_ref, out_ref):
    rows = qkv_ref.shape[1]
    keys = k_ref.shape[0]
    allowed = mask_ref[...] > 0
    for h in range(qkv_ref.shape[2] // HEAD_DIM):
        at = slice(h * HEAD_DIM, (h + 1) * HEAD_DIM)
        scores = dot(qkv_ref[0, :, at], k_ref[:, at], ((1,), (1,))) * (1.0 / math.sqrt(HEAD_DIM))
        expo = jnp.where(allowed, jnp.exp(scores), 0.0)
        top = dot(expo.astype(BF16), v_ref[:, at])
        out_ref[:, at] = (top / jnp.sum(expo, axis=-1, keepdims=True)).astype(BF16)


def attend(qkv, keys, values, mask):
    return call(attend_body, [(qkv.shape[1:], BF16)])(mask, qkv, keys, values)[0]


def output_body(a_ref, w_ref, even_ref, odd_ref):
    half = even_ref.shape[0]
    out = dot(a_ref[...], w_ref[...])
    even_ref[...] = out[:half].astype(BF16)
    odd_ref[...] = out[half:].astype(BF16)


def output_project(attended, weights):
    rows, depth = attended.shape
    width = weights.shape[1]
    step = min(width, 1024)
    out = jax.ShapeDtypeStruct((rows // 2, width), BF16)
    out_spec = pl.BlockSpec((rows // 2, step), lambda n: (0, n))
    return pl.pallas_call(
        output_body,
        grid=(width // step,),
        in_specs=[
            pl.BlockSpec((rows, depth), lambda n: (0, 0)),
            pl.BlockSpec((depth, step), lambda n: (0, n)),
        ],
        out_specs=[out_spec, out_spec],
        out_shape=[out, out],
        compiler_params=params(24),
    )(attended, weights)


def pair_sum_body(mine_ref, other_ref, own_ref, *send_refs):
    patches = own_ref.shape[0]
    total = mine_ref[...].astype(F32) + other_ref[...].astype(F32)
    own_ref[...] = total[:patches]
    for index, ref in enumerate(send_refs):
        ref[...] = total[(index + 1) * patches : (index + 2) * patches].astype(BF16)


def scatter_sum(even, odd, patches):
    blocks = even.shape[0] // patches
    block = (patches, even.shape[1])
    pieces = call(pair_sum_body, [(block, F32)] + [(block, BF16)] * (blocks - 1))(
        even, swap(odd, 1)
    )
    return [pieces[0]] + [swap(piece, 2 * (index + 1)) for index, piece in enumerate(pieces[1:])]


def block_sum_body(*refs):
    (*terms, out_ref, last_ref) = refs
    total = terms[0][...]
    for term in terms[1:]:
        total += term[...].astype(F32)
    total = total.astype(BF16).astype(F32)
    out_ref[...] = total
    last_ref[...] = total[-1:].astype(BF16)


def state_body(patch_ref, prev_ref, local_ref, state_ref, normed_ref, wide):
    patches = patch_ref.shape[0]
    width = state_ref.shape[1]
    first = lax.broadcasted_iota(jnp.int32, (patches, 1), 0) == 0
    chunks = width // LANES
    for b in range(PATCH):
        at = slice(b * width, (b + 1) * width)
        rolled = pltpu.roll(patch_ref[:, at], 1, 0)
        part = jnp.where(first, prev_ref[:, at].astype(F32), rolled)
        for c in range(chunks):
            wide[c, pl.ds(b, patches, stride=PATCH), :] = part[:, c * LANES : (c + 1) * LANES]
    context = jnp.concatenate([wide[c] for c in range(chunks)], axis=1)
    state = local_ref[...].astype(F32) + context
    state_ref[...] = state
    mean = jnp.mean(state * state, axis=-1, keepdims=True)
    normed_ref[...] = (state * lax.rsqrt(mean + EPS)).astype(BF16)


def unit(x):
    scale = lax.rsqrt(jnp.mean(x * x, axis=-1, keepdims=True) + EPS)
    return x * scale, scale


def unit_back(grad, y, scale):
    return scale * (grad - y * jnp.mean(grad * y, axis=-1, keepdims=True))


def local_body(order, head_ref, *refs):
    count = len(order)
    x_refs = refs[:count]
    (gb_ref, wq_ref, wk_ref, wv_ref, wo_ref, ab_ref, gqkv_ref, gout_ref, gqkv, gout) = refs[count:]
    rows = x_refs[0].shape[0]
    me = head_ref[1]
    row = lax.broadcasted_iota(jnp.int32, (rows, rows), 0)
    column = lax.broadcasted_iota(jnp.int32, (rows, rows), 1)
    allowed = (row // PATCH == column // PATCH) & (column <= row)
    root = 1.0 / math.sqrt(LOCAL_HEAD_DIM)
    weights = jnp.concatenate([wq_ref[0], wk_ref[0], wv_ref[0]], axis=1)
    wo = wo_ref[0]
    d = LOCAL_HEAD_DIM
    ab_ref[...] = jnp.zeros_like(ab_ref)
    for index, bits in enumerate(order):
        peer = me ^ bits
        x = x_refs[index][...]
        gb = gb_ref[pl.ds(pl.multiple_of(peer * rows, rows), rows), :]
        qkv = dot(x, weights)
        grad = dot(gb, wo, ((1,), (1,)))
        q, q_scale = unit(qkv[:, :d])
        k, k_scale = unit(qkv[:, d : 2 * d])
        qb, kb, vb, gradb = q.astype(BF16), k.astype(BF16), qkv[:, 2 * d :].astype(BF16), grad.astype(BF16)
        expo = jnp.where(allowed, jnp.exp(dot(qb, kb, ((1,), (1,))) * root), 0.0)
        weight = expo / jnp.sum(expo, axis=-1, keepdims=True)
        wb = weight.astype(BF16)
        ab = dot(wb, vb).astype(BF16)
        ab_ref[peer] = ab
        grad_v = dot(wb, gradb, ((0,), (0,)))
        grad_w = dot(gradb, vb, ((1,), (1,)))
        mean = jnp.sum(weight * grad_w, axis=-1, keepdims=True)
        grad_s = (weight * (grad_w - mean) * root).astype(BF16)
        grad_q = unit_back(dot(grad_s, kb), q, q_scale)
        grad_k = unit_back(dot(grad_s, qb, ((0,), (0,))), k, k_scale)
        gq = jnp.concatenate([grad_q, grad_k, grad_v], axis=1).astype(BF16)
        term_qkv = dot(x, gq, ((0,), (0,)))
        term_out = dot(ab, gb, ((0,), (0,)))
        if index == 0:
            gqkv[...] = term_qkv
            gout[...] = term_out
        else:
            gqkv[...] += term_qkv
            gout[...] += term_out
    gqkv_ref[...] = gqkv[...].astype(BF16)
    gout_ref[...] = jnp.zeros_like(gout_ref)
    share = gout_ref.shape[1]
    pieces = d // share
    base = head_ref[2]
    for piece in range(pieces):
        gout_ref[base + piece] = gout[piece * share : (piece + 1) * share, :].astype(BF16)


def local_layer(blocks, order, gb_all, local_qkv, local_out, head_info, tp_count, share):
    rows, width = blocks[0].shape
    count = len(blocks)
    d = LOCAL_HEAD_DIM
    heads = LOCAL_HEADS

    def whole(shape):
        return pl.BlockSpec(shape, lambda i, info: (0,) * len(shape))

    def qkv_spec(kind):
        return pl.BlockSpec((1, width, d), lambda i, info: (0, 0, kind * heads + info[0]))

    outs = [((tp_count, rows, d), BF16), ((width, 3 * d), BF16), ((tp_count, share, width), BF16)]
    return pl.pallas_call(
        functools.partial(local_body, order),
        grid_spec=pltpu.PrefetchScalarGridSpec(
            num_scalar_prefetch=1,
            grid=(1,),
            in_specs=[whole((rows, width))] * count
            + [whole(gb_all.shape)]
            + [qkv_spec(0), qkv_spec(1), qkv_spec(2)]
            + [pl.BlockSpec((1, d, width), lambda i, info: (0, info[0], 0))],
            out_specs=[whole(shape) for shape, _ in outs],
            scratch_shapes=[pltpu.VMEM((width, 3 * d), F32), pltpu.VMEM((d, width), F32)],
        ),
        out_shape=[jax.ShapeDtypeStruct(shape, dtype) for shape, dtype in outs],
        compiler_params=params(48),
    )(head_info, *blocks, gb_all, local_qkv, local_qkv, local_qkv, local_out)


def hidden_body(state_ref, ab_ref, w_ref, out_ref):
    d = ab_ref.shape[2]
    total = state_ref[...]
    for h in range(ab_ref.shape[0]):
        total += dot(ab_ref[h], w_ref[0, h * d : (h + 1) * d, :])
    out_ref[...] = total.astype(BF16)


def grad_qkv_body(heads, parts_ref, out_ref):
    d = LOCAL_HEAD_DIM
    sources = parts_ref.shape[0]
    for h in range(heads):
        total = parts_ref[h].astype(F32)
        for source in range(h + heads, sources, heads):
            total += parts_ref[source].astype(F32)
        for kind in range(3):
            at = (kind * heads + h) * d
            out_ref[0, :, at : at + d] = total[:, kind * d : (kind + 1) * d]


def plane_sum_body(groups, parts_ref, out_ref):
    for plane, sources in enumerate(groups):
        total = parts_ref[sources[0]].astype(F32)
        for source in sources[1:]:
            total += parts_ref[source].astype(F32)
        out_ref[plane] = total.astype(BF16)


def final_sum_body(parts_ref, out_ref):
    total = parts_ref[0].astype(F32)
    for source in range(1, parts_ref.shape[0]):
        total += parts_ref[source].astype(F32)
    out_ref[0] = total


def per_device(byte_embeds, local_embeds, global_qkv, global_out, local_qkv, local_out, cotangent):
    byte_count, width = byte_embeds.shape
    patches = byte_count // PATCH
    planes, tp_count = lax.axis_size("ctx"), lax.axis_size("tp")
    plane, me = lax.axis_index("ctx"), lax.axis_index("tp")
    order = block_order(tp_count)
    shard_rows = tp_count * patches

    low, high = patch_norm(byte_embeds)
    total = project(jnp.concatenate(gather(low, tp_count), axis=0), global_qkv)
    qkv = project(jnp.concatenate(gather(high, tp_count), axis=0), global_qkv, total)

    place = (
        (me ^ jnp.array(order, jnp.int32))[:, None] * patches
        + jnp.arange(patches, dtype=jnp.int32)[None, :]
    ).reshape(-1)
    keys = lax.all_gather(qkv[1], "ctx", axis=0, tiled=True)
    values = lax.all_gather(qkv[2], "ctx", axis=0, tiled=True)
    key_place = (jnp.arange(planes, dtype=jnp.int32)[:, None] * shard_rows + place[None, :]).reshape(-1)
    mask = (key_place[None, :] <= (plane * shard_rows + place)[:, None]).astype(F32)
    attended = attend(qkv, keys, values, mask)

    even, odd = output_project(attended, global_out)
    terms = scatter_sum(even, odd, patches)
    patch_out, last = call(
        block_sum_body, [(terms[0].shape, F32), ((1, terms[0].shape[1]), BF16)]
    )(*terms)
    devices = planes * tp_count
    prev = lax.ppermute(last, ("ctx", "tp"), [(d, d + 1) for d in range(devices - 1)])
    state, normed = call(
        state_body,
        [((byte_count, width), F32), ((byte_count, width), BF16)],
        [pltpu.VMEM((width // LANES, byte_count, LANES), F32)],
    )(patch_out, prev, local_embeds)

    group = min(tp_count, LOCAL_HEADS)
    share = width // devices
    pieces = LOCAL_HEAD_DIM // share
    plane_heads = LOCAL_HEADS // planes
    head = me % group
    gb_all = lax.all_gather(cotangent, "tp", axis=0, tiled=True)
    head_info = jnp.stack([head, me, (head % plane_heads) * pieces]).astype(jnp.int32)
    ab, grad_qkv, grad_out = local_layer(
        gather(normed, group), block_order(group), gb_all, local_qkv, local_out, head_info, tp_count, share
    )

    grad_qkv = lax.all_to_all(grad_qkv, ("ctx", "tp"), 0, 0, tiled=True)
    ab = lax.all_to_all(ab, "tp", 0, 0, tiled=True)
    grad_out = lax.all_to_all(grad_out, "tp", 0, 0, tiled=True)
    if group < tp_count:
        ab = lax.dynamic_slice_in_dim(ab, (me // group) * group, group, 0)
    hidden = call(hidden_body, [((byte_count, width), BF16)])(state, ab, local_out)[0]
    groups = [
        [t for t in range(tp_count) if (t % group) // plane_heads == c] for c in range(planes)
    ]
    grad_out = call(
        functools.partial(plane_sum_body, groups), [((planes, share, width), BF16)]
    )(grad_out)[0]
    grad_out = lax.all_to_all(grad_out, "ctx", 0, 0, tiled=True)
    grad_out = call(final_sum_body, [((1, share, width), F32)])(grad_out)[0]
    grad_qkv = call(functools.partial(grad_qkv_body, LOCAL_HEADS), [((1, share, 3 * width), F32)])(
        grad_qkv.reshape(devices, share, 3 * LOCAL_HEAD_DIM)
    )[0]
    return (hidden, grad_qkv, grad_out)


def solution(mesh):
    in_specs = (
        P(("ctx", "tp"), None),
        P(("ctx", "tp"), None),
        P(None, None, "tp"),
        P("tp", None),
        P(),
        P(),
        P(("ctx", "tp"), None),
    )
    out_specs = (P(("ctx", "tp"), None), P(None, ("ctx", "tp"), None), P(None, ("ctx", "tp"), None))
    return jax.shard_map(
        per_device, mesh=mesh, in_specs=in_specs, out_specs=out_specs, check_vma=False
    )
```

time: 424 us -> 246 us (0.58)
  waiting for transfers between devices: 293 us -> 75.9 us
  matrix products: 44.3 us -> 0 us
  Pallas kernels: 0 us -> 37.9 us
  starting transfers between devices: 2.18 us -> 29.2 us
  blocking collectives: 37.7 us -> 60.3 us
  other arithmetic: 12.1 us -> 0.35 us
  local copies, waits for them, and re-layouts: 19.6 us -> 26.9 us
    reduce_scatter x5 -> x0, waiting for transfers between devices: 258 us -> none  [the longest x1 112 us: per_device(): lax.psum_scatter(grad_qkv.astype(jnp.bfloat16), 'ctx', scatter_dimension=...]
    ppermute x1 -> x26, waiting for transfers between devices: 0.01 us -> 50.6 us  [the longest x25 49.9 us: swap(): lax.ppermute(value, 'tp', [(source, source ^ bits) for source in range(co...]
    dot_general x15 -> x0, matrix products: 44.3 us -> none  [the longest x1 11.7 us: per_device(): jnp.einsum('nd,cdh->nch', lax.all_gather(normed, 'tp', axis=0, tiled=True...]
    pallas_call x0 -> x13, Pallas kernels: none -> 37.9 us  [the longest x1 17.1 us: local_layer(): pl.pallas_call(functools.partial(local_body, order), grid_spec=pltpu.Pref...]
    all_gather x1, waiting for transfers between devices: 34.3 us -> 0.01 us  [per_device(): gb_all = lax.all_gather(cotangent, 'tp', axis=0, tiled=True)]
    all_to_all x0 -> x2, waiting for transfers between devices: none -> 25.3 us  [the longest x1 17.1 us: per_device(): grad_qkv = lax.all_to_all(grad_qkv, ('ctx', 'tp'), 0, 0, tiled=True)]
    unnamed x42 -> x35, local copies, waits for them, and re-layouts: 2.5 us -> 26.7 us
    all_to_all x0 -> x2, blocking collectives: none -> 22.3 us  [the longest x1 12.1 us: per_device(): grad_out = lax.all_to_all(grad_out, 'tp', 0, 0, tiled=True)]
  transfers between devices with their start and end apart: 7 -> 29, of which waited for: 6 -> 18; matrix products, arithmetic and copies ran while one was open for 8% -> 3% of each run, Pallas kernels for 0% -> 8%
where the time goes in v1:
time: 246 us; the launch traced here: 245 us
  waiting for transfers between devices  75.9 us (31%)
  blocking collectives  60.3 us (25%)
  Pallas kernels  37.9 us (15%)
  starting transfers between devices  29.2 us (12%)
  local copies, waits for them, and re-layouts  26.9 us (11%)
  between operations  14.4 us (6%)
    ppermute x25, waiting for transfers between devices, swap(): lax.ppermute(value, 'tp', [(source, source ^ bits) for source in range(co...  49.9 us
    unnamed x35, local copies, waits for them, and re-layouts  26.7 us
    ppermute x25, starting transfers between devices, swap(): lax.ppermute(value, 'tp', [(source, source ^ bits) for source in range(co...  20.5 us
    all_gather x1, blocking collectives, per_device(): keys = lax.all_gather(qkv[1], 'ctx', axis=0, tiled=True)  19.8 us
    all_gather x1, blocking collectives, per_device(): values = lax.all_gather(qkv[2], 'ctx', axis=0, tiled=True)  18.2 us
    pallas_call x1, Pallas kernels, local_layer(): pl.pallas_call(functools.partial(local_body, order), grid_spec=pltpu.Pref...  17.1 us
    all_to_all x1, waiting for transfers between devices, per_device(): grad_qkv = lax.all_to_all(grad_qkv, ('ctx', 'tp'), 0, 0, tiled=True)  17.1 us
    all_to_all x1, blocking collectives, per_device(): grad_out = lax.all_to_all(grad_out, 'tp', 0, 0, tiled=True)  12.1 us
  transfers between devices with their start and end apart: 29, of which 18 were waited for; matrix products, arithmetic and copies ran while one was open for 3% of the time, Pallas kernels for 8%

profile of v1, /device:TPU:0, one launch (start us, length us, event | category | flops | bytes accessed | tf_op | source)
XLA Modules:
  0.0 245.0 jit_solution(9507568690221832187)
XLA Ops:
  7.2 1.0 copy-done.6
  8.2 1.0 shard_map.103
  9.2 2.9 %collective-permute-start = (bf16[24,4096]{1,0:T(8,128)(2,1)}, bf16[24,4096]{1,0:T(8,128)(2,1)}, u32[]{:S(2)}, u32[]{:S(2)}) collective-permute-start(bf16[24,4096]{1,0:T(8,128)(2,1)} %get-tuple-element.18), channel_id=1, source_target_pairs={{0,2},{1,3},{2,0},{3,1},{4,6},{5,7},{6,4},{7,5},{8,10},{9,11},{10,... | collective-permute-start | bytes 589832 | tf_op jit(solution)/shard_map/ppermute | solution.py:41
  12.2 1.5 collective-permute-start.1
  13.7 2.0 collective-permute-start.7
  15.7 1.1 constant_dynamic-update-slice_fusion.7
  17.2 1.0 collective-permute-done
  18.2 2.1 collective-permute-start.8
  20.3 0.9 constant_dynamic-update-slice_fusion.6
  21.3 2.2 collective-permute-done.1
  24.0 1.0 constant_dynamic-update-slice_fusion.5
  25.1 0.9 constant_dynamic-update-slice_fusion.4
  26.6 0.9 constant_dynamic-update-slice_fusion.3
  28.2 0.9 constant_dynamic-update-slice_fusion.14
  29.1 3.9 %collective-permute-done.8 = bf16[24,4096]{1,0:T(8,128)(2,1)S(1)} collective-permute-done((bf16[24,4096]{1,0:T(8,128)(2,1)}, bf16[24,4096]{1,0:T(8,128)(2,1)S(1)}, u32[]{:S(2)}, u32[]{:S(2)}) %collective-permute-start.8) | collective-permute-done | bytes 196640 | tf_op jit(solution)/shard_map/ppermute | solution.py:41
  33.0 2.4 collective-permute-done.9
  36.2 0.9 collective-permute-done.11
  37.6 8.7 %copy-done = bf16[3,8192,512]{2,1,0:T(8,128)(2,1)S(1)} copy-done((bf16[3,8192,512]{2,1,0:T(8,128)(2,1)S(1)}, bf16[3,8192,512]{2,1,0:T(8,128)(2,1)}, u32[]{:S(2)}) %copy-start) | copy-done | bytes 25165848
  46.3 5.0 %shard_map.104.low_ref = f32[3,192,512]{2,1,0:T(8,128)S(1)} custom-call(bf16[192,4096]{1,0:T(8,128)(2,1)S(1)} %constant_dynamic-update-slice_fusion.8.x_ref, bf16[3,8192,512]{2,1,0:T(8,128)(2,1)S(1)} %copy-done), custom_call_target="tpu_custom_call" | custom-call | flops 2415919104 | bytes 12582912 | tf_op jit(solution)/shard_map/pallas_call | solution.py:140
  51.4 8.2 %copy-done.1 = bf16[3,8192,512]{2,1,0:T(8,128)(2,1)S(1)} copy-done((bf16[3,8192,512]{2,1,0:T(8,128)(2,1)S(1)}, bf16[3,8192,512]{2,1,0:T(8,128)(2,1)}, u32[]{:S(2)}) %copy-start.1) | copy-done | bytes 25165848
  59.6 5.4 %shard_map.105.qkv_ref = bf16[3,192,512]{2,1,0:T(8,128)(2,1)S(1)} custom-call(bf16[192,4096]{1,0:T(8,128)(2,1)S(1)} %constant_dynamic-update-slice_fusion.x_ref, f32[3,192,512]{2,1,0:T(8,128)S(1)} %shard_map.104.low_ref, bf16[3,8192,512]{2,1,0:T(8,128)(2,1)S(1)} %copy-done.1), custom_call_target="tpu_custom_call" | custom-call | flops 2415919104 | bytes 12582912 | tf_op jit(solution)/shard_map/pallas_call | solution.py:140
  65.1 19.8 %all-gather = bf16[1,768,512]{2,1,0:T(8,128)(2,1)S(1)} all-gather(bf16[1,192,512]{2,1,0:T(8,128)(2,1)S(1)} %get-tuple-element.34), channel_id=2, replica_groups=mesh['ctx'=4,'tp'=8] {'ctx'}, dimensions={1}, use_global_device_ids=true | all-gather | bytes 983040 | tf_op jit(solution)/shard_map/all_gather | solution.py:385
  84.9 18.2 %all-gather.1 = bf16[1,768,512]{2,1,0:T(8,128)(2,1)S(1)} all-gather(bf16[1,192,512]{2,1,0:T(8,128)(2,1)S(1)} %get-tuple-element.33), channel_id=3, replica_groups=mesh['ctx'=4,'tp'=8] {'ctx'}, dimensions={1}, use_global_device_ids=true | all-gather | bytes 983040 | tf_op jit(solution)/shard_map/all_gather | solution.py:386
  103.1 1.1 shard_map.106.a_ref
  104.3 3.9 %shard_map.107 = (bf16[96,8192]{1,0:T(8,128)(2,1)S(1)}, bf16[96,8192]{1,0:T(8,128)(2,1)S(1)}) custom-call(bf16[192,512]{1,0:T(8,128)(2,1)S(1)} %shard_map.106.a_ref, bf16[512,8192]{1,0:T(8,128)(2,1)S(1)} %bitcast.7), custom_call_target="tpu_custom_call" | custom-call | tf_op jit(solution)/shard_map/pallas_call | solution.py:185
  108.2 3.4 %collective-permute-done.14.other_ref = bf16[96,8192]{1,0:T(8,128)(2,1)S(1)} collective-permute-done((bf16[96,8192]{1,0:T(8,128)(2,1)S(1)}, bf16[96,8192]{1,0:T(8,128)(2,1)S(1)}, u32[]{:S(2)}, u32[]{:S(2)}) %collective-permute-start.14) | collective-permute-done | bytes 1572896 | tf_op jit(solution)/shard_map/ppermute | solution.py:41
  112.0 1.5 collective-permute-start.15
  114.0 1.5 collective-permute-start.17
  115.5 8.5 %collective-permute-done.15.refs_1_ = bf16[24,8192]{1,0:T(8,128)(2,1)S(1)} collective-permute-done((bf16[24,8192]{1,0:T(8,128)(2,1)S(1)}, bf16[24,8192]{1,0:T(8,128)(2,1)S(1)}, u32[]{:S(2)}, u32[]{:S(2)}) %collective-permute-start.15) | collective-permute-done | bytes 393248 | tf_op jit(solution)/shard_map/ppermute | solution.py:41
  124.0 8.8 %collective-permute-done.16.refs_2_ = bf16[24,8192]{1,0:T(8,128)(2,1)S(1)} collective-permute-done((bf16[24,8192]{1,0:T(8,128)(2,1)S(1)}, bf16[24,8192]{1,0:T(8,128)(2,1)S(1)}, u32[]{:S(2)}, u32[]{:S(2)}) %collective-permute-start.16) | collective-permute-done | bytes 393248 | tf_op jit(solution)/shard_map/ppermute | solution.py:41
  133.0 1.5 collective-permute-start.18
  135.6 0.9 copy-done.3
  136.5 3.7 %collective-permute-start.19 = (bf16[192,1024]{1,0:T(8,128)(2,1)S(1)}, bf16[192,1024]{1,0:T(8,128)(2,1)S(1)}, u32[]{:S(2)}, u32[]{:S(2)}) collective-permute-start(bf16[192,1024]{1,0:T(8,128)(2,1)S(1)} %get-tuple-element.29.refs_0_), channel_id=1, source_target_pairs={{0,2},{1,3},{2,0},{3,1},{4,6},{5,7},{6,4},{7,5},{8,10},{9,11},{10,... | collective-permute-start | bytes 1179656 | tf_op jit(solution)/shard_map/ppermute | solution.py:41
  140.2 1.1 collective-permute-start.20
  141.4 1.2 collective-permute-start.21
  142.6 7.6 %collective-permute-done.19.refs_1_ = bf16[192,1024]{1,0:T(8,128)(2,1)S(1)} collective-permute-done((bf16[192,1024]{1,0:T(8,128)(2,1)S(1)}, bf16[192,1024]{1,0:T(8,128)(2,1)S(1)}, u32[]{:S(2)}, u32[]{:S(2)}) %collective-permute-start.19) | collective-permute-done | bytes 393248 | tf_op jit(solution)/shard_map/ppermute | solution.py:41
  150.2 8.4 %collective-permute-done.20.refs_2_ = bf16[192,1024]{1,0:T(8,128)(2,1)S(1)} collective-permute-done((bf16[192,1024]{1,0:T(8,128)(2,1)S(1)}, bf16[192,1024]{1,0:T(8,128)(2,1)S(1)}, u32[]{:S(2)}, u32[]{:S(2)}) %collective-permute-start.20) | collective-permute-done | bytes 393248 | tf_op jit(solution)/shard_map/ppermute | solution.py:41
  159.2 1.1 collective-permute-done.24.refs_6_
  160.9 17.1 %shard_map.111 = (bf16[8,192,128]{2,1,0:T(8,128)(2,1)}, bf16[1024,384]{1,0:T(8,128)(2,1)S(1)}, bf16[8,32,1024]{2,1,0:T(8,128)(2,1)S(1)}) custom-call(s32[3]{0:T(128)S(1)} %pad_add_fusion.head_ref, bf16[192,1024]{1,0:T(8,128)(2,1)S(1)} %get-tuple-element.29.refs_0_, bf16[192,1024]{1,0:T(8,128)(2,1)S(1)} %collective-permute-done.19.refs_1_, ...), custom_call_target="tpu_custom_call" | custom-call | tf_op jit(solution)/shard_map/pallas_call | solution.py:317
  178.0 0.9 copy-done.5
  178.9 12.1 %all_to_all.24.parts_ref = bf16[8,32,1024]{2,1,0:T(8,128)(2,1)S(1)} all-to-all(bf16[8,32,1024]{2,1,0:T(8,128)(2,1)S(1)} %get-tuple-element.32), channel_id=1, replica_groups=mesh['ctx'=4,'tp'=8] {'tp'}, dimensions={0} | all-to-all | bytes 1048576 | tf_op jit(solution)/shard_map/all_to_all | solution.py:417
  191.0 3.5 %all-to-all-start = ((bf16[8,192,128]{2,1,0:T(8,128)(2,1)}), bf16[8,192,128]{2,1,0:T(8,128)(2,1)S(1)}, u32[]{:S(2)}, u32[]{:S(2)}) async-start(bf16[8,192,128]{2,1,0:T(8,128)(2,1)} %get-tuple-element.30), calls=%async_computation | async-start | bytes 786432 | tf_op jit(solution)/shard_map/all_to_all | solution.py:416
  194.6 8.2 %all-to-all-done.ab_ref = bf16[8,192,128]{2,1,0:T(8,128)(2,1)S(1)} async-done(((bf16[8,192,128]{2,1,0:T(8,128)(2,1)}), bf16[8,192,128]{2,1,0:T(8,128)(2,1)S(1)}, u32[]{:S(2)}, u32[]{:S(2)}) %all-to-all-start) | async-done | bytes 393248 | tf_op jit(solution)/shard_map/all_to_all | solution.py:416
  202.8 10.1 %all_to_all.25.parts_ref = bf16[4,32,1024]{2,1,0:T(8,128)(2,1)S(1)} all-to-all(bf16[4,32,1024]{2,1,0:T(8,128)(2,1)S(1)} %shard_map.114), channel_id=1, replica_groups=mesh['ctx'=4,'tp'=8] {'ctx'}, dimensions={0} | all-to-all | bytes 524288 | tf_op jit(solution)/shard_map/all_to_all | solution.py:427
  212.9 3.8 %all-to-all-start.1 = ((bf16[32,32,384]{2,1,0:T(8,128)(2,1)}), bf16[32,32,384]{2,1,0:T(8,128)(2,1)S(1)}, u32[]{:S(2)}, u32[]{:S(2)}) async-start(bf16[32,32,384]{2,1,0:T(8,128)(2,1)} %bitcast.10), calls=%async_computation.1 | async-start | bytes 1572864 | tf_op jit(solution)/shard_map/all_to_all | solution.py:415
  216.7 1.1 copy-done.4
  217.8 1.7 shard_map.112
  220.2 17.1 %all-to-all-done.1.parts_ref = bf16[32,32,384]{2,1,0:T(8,128)(2,1)S(1)} async-done(((bf16[32,32,384]{2,1,0:T(8,128)(2,1)}), bf16[32,32,384]{2,1,0:T(8,128)(2,1)S(1)}, u32[]{:S(2)}, u32[]{:S(2)}) %all-to-all-start.1) | async-done | bytes 786464 | tf_op jit(solution)/shard_map/all_to_all | solution.py:415
  (76 shorter events, 8.7 us)
Async XLA Ops:
  7.2 9.6 %copy-start.8 = (s32[8]{0:T(128)S(1)}, s32[8]{0:T(128)}, u32[]{:S(2)}) copy-start(s32[8]{0:T(128)} %constant.40.clone) | copy-start | bytes 100
  7.2 153.7 %all-gather.4.cloned.1.call-start = ((), (), s32[]{:S(2)}) async-start(), calls=%async_computation.4 | async-start | bytes 3538944 | tf_op jit(solution)/shard_map/all_gather | solution.py:409
  7.2 1.0 copy-start.6
  9.2 9.0 %collective-permute-start = (bf16[24,4096]{1,0:T(8,128)(2,1)}, bf16[24,4096]{1,0:T(8,128)(2,1)}, u32[]{:S(2)}, u32[]{:S(2)}) collective-permute-start(bf16[24,4096]{1,0:T(8,128)(2,1)} %get-tuple-element.18), channel_id=1, source_target_pairs={{0,2},{1,3},{2,0},{3,1},{4,6},{5,7},{6,4},{7,5},{8,10},{9,11},{10,... | collective-permute-start | bytes 589832 | tf_op jit(solution)/shard_map/ppermute | solution.py:41
  12.2 11.3 %collective-permute-start.1 = (bf16[24,4096]{1,0:T(8,128)(2,1)}, bf16[24,4096]{1,0:T(8,128)(2,1)}, u32[]{:S(2)}, u32[]{:S(2)}) collective-permute-start(bf16[24,4096]{1,0:T(8,128)(2,1)} %get-tuple-element.18), channel_id=1, source_target_pairs={{0,4},{1,5},{2,6},{3,7},{4,0},{5,1},{6,2},{7,3},{8,12},{9,13},{10,... | collective-permute-start | bytes 589832 | tf_op jit(solution)/shard_map/ppermute | solution.py:41
  13.7 11.3 %collective-permute-start.2 = (bf16[24,4096]{1,0:T(8,128)(2,1)}, bf16[24,4096]{1,0:T(8,128)(2,1)}, u32[]{:S(2)}, u32[]{:S(2)}) collective-permute-start(bf16[24,4096]{1,0:T(8,128)(2,1)} %get-tuple-element.18), channel_id=1, source_target_pairs={{0,6},{1,7},{2,4},{3,5},{4,2},{5,3},{6,0},{7,1},{8,14},{9,15},{10,... | collective-permute-start | bytes 589832 | tf_op jit(solution)/shard_map/ppermute | solution.py:41
  13.7 12.3 %collective-permute-start.3 = (bf16[24,4096]{1,0:T(8,128)(2,1)}, bf16[24,4096]{1,0:T(8,128)(2,1)}, u32[]{:S(2)}, u32[]{:S(2)}) collective-permute-start(bf16[24,4096]{1,0:T(8,128)(2,1)} %get-tuple-element.18), channel_id=1, source_target_pairs={{0,1},{1,0},{2,3},{3,2},{4,5},{5,4},{6,7},{7,6},{8,9},{9,8},{10,11... | collective-permute-start | bytes 589832 | tf_op jit(solution)/shard_map/ppermute | solution.py:41
  13.7 14.5 %collective-permute-start.7 = (bf16[24,4096]{1,0:T(8,128)(2,1)}, bf16[24,4096]{1,0:T(8,128)(2,1)}, u32[]{:S(2)}, u32[]{:S(2)}) collective-permute-start(bf16[24,4096]{1,0:T(8,128)(2,1)} %get-tuple-element.19), channel_id=1, source_target_pairs={{0,2},{1,3},{2,0},{3,1},{4,6},{5,7},{6,4},{7,5},{8,10},{9,11},{10,... | collective-permute-start | bytes 589832 | tf_op jit(solution)/shard_map/ppermute | solution.py:41
  18.2 14.8 %collective-permute-start.8 = (bf16[24,4096]{1,0:T(8,128)(2,1)}, bf16[24,4096]{1,0:T(8,128)(2,1)S(1)}, u32[]{:S(2)}, u32[]{:S(2)}) collective-permute-start(bf16[24,4096]{1,0:T(8,128)(2,1)} %get-tuple-element.19), channel_id=1, source_target_pairs={{0,4},{1,5},{2,6},{3,7},{4,0},{5,1},{6,2},{7,3},{8,12},{9,13},{10,... | collective-permute-start | bytes 589832 | tf_op jit(solution)/shard_map/ppermute | solution.py:41
  23.5 12.0 %collective-permute-start.9 = (bf16[24,4096]{1,0:T(8,128)(2,1)}, bf16[24,4096]{1,0:T(8,128)(2,1)S(1)}, u32[]{:S(2)}, u32[]{:S(2)}) collective-permute-start(bf16[24,4096]{1,0:T(8,128)(2,1)} %get-tuple-element.19), channel_id=1, source_target_pairs={{0,6},{1,7},{2,4},{3,5},{4,2},{5,3},{6,0},{7,1},{8,14},{9,15},{10,... | collective-permute-start | bytes 589832 | tf_op jit(solution)/shard_map/ppermute | solution.py:41
  25.0 10.5 %collective-permute-start.10 = (bf16[24,4096]{1,0:T(8,128)(2,1)}, bf16[24,4096]{1,0:T(8,128)(2,1)S(1)}, u32[]{:S(2)}, u32[]{:S(2)}) collective-permute-start(bf16[24,4096]{1,0:T(8,128)(2,1)} %get-tuple-element.19), channel_id=1, source_target_pairs={{0,1},{1,0},{2,3},{3,2},{4,5},{5,4},{6,7},{7,6},{8,9},{9,8},{10,11... | collective-permute-start | bytes 589832 | tf_op jit(solution)/shard_map/ppermute | solution.py:41
  26.0 10.1 %collective-permute-start.4 = (bf16[24,4096]{1,0:T(8,128)(2,1)}, bf16[24,4096]{1,0:T(8,128)(2,1)S(1)}, u32[]{:S(2)}, u32[]{:S(2)}) collective-permute-start(bf16[24,4096]{1,0:T(8,128)(2,1)} %collective-permute-done), channel_id=1, source_target_pairs={{0,1},{1,0},{2,3},{3,2},{4,5},{5,4},{6,7},{7,6},{8,9},{9,8},{10,11... | collective-permute-start | bytes 589832 | tf_op jit(solution)/shard_map/ppermute | solution.py:41
  28.2 8.0 %collective-permute-start.5 = (bf16[24,4096]{1,0:T(8,128)(2,1)}, bf16[24,4096]{1,0:T(8,128)(2,1)S(1)}, u32[]{:S(2)}, u32[]{:S(2)}) collective-permute-start(bf16[24,4096]{1,0:T(8,128)(2,1)} %collective-permute-done.1), channel_id=1, source_target_pairs={{0,1},{1,0},{2,3},{3,2},{4,5},{5,4},{6,7},{7,6},{8,9},{9,8},{10,11... | collective-permute-start | bytes 589832 | tf_op jit(solution)/shard_map/ppermute | solution.py:41
  33.0 18.3 %collective-permute-start.6 = (bf16[24,4096]{1,0:T(8,128)(2,1)}, bf16[24,4096]{1,0:T(8,128)(2,1)S(1)}, u32[]{:S(2)}, u32[]{:S(2)}) collective-permute-start(bf16[24,4096]{1,0:T(8,128)(2,1)} %collective-permute-done.2), channel_id=1, source_target_pairs={{0,1},{1,0},{2,3},{3,2},{4,5},{5,4},{6,7},{7,6},{8,9},{9,8},{10,11... | collective-permute-start | bytes 589832 | tf_op jit(solution)/shard_map/ppermute | solution.py:41
  35.4 1.7 collective-permute-start.11
  35.5 1.7 collective-permute-start.12
  36.1 1.5 collective-permute-start.13
  37.6 8.7 %copy-start = (bf16[3,8192,512]{2,1,0:T(8,128)(2,1)S(1)}, bf16[3,8192,512]{2,1,0:T(8,128)(2,1)}, u32[]{:S(2)}) copy-start(bf16[3,8192,512]{2,1,0:T(8,128)(2,1)} %w_ref.5) | copy-start | bytes 75497472
  46.3 58.0 %slice-start = ((s8[8388608]{0:T(1024)(128)(4,1)}), s8[4194304]{0:T(1024)(128)(4,1)S(1)}, s32[]{:S(2)}) async-start(s8[8388608]{0:T(1024)(128)(4,1)} %bitcast.6), calls=%async_computation.5 | async-start | bytes 8388608
  51.4 8.2 %copy-start.1 = (bf16[3,8192,512]{2,1,0:T(8,128)(2,1)S(1)}, bf16[3,8192,512]{2,1,0:T(8,128)(2,1)}, u32[]{:S(2)}) copy-start(bf16[3,8192,512]{2,1,0:T(8,128)(2,1)} %w_ref.5) | copy-start | bytes 75497472
  59.6 44.7 %slice-start.1 = ((s8[8388608]{0:T(1024)(128)(4,1)}), s8[4194304]{0:T(1024)(128)(4,1)S(1)}, s32[]{:S(2)}) async-start(s8[8388608]{0:T(1024)(128)(4,1)} %bitcast.6), calls=%async_computation.6 | async-start | bytes 8388608
  108.2 3.5 %collective-permute-start.14 = (bf16[96,8192]{1,0:T(8,128)(2,1)S(1)}, bf16[96,8192]{1,0:T(8,128)(2,1)S(1)}, u32[]{:S(2)}, u32[]{:S(2)}) collective-permute-start(bf16[96,8192]{1,0:T(8,128)(2,1)S(1)} %get-tuple-element.21), channel_id=1, source_target_pairs={{0,1},{1,0},{2,3},{3,2},{4,5},{5,4},{6,7},{7,6},{8,9},{9,8},{10,11... | collective-permute-start | bytes 4718600 | tf_op jit(solution)/shard_map/ppermute | solution.py:41
  112.0 23.2 %copy-start.7 = (bf16[192,1024]{1,0:T(8,128)(2,1)S(1)}, bf16[192,1024]{1,0:T(8,128)(2,1)}, u32[]{:S(2)}) copy-start(bf16[192,1024]{1,0:T(8,128)(2,1)} %local_ref.1) | copy-start | bytes 1179652
  112.0 12.0 %collective-permute-start.15 = (bf16[24,8192]{1,0:T(8,128)(2,1)S(1)}, bf16[24,8192]{1,0:T(8,128)(2,1)S(1)}, u32[]{:S(2)}, u32[]{:S(2)}) collective-permute-start(bf16[24,8192]{1,0:T(8,128)(2,1)S(1)} %get-tuple-element.23), channel_id=1, source_target_pairs={{0,2},{1,3},{2,0},{3,1},{4,6},{5,7},{6,4},{7,5},{8,10},{9,11},{10,... | collective-permute-start | bytes 1179656 | tf_op jit(solution)/shard_map/ppermute | solution.py:41
  113.5 19.3 %collective-permute-start.16 = (bf16[24,8192]{1,0:T(8,128)(2,1)S(1)}, bf16[24,8192]{1,0:T(8,128)(2,1)S(1)}, u32[]{:S(2)}, u32[]{:S(2)}) collective-permute-start(bf16[24,8192]{1,0:T(8,128)(2,1)S(1)} %get-tuple-element.24), channel_id=1, source_target_pairs={{0,4},{1,5},{2,6},{3,7},{4,0},{5,1},{6,2},{7,3},{8,12},{9,13},{10,... | collective-permute-start | bytes 1179656 | tf_op jit(solution)/shard_map/ppermute | solution.py:41
  114.0 18.7 %collective-permute-start.17 = (bf16[24,8192]{1,0:T(8,128)(2,1)S(1)}, bf16[24,8192]{1,0:T(8,128)(2,1)S(1)}, u32[]{:S(2)}, u32[]{:S(2)}) collective-permute-start(bf16[24,8192]{1,0:T(8,128)(2,1)S(1)} %get-tuple-element.25), channel_id=1, source_target_pairs={{0,6},{1,7},{2,4},{3,5},{4,2},{5,3},{6,0},{7,1},{8,14},{9,15},{10,... | collective-permute-start | bytes 1179656 | tf_op jit(solution)/shard_map/ppermute | solution.py:41
  133.0 2.1 collective-permute-start.18
  135.6 0.9 copy-start.3
  136.5 13.7 %collective-permute-start.19 = (bf16[192,1024]{1,0:T(8,128)(2,1)S(1)}, bf16[192,1024]{1,0:T(8,128)(2,1)S(1)}, u32[]{:S(2)}, u32[]{:S(2)}) collective-permute-start(bf16[192,1024]{1,0:T(8,128)(2,1)S(1)} %get-tuple-element.29.refs_0_), channel_id=1, source_target_pairs={{0,2},{1,3},{2,0},{3,1},{4,6},{5,7},{6,4},{7,5},{8,10},{9,11},{10,... | collective-permute-start | bytes 1179656 | tf_op jit(solution)/shard_map/ppermute | solution.py:41
  140.2 18.4 %collective-permute-start.20 = (bf16[192,1024]{1,0:T(8,128)(2,1)S(1)}, bf16[192,1024]{1,0:T(8,128)(2,1)S(1)}, u32[]{:S(2)}, u32[]{:S(2)}) collective-permute-start(bf16[192,1024]{1,0:T(8,128)(2,1)S(1)} %get-tuple-element.29.refs_0_), channel_id=1, source_target_pairs={{0,4},{1,5},{2,6},{3,7},{4,0},{5,1},{6,2},{7,3},{8,12},{9,13},{10,... | collective-permute-start | bytes 1179656 | tf_op jit(solution)/shard_map/ppermute | solution.py:41
  141.4 17.3 %collective-permute-start.21 = (bf16[192,1024]{1,0:T(8,128)(2,1)S(1)}, bf16[192,1024]{1,0:T(8,128)(2,1)S(1)}, u32[]{:S(2)}, u32[]{:S(2)}) collective-permute-start(bf16[192,1024]{1,0:T(8,128)(2,1)S(1)} %get-tuple-element.29.refs_0_), channel_id=1, source_target_pairs={{0,6},{1,7},{2,4},{3,5},{4,2},{5,3},{6,0},{7,1},{8,14},{9,15},{10,... | collective-permute-start | bytes 1179656 | tf_op jit(solution)/shard_map/ppermute | solution.py:41
  142.5 16.7 %collective-permute-start.22 = (bf16[192,1024]{1,0:T(8,128)(2,1)S(1)}, bf16[192,1024]{1,0:T(8,128)(2,1)S(1)}, u32[]{:S(2)}, u32[]{:S(2)}) collective-permute-start(bf16[192,1024]{1,0:T(8,128)(2,1)S(1)} %get-tuple-element.29.refs_0_), channel_id=1, source_target_pairs={{0,1},{1,0},{2,3},{3,2},{4,5},{5,4},{6,7},{7,6},{8,9},{9,8},{10,11... | collective-permute-start | bytes 1179656 | tf_op jit(solution)/shard_map/ppermute | solution.py:41
  150.2 9.0 %collective-permute-start.23 = (bf16[192,1024]{1,0:T(8,128)(2,1)S(1)}, bf16[192,1024]{1,0:T(8,128)(2,1)S(1)}, u32[]{:S(2)}, u32[]{:S(2)}) collective-permute-start(bf16[192,1024]{1,0:T(8,128)(2,1)S(1)} %collective-permute-done.19.refs_1_), channel_id=1, source_target_pairs={{0,1},{1,0},{2,3},{3,2},{4,5},{5,4},{6,7},{7,6},{8,9},{9,8},{10,11... | collective-permute-start | bytes 1179656 | tf_op jit(solution)/shard_map/ppermute | solution.py:41
  158.6 1.7 collective-permute-start.24
  158.6 2.3 collective-permute-start.25
  178.0 0.9 copy-start.5
  191.0 11.7 %all-to-all-start = ((bf16[8,192,128]{2,1,0:T(8,128)(2,1)}), bf16[8,192,128]{2,1,0:T(8,128)(2,1)S(1)}, u32[]{:S(2)}, u32[]{:S(2)}) async-start(bf16[8,192,128]{2,1,0:T(8,128)(2,1)} %get-tuple-element.30), calls=%async_computation | async-start | bytes 786432 | tf_op jit(solution)/shard_map/all_to_all | solution.py:416
  194.5 22.2 %copy-start.2 = (bf16[1,1024,1024]{2,1,0:T(8,128)(2,1)S(1)}, bf16[1,1024,1024]{2,1,0:T(8,128)(2,1)}, u32[]{:S(2)}) copy-start(bf16[1,1024,1024]{2,1,0:T(8,128)(2,1)} %w_ref.7) | copy-start | bytes 6291460
  212.9 24.4 %all-to-all-start.1 = ((bf16[32,32,384]{2,1,0:T(8,128)(2,1)}), bf16[32,32,384]{2,1,0:T(8,128)(2,1)S(1)}, u32[]{:S(2)}, u32[]{:S(2)}) async-start(bf16[32,32,384]{2,1,0:T(8,128)(2,1)} %bitcast.10), calls=%async_computation.1 | async-start | bytes 1572864 | tf_op jit(solution)/shard_map/all_to_all | solution.py:415
  216.7 1.1 copy-start.4
Sparse Core Ops, SparseCore 0:
  15.8 37.8 all-gather.3

commit v2 on v1

--- a/solution.py
+++ b/solution.py
@@ -98,8 +98,13 @@
         out_ref[0] = total[...]
 
 
-def project_high_body(x_ref, low_ref, w_ref, out_ref, total):
+def project_high_body(x_ref, low_ref, pass_ref, w_ref, out_ref, passed_ref, total):
     which, step = pl.program_id(0), pl.program_id(1)
+
+    @pl.when((which == 0) & (step == 0))
+    def _():
+        passed_ref[...] = pass_ref[...]
+
     depth = w_ref.shape[1]
     x = x_ref[:, pl.ds(pl.multiple_of(step * depth, depth), depth)]
 
@@ -127,7 +132,7 @@
         out_ref[0] = total[...].astype(BF16)
 
 
-def project(x, weights, low=None):
+def project(x, weights, low=None, passed=None):
     rows, half = x.shape
     kinds, _, width = weights.shape
     depth = min(half, 1024)
@@ -136,21 +141,37 @@
     x_spec = pl.BlockSpec((rows, half), lambda c, k: (0, 0))
     w_spec = pl.BlockSpec((1, depth, width), lambda c, k: (c, k + offset, 0))
     out_spec = pl.BlockSpec((1, rows, width), lambda c, k: (c, 0, 0))
-    first = low is None
+    cost = pl.CostEstimate(
+        flops=2 * rows * half * kinds * width,
+        bytes_accessed=2 * half * kinds * width,
+        transcendentals=0,
+    )
+    scratch = [pltpu.VMEM((rows, width), F32)]
+    if low is None:
+        return pl.pallas_call(
+            project_low_body,
+            grid=(kinds, steps),
+            in_specs=[x_spec, w_spec],
+            out_specs=out_spec,
+            out_shape=jax.ShapeDtypeStruct((kinds, rows, width), F32),
+            scratch_shapes=scratch,
+            compiler_params=params(60),
+            cost_estimate=cost,
+        )(x, weights)
+    pass_spec = pl.BlockSpec(passed.shape, lambda c, k: (0, 0))
     return pl.pallas_call(
-        project_low_body if first else project_high_body,
+        project_high_body,
         grid=(kinds, steps),
-        in_specs=[x_spec, w_spec] if first else [x_spec, out_spec, w_spec],
-        out_specs=out_spec,
-        out_shape=jax.ShapeDtypeStruct((kinds, rows, width), F32 if first else BF16),
-        scratch_shapes=[pltpu.VMEM((rows, width), F32)],
-        compiler_params=params(24),
-        cost_estimate=pl.CostEstimate(
-            flops=2 * rows * half * kinds * width,
-            bytes_accessed=2 * half * kinds * width,
-            transcendentals=0,
-        ),
-    )(*((x, weights) if first else (x, low, weights)))
+        in_specs=[x_spec, out_spec, pass_spec, w_spec],
+        out_specs=[out_spec, pass_spec],
+        out_shape=[
+            jax.ShapeDtypeStruct((kinds, rows, width), BF16),
+            jax.ShapeDtypeStruct(passed.shape, passed.dtype),
+        ],
+        scratch_shapes=scratch,
+        compiler_params=params(60),
+        cost_estimate=cost,
+    )(x, low, passed, weights)
 
 
 def attend_body(mask_ref, qkv_ref, k_ref, v_ref, out_ref):
@@ -249,63 +270,120 @@
     return scale * (grad - y * jnp.mean(grad * y, axis=-1, keepdims=True))
 
 
-def local_body(order, head_ref, *refs):
+def core_grad_body(head_ref, gb_ref, wo_ref, out_ref):
+    out_ref[...] = dot(gb_ref[...], wo_ref[0], ((1,), (1,))).astype(BF16)
+
+
+def core_grad(head_info, gb_all, local_out):
+    rows, width = gb_all.shape
+    d = LOCAL_HEAD_DIM
+    return pl.pallas_call(
+        core_grad_body,
+        grid_spec=pltpu.PrefetchScalarGridSpec(
+            num_scalar_prefetch=1,
+            grid=(1,),
+            in_specs=[
+                pl.BlockSpec((rows, width), lambda i, info: (0, 0)),
+                pl.BlockSpec((1, d, width), lambda i, info: (0, info[0], 0)),
+            ],
+            out_specs=pl.BlockSpec((rows, d), lambda i, info: (0, 0)),
+        ),
+        out_shape=jax.ShapeDtypeStruct((rows, d), BF16),
+        compiler_params=params(24),
+    )(head_info, gb_all, local_out)
+
+
+def local_body(orders, step, head_ref, *refs):
+    refs = list(refs)
+
+    def take(count):
+        taken = refs[:count]
+        del refs[:count]
+        return taken
+
+    order = orders[step]
     count = len(order)
-    x_refs = refs[:count]
-    (gb_ref, wq_ref, wk_ref, wv_ref, wo_ref, ab_ref, gqkv_ref, gout_ref, gqkv, gout) = refs[count:]
+    last = step == len(orders) - 1
+    x_refs = take(count)
+    gb_ref, gcore_ref, wq_ref, wk_ref, wv_ref = take(5)
+    carry = take(2) if step else None
+    earlier = take(step) if last else []
     rows = x_refs[0].shape[0]
     me = head_ref[1]
+    d = LOCAL_HEAD_DIM
     row = lax.broadcasted_iota(jnp.int32, (rows, rows), 0)
     column = lax.broadcasted_iota(jnp.int32, (rows, rows), 1)
     allowed = (row // PATCH == column // PATCH) & (column <= row)
-    root = 1.0 / math.sqrt(LOCAL_HEAD_DIM)
+    root = 1.0 / math.sqrt(d)
+
+    def block_of(ref, bits):
+        return ref[pl.ds(pl.multiple_of((me ^ bits) * rows, rows), rows), :]
+
+    x = jnp.concatenate([ref[...] for ref in x_refs], axis=0)
+    gb = jnp.concatenate([block_of(gb_ref, bits) for bits in order], axis=0)
     weights = jnp.concatenate([wq_ref[0], wk_ref[0], wv_ref[0]], axis=1)
-    wo = wo_ref[0]
-    d = LOCAL_HEAD_DIM
-    ab_ref[...] = jnp.zeros_like(ab_ref)
+    qkv = dot(x, weights)
+    abs_, gqs = [], []
     for index, bits in enumerate(order):
-        peer = me ^ bits
-        x = x_refs[index][...]
-        gb = gb_ref[pl.ds(pl.multiple_of(peer * rows, rows), rows), :]
-        qkv = dot(x, weights)
-        grad = dot(gb, wo, ((1,), (1,)))
-        q, q_scale = unit(qkv[:, :d])
-        k, k_scale = unit(qkv[:, d : 2 * d])
-        qb, kb, vb, gradb = q.astype(BF16), k.astype(BF16), qkv[:, 2 * d :].astype(BF16), grad.astype(BF16)
+        at = slice(index * rows, (index + 1) * rows)
+        gradb = block_of(gcore_ref, bits)
+        q, q_scale = unit(qkv[at, :d])
+        k, k_scale = unit(qkv[at, d : 2 * d])
+        qb, kb, vb = q.astype(BF16), k.astype(BF16), qkv[at, 2 * d :].astype(BF16)
         expo = jnp.where(allowed, jnp.exp(dot(qb, kb, ((1,), (1,))) * root), 0.0)
         weight = expo / jnp.sum(expo, axis=-1, keepdims=True)
         wb = weight.astype(BF16)
-        ab = dot(wb, vb).astype(BF16)
-        ab_ref[peer] = ab
+        abs_.append(dot(wb, vb).astype(BF16))
         grad_v = dot(wb, gradb, ((0,), (0,)))
         grad_w = dot(gradb, vb, ((1,), (1,)))
         mean = jnp.sum(weight * grad_w, axis=-1, keepdims=True)
         grad_s = (weight * (grad_w - mean) * root).astype(BF16)
         grad_q = unit_back(dot(grad_s, kb), q, q_scale)
         grad_k = unit_back(dot(grad_s, qb, ((0,), (0,))), k, k_scale)
-        gq = jnp.concatenate([grad_q, grad_k, grad_v], axis=1).astype(BF16)
-        term_qkv = dot(x, gq, ((0,), (0,)))
-        term_out = dot(ab, gb, ((0,), (0,)))
-        if index == 0:
-            gqkv[...] = term_qkv
-            gout[...] = term_out
-        else:
-            gqkv[...] += term_qkv
-            gout[...] += term_out
-    gqkv_ref[...] = gqkv[...].astype(BF16)
-    gout_ref[...] = jnp.zeros_like(gout_ref)
-    share = gout_ref.shape[1]
-    pieces = d // share
-    base = head_ref[2]
-    for piece in range(pieces):
-        gout_ref[base + piece] = gout[piece * share : (piece + 1) * share, :].astype(BF16)
-
-
-def local_layer(blocks, order, gb_all, local_qkv, local_out, head_info, tp_count, share):
+        gqs.append(jnp.concatenate([grad_q, grad_k, grad_v], axis=1).astype(BF16))
+    gqkv = dot(jnp.concatenate(gqs, axis=0), x, ((0,), (0,)))
+    gout = dot(jnp.concatenate(abs_, axis=0), gb, ((0,), (0,)))
+    if carry:
+        gqkv += carry[0][...]
+        gout += carry[1][...]
+    if not last:
+        gqkv_ref, gout_ref, ab_ref = refs
+        gqkv_ref[...] = gqkv
+        gout_ref[...] = gout
+        for index, ab in enumerate(abs_):
+            ab_ref[index] = ab
+        return
+    *plane_refs, send_ref, gqkv_total, gout_total = refs
+    gqkv_total[...] = gqkv
+    gout_total[...] = gout
+    piece = plane_refs[0].shape[1]
+    for k, ref in enumerate(plane_refs):
+        at = pl.multiple_of((head_ref[3] ^ k) * piece, piece)
+        ref[...] = gqkv_total[:, pl.ds(at, piece)].astype(BF16)
+    send_ref[...] = jnp.zeros_like(send_ref)
+    for ref, bits_list in zip(earlier, orders):
+        for index, bits in enumerate(bits_list):
+            send_ref[me ^ bits, :rows, :] = ref[index]
+    for bits, ab in zip(order, abs_):
+        send_ref[me ^ bits, :rows, :] = ab
+    chunks = gout_total.shape[1] // d
+    share = (send_ref.shape[1] - rows) // chunks
+    for part in range(d // share):
+        for c in range(chunks):
+            send_ref[head_ref[2] + part, rows + c * share : rows + (c + 1) * share, :] = gout_total[
+                part * share : (part + 1) * share, c * d : (c + 1) * d
+            ].astype(BF16)
+
+
+def local_layer(blocks, gb_all, gcore, local_qkv, head_info, tp_count, planes):
     rows, width = blocks[0].shape
-    count = len(blocks)
+    group = len(blocks)
+    order = block_order(group)
+    by_bits = dict(zip(order, blocks))
+    orders = [part for part in ([0, 1], [2, 3], list(range(4, group))) if part and part[0] < group]
     d = LOCAL_HEAD_DIM
     heads = LOCAL_HEADS
+    share = width // (planes * tp_count)
 
     def whole(shape):
         return pl.BlockSpec(shape, lambda i, info: (0,) * len(shape))
@@ -313,30 +391,69 @@
     def qkv_spec(kind):
         return pl.BlockSpec((1, width, d), lambda i, info: (0, 0, kind * heads + info[0]))
 
-    outs = [((tp_count, rows, d), BF16), ((width, 3 * d), BF16), ((tp_count, share, width), BF16)]
-    return pl.pallas_call(
-        functools.partial(local_body, order),
-        grid_spec=pltpu.PrefetchScalarGridSpec(
-            num_scalar_prefetch=1,
-            grid=(1,),
-            in_specs=[whole((rows, width))] * count
-            + [whole(gb_all.shape)]
-            + [qkv_spec(0), qkv_spec(1), qkv_spec(2)]
-            + [pl.BlockSpec((1, d, width), lambda i, info: (0, info[0], 0))],
-            out_specs=[whole(shape) for shape, _ in outs],
-            scratch_shapes=[pltpu.VMEM((width, 3 * d), F32), pltpu.VMEM((d, width), F32)],
-        ),
-        out_shape=[jax.ShapeDtypeStruct(shape, dtype) for shape, dtype in outs],
-        compiler_params=params(48),
-    )(head_info, *blocks, gb_all, local_qkv, local_qkv, local_qkv, local_out)
-
-
-def hidden_body(state_ref, ab_ref, w_ref, out_ref):
-    d = ab_ref.shape[2]
-    total = state_ref[...]
-    for h in range(ab_ref.shape[0]):
-        total += dot(ab_ref[h], w_ref[0, h * d : (h + 1) * d, :])
-    out_ref[...] = total.astype(BF16)
+    carry, abs_ = [], []
+    for step, part in enumerate(orders):
+        last = step == len(orders) - 1
+        plain = [by_bits[bits] for bits in part] + [gb_all, gcore]
+        extra = carry + (abs_ if last else [])
+        totals = [((3 * d, width), F32), ((d, width), F32)]
+        if last:
+            outs = [((3 * d, width // planes), BF16)] * planes
+            outs += [((tp_count, rows + share * (width // d), d), BF16)]
+        else:
+            outs = totals + [((len(part), rows, d), BF16)]
+        result = pl.pallas_call(
+            functools.partial(local_body, orders, step),
+            grid_spec=pltpu.PrefetchScalarGridSpec(
+                num_scalar_prefetch=1,
+                grid=(1,),
+                in_specs=[whole(a.shape) for a in plain]
+                + [qkv_spec(0), qkv_spec(1), qkv_spec(2)]
+                + [whole(a.shape) for a in extra],
+                out_specs=[whole(shape) for shape, _ in outs],
+                scratch_shapes=[pltpu.VMEM(s, t) for s, t in totals] if last else [],
+            ),
+            out_shape=[jax.ShapeDtypeStruct(shape, dtype) for shape, dtype in outs],
+            compiler_params=params(48),
+        )(head_info, *plain, local_qkv, local_qkv, local_qkv, *extra)
+        if not last:
+            carry = list(result[:2])
+            abs_.append(result[2])
+    return result[:-1], result[-1]
+
+
+def hidden_body(rows, state_ref, parts_ref, w_ref, out_ref):
+    ab = jnp.concatenate([parts_ref[h, :rows, :] for h in range(parts_ref.shape[0])], axis=1)
+    out_ref[...] = (state_ref[...] + dot(ab, w_ref[0])).astype(BF16)
+
+
+def plane_sum_body(groups, rows, info_ref, parts_ref, *refs):
+    *out_refs, sums = refs
+    for plane, sources in enumerate(groups):
+        total = parts_ref[sources[0], rows:, :].astype(F32)
+        for source in sources[1:]:
+            total += parts_ref[source, rows:, :].astype(F32)
+        sums[plane] = total
+    for k, ref in enumerate(out_refs):
+        ref[...] = sums[info_ref[3] ^ k].astype(BF16)
+
+
+def grad_out_body(*refs):
+    *terms, out_ref = refs
+    total = terms[0][...].astype(F32)
+    for term in terms[1:]:
+        total += term[...].astype(F32)
+    share = out_ref.shape[1]
+    for c in range(out_ref.shape[2] // LANES):
+        out_ref[0, :, c * LANES : (c + 1) * LANES] = total[c * share : (c + 1) * share]
+
+
+def turn_body(*refs):
+    *terms, out_ref = refs
+    total = terms[0][...].astype(F32)
+    for term in terms[1:]:
+        total += term[...].astype(F32)
+    out_ref[...] = total.T.astype(BF16)
 
 
 def grad_qkv_body(heads, parts_ref, out_ref):
@@ -351,19 +468,11 @@
             out_ref[0, :, at : at + d] = total[:, kind * d : (kind + 1) * d]
 
 
-def plane_sum_body(groups, parts_ref, out_ref):
-    for plane, sources in enumerate(groups):
-        total = parts_ref[sources[0]].astype(F32)
-        for source in sources[1:]:
-            total += parts_ref[source].astype(F32)
-        out_ref[plane] = total.astype(BF16)
-
-
-def final_sum_body(parts_ref, out_ref):
-    total = parts_ref[0].astype(F32)
-    for source in range(1, parts_ref.shape[0]):
-        total += parts_ref[source].astype(F32)
-    out_ref[0] = total
+def swap_planes(pieces):
+    count = len(pieces)
+    return [pieces[0]] + [
+        lax.ppermute(pieces[k], "ctx", [(c, c ^ k) for c in range(count)]) for k in range(1, count)
+    ]
 
 
 def per_device(byte_embeds, local_embeds, global_qkv, global_out, local_qkv, local_out, cotangent):
@@ -376,7 +485,9 @@
 
     low, high = patch_norm(byte_embeds)
     total = project(jnp.concatenate(gather(low, tp_count), axis=0), global_qkv)
-    qkv = project(jnp.concatenate(gather(high, tp_count), axis=0), global_qkv, total)
+    qkv, gb = project(
+        jnp.concatenate(gather(high, tp_count), axis=0), global_qkv, total, cotangent
+    )
 
     place = (
         (me ^ jnp.array(order, jnp.int32))[:, None] * patches
@@ -406,28 +517,40 @@
     pieces = LOCAL_HEAD_DIM // share
     plane_heads = LOCAL_HEADS // planes
     head = me % group
-    gb_all = lax.all_gather(cotangent, "tp", axis=0, tiled=True)
-    head_info = jnp.stack([head, me, (head % plane_heads) * pieces]).astype(jnp.int32)
-    ab, grad_qkv, grad_out = local_layer(
-        gather(normed, group), block_order(group), gb_all, local_qkv, local_out, head_info, tp_count, share
-    )
-
-    grad_qkv = lax.all_to_all(grad_qkv, ("ctx", "tp"), 0, 0, tiled=True)
-    ab = lax.all_to_all(ab, "tp", 0, 0, tiled=True)
-    grad_out = lax.all_to_all(grad_out, "tp", 0, 0, tiled=True)
-    if group < tp_count:
-        ab = lax.dynamic_slice_in_dim(ab, (me // group) * group, group, 0)
-    hidden = call(hidden_body, [((byte_count, width), BF16)])(state, ab, local_out)[0]
+    gb_all = lax.all_gather(gb, "tp", axis=0, tiled=True)
+    head_info = jnp.stack([head, me, (head % plane_heads) * pieces, plane]).astype(jnp.int32)
+    gcore = core_grad(head_info, gb_all, local_out)
+    plane_pieces, send = local_layer(
+        gather(normed, group), gb_all, gcore, local_qkv, head_info, tp_count, planes
+    )
+
+    plane_pieces = swap_planes(plane_pieces)
+    parts = lax.all_to_all(send, "tp", 0, 0, tiled=True)
     groups = [
         [t for t in range(tp_count) if (t % group) // plane_heads == c] for c in range(planes)
     ]
-    grad_out = call(
-        functools.partial(plane_sum_body, groups), [((planes, share, width), BF16)]
-    )(grad_out)[0]
-    grad_out = lax.all_to_all(grad_out, "ctx", 0, 0, tiled=True)
-    grad_out = call(final_sum_body, [((1, share, width), F32)])(grad_out)[0]
+    flat = share * width // LANES
+    out_pieces = pl.pallas_call(
+        functools.partial(plane_sum_body, groups, byte_count),
+        in_specs=[pl.BlockSpec(memory_space=pltpu.SMEM), pl.BlockSpec(memory_space=pltpu.VMEM)],
+        out_shape=[jax.ShapeDtypeStruct((flat, LANES), BF16)] * planes,
+        scratch_shapes=[pltpu.VMEM((planes, flat, LANES), F32)],
+        compiler_params=params(32),
+    )(head_info, parts)
+    out_pieces = swap_planes(out_pieces)
+    mine = parts
+    if group < tp_count:
+        mine = lax.dynamic_slice_in_dim(parts, (me // group) * group, group, 0)
+    hidden = call(functools.partial(hidden_body, byte_count), [((byte_count, width), BF16)])(
+        state, mine, local_out
+    )[0]
+    grad_out = call(grad_out_body, [((1, share, width), F32)])(*out_pieces)[0]
+    turned = call(turn_body, [((tp_count * share, 3 * LOCAL_HEAD_DIM), BF16)])(*plane_pieces)[0]
+    grad_qkv = lax.all_to_all(
+        turned.reshape(tp_count, share, 3 * LOCAL_HEAD_DIM), "tp", 0, 0, tiled=True
+    )
     grad_qkv = call(functools.partial(grad_qkv_body, LOCAL_HEADS), [((1, share, 3 * width), F32)])(
-        grad_qkv.reshape(devices, share, 3 * LOCAL_HEAD_DIM)
+        grad_qkv
     )[0]
     return (hidden, grad_qkv, grad_out)
 

time: 246 us -> 232 us (0.943)
  blocking collectives: 60.3 us -> 37.5 us
  Pallas kernels: 37.9 us -> 57.2 us
  local copies, waits for them, and re-layouts: 26.9 us -> 13.8 us
  starting transfers between devices: 29.2 us -> 41.7 us
  waiting for transfers between devices: 75.9 us -> 65.9 us
    all_to_all x2, waiting for transfers between devices: 25.3 us -> 0.01 us  [the longest x1 0.01 us: per_device(): parts = lax.all_to_all(send, 'tp', 0, 0, tiled=True)]
    all_to_all x2 -> x0, blocking collectives: 22.3 us -> none  [the longest x1 12.1 us: per_device(): grad_out = lax.all_to_all(grad_out, 'tp', 0, 0, tiled=True)]
    pallas_call x6 -> x10, Pallas kernels: 30 us -> 49.3 us  [the longest x3 18.3 us: local_layer(): pl.pallas_call(functools.partial(local_body, orders, step), grid_spec=plt...]
    ppermute x0 -> x6, waiting for transfers between devices: none -> 15.6 us  [swap_planes(): lax.ppermute(pieces[k], 'ctx', [(c, c ^ k) for c in range(count)])]
    unnamed x35 -> x41, local copies, waits for them, and re-layouts: 26.7 us -> 12.5 us
    ppermute x0 -> x6, starting transfers between devices: none -> 11.1 us  [swap_planes(): lax.ppermute(pieces[k], 'ctx', [(c, c ^ k) for c in range(count)])]
  transfers between devices with their start and end apart: 29 -> 35, of which waited for: 18 -> 17; matrix products, arithmetic and copies ran while one was open for 3% -> 1% of each run, Pallas kernels for 8% -> 16%
where the time goes in v2:
time: 232 us; the launch traced here: 231 us
  waiting for transfers between devices  65.9 us (28%)
  Pallas kernels  57.2 us (25%)
  starting transfers between devices  41.7 us (18%)
  blocking collectives  37.5 us (16%)
  between operations  14.4 us (6%)
  local copies, waits for them, and re-layouts  13.8 us (6%)
    ppermute x25, waiting for transfers between devices, swap(): lax.ppermute(value, 'tp', [(source, source ^ bits) for source in range(co...  49.7 us
    ppermute x25, starting transfers between devices, swap(): lax.ppermute(value, 'tp', [(source, source ^ bits) for source in range(co...  21.3 us
    all_gather x1, blocking collectives, per_device(): keys = lax.all_gather(qkv[1], 'ctx', axis=0, tiled=True)  19.8 us
    pallas_call x3, Pallas kernels, local_layer(): pl.pallas_call(functools.partial(local_body, orders, step), grid_spec=plt...  18.3 us
    all_gather x1, blocking collectives, per_device(): values = lax.all_gather(qkv[2], 'ctx', axis=0, tiled=True)  17.7 us
    ppermute x6, waiting for transfers between devices, swap_planes(): lax.ppermute(pieces[k], 'ctx', [(c, c ^ k) for c in range(count)])  15.6 us
    pallas_call x1, Pallas kernels, project(): pl.pallas_call(project_high_body, grid=(kinds, steps), in_specs=[x_spec,...  13 us
    unnamed x41, local copies, waits for them, and re-layouts  12.5 us
  transfers between devices with their start and end apart: 35, of which 17 were waited for; matrix products, arithmetic and copies ran while one was open for 1% of the time, Pallas kernels for 16%

profile of v2, /device:TPU:0, one launch (start us, length us, event | category | flops | bytes accessed | tf_op | source)
XLA Modules:
  0.0 230.8 jit_solution(13307239824996583759)
XLA Ops:
  7.2 1.0 copy-done.7
  8.5 3.0 %collective-permute-start.7 = (bf16[24,4096]{1,0:T(8,128)(2,1)S(1)}, bf16[24,4096]{1,0:T(8,128)(2,1)S(1)}, u32[]{:S(2)}, u32[]{:S(2)}) collective-permute-start(bf16[24,4096]{1,0:T(8,128)(2,1)S(1)} %get-tuple-element.33), channel_id=1, source_target_pairs={{0,2},{1,3},{2,0},{3,1},{4,6},{5,7},{6,4},{7,5},{8,10},{9,11},{10,... | collective-permute-start | bytes 589832 | tf_op jit(solution)/shard_map/ppermute | solution.py:41
  11.5 1.5 collective-permute-start.8
  13.1 1.9 collective-permute-start
  15.1 2.2 collective-permute-done.7
  17.3 2.1 collective-permute-start.1
  19.4 3.1 %collective-permute-done.8 = bf16[24,4096]{1,0:T(8,128)(2,1)S(1)} collective-permute-done((bf16[24,4096]{1,0:T(8,128)(2,1)S(1)}, bf16[24,4096]{1,0:T(8,128)(2,1)S(1)}, u32[]{:S(2)}, u32[]{:S(2)}) %collective-permute-start.8) | collective-permute-done | bytes 196640 | tf_op jit(solution)/shard_map/ppermute | solution.py:41
  23.7 2.0 collective-permute-done
  25.8 4.8 %collective-permute-done.1 = bf16[24,4096]{1,0:T(8,128)(2,1)S(1)} collective-permute-done((bf16[24,4096]{1,0:T(8,128)(2,1)S(1)}, bf16[24,4096]{1,0:T(8,128)(2,1)S(1)}, u32[]{:S(2)}, u32[]{:S(2)}) %collective-permute-start.1) | collective-permute-done | bytes 196640 | tf_op jit(solution)/shard_map/ppermute | solution.py:41
  33.2 12.3 %shard_map.104.low_ref = f32[3,192,512]{2,1,0:T(8,128)} custom-call(bf16[192,4096]{1,0:T(8,128)(2,1)} %copy-done.12, bf16[3,8192,512]{2,1,0:T(8,128)(2,1)} %w_ref.5), custom_call_target="tpu_custom_call" | custom-call | flops 2415919104 | bytes 12582912 | tf_op jit(solution)/shard_map/pallas_call | solution.py:151
  45.6 1.2 copy-done.11
  46.8 13.0 %shard_map.105 = (bf16[3,192,512]{2,1,0:T(8,128)(2,1)}, bf16[192,1024]{1,0:T(8,128)(2,1)}) custom-call(bf16[192,4096]{1,0:T(8,128)(2,1)} %copy-done.11, f32[3,192,512]{2,1,0:T(8,128)} %shard_map.104.low_ref, bf16[192,1024]{1,0:T(8,128)(2,1)} %pass_ref.1, bf16[3,8192,512]{2,1,0:T(8,128)(2,1)} %w_ref.5), custom_call_target="tpu_custom_call" | custom-call | flops 2415919104 | bytes 12582912 | tf_op jit(solution)/shard_map/pallas_call | solution.py:162
  60.2 1.1 fusion
  61.3 19.8 %all-gather = bf16[1,768,512]{2,1,0:T(8,128)(2,1)S(1)} all-gather(bf16[1,192,512]{2,1,0:T(8,128)(2,1)S(1)} %get-tuple-element.62), channel_id=2, replica_groups=mesh['ctx'=4,'tp'=8] {'ctx'}, dimensions={1}, use_global_device_ids=true | all-gather | bytes 983040 | tf_op jit(solution)/shard_map/all_gather | solution.py:496
  81.1 17.7 %all-gather.1 = bf16[1,768,512]{2,1,0:T(8,128)(2,1)S(1)} all-gather(bf16[1,192,512]{2,1,0:T(8,128)(2,1)S(1)} %get-tuple-element.61), channel_id=3, replica_groups=mesh['ctx'=4,'tp'=8] {'ctx'}, dimensions={1}, use_global_device_ids=true | all-gather | bytes 983040 | tf_op jit(solution)/shard_map/all_gather | solution.py:497
  98.9 1.1 shard_map.106.a_ref
  100.0 3.4 %copy-done.2 = bf16[512,8192]{1,0:T(8,128)(2,1)S(1)} copy-done((bf16[512,8192]{1,0:T(8,128)(2,1)S(1)}, bf16[512,8192]{1,0:T(8,128)(2,1)}, u32[]{:S(2)}) %copy-start.2) | copy-done | bytes 8388632
  103.4 3.9 %shard_map.107 = (bf16[96,8192]{1,0:T(8,128)(2,1)S(1)}, bf16[96,8192]{1,0:T(8,128)(2,1)S(1)}) custom-call(bf16[192,512]{1,0:T(8,128)(2,1)S(1)} %shard_map.106.a_ref, bf16[512,8192]{1,0:T(8,128)(2,1)S(1)} %copy-done.2), custom_call_target="tpu_custom_call" | custom-call | tf_op jit(solution)/shard_map/pallas_call | solution.py:206
  107.3 3.4 %collective-permute-done.14.other_ref = bf16[96,8192]{1,0:T(8,128)(2,1)S(1)} collective-permute-done((bf16[96,8192]{1,0:T(8,128)(2,1)S(1)}, bf16[96,8192]{1,0:T(8,128)(2,1)S(1)}, u32[]{:S(2)}, u32[]{:S(2)}) %collective-permute-start.14) | collective-permute-done | bytes 1572896 | tf_op jit(solution)/shard_map/ppermute | solution.py:41
  111.1 1.3 collective-permute-start.15
  113.2 1.4 collective-permute-start.17
  114.7 8.5 %collective-permute-done.15.refs_1_ = bf16[24,8192]{1,0:T(8,128)(2,1)S(1)} collective-permute-done((bf16[24,8192]{1,0:T(8,128)(2,1)S(1)}, bf16[24,8192]{1,0:T(8,128)(2,1)S(1)}, u32[]{:S(2)}, u32[]{:S(2)}) %collective-permute-start.15) | collective-permute-done | bytes 393248 | tf_op jit(solution)/shard_map/ppermute | solution.py:41
  123.1 7.0 %collective-permute-done.16.refs_2_ = bf16[24,8192]{1,0:T(8,128)(2,1)S(1)} collective-permute-done((bf16[24,8192]{1,0:T(8,128)(2,1)S(1)}, bf16[24,8192]{1,0:T(8,128)(2,1)S(1)}, u32[]{:S(2)}, u32[]{:S(2)}) %collective-permute-start.16) | collective-permute-done | bytes 393248 | tf_op jit(solution)/shard_map/ppermute | solution.py:41
  130.1 1.6 collective-permute-done.17.refs_3_
  131.9 1.6 collective-permute-start.18
  134.2 1.2 shard_map.110
  136.3 3.9 %collective-permute-start.23 = (bf16[192,1024]{1,0:T(8,128)(2,1)}, bf16[192,1024]{1,0:T(8,128)(2,1)S(1)}, u32[]{:S(2)}, u32[]{:S(2)}) collective-permute-start(bf16[192,1024]{1,0:T(8,128)(2,1)} %get-tuple-element.44.refs_0_), channel_id=1, source_target_pairs={{0,2},{1,3},{2,0},{3,1},{4,6},{5,7},{6,4},{7,5},{8,10},{9,11},{10,... | collective-permute-start | bytes 1179656 | tf_op jit(solution)/shard_map/ppermute | solution.py:41
  140.2 1.5 collective-permute-start.19
  142.6 7.8 %collective-permute-done.23.refs_0_ = bf16[192,1024]{1,0:T(8,128)(2,1)S(1)} collective-permute-done((bf16[192,1024]{1,0:T(8,128)(2,1)}, bf16[192,1024]{1,0:T(8,128)(2,1)S(1)}, u32[]{:S(2)}, u32[]{:S(2)}) %collective-permute-start.23) | collective-permute-done | bytes 393248 | tf_op jit(solution)/shard_map/ppermute | solution.py:41
  150.4 8.5 %collective-permute-done.19.refs_0_ = bf16[192,1024]{1,0:T(8,128)(2,1)S(1)} collective-permute-done((bf16[192,1024]{1,0:T(8,128)(2,1)}, bf16[192,1024]{1,0:T(8,128)(2,1)S(1)}, u32[]{:S(2)}, u32[]{:S(2)}) %collective-permute-start.19) | collective-permute-done | bytes 393248 | tf_op jit(solution)/shard_map/ppermute | solution.py:41
  159.5 1.9 copy-done
  161.4 1.5 shard_map.111.refs_3_.refs_5_
  162.9 5.6 %shard_map.112 = (f32[384,1024]{1,0:T(8,128)S(1)}, f32[128,1024]{1,0:T(8,128)S(1)}, bf16[2,192,128]{2,1,0:T(8,128)(2,1)S(1)}) custom-call(s32[4]{0:T(128)S(1)} %pad_add_fusion.head_ref.info_ref, bf16[192,1024]{1,0:T(8,128)(2,1)} %get-tuple-element.44.refs_0_, bf16[192,1024]{1,0:T(8,128)(2,1)} %collective-permute-done.25.refs_1_, ...), custom_call_target="tpu_custom_call" | custom-call | tf_op jit(solution)/shard_map/pallas_call | solution.py:405
  168.5 5.5 %shard_map.113 = (f32[384,1024]{1,0:T(8,128)S(1)}, f32[128,1024]{1,0:T(8,128)S(1)}, bf16[2,192,128]{2,1,0:T(8,128)(2,1)S(1)}) custom-call(s32[4]{0:T(128)S(1)} %pad_add_fusion.head_ref.info_ref, bf16[192,1024]{1,0:T(8,128)(2,1)S(1)} %collective-permute-done.23.refs_0_, bf16[192,1024]{1,0:T(8,128)(2,1)} %collective-permute-done.24.refs_1_, ...), custom_call_target="tpu_custom_call" | custom-call | tf_op jit(solution)/shard_map/pallas_call | solution.py:405
  174.0 7.3 %shard_map.114 = (bf16[384,256]{1,0:T(8,128)(2,1)S(1)}, bf16[384,256]{1,0:T(8,128)(2,1)S(1)}, bf16[384,256]{1,0:T(8,128)(2,1)S(1)}, bf16[384,256]{1,0:T(8,128)(2,1)S(1)}, bf16[8,448,128]{2,1,0:T(8,128)(2,1)S(1)}) custom-call(s32[4]{0:T(128)S(1)} %pad_add_fusion.head_ref.info_ref, bf16[192,1024]{1,0:T(8,128)(2,1)S(1)} %collective-permute-done.19.refs_0_, ...), custom_call_target="tpu_custom_call" | custom-call | tf_op jit(solution)/shard_map/pallas_call | solution.py:405
  183.6 3.6 %all-to-all-start = ((bf16[8,448,128]{2,1,0:T(8,128)(2,1)}), bf16[8,448,128]{2,1,0:T(8,128)(2,1)S(1)}, u32[]{:S(2)}, u32[]{:S(2)}) async-start(bf16[8,448,128]{2,1,0:T(8,128)(2,1)} %copy-done.4), calls=%async_computation | async-start | bytes 1835008 | tf_op jit(solution)/shard_map/all_to_all | solution.py:528
  187.5 2.6 %collective-permute-start.27 = (bf16[384,256]{1,0:T(8,128)(2,1)}, bf16[384,256]{1,0:T(8,128)(2,1)S(1)}, u32[]{:S(2)}, u32[]{:S(2)}) collective-permute-start(bf16[384,256]{1,0:T(8,128)(2,1)} %copy-done.9), channel_id=1, source_target_pairs={{0,16},{8,24},{16,0},{24,8},{1,17},{9,25},{17,1},{25,9},{2,18},{10... | collective-permute-start | bytes 589832 | tf_op jit(solution)/shard_map/ppermute | solution.py:474
  190.1 1.5 collective-permute-start.28
  191.6 6.9 %collective-permute-done.26.refs_1_ = bf16[384,256]{1,0:T(8,128)(2,1)S(1)} collective-permute-done((bf16[384,256]{1,0:T(8,128)(2,1)}, bf16[384,256]{1,0:T(8,128)(2,1)S(1)}, u32[]{:S(2)}, u32[]{:S(2)}) %collective-permute-start.26) | collective-permute-done | bytes 196640 | tf_op jit(solution)/shard_map/ppermute | solution.py:474
  198.5 6.3 %collective-permute-done.27.refs_2_ = bf16[384,256]{1,0:T(8,128)(2,1)S(1)} collective-permute-done((bf16[384,256]{1,0:T(8,128)(2,1)}, bf16[384,256]{1,0:T(8,128)(2,1)S(1)}, u32[]{:S(2)}, u32[]{:S(2)}) %collective-permute-start.27) | collective-permute-done | bytes 196640 | tf_op jit(solution)/shard_map/ppermute | solution.py:474
  205.7 4.0 %all-to-all-start.1 = ((bf16[8,32,384]{2,1,0:T(8,128)(2,1)}), bf16[8,32,384]{2,1,0:T(8,128)(2,1)S(1)}, u32[]{:S(2)}, u32[]{:S(2)}) async-start(bf16[8,32,384]{2,1,0:T(8,128)(2,1)} %bitcast.6), calls=%async_computation.1 | async-start | bytes 393216 | tf_op jit(solution)/shard_map/all_to_all | solution.py:549
  209.7 1.3 shard_map.118
  211.0 3.7 %collective-permute-start.29 = (bf16[256,128]{1,0:T(8,128)(2,1)}, bf16[256,128]{1,0:T(8,128)(2,1)S(1)}, u32[]{:S(2)}, u32[]{:S(2)}) collective-permute-start(bf16[256,128]{1,0:T(8,128)(2,1)} %get-tuple-element.58), channel_id=1, source_target_pairs={{0,8},{8,0},{16,24},{24,16},{1,9},{9,1},{17,25},{25,17},{2,10},{10... | collective-permute-start | bytes 196616 | tf_op jit(solution)/shard_map/ppermute | solution.py:474
  214.7 1.5 collective-permute-start.30
  216.2 1.5 collective-permute-start.31
  218.5 1.1 copy-done.6
  219.6 1.3 shard_map.115
  220.9 2.3 %collective-permute-done.31.refs_3_ = bf16[256,128]{1,0:T(8,128)(2,1)S(1)} collective-permute-done((bf16[256,128]{1,0:T(8,128)(2,1)S(1)}, bf16[256,128]{1,0:T(8,128)(2,1)S(1)}, u32[]{:S(2)}, u32[]{:S(2)}) %collective-permute-start.31) | collective-permute-done | bytes 65568 | tf_op jit(solution)/shard_map/ppermute | solution.py:474
  (95 shorter events, 14.2 us)
Async XLA Ops:
  7.2 152.3 %all-gather.4.cloned.1.call-start = ((), (), s32[]{:S(2)}) async-start(), calls=%async_computation.2 | async-start | bytes 3538944 | tf_op jit(solution)/shard_map/all_gather | solution.py:520
  7.2 1.0 copy-start.7
  8.5 8.7 %collective-permute-start.7 = (bf16[24,4096]{1,0:T(8,128)(2,1)S(1)}, bf16[24,4096]{1,0:T(8,128)(2,1)S(1)}, u32[]{:S(2)}, u32[]{:S(2)}) collective-permute-start(bf16[24,4096]{1,0:T(8,128)(2,1)S(1)} %get-tuple-element.33), channel_id=1, source_target_pairs={{0,2},{1,3},{2,0},{3,1},{4,6},{5,7},{6,4},{7,5},{8,10},{9,11},{10,... | collective-permute-start | bytes 589832 | tf_op jit(solution)/shard_map/ppermute | solution.py:41
  11.5 11.0 %collective-permute-start.8 = (bf16[24,4096]{1,0:T(8,128)(2,1)S(1)}, bf16[24,4096]{1,0:T(8,128)(2,1)S(1)}, u32[]{:S(2)}, u32[]{:S(2)}) collective-permute-start(bf16[24,4096]{1,0:T(8,128)(2,1)S(1)} %get-tuple-element.33), channel_id=1, source_target_pairs={{0,4},{1,5},{2,6},{3,7},{4,0},{5,1},{6,2},{7,3},{8,12},{9,13},{10,... | collective-permute-start | bytes 589832 | tf_op jit(solution)/shard_map/ppermute | solution.py:41
  13.1 10.0 %collective-permute-start.9 = (bf16[24,4096]{1,0:T(8,128)(2,1)S(1)}, bf16[24,4096]{1,0:T(8,128)(2,1)S(1)}, u32[]{:S(2)}, u32[]{:S(2)}) collective-permute-start(bf16[24,4096]{1,0:T(8,128)(2,1)S(1)} %get-tuple-element.33), channel_id=1, source_target_pairs={{0,6},{1,7},{2,4},{3,5},{4,2},{5,3},{6,0},{7,1},{8,14},{9,15},{10,... | collective-permute-start | bytes 589832 | tf_op jit(solution)/shard_map/ppermute | solution.py:41
  13.1 10.1 %collective-permute-start.10 = (bf16[24,4096]{1,0:T(8,128)(2,1)S(1)}, bf16[24,4096]{1,0:T(8,128)(2,1)S(1)}, u32[]{:S(2)}, u32[]{:S(2)}) collective-permute-start(bf16[24,4096]{1,0:T(8,128)(2,1)S(1)} %get-tuple-element.33), channel_id=1, source_target_pairs={{0,1},{1,0},{2,3},{3,2},{4,5},{5,4},{6,7},{7,6},{8,9},{9,8},{10,11... | collective-permute-start | bytes 589832 | tf_op jit(solution)/shard_map/ppermute | solution.py:41
  13.1 12.7 %collective-permute-start = (bf16[24,4096]{1,0:T(8,128)(2,1)S(1)}, bf16[24,4096]{1,0:T(8,128)(2,1)S(1)}, u32[]{:S(2)}, u32[]{:S(2)}) collective-permute-start(bf16[24,4096]{1,0:T(8,128)(2,1)S(1)} %get-tuple-element.32), channel_id=1, source_target_pairs={{0,2},{1,3},{2,0},{3,1},{4,6},{5,7},{6,4},{7,5},{8,10},{9,11},{10,... | collective-permute-start | bytes 589832 | tf_op jit(solution)/shard_map/ppermute | solution.py:41
  17.3 13.3 %collective-permute-start.1 = (bf16[24,4096]{1,0:T(8,128)(2,1)S(1)}, bf16[24,4096]{1,0:T(8,128)(2,1)S(1)}, u32[]{:S(2)}, u32[]{:S(2)}) collective-permute-start(bf16[24,4096]{1,0:T(8,128)(2,1)S(1)} %get-tuple-element.32), channel_id=1, source_target_pairs={{0,4},{1,5},{2,6},{3,7},{4,0},{5,1},{6,2},{7,3},{8,12},{9,13},{10,... | collective-permute-start | bytes 589832 | tf_op jit(solution)/shard_map/ppermute | solution.py:41
  22.5 8.1 %collective-permute-start.2 = (bf16[24,4096]{1,0:T(8,128)(2,1)S(1)}, bf16[24,4096]{1,0:T(8,128)(2,1)S(1)}, u32[]{:S(2)}, u32[]{:S(2)}) collective-permute-start(bf16[24,4096]{1,0:T(8,128)(2,1)S(1)} %get-tuple-element.32), channel_id=1, source_target_pairs={{0,6},{1,7},{2,4},{3,5},{4,2},{5,3},{6,0},{7,1},{8,14},{9,15},{10,... | collective-permute-start | bytes 589832 | tf_op jit(solution)/shard_map/ppermute | solution.py:41
  23.1 8.1 %collective-permute-start.3 = (bf16[24,4096]{1,0:T(8,128)(2,1)S(1)}, bf16[24,4096]{1,0:T(8,128)(2,1)S(1)}, u32[]{:S(2)}, u32[]{:S(2)}) collective-permute-start(bf16[24,4096]{1,0:T(8,128)(2,1)S(1)} %get-tuple-element.32), channel_id=1, source_target_pairs={{0,1},{1,0},{2,3},{3,2},{4,5},{5,4},{6,7},{7,6},{8,9},{9,8},{10,11... | collective-permute-start | bytes 589832 | tf_op jit(solution)/shard_map/ppermute | solution.py:41
  23.1 8.1 %collective-permute-start.11 = (bf16[24,4096]{1,0:T(8,128)(2,1)S(1)}, bf16[24,4096]{1,0:T(8,128)(2,1)S(1)}, u32[]{:S(2)}, u32[]{:S(2)}) collective-permute-start(bf16[24,4096]{1,0:T(8,128)(2,1)S(1)} %collective-permute-done.7), channel_id=1, source_target_pairs={{0,1},{1,0},{2,3},{3,2},{4,5},{5,4},{6,7},{7,6},{8,9},{9,8},{10,11... | collective-permute-start | bytes 589832 | tf_op jit(solution)/shard_map/ppermute | solution.py:41
  25.8 6.1 %collective-permute-start.12 = (bf16[24,4096]{1,0:T(8,128)(2,1)S(1)}, bf16[24,4096]{1,0:T(8,128)(2,1)S(1)}, u32[]{:S(2)}, u32[]{:S(2)}) collective-permute-start(bf16[24,4096]{1,0:T(8,128)(2,1)S(1)} %collective-permute-done.8), channel_id=1, source_target_pairs={{0,1},{1,0},{2,3},{3,2},{4,5},{5,4},{6,7},{7,6},{8,9},{9,8},{10,11... | collective-permute-start | bytes 589832 | tf_op jit(solution)/shard_map/ppermute | solution.py:41
  30.5 1.4 collective-permute-start.13
  30.6 1.7 collective-permute-start.4
  31.2 1.5 collective-permute-start.5
  31.3 14.2 %collective-permute-start.6 = (bf16[24,4096]{1,0:T(8,128)(2,1)S(1)}, bf16[24,4096]{1,0:T(8,128)(2,1)S(1)}, u32[]{:S(2)}, u32[]{:S(2)}) collective-permute-start(bf16[24,4096]{1,0:T(8,128)(2,1)S(1)} %collective-permute-done.2), channel_id=1, source_target_pairs={{0,1},{1,0},{2,3},{3,2},{4,5},{5,4},{6,7},{7,6},{8,9},{9,8},{10,11... | collective-permute-start | bytes 589832 | tf_op jit(solution)/shard_map/ppermute | solution.py:41
  32.0 1.2 copy-start.12
  45.6 1.2 copy-start.11
  46.8 13.0 %copy-start.13 = (s32[8]{0:T(128)S(1)}, s32[8]{0:T(128)}, u32[]{:S(2)}) copy-start(s32[8]{0:T(128)} %constant.40.clone) | copy-start | bytes 100
  60.1 38.8 %copy-start.3 = (bf16[3,192,512]{2,1,0:T(8,128)(2,1)S(1)}, bf16[3,192,512]{2,1,0:T(8,128)(2,1)}, u32[]{:S(2)}) copy-start(bf16[3,192,512]{2,1,0:T(8,128)(2,1)} %get-tuple-element.34.qkv_ref) | copy-start | bytes 1769476
  100.0 3.4 %copy-start.2 = (bf16[512,8192]{1,0:T(8,128)(2,1)S(1)}, bf16[512,8192]{1,0:T(8,128)(2,1)}, u32[]{:S(2)}) copy-start(bf16[512,8192]{1,0:T(8,128)(2,1)} %w_ref.6) | copy-start | bytes 25165828
  107.3 3.5 %collective-permute-start.14 = (bf16[96,8192]{1,0:T(8,128)(2,1)S(1)}, bf16[96,8192]{1,0:T(8,128)(2,1)S(1)}, u32[]{:S(2)}, u32[]{:S(2)}) collective-permute-start(bf16[96,8192]{1,0:T(8,128)(2,1)S(1)} %get-tuple-element.36), channel_id=1, source_target_pairs={{0,1},{1,0},{2,3},{3,2},{4,5},{5,4},{6,7},{7,6},{8,9},{9,8},{10,11... | collective-permute-start | bytes 4718600 | tf_op jit(solution)/shard_map/ppermute | solution.py:41
  111.1 23.1 %copy-start.8 = (bf16[192,1024]{1,0:T(8,128)(2,1)S(1)}, bf16[192,1024]{1,0:T(8,128)(2,1)}, u32[]{:S(2)}) copy-start(bf16[192,1024]{1,0:T(8,128)(2,1)} %local_ref.1) | copy-start | bytes 1179652
  111.1 12.0 %collective-permute-start.15 = (bf16[24,8192]{1,0:T(8,128)(2,1)S(1)}, bf16[24,8192]{1,0:T(8,128)(2,1)S(1)}, u32[]{:S(2)}, u32[]{:S(2)}) collective-permute-start(bf16[24,8192]{1,0:T(8,128)(2,1)S(1)} %get-tuple-element.38), channel_id=1, source_target_pairs={{0,2},{1,3},{2,0},{3,1},{4,6},{5,7},{6,4},{7,5},{8,10},{9,11},{10,... | collective-permute-start | bytes 1179656 | tf_op jit(solution)/shard_map/ppermute | solution.py:41
  112.4 17.7 %collective-permute-start.16 = (bf16[24,8192]{1,0:T(8,128)(2,1)S(1)}, bf16[24,8192]{1,0:T(8,128)(2,1)S(1)}, u32[]{:S(2)}, u32[]{:S(2)}) collective-permute-start(bf16[24,8192]{1,0:T(8,128)(2,1)S(1)} %get-tuple-element.39), channel_id=1, source_target_pairs={{0,4},{1,5},{2,6},{3,7},{4,0},{5,1},{6,2},{7,3},{8,12},{9,13},{10,... | collective-permute-start | bytes 1179656 | tf_op jit(solution)/shard_map/ppermute | solution.py:41
  113.2 18.5 %collective-permute-start.17 = (bf16[24,8192]{1,0:T(8,128)(2,1)S(1)}, bf16[24,8192]{1,0:T(8,128)(2,1)S(1)}, u32[]{:S(2)}, u32[]{:S(2)}) collective-permute-start(bf16[24,8192]{1,0:T(8,128)(2,1)S(1)} %get-tuple-element.40), channel_id=1, source_target_pairs={{0,6},{1,7},{2,4},{3,5},{4,2},{5,3},{6,0},{7,1},{8,14},{9,15},{10,... | collective-permute-start | bytes 1179656 | tf_op jit(solution)/shard_map/ppermute | solution.py:41
  131.7 27.8 %copy-start.1 = (bf16[1,1024,1024]{2,1,0:T(8,128)(2,1)S(1)}, bf16[1,1024,1024]{2,1,0:T(8,128)(2,1)}, u32[]{:S(2)}) copy-start(bf16[1,1024,1024]{2,1,0:T(8,128)(2,1)} %w_ref.7) | copy-start | bytes 6291460
  131.9 2.3 collective-permute-start.18
  135.4 0.9 copy-start.5
  136.3 14.1 %collective-permute-start.23 = (bf16[192,1024]{1,0:T(8,128)(2,1)}, bf16[192,1024]{1,0:T(8,128)(2,1)S(1)}, u32[]{:S(2)}, u32[]{:S(2)}) collective-permute-start(bf16[192,1024]{1,0:T(8,128)(2,1)} %get-tuple-element.44.refs_0_), channel_id=1, source_target_pairs={{0,2},{1,3},{2,0},{3,1},{4,6},{5,7},{6,4},{7,5},{8,10},{9,11},{10,... | collective-permute-start | bytes 1179656 | tf_op jit(solution)/shard_map/ppermute | solution.py:41
  140.2 18.7 %collective-permute-start.19 = (bf16[192,1024]{1,0:T(8,128)(2,1)}, bf16[192,1024]{1,0:T(8,128)(2,1)S(1)}, u32[]{:S(2)}, u32[]{:S(2)}) collective-permute-start(bf16[192,1024]{1,0:T(8,128)(2,1)} %get-tuple-element.44.refs_0_), channel_id=1, source_target_pairs={{0,4},{1,5},{2,6},{3,7},{4,0},{5,1},{6,2},{7,3},{8,12},{9,13},{10,... | collective-permute-start | bytes 1179656 | tf_op jit(solution)/shard_map/ppermute | solution.py:41
  141.7 17.2 %collective-permute-start.21 = (bf16[192,1024]{1,0:T(8,128)(2,1)}, bf16[192,1024]{1,0:T(8,128)(2,1)S(1)}, u32[]{:S(2)}, u32[]{:S(2)}) collective-permute-start(bf16[192,1024]{1,0:T(8,128)(2,1)} %get-tuple-element.44.refs_0_), channel_id=1, source_target_pairs={{0,6},{1,7},{2,4},{3,5},{4,2},{5,3},{6,0},{7,1},{8,14},{9,15},{10,... | collective-permute-start | bytes 1179656 | tf_op jit(solution)/shard_map/ppermute | solution.py:41
  142.6 20.3 %collective-permute-start.25 = (bf16[192,1024]{1,0:T(8,128)(2,1)}, bf16[192,1024]{1,0:T(8,128)(2,1)}, u32[]{:S(2)}, u32[]{:S(2)}) collective-permute-start(bf16[192,1024]{1,0:T(8,128)(2,1)} %get-tuple-element.44.refs_0_), channel_id=1, source_target_pairs={{0,1},{1,0},{2,3},{3,2},{4,5},{5,4},{6,7},{7,6},{8,9},{9,8},{10,11... | collective-permute-start | bytes 1179656 | tf_op jit(solution)/shard_map/ppermute | solution.py:41
  150.4 18.1 %collective-permute-start.24 = (bf16[192,1024]{1,0:T(8,128)(2,1)S(1)}, bf16[192,1024]{1,0:T(8,128)(2,1)}, u32[]{:S(2)}, u32[]{:S(2)}) collective-permute-start(bf16[192,1024]{1,0:T(8,128)(2,1)S(1)} %collective-permute-done.23.refs_0_), channel_id=1, source_target_pairs={{0,1},{1,0},{2,3},{3,2},{4,5},{5,4},{6,7},{7,6},{8,9},{9,8},{10,11... | collective-permute-start | bytes 1179656 | tf_op jit(solution)/shard_map/ppermute | solution.py:41
  158.9 15.1 %collective-permute-start.20 = (bf16[192,1024]{1,0:T(8,128)(2,1)S(1)}, bf16[192,1024]{1,0:T(8,128)(2,1)}, u32[]{:S(2)}, u32[]{:S(2)}) collective-permute-start(bf16[192,1024]{1,0:T(8,128)(2,1)S(1)} %collective-permute-done.19.refs_0_), channel_id=1, source_target_pairs={{0,1},{1,0},{2,3},{3,2},{4,5},{5,4},{6,7},{7,6},{8,9},{9,8},{10,11... | collective-permute-start | bytes 1179656 | tf_op jit(solution)/shard_map/ppermute | solution.py:41
  158.9 15.1 %collective-permute-start.22 = (bf16[192,1024]{1,0:T(8,128)(2,1)S(1)}, bf16[192,1024]{1,0:T(8,128)(2,1)}, u32[]{:S(2)}, u32[]{:S(2)}) collective-permute-start(bf16[192,1024]{1,0:T(8,128)(2,1)S(1)} %collective-permute-done.21.refs_2_), channel_id=1, source_target_pairs={{0,1},{1,0},{2,3},{3,2},{4,5},{5,4},{6,7},{7,6},{8,9},{9,8},{10,11... | collective-permute-start | bytes 1179656 | tf_op jit(solution)/shard_map/ppermute | solution.py:41
  159.5 1.9 copy-start
  181.3 1.0 copy-start.4
  182.2 0.7 copy-start.9
  183.6 22.1 %all-to-all-start = ((bf16[8,448,128]{2,1,0:T(8,128)(2,1)}), bf16[8,448,128]{2,1,0:T(8,128)(2,1)S(1)}, u32[]{:S(2)}, u32[]{:S(2)}) async-start(bf16[8,448,128]{2,1,0:T(8,128)(2,1)} %copy-done.4), calls=%async_computation | async-start | bytes 1835008 | tf_op jit(solution)/shard_map/all_to_all | solution.py:528
  187.1 11.4 %collective-permute-start.26 = (bf16[384,256]{1,0:T(8,128)(2,1)}, bf16[384,256]{1,0:T(8,128)(2,1)S(1)}, u32[]{:S(2)}, u32[]{:S(2)}) collective-permute-start(bf16[384,256]{1,0:T(8,128)(2,1)} %copy-done.10), channel_id=1, source_target_pairs={{0,8},{8,0},{16,24},{24,16},{1,9},{9,1},{17,25},{25,17},{2,10},{10... | collective-permute-start | bytes 589832 | tf_op jit(solution)/shard_map/ppermute | solution.py:474
  187.5 17.3 %collective-permute-start.27 = (bf16[384,256]{1,0:T(8,128)(2,1)}, bf16[384,256]{1,0:T(8,128)(2,1)S(1)}, u32[]{:S(2)}, u32[]{:S(2)}) collective-permute-start(bf16[384,256]{1,0:T(8,128)(2,1)} %copy-done.9), channel_id=1, source_target_pairs={{0,16},{8,24},{16,0},{24,8},{1,17},{9,25},{17,1},{25,9},{2,18},{10... | collective-permute-start | bytes 589832 | tf_op jit(solution)/shard_map/ppermute | solution.py:474
  190.1 14.8 %collective-permute-start.28 = (bf16[384,256]{1,0:T(8,128)(2,1)S(1)}, bf16[384,256]{1,0:T(8,128)(2,1)S(1)}, u32[]{:S(2)}, u32[]{:S(2)}) collective-permute-start(bf16[384,256]{1,0:T(8,128)(2,1)S(1)} %get-tuple-element.56), channel_id=1, source_target_pairs={{0,24},{8,16},{16,8},{24,0},{1,25},{9,17},{17,9},{25,1},{2,26},{10... | collective-permute-start | bytes 589832 | tf_op jit(solution)/shard_map/ppermute | solution.py:474
  205.7 12.0 %all-to-all-start.1 = ((bf16[8,32,384]{2,1,0:T(8,128)(2,1)}), bf16[8,32,384]{2,1,0:T(8,128)(2,1)S(1)}, u32[]{:S(2)}, u32[]{:S(2)}) async-start(bf16[8,32,384]{2,1,0:T(8,128)(2,1)} %bitcast.6), calls=%async_computation.1 | async-start | bytes 393216 | tf_op jit(solution)/shard_map/all_to_all | solution.py:549
  211.0 9.9 %collective-permute-start.29 = (bf16[256,128]{1,0:T(8,128)(2,1)}, bf16[256,128]{1,0:T(8,128)(2,1)S(1)}, u32[]{:S(2)}, u32[]{:S(2)}) collective-permute-start(bf16[256,128]{1,0:T(8,128)(2,1)} %get-tuple-element.58), channel_id=1, source_target_pairs={{0,8},{8,0},{16,24},{24,16},{1,9},{9,1},{17,25},{25,17},{2,10},{10... | collective-permute-start | bytes 196616 | tf_op jit(solution)/shard_map/ppermute | solution.py:474
  214.7 6.2 %collective-permute-start.30 = (bf16[256,128]{1,0:T(8,128)(2,1)}, bf16[256,128]{1,0:T(8,128)(2,1)S(1)}, u32[]{:S(2)}, u32[]{:S(2)}) collective-permute-start(bf16[256,128]{1,0:T(8,128)(2,1)} %get-tuple-element.59), channel_id=1, source_target_pairs={{0,16},{8,24},{16,0},{24,8},{1,17},{9,25},{17,1},{25,9},{2,18},{10... | collective-permute-start | bytes 196616 | tf_op jit(solution)/shard_map/ppermute | solution.py:474
  216.2 7.1 %collective-permute-start.31 = (bf16[256,128]{1,0:T(8,128)(2,1)S(1)}, bf16[256,128]{1,0:T(8,128)(2,1)S(1)}, u32[]{:S(2)}, u32[]{:S(2)}) collective-permute-start(bf16[256,128]{1,0:T(8,128)(2,1)S(1)} %get-tuple-element.60), channel_id=1, source_target_pairs={{0,24},{8,16},{16,8},{24,0},{1,25},{9,17},{17,9},{25,1},{2,26},{10... | collective-permute-start | bytes 196616 | tf_op jit(solution)/shard_map/ppermute | solution.py:474
  218.5 1.1 copy-start.6
  (1 other events, 0.7 us)
Sparse Core Ops, SparseCore 0:
  59.9 32.6 all-gather.3

commit v3 on v0

v3 whole, which is shorter than its diff:
```python
import functools
import math

import jax
import jax.numpy as jnp
from jax import lax
from jax.experimental import pallas as pl
from jax.experimental.pallas import tpu as pltpu
from jax.sharding import PartitionSpec as P

PATCH = 8
HEAD_DIM = 128
LOCAL_HEADS = 8
LOCAL_HEAD_DIM = 128
EPS = 1e-06
F32 = jnp.float32
BF16 = jnp.bfloat16
MIB = 1 << 20
LARGE = 60
TOKEN = jax.ShapeDtypeStruct((8, 128), jnp.float32)
LANES = 128


def params(mib):
    return pltpu.CompilerParams(vmem_limit_bytes=mib * MIB)


def call(body, outs, scratch=(), mib=32):
    return pl.pallas_call(
        body,
        out_shape=[jax.ShapeDtypeStruct(shape, dtype) for shape, dtype in outs],
        scratch_shapes=list(scratch),
        compiler_params=params(mib),
    )


class Held:
    def __init__(self, source, target, sem):
        self.ref, self.copy, self.waited = target, pltpu.make_async_copy(source, target, sem), False
        self.copy.start()

    def __call__(self):
        if not self.waited:
            self.copy.wait()
            self.waited = True
        return self.ref


class Sent:
    def __init__(self, source, target, sem):
        self.ref, self.copy, self.started = source, pltpu.make_async_copy(source, target, sem), False

    def send(self):
        self.copy.start()
        self.started = True


def staged(body, args, sent, outs=(), scratch=(), info=None, mib=16, flops=0, after=None, held=()):
    tokens = [] if after is None else [after]
    counts = [len(args), len(held), len(tokens), len(sent), len(outs)]
    counts += [len(held), len(sent), len(scratch)]

    def kernel(*refs):
        refs = list(refs)
        info_ref = [refs.pop(0)] if info is not None else []
        groups = []
        for count in counts:
            groups.append(refs[:count])
            del refs[:count]
        in_refs, held_far, _, sent_far, out_refs, held_near, sent_near, own = groups
        in_sems, out_sems = refs
        inputs = [Held(f, n, in_sems.at[i]) for i, (f, n) in enumerate(zip(held_far, held_near))]
        outputs = [Sent(n, f, out_sems.at[i]) for i, (f, n) in enumerate(zip(sent_far, sent_near))]
        body(*info_ref, *in_refs, *inputs, *outputs, *out_refs, *own)
        for output in outputs:
            if not output.started:
                output.send()
        for value in inputs:
            value()
        for output in outputs:
            output.copy.wait()

    here, there = pl.BlockSpec(memory_space=pltpu.VMEM), pl.BlockSpec(memory_space=pltpu.HBM)
    free = pl.BlockSpec(memory_space=pl.ANY)
    scalars = [] if info is None else [info]
    return pl.pallas_call(
        kernel,
        in_specs=[pl.BlockSpec(memory_space=pltpu.SMEM)] * len(scalars)
        + [here] * len(args)
        + [free] * (len(held) + len(tokens)),
        out_specs=[there] * len(sent) + [here] * len(outs),
        out_shape=[pltpu.HBM(shape, dtype) for shape, dtype in sent]
        + [jax.ShapeDtypeStruct(shape, dtype) for shape, dtype in outs],
        scratch_shapes=[pltpu.VMEM(value.shape, value.dtype) for value in held]
        + [pltpu.VMEM(shape, dtype) for shape, dtype in sent]
        + list(scratch)
        + [pltpu.SemaphoreType.DMA((max(1, count),)) for count in (len(held), len(sent))],
        compiler_params=params(mib),
        cost_estimate=pl.CostEstimate(flops=flops, bytes_accessed=1 << 22, transcendentals=0),
    )(*scalars, *args, *held, *tokens)


def dot(a, b, dims=((1,), (0,))):
    return lax.dot_general(a, b, (dims, ((), ())), preferred_element_type=F32)


def swap(value, bits):
    count = lax.axis_size("tp")
    return lax.ppermute(value, "tp", [(source, source ^ bits) for source in range(count)])


def block_order(size):
    return list(range(0, size, 2)) + list(range(1, size, 2))


def gather(value, size):
    even = [value] + [swap(value, bits) for bits in range(2, size, 2)]
    return even + [swap(piece, 1) for piece in even]


def tie_body(*refs):
    pass


def tie(value, *after):
    there = pl.BlockSpec(memory_space=pl.ANY)
    return pl.pallas_call(
        tie_body,
        in_specs=[there] * (1 + len(after)),
        out_specs=there,
        out_shape=jax.ShapeDtypeStruct(value.shape, value.dtype),
        input_output_aliases={0: 0},
        compiler_params=params(1),
    )(value, *after)


def preload_body(parts, info_ref, w_ref, _, out_ref, info_out, sems):
    for index in range(info_ref.shape[0]):
        info_out[index] = info_ref[index]
    source = w_ref.at[0] if len(w_ref.shape) == 3 else w_ref
    size = source.shape[0] // parts
    copies = []
    for part in range(parts):
        at = pl.ds(part * size, size)
        copies.append(pltpu.make_async_copy(source.at[at], out_ref.at[at], sems.at[part]))
        copies[-1].start()
    for copy in copies:
        copy.wait()


def preload(weights, info, after, parts=8):
    there = pl.BlockSpec(memory_space=pl.ANY)
    scalar = pl.BlockSpec(memory_space=pltpu.SMEM)
    shape = weights.shape[-2:]
    return pl.pallas_call(
        functools.partial(preload_body, parts),
        in_specs=[scalar, there, there],
        out_specs=[pl.BlockSpec(memory_space=pltpu.VMEM), scalar],
        out_shape=[
            pltpu.VMEM(shape, weights.dtype),
            jax.ShapeDtypeStruct(info.shape, info.dtype),
        ],
        scratch_shapes=[pltpu.SemaphoreType.DMA((parts,))],
        compiler_params=params(50),
        cost_estimate=pl.CostEstimate(
            flops=0, bytes_accessed=2 * math.prod(shape), transcendentals=0
        ),
    )(info, weights, after)


def patch_norm_body(x_ref, out_ref, wide):
    patches = out_ref.shape[0]
    width = x_ref.shape[1]
    total = jnp.zeros((patches, LANES), F32)
    for c in range(width // LANES):
        wide[c] = x_ref[:, c * LANES : (c + 1) * LANES].astype(F32)
    for c in range(width // LANES):
        for b in range(PATCH):
            part = wide[c, pl.ds(b, patches, stride=PATCH), :]
            total += part * part
    scale = lax.rsqrt(jnp.sum(total, axis=-1, keepdims=True) / (PATCH * width) + EPS)
    for b in range(PATCH):
        for c in range(width // LANES):
            part = wide[c, pl.ds(b, patches, stride=PATCH), :]
            at = b * width + c * LANES
            out_ref[:, at : at + LANES] = (part * scale).astype(BF16)


def patch_norm(byte_embeds):
    rows, width = byte_embeds.shape
    return call(
        patch_norm_body,
        [((rows // PATCH, PATCH * width), BF16)],
        [pltpu.VMEM((width // LANES, rows, LANES), F32)],
        16,
    )(byte_embeds)[0]


def stack(refs):
    return jnp.concatenate([ref[...].astype(F32) for ref in refs], axis=0).astype(BF16)


def project_body(count, *refs):
    x_refs, refs = refs[:count], refs[count:]
    first_ref, pass_ref, w_ref, q, kv, passed, held, sems = refs
    kinds, rows, _ = held.shape
    depth = math.gcd(rows, 1024)
    copies = {}
    for c in range(kinds):
        for k in range(0, rows, depth):
            at = pl.ds(k, depth)
            copies[c, k] = pltpu.make_async_copy(
                w_ref.at[c + 1, at], held.at[c, at], sems.at[len(copies)]
            )
            copies[c, k].start()
    x = stack(x_refs)
    passed.ref[...] = pass_ref[...]
    passed.send()
    for c in range(kinds + 1):
        total = None
        for k in range(0, rows, depth):
            if c:
                copies[c - 1, k].wait()
                w = held[c - 1, k : k + depth, :]
            else:
                w = first_ref[k : k + depth, :]
            term = dot(x[:, k : k + depth], w)
            total = term if total is None else total + term
        for h in range(total.shape[1] // HEAD_DIM):
            at = slice(h * HEAD_DIM, (h + 1) * HEAD_DIM)
            part = total[:, at]
            if c < 2:
                part = part * lax.rsqrt(jnp.mean(part * part, axis=-1, keepdims=True) + EPS)
            if c == 0:
                q.ref[:, at] = part.astype(BF16)
            else:
                kv.ref[c - 1, :, at] = part.astype(BF16)
        if c == 0:
            q.send()


def project(pieces, first, weights, passed):
    rows = sum(piece.shape[0] for piece in pieces)
    kinds, deep, width = weights.shape
    here, there = pl.BlockSpec(memory_space=pltpu.VMEM), pl.BlockSpec(memory_space=pltpu.HBM)
    outs = [((rows, width), BF16), ((kinds - 1, rows, width), BF16), (passed.shape, passed.dtype)]
    count = len(pieces)

    def body(*refs):
        in_refs, far, near = refs[: count + 3], refs[count + 3 : count + 6], refs[count + 6 : count + 9]
        held, sems, out_sems = refs[count + 9 :]
        outputs = [Sent(n, f, out_sems.at[i]) for i, (f, n) in enumerate(zip(far, near))]
        project_body(count, *in_refs, *outputs, held, sems)
        outputs[1].send()
        for output in outputs:
            output.copy.wait()

    return pl.pallas_call(
        body,
        in_specs=[here] * (count + 2) + [pl.BlockSpec(memory_space=pl.ANY)],
        out_specs=[there] * 3,
        out_shape=[pltpu.HBM(shape, dtype) for shape, dtype in outs],
        scratch_shapes=[pltpu.VMEM(shape, dtype) for shape, dtype in outs]
        + [
            pltpu.VMEM((kinds - 1, deep, width), BF16),
            pltpu.SemaphoreType.DMA(((kinds - 1) * deep // math.gcd(deep, 1024),)),
            pltpu.SemaphoreType.DMA((3,)),
        ],
        compiler_params=params(40),
    )(*pieces, first, passed, weights)


def heads_of(ref_width):
    return [slice(at, at + HEAD_DIM) for at in range(0, ref_width, HEAD_DIM)]


def last_row(info_ref, rows, tp_count):
    return block_place(info_ref[1] ^ (tp_count - 1), tp_count) * (rows // tp_count) + (
        rows // tp_count - 1
    )


def block_place(bits, size):
    return bits // 2 + (bits % 2) * (size // 2)


def split_den(dens, count):
    high = dens.astype(BF16).astype(F32)
    return high + pltpu.roll(dens - high, count, 1)


def attend_body(tp_count, info_ref, kv_in_ref, q3_ref, q2_ref, mask_ref, *refs):
    q_in, kv_here, back3, back2, top_ref, den_ref, far_top, far_den = refs
    back3_ref, back2_ref = back3.ref, back2.ref
    q_ref, kv_ref = q_in(), kv_here()
    rows, width = q_ref.shape
    root = 1.0 / math.sqrt(HEAD_DIM)
    allowed = mask_ref[...] > 0
    linked = jnp.where(info_ref[3] % 2 == 1, 1.0, 0.0)
    heads = heads_of(width)
    count = len(heads)
    lane = lax.broadcasted_iota(jnp.int32, (rows, LANES), 1)
    dens = jnp.zeros((rows, LANES), F32)
    far_dens = [dens, dens]
    for h, at in enumerate(heads):
        q, k, v = q_ref[:, at], kv_ref[0, :, at], kv_ref[1, :, at]
        k_in, v_in = kv_in_ref[0, :, at], kv_in_ref[1, :, at]
        own = jnp.where(allowed, jnp.exp(dot(q, k, ((1,), (1,))) * root), 0.0)
        other = jnp.exp(dot(q, k_in, ((1,), (1,))) * root) * linked
        top_ref[:, at] = dot(own.astype(BF16), v) + dot(other.astype(BF16), v_in)
        den = jnp.sum(own, axis=-1, keepdims=True) + jnp.sum(other, axis=-1, keepdims=True)
        dens = jnp.where(lane == h, den, dens)
        for index, far_ref in enumerate((q3_ref, q2_ref)):
            far = far_ref[:, at]
            own = jnp.exp(dot(far, k, ((1,), (1,))) * root)
            other = jnp.exp(dot(far, k_in, ((1,), (1,))) * root)
            far_top[index, :, at] = dot(own.astype(BF16), v) + dot(other.astype(BF16), v_in)
            den = jnp.sum(own, axis=-1, keepdims=True) + jnp.sum(other, axis=-1, keepdims=True)
            far_dens[index] = jnp.where(lane == h, den, far_dens[index])
    den_ref[...] = dens
    last = last_row(info_ref, rows, tp_count)
    edge_rows = EDGE_ROWS

    def fill(ref, at, top, den):
        ref[at, :width] = top.astype(BF16)
        ref[at, width:] = split_den(den, count).astype(BF16)

    def spread(row):
        return jnp.broadcast_to(row, (edge_rows, row.shape[1]))

    far_den[...] = far_dens[1]
    fill(back3_ref, slice(0, rows), far_top[0], far_dens[0])
    fill(
        back3_ref,
        slice(rows, rows + edge_rows),
        spread(far_top[1, pl.ds(last, 1), :]),
        spread(far_den[pl.ds(last, 1), :]),
    )
    back3.send()
    fill(back2_ref, slice(0, rows), far_top[1], far_dens[1])
    fill(
        back2_ref,
        slice(rows, rows + edge_rows),
        spread(top_ref[pl.ds(last, 1), :]),
        spread(den_ref[pl.ds(last, 1), :]),
    )


EDGE_ROWS = 16


def attend_paired(info, q, kv, mask, tp_count):
    kv_in = lax.ppermute(kv, "ctx", [(0, 1), (2, 3)])
    far = [lax.ppermute(q, "ctx", [(c, 1)]) for c in (3, 2)]
    rows, width = q.shape
    back = ((rows + EDGE_ROWS, width + LANES), BF16)
    back3, back2, top, den = staged(
        functools.partial(attend_body, tp_count),
        [kv_in, *far, mask],
        [back, back],
        [((rows, width), F32), ((rows, LANES), F32)],
        [pltpu.VMEM((2, rows, width), F32), pltpu.VMEM((rows, LANES), F32)],
        info,
        held=[q, kv],
    )
    back3 = lax.ppermute(back3, "ctx", [(1, 3)])
    back2 = lax.ppermute(back2, "ctx", [(c, c + 1) for c in range(3)])
    return top, den, [back2, back3]


def attend_all_body(tp_count, info_ref, mask_ref, q_ref, k_ref, v_ref, top_ref, den_ref, edge_ref):
    rows, width = q_ref.shape
    allowed = mask_ref[...] > 0
    lane = lax.broadcasted_iota(jnp.int32, den_ref.shape, 1)
    dens = jnp.zeros(den_ref.shape, F32)
    heads = heads_of(width)
    for h, at in enumerate(heads):
        scores = dot(q_ref[:, at], k_ref[:, at], ((1,), (1,))) * (1.0 / math.sqrt(HEAD_DIM))
        expo = jnp.where(allowed, jnp.exp(scores), 0.0)
        top_ref[:, at] = dot(expo.astype(BF16), v_ref[:, at])
        dens = jnp.where(lane == h, jnp.sum(expo, axis=-1, keepdims=True), dens)
    den_ref[...] = dens
    last = last_row(info_ref, rows, tp_count)
    count = edge_ref.shape[0]
    top = jnp.broadcast_to(top_ref[pl.ds(last, 1), :], (count, width))
    den = jnp.broadcast_to(den_ref[pl.ds(last, 1), :], (count, LANES))
    edge_ref[:, :width] = top.astype(BF16)
    edge_ref[:, width:] = split_den(den, len(heads)).astype(BF16)


def attend_all(info, q, kv, mask, tp_count):
    planes = lax.axis_size("ctx")
    keys = lax.all_gather(kv[0], "ctx", axis=0, tiled=True)
    values = lax.all_gather(kv[1], "ctx", axis=0, tiled=True)
    rows, width = q.shape
    here = pl.BlockSpec(memory_space=pltpu.VMEM)
    outs = [((rows, width), F32), ((rows, LANES), F32), ((EDGE_ROWS, width + LANES), BF16)]
    top, den, edge = pl.pallas_call(
        functools.partial(attend_all_body, tp_count),
        in_specs=[pl.BlockSpec(memory_space=pltpu.SMEM)] + [here] * 4,
        out_specs=[here] * 3,
        out_shape=[jax.ShapeDtypeStruct(shape, dtype) for shape, dtype in outs],
        compiler_params=params(48),
    )(info, mask, q, keys, values)
    back = jnp.concatenate([jnp.zeros((rows, width + LANES), BF16), edge], axis=0)
    return top, den, [lax.ppermute(back, "ctx", [(c, c + 1) for c in range(planes - 1)])]


def output_body(count, tp_count, info_ref, *refs):
    back_refs = refs[:count]
    top_ref, den_ref, w_ref, odd_out, even_ref, whole, odd_ref, out_sems = refs[count:]
    depth = w_ref.shape[0]
    blocks, _, step = odd_ref.shape
    rows = top_ref.shape[0]
    heads = heads_of(depth)
    edges = []

    def column(ref, at, h):
        high, low = depth + h, depth + len(heads) + h
        return ref[at, high : high + 1].astype(F32) + ref[at, low : low + 1].astype(F32)

    for h, lanes in enumerate(heads):
        top, den = top_ref[:, lanes], den_ref[:, h : h + 1]
        edge, edge_den = 0.0, 0.0
        for index, ref in enumerate(back_refs):
            mine, mine_den = ref[:rows, lanes].astype(F32), column(ref, slice(0, rows), h)
            if index == 0:
                taken = info_ref[3] == 2
                mine, mine_den = jnp.where(taken, mine, 0.0), jnp.where(taken, mine_den, 0.0)
            top += mine
            den += mine_den
            edge += ref[rows:, lanes].astype(F32)
            edge_den += column(ref, slice(rows, None), h)
        whole[:, lanes] = top / den
        edges.append(jnp.where(edge_den > 0, edge / jnp.where(edge_den > 0, edge_den, 1.0), 0.0))
    edge = jnp.concatenate(edges, axis=1)[:1]
    patches = rows // tp_count
    me = info_ref[1]
    before = []
    for bits in block_order(tp_count):
        peer = me ^ bits
        source = block_place(me ^ ((peer + tp_count - 1) % tp_count), tp_count)
        row = whole[pl.ds(source * patches + patches - 1, 1), :]
        before.append(jnp.where(peer == 0, edge, row))
    for index, row in enumerate(before):
        at = index * patches + patches - 1
        whole[at : at + 1, :] = row
    attended = whole[...].astype(BF16)
    half = rows // 2
    sends = []
    for n in range(blocks):
        at = pl.ds(n * step, step)
        out = dot(attended, w_ref[:, at])
        odd_ref[n] = out[half:].astype(BF16)
        sends.append(pltpu.make_async_copy(odd_ref.at[n], odd_out.at[:, at], out_sems.at[n]))
        sends[-1].start()
        even_ref[:, at] = out[:half].astype(BF16)
    for copy in sends:
        copy.wait()


def output_project(info, top, den, back, weights, tp_count):
    rows, depth = top.shape
    width = weights.shape[1]
    step = min(width, 1024)
    here, there = pl.BlockSpec(memory_space=pltpu.VMEM), pl.BlockSpec(memory_space=pltpu.HBM)
    blocks = width // step
    odd, even = pl.pallas_call(
        functools.partial(output_body, len(back), tp_count),
        in_specs=[pl.BlockSpec(memory_space=pltpu.SMEM)] + [here] * (3 + len(back)),
        out_specs=[there, here],
        out_shape=[
            pltpu.HBM((rows // 2, width), BF16),
            jax.ShapeDtypeStruct((rows // 2, width), BF16),
        ],
        scratch_shapes=[
            pltpu.VMEM((rows, depth), F32),
            pltpu.VMEM((blocks, rows // 2, step), BF16),
            pltpu.SemaphoreType.DMA((blocks,)),
        ],
        compiler_params=params(16),
    )(info, *back, top, den, weights)
    return even, odd


def pair_sum_body(mine_ref, other_ref, own_ref, *send_refs):
    patches = own_ref.shape[0]
    total = mine_ref[...].astype(F32) + other_ref[...].astype(F32)
    own_ref[...] = total[:patches]
    for index, ref in enumerate(send_refs):
        ref[...] = total[(index + 1) * patches : (index + 2) * patches].astype(BF16)


def scatter_sum(even, odd, patches):
    blocks = even.shape[0] // patches
    block = (patches, even.shape[1])
    pieces = call(pair_sum_body, [(block, F32)] + [(block, BF16)] * (blocks - 1))(
        even, swap(odd, 1)
    )
    return [pieces[0]] + [swap(piece, 2 * (index + 1)) for index, piece in enumerate(pieces[1:])]


def state_body(count, *refs):
    terms = refs[:count]
    local_ref, normed, state_out, normed_ref, wide = refs[count:]
    patches = terms[0].shape[0]
    width = normed_ref.shape[1]
    chunks = width // LANES
    for b in range(PATCH):
        at = slice(b * width, (b + 1) * width)
        total = terms[0][:, at]
        for term in terms[1:]:
            total += term[:, at].astype(F32)
        part = pltpu.roll(total.astype(BF16).astype(F32), 1, 0)
        for c in range(chunks):
            wide[c, pl.ds(b, patches, stride=PATCH), :] = part[:, c * LANES : (c + 1) * LANES]
    context = jnp.concatenate([wide[c] for c in range(chunks)], axis=1)
    state = local_ref[...].astype(F32) + context
    state_out.ref[...] = state
    state_out.send()
    mean = jnp.mean(state * state, axis=-1, keepdims=True)
    normed_ref[...] = (state * lax.rsqrt(mean + EPS)).astype(BF16)
    normed.ref[...] = normed_ref[...]


def byte_state(terms, local_embeds, after):
    rows, width = local_embeds.shape
    normed, state, normed_near = staged(
        functools.partial(state_body, len(terms)),
        [*terms, local_embeds],
        [((rows, width), BF16), ((rows, width), F32)],
        [((rows, width), BF16)],
        [pltpu.VMEM((width // LANES, rows, LANES), F32)],
        after=after,
    )
    return state, normed, normed_near


def unit(x):
    scale = lax.rsqrt(jnp.mean(x * x, axis=-1, keepdims=True) + EPS)
    return x * scale, scale


def unit_back(grad, y, scale):
    return scale * (grad - y * jnp.mean(grad * y, axis=-1, keepdims=True))


def prepare_body(parts, info_ref, gb_ref, wq_ref, wk_ref, wv_ref, wo_ref, *refs):
    weights_ref = refs[0]
    d = LOCAL_HEAD_DIM
    rows = refs[1].shape[0] // len(parts[0])
    for kind, ref in enumerate((wq_ref, wk_ref, wv_ref)):
        weights_ref[:, kind * d : (kind + 1) * d] = ref[0]
    for index, part in enumerate(parts):
        out_ref, core_ref = refs[1 + 2 * index : 3 + 2 * index]
        for place, bits in enumerate(part):
            at = pl.multiple_of((info_ref[1] ^ bits) * rows, rows)
            out_ref[place * rows : (place + 1) * rows, :] = gb_ref[pl.ds(at, rows), :]
        core_ref[...] = dot(out_ref[...], wo_ref[0], ((1,), (1,))).astype(BF16)


def prepare(info, gb_all, local_qkv, local_out, rows, parts):
    width = gb_all.shape[1]
    d = LOCAL_HEAD_DIM
    heads = LOCAL_HEADS

    def qkv_spec(kind):
        return pl.BlockSpec((1, width, d), lambda i, info: (0, 0, kind * heads + info[0]))

    outs = [(width, 3 * d)]
    for part in parts:
        outs += [(len(part) * rows, width), (len(part) * rows, d)]
    weights, *blocks = pl.pallas_call(
        functools.partial(prepare_body, parts),
        grid_spec=pltpu.PrefetchScalarGridSpec(
            num_scalar_prefetch=1,
            grid=(1,),
            in_specs=[
                pl.BlockSpec(gb_all.shape, lambda i, info: (0, 0)),
                qkv_spec(0),
                qkv_spec(1),
                qkv_spec(2),
                pl.BlockSpec((1, d, width), lambda i, info: (0, info[0], 0)),
            ],
            out_specs=[pl.BlockSpec(shape, lambda i, info: (0, 0)) for shape in outs],
        ),
        out_shape=[jax.ShapeDtypeStruct(shape, BF16) for shape in outs],
        compiler_params=params(LARGE),
    )(info, gb_all, local_qkv, local_qkv, local_qkv, local_out)
    return weights, blocks[0::2], blocks[1::2]


def window(rows):
    row = lax.broadcasted_iota(jnp.int32, (rows, rows), 0)
    column = lax.broadcasted_iota(jnp.int32, (rows, rows), 1)
    return (row // PATCH == column // PATCH) & (column <= row)


def core_weights(qkv, allowed):
    d = LOCAL_HEAD_DIM
    q, q_scale = unit(qkv[:, :d])
    k, k_scale = unit(qkv[:, d : 2 * d])
    qb, kb, vb = q.astype(BF16), k.astype(BF16), qkv[:, 2 * d :].astype(BF16)
    expo = jnp.where(allowed, jnp.exp(dot(qb, kb, ((1,), (1,))) * (1.0 / math.sqrt(d))), 0.0)
    weight = expo / jnp.sum(expo, axis=-1, keepdims=True)
    return (q, q_scale, qb), (k, k_scale, kb), vb, weight


def core_forward(weight, vb):
    return dot(weight.astype(BF16), vb).astype(BF16)


def core_backward(query, key, vb, weight, gradb):
    q, q_scale, qb = query
    k, k_scale, kb = key
    grad_v = dot(weight.astype(BF16), gradb, ((0,), (0,)))
    grad_w = dot(gradb, vb, ((1,), (1,)))
    mean = jnp.sum(weight * grad_w, axis=-1, keepdims=True)
    grad_s = (weight * (grad_w - mean) * (1.0 / math.sqrt(LOCAL_HEAD_DIM))).astype(BF16)
    grad_q = unit_back(dot(grad_s, kb), q, q_scale)
    grad_k = unit_back(dot(grad_s, qb, ((0,), (0,))), k, k_scale)
    return jnp.concatenate([grad_q, grad_k, grad_v], axis=1).astype(BF16)


def chunks_in(piece):
    return jnp.concatenate(
        [piece[:, at : at + LANES] for at in range(0, piece.shape[1], LANES)], axis=0
    )


def chunks_out(value, rows):
    return jnp.concatenate(
        [value[at : at + rows] for at in range(0, value.shape[0], rows)], axis=1
    )


def rows_of(refs):
    return jnp.concatenate([ref[...] for ref in refs], axis=0)


def local_body(count, *refs):
    x_refs, refs = refs[:count], refs[count:]
    (gb_ref, core_ref, w_ref), refs = refs[:3], refs[3:]
    carry, (gqkv_ref, gout_ref, ab_ref, token_ref) = refs[:-4], refs[-4:]
    token_ref[...] = jnp.zeros_like(token_ref)
    gqkv, gout, abs_ = local_grads(x_refs, gb_ref, core_ref, w_ref, carry)
    gqkv_ref[...] = gqkv
    gout_ref[...] = gout
    ab_ref[...] = jnp.concatenate(abs_, axis=0)


def local_grads(x_refs, gb_ref, core_ref, w_ref, carry):
    x = rows_of(x_refs)
    rows = x_refs[0].shape[0]
    allowed = window(rows)
    qkv = dot(x, w_ref[...])
    abs_, gqs = [], []
    for index in range(len(x_refs)):
        at = slice(index * rows, (index + 1) * rows)
        query, key, vb, weight = core_weights(qkv[at], allowed)
        abs_.append(core_forward(weight, vb))
        gqs.append(core_backward(query, key, vb, weight, core_ref[at, :]))
    gqkv = dot(jnp.concatenate(gqs, axis=0), x, ((0,), (0,)))
    gout = dot(jnp.concatenate(abs_, axis=0), gb_ref[...], ((0,), (0,)))
    if carry:
        gqkv += carry[0][...]
        gout += carry[1][...]
    return gqkv, gout, abs_


def local_last_body(count, info_ref, *refs):
    x_refs, refs = refs[:count], refs[count:]
    gb_ref, core_ref, w_ref, *carry, ab0_ref, gqkv_out, message, kept_ref, held = refs
    gqkv, gout, abs_ = local_grads(x_refs, gb_ref, core_ref, w_ref, carry)
    gqkv_out.ref[...] = gqkv.T.astype(BF16)
    gqkv_out.send()
    held[...] = gout
    rows = x_refs[0].shape[0]
    message.ref[:rows, :] = ab0_ref[rows:, :]
    for index, ab in enumerate(abs_):
        message.ref[(index + 1) * rows : (index + 2) * rows, :] = ab
    deep = kept_ref.shape[1]
    piece_rows = deep * LANES // held.shape[1]
    for k in range(held.shape[0] // piece_rows):
        at = pl.multiple_of((info_ref[2] ^ k) * piece_rows, piece_rows)
        piece = chunks_in(held[pl.ds(at, piece_rows), :]).astype(BF16)
        if k % 2:
            start = (count + 1) * rows + k // 2 * deep
            message.ref[start : start + deep, :] = piece
        else:
            kept_ref[k // 2] = piece


def relay_body(count, ab0_ref, ab1_ref, kept_ref, there_ref, *refs):
    rows = ab0_ref.shape[0] // 2
    deep = kept_ref.shape[1]
    *messages, own = refs
    for k, message in enumerate([own, *messages]):
        parts = []
        if k <= count:
            parts.append(ab0_ref[:rows, :] if k == 0 else ab1_ref[(k - 1) * rows : k * rows, :])
            parts.append(there_ref[k * rows : (k + 1) * rows, :])
        if k < kept_ref.shape[0]:
            start = (count + 1) * rows + k * deep
            parts.append(kept_ref[k])
            parts.append(there_ref[start : start + deep, :])
        at = 0
        target = message if k == 0 else message.ref
        for part in parts:
            target[at : at + part.shape[0], :] = part
            at += part.shape[0]
        if k:
            message.send()


def local_layer(normed, normed_near, info, parts, gbs, cores, weights, rounds, tp_count):
    rows, width = normed.shape
    d = LOCAL_HEAD_DIM
    near = [swap(normed, bits) for bits in parts[1]]
    count = len(near)
    totals = [((3 * d, width), F32), ((d, width), F32)]

    def step(index, xs, carry):
        return staged(
            functools.partial(local_body, len(xs)),
            [*xs, gbs[index], cores[index], weights, *carry],
            [],
            [*totals, ((len(xs) * rows, d), BF16), (TOKEN.shape, F32)],
            flops=1 << 34,
            mib=20,
        )

    *carry, ab0, done = step(0, [normed_near, swap(normed, 1)], [])
    near = [tie(block, done) for block in near]
    far = [swap(block, 1) for block in near]
    *carry, ab1, _ = step(1, near, carry)
    deep = d // rounds * width // LANES
    halves = rounds // 2
    length = (count + 1) * rows + halves * deep
    grad_qkv, message, kept = staged(
        functools.partial(local_last_body, count),
        [*far, gbs[2], cores[2], weights, *carry, ab0],
        [((width, 3 * d), BF16), ((length, d), BF16)],
        [((halves, deep, d), BF16)],
        [pltpu.VMEM((d, width), F32)],
        info,
        flops=1 << 34,
        mib=20,
    )
    sizes = [2 * rows * (k <= count) + 2 * deep * (k < halves) for k in range(max(count + 1, halves))]
    *messages, own = staged(
        functools.partial(relay_body, count),
        [ab0, ab1, kept, swap(message, 1)],
        [((size, d), BF16) for size in sizes[1:]],
        [((sizes[0], d), BF16)],
    )
    messages = [own] + [swap(value, 2 * (k + 1)) for k, value in enumerate(messages)]
    return messages, grad_qkv


def hidden_body(heads, count, info_ref, state_ref, w_ref, *refs):
    *messages, out_ref, token_ref = refs
    token_ref[...] = jnp.zeros_like(token_ref)
    rows = state_ref.shape[0]
    d = LOCAL_HEAD_DIM
    total = state_ref[...]
    for bits in range(2 * count + 2):
        at = bits % 2 * rows
        head = heads(info_ref[1] ^ bits)
        weights = w_ref[0, pl.ds(pl.multiple_of(head * d, d), d), :]
        total += dot(messages[bits // 2][at : at + rows, :], weights)
    out_ref[...] = total.astype(BF16)


def planes_body(planes, count, rounds, rows, info_ref, *refs):
    half = rounds // 2
    messages, outs, held = refs[:half], refs[half:-1], refs[-1]
    deep = held.shape[1]
    for k in range(rounds):
        start = 2 * rows * (k // 2 <= count) + k % 2 * deep
        held[k] = messages[k // 2][start : start + deep, :].astype(F32)
    for z, out in enumerate(outs):
        total = None
        for outer in range(rounds // planes):
            term = held[info_ref[2] ^ ((info_ref[3] ^ z) + outer * planes)]
            total = term if total is None else total + term
        out.ref[...] = total.astype(BF16)
        out.send()


def final_body(heads, parts_ref, *refs):
    *terms, gqkv_ref, gout_ref = refs
    gout = sum(term[...].astype(F32) for term in terms)
    gout_ref[0] = chunks_out(gout, gout_ref.shape[1])
    d = LOCAL_HEAD_DIM
    tp_count = len(heads)
    for h in range(LOCAL_HEADS):
        total = None
        for source in range(parts_ref.shape[0]):
            if heads[source % tp_count] == h:
                term = parts_ref[source].astype(F32)
                total = term if total is None else total + term
        for kind in range(3):
            at = (kind * LOCAL_HEADS + h) * d
            gqkv_ref[0, :, at : at + d] = total[:, kind * d : (kind + 1) * d]


def swap_planes(pieces):
    count = len(pieces)
    return [pieces[0]] + [
        lax.ppermute(pieces[k], "ctx", [(c, c ^ k) for c in range(count)]) for k in range(1, count)
    ]


def per_device(byte_embeds, local_embeds, global_qkv, global_out, local_qkv, local_out, cotangent):
    byte_count, width = byte_embeds.shape
    patches = byte_count // PATCH
    planes, tp_count = lax.axis_size("ctx"), lax.axis_size("tp")
    plane, me = lax.axis_index("ctx"), lax.axis_index("tp")
    order = block_order(tp_count)
    shard_rows = tp_count * patches
    devices = planes * tp_count

    group = min(tp_count, LOCAL_HEADS)
    share = width // devices
    rounds = LOCAL_HEAD_DIM // share
    plane_heads = LOCAL_HEADS // planes

    def head_of(t):
        return (t % rounds) % planes * plane_heads + t // rounds

    heads = [head_of(t) for t in range(tp_count)]
    head_info = jnp.stack([head_of(me), me, me % rounds, plane]).astype(jnp.int32)

    patch_in = patch_norm(byte_embeds)
    mine = swap(patch_in, 1)
    weights_in, head_info = preload(global_qkv, head_info, mine)
    even = [tie(swap(patch_in, bits), head_info) for bits in range(2, tp_count, 2)]
    pieces = [patch_in, *even, mine, *(swap(piece, 1) for piece in even)]
    q, kv, gb = project(pieces, weights_in, global_qkv, cotangent)

    place = (
        (me ^ jnp.array(order, jnp.int32))[:, None] * patches
        + jnp.arange(patches, dtype=jnp.int32)[None, :]
    ).reshape(-1)
    weights_out, head_info = preload(global_out, head_info, q)
    if planes == 4:
        mask = (place[None, :] <= place[:, None]).astype(F32)
        top, den, back = attend_paired(
            head_info, q, kv, mask, tp_count
        )
    else:
        key_place = (
            jnp.arange(planes, dtype=jnp.int32)[:, None] * shard_rows + place[None, :]
        ).reshape(-1)
        mask = (key_place[None, :] <= (plane * shard_rows + place)[:, None]).astype(F32)
        top, den, back = attend_all(head_info, q, kv, mask, tp_count)

    even, odd = output_project(head_info, top, den, back, weights_out, tp_count)

    parts = [[0, 1], list(range(2, group, 2)), list(range(3, group, 2))]
    gb_all = lax.all_gather(gb, "tp", axis=0, tiled=True)
    weights, gbs, cores = prepare(head_info, gb_all, local_qkv, local_out, byte_count, parts)
    state, normed, normed_near = byte_state(scatter_sum(even, odd, patches), local_embeds, cores[0])
    messages, grad_qkv = local_layer(
        normed, normed_near, head_info, parts, gbs, cores, weights, rounds, tp_count
    )
    grad_qkv = lax.all_to_all(grad_qkv, ("ctx", "tp"), 0, 0, tiled=True)
    flat = (share * width // LANES, LANES)
    count = group // 2 - 1
    out_pieces = staged(
        functools.partial(planes_body, planes, count, rounds, byte_count),
        messages[: rounds // 2],
        [(flat, BF16)] * planes,
        scratch=[pltpu.VMEM((rounds,) + flat, F32)],
        info=head_info,
    )
    out_pieces = swap_planes(out_pieces)
    here = pl.BlockSpec(memory_space=pltpu.VMEM)
    hidden, done = pl.pallas_call(
        functools.partial(hidden_body, head_of, count),
        in_specs=[pl.BlockSpec(memory_space=pltpu.SMEM)] + [here] * (3 + count),
        out_specs=[here, here],
        out_shape=[jax.ShapeDtypeStruct((byte_count, width), BF16), TOKEN],
        compiler_params=params(LARGE),
    )(head_info, state, local_out, *messages[: count + 1])
    out_pieces[0] = tie(out_pieces[0], done)
    grad_qkv, grad_out = call(
        functools.partial(final_body, heads),
        [((1, share, 3 * width), F32), ((1, share, width), F32)],
        mib=LARGE,
    )(grad_qkv.reshape(devices, share, 3 * LOCAL_HEAD_DIM), *out_pieces)
    return (hidden, grad_qkv, grad_out)


def solution(mesh):
    in_specs = (
        P(("ctx", "tp"), None),
        P(("ctx", "tp"), None),
        P(None, None, "tp"),
        P("tp", None),
        P(),
        P(),
        P(("ctx", "tp"), None),
    )
    out_specs = (P(("ctx", "tp"), None), P(None, ("ctx", "tp"), None), P(None, ("ctx", "tp"), None))
    return jax.shard_map(
        per_device, mesh=mesh, in_specs=in_specs, out_specs=out_specs, check_vma=False
    )
```

time: 424 us -> 183 us (0.43)
  waiting for transfers between devices: 293 us -> 60.8 us
  Pallas kernels: 0 us -> 53.6 us
  matrix products: 44.3 us -> 0 us
  starting transfers between devices: 2.18 us -> 43.6 us
  blocking collectives: 37.7 us -> 0 us
  other arithmetic: 12.1 us -> 0.82 us
  local copies, waits for them, and re-layouts: 19.6 us -> 8.91 us
    reduce_scatter x5 -> x0, waiting for transfers between devices: 258 us -> none  [the longest x1 112 us: per_device(): lax.psum_scatter(grad_qkv.astype(jnp.bfloat16), 'ctx', scatter_dimension=...]
    ppermute x1 -> x30, waiting for transfers between devices: 0.01 us -> 60.7 us  [the longest x22 53.1 us: swap(): lax.ppermute(value, 'tp', [(source, source ^ bits) for source in range(co...]
    pallas_call x0 -> x23, Pallas kernels: none -> 53.6 us  [the longest x7 19.4 us: staged(): pl.pallas_call(kernel, in_specs=[pl.BlockSpec(memory_space=pltpu.SMEM)] *...]
    dot_general x15 -> x0, matrix products: 44.3 us -> none  [the longest x1 11.7 us: per_device(): jnp.einsum('nd,cdh->nch', lax.all_gather(normed, 'tp', axis=0, tiled=True...]
    all_gather x2 -> x0, blocking collectives: 37.7 us -> none  [the longest x1 19.5 us: per_device(): key_piece = lax.all_gather(keys_mine, 'ctx', axis=0, tiled=True)]
    all_gather x1, waiting for transfers between devices: 34.3 us -> 0.01 us  [per_device(): gb_all = lax.all_gather(gb, 'tp', axis=0, tiled=True)]
    ppermute x1 -> x30, starting transfers between devices: 1.94 us -> 33.6 us  [the longest x22 16.8 us: swap(): lax.ppermute(value, 'tp', [(source, source ^ bits) for source in range(co...]
    all_to_all x0 -> x1, starting transfers between devices: none -> 10 us  [per_device(): grad_qkv = lax.all_to_all(grad_qkv, ('ctx', 'tp'), 0, 0, tiled=True)]
  transfers between devices with their start and end apart: 7 -> 32, of which waited for: 6 -> 14; matrix products, arithmetic and copies ran while one was open for 8% -> 0% of each run, Pallas kernels for 0% -> 19%
where the time goes in v3:
time: 183 us; the launch traced here: 182 us
  waiting for transfers between devices  60.8 us (33%)
  Pallas kernels  53.6 us (29%)
  starting transfers between devices  43.6 us (24%)
  between operations  14.5 us (8%)
  local copies, waits for them, and re-layouts  8.91 us (5%)
    ppermute x22, waiting for transfers between devices, swap(): lax.ppermute(value, 'tp', [(source, source ^ bits) for source in range(co...  53.1 us
    pallas_call x7, Pallas kernels, staged(): pl.pallas_call(kernel, in_specs=[pl.BlockSpec(memory_space=pltpu.SMEM)] *...  19.4 us
    ppermute x22, starting transfers between devices, swap(): lax.ppermute(value, 'tp', [(source, source ^ bits) for source in range(co...  16.8 us
    all_to_all x1, starting transfers between devices, per_device(): grad_qkv = lax.all_to_all(grad_qkv, ('ctx', 'tp'), 0, 0, tiled=True)  10 us
    pallas_call x2, Pallas kernels, preload(): pl.pallas_call(functools.partial(preload_body, parts), in_specs=[scalar,...  9.84 us
    pallas_call x1, Pallas kernels, project(): pl.pallas_call(body, in_specs=[here] * (count + 2) + [pl.BlockSpec(memory...  8.96 us
    unnamed x64, local copies, waits for them, and re-layouts  8.83 us
    ppermute x1, starting transfers between devices, attend_paired(): back2 = lax.ppermute(back2, 'ctx', [(c, c + 1) for c in range(3)])  6.65 us
  transfers between devices with their start and end apart: 32, of which 14 were waited for; matrix products, arithmetic and copies ran while one was open for 0% of the time, Pallas kernels for 19%

profile of v3, /device:TPU:0, one launch (start us, length us, event | category | flops | bytes accessed | tf_op | source)
XLA Modules:
  0.0 182.2 jit_solution(9648874808526598249)
XLA Ops:
  7.2 1.0 copy-done.7
  9.1 2.6 %collective-permute-start.1 = (bf16[24,8192]{1,0:T(8,128)(2,1)S(1)}, bf16[24,8192]{1,0:T(8,128)(2,1)S(1)}, u32[]{:S(2)}, u32[]{:S(2)}) collective-permute-start(bf16[24,8192]{1,0:T(8,128)(2,1)S(1)} %shard_map.103.refs_0_), channel_id=1, source_target_pairs={{0,2},{1,3},{2,0},{3,1},{4,6},{5,7},{6,4},{7,5},{8,10},{9,11},{10,... | collective-permute-start | bytes 1179656 | tf_op jit(solution)/shard_map/ppermute | solution.py:109
  11.6 1.5 collective-permute-start.2
  13.8 0.7 copy-done
  14.6 4.7 %shard_map.104 = (bf16[8192,512]{1,0:T(8,128)(2,1)S(1)}, s32[4]{0:T(128)}) custom-call(s32[4]{0:T(128)} %pad_add_fusion.info_ref, bf16[3,8192,512]{2,1,0:T(8,128)(2,1)} %refs_10_.1, bf16[24,8192]{1,0:T(8,128)(2,1)} %copy-done), custom_call_target="tpu_custom_call" | custom-call | bytes 8388608 | tf_op jit(solution)/shard_map/pallas_call | solution.py:155
  19.3 2.3 %collective-permute-done.1.refs_0_ = bf16[24,8192]{1,0:T(8,128)(2,1)S(1)} collective-permute-done((bf16[24,8192]{1,0:T(8,128)(2,1)S(1)}, bf16[24,8192]{1,0:T(8,128)(2,1)S(1)}, u32[]{:S(2)}, u32[]{:S(2)}) %collective-permute-start.1) | collective-permute-done | bytes 393248 | tf_op jit(solution)/shard_map/ppermute | solution.py:109
  22.3 9.0 %collective-permute-done.2.refs_0_ = bf16[24,8192]{1,0:T(8,128)(2,1)S(1)} collective-permute-done((bf16[24,8192]{1,0:T(8,128)(2,1)S(1)}, bf16[24,8192]{1,0:T(8,128)(2,1)S(1)}, u32[]{:S(2)}, u32[]{:S(2)}) %collective-permute-start.2) | collective-permute-done | bytes 393248 | tf_op jit(solution)/shard_map/ppermute | solution.py:109
  33.6 0.8 collective-permute-done.6.refs_7_
  34.4 9.0 %shard_map.108 = (bf16[192,512]{1,0:T(8,128)(2,1)}, bf16[2,192,512]{2,1,0:T(8,128)(2,1)}, bf16[192,1024]{1,0:T(8,128)(2,1)}) custom-call(bf16[24,8192]{1,0:T(8,128)(2,1)S(1)} %shard_map.103.refs_0_, bf16[24,8192]{1,0:T(8,128)(2,1)S(1)} %shard_map.105.refs_1_, bf16[24,8192]{1,0:T(8,128)(2,1)S(1)} %shard_map.106.refs_2_, ...), custom_call_target="tpu_custom_call" | custom-call | tf_op jit(solution)/shard_map/pallas_call | solution.py:258
  43.4 3.5 %collective-permute-start.7 = (bf16[2,192,512]{2,1,0:T(8,128)(2,1)}, bf16[2,192,512]{2,1,0:T(8,128)(2,1)S(1)}, u32[]{:S(2)}, u32[]{:S(2)}) collective-permute-start(bf16[2,192,512]{2,1,0:T(8,128)(2,1)} %get-tuple-element.56.refs_6_), channel_id=1, source_target_pairs={{0,8},{16,24},{1,9},{17,25},{2,10},{18,26},{3,11},{19,27},{4,12},{... | collective-permute-start | bytes 1179656 | tf_op jit(solution)/shard_map/ppermute | solution.py:353
  47.8 0.7 collective-permute-start.9
  48.6 5.2 %shard_map.109 = (bf16[512,8192]{1,0:T(8,128)(2,1)S(1)}, s32[4]{0:T(128)}) custom-call(s32[4]{0:T(128)} %get-tuple-element.52.refs_1_.info_ref, bf16[512,8192]{1,0:T(8,128)(2,1)} %w_ref.4, bf16[192,512]{1,0:T(8,128)(2,1)} %get-tuple-element.54._.refs_5_), custom_call_target="tpu_custom_call" | custom-call | bytes 8388608 | tf_op jit(solution)/shard_map/pallas_call | solution.py:155
  53.8 2.3 %collective-permute-done.7.refs_1_ = bf16[2,192,512]{2,1,0:T(8,128)(2,1)S(1)} collective-permute-done((bf16[2,192,512]{2,1,0:T(8,128)(2,1)}, bf16[2,192,512]{2,1,0:T(8,128)(2,1)S(1)}, u32[]{:S(2)}, u32[]{:S(2)}) %collective-permute-start.7) | collective-permute-done | bytes 393248 | tf_op jit(solution)/shard_map/ppermute | solution.py:353
  56.8 3.6 %shard_map.110 = (bf16[208,640]{1,0:T(8,128)(2,1)}, bf16[208,640]{1,0:T(8,128)(2,1)}, f32[192,512]{1,0:T(8,128)S(1)}, f32[192,128]{1,0:T(8,128)S(1)}) custom-call(s32[4]{0:T(128)S(1)} %copy-done.13, bf16[2,192,512]{2,1,0:T(8,128)(2,1)S(1)} %collective-permute-done.7.refs_1_, bf16[192,512]{1,0:T(8,128)(2,1)S(1)} %collective-permute-done.8.refs_2_, ...), custom_call_target="tpu_custom_call" | custom-call | bytes 4194304 | tf_op jit(solution)/shard_map/pallas_call | solution.py:86
  60.4 6.6 %collective-permute-start.10 = (bf16[208,640]{1,0:T(8,128)(2,1)}, bf16[208,640]{1,0:T(8,128)(2,1)S(1)}, u32[]{:S(2)}, u32[]{:S(2)}) collective-permute-start(bf16[208,640]{1,0:T(8,128)(2,1)} %get-tuple-element.57), channel_id=1, source_target_pairs={{0,8},{8,16},{16,24},{1,9},{9,17},{17,25},{2,10},{10,18},{18,26},{... | collective-permute-start | bytes 798728 | tf_op jit(solution)/shard_map/ppermute | solution.py:367
  67.1 0.9 collective-permute-start.11
  67.9 5.3 %collective-permute-done.10.refs_0_ = bf16[208,640]{1,0:T(8,128)(2,1)S(1)} collective-permute-done((bf16[208,640]{1,0:T(8,128)(2,1)}, bf16[208,640]{1,0:T(8,128)(2,1)S(1)}, u32[]{:S(2)}, u32[]{:S(2)}) %collective-permute-start.10) | collective-permute-done | bytes 266272 | tf_op jit(solution)/shard_map/ppermute | solution.py:367
  73.2 3.4 %shard_map.111 = (bf16[96,8192]{1,0:T(8,128)(2,1)}, bf16[96,8192]{1,0:T(8,128)(2,1)S(1)}) custom-call(s32[4]{0:T(128)S(1)} %copy-done.13, bf16[208,640]{1,0:T(8,128)(2,1)S(1)} %collective-permute-done.10.refs_0_, bf16[208,640]{1,0:T(8,128)(2,1)S(1)} %collective-permute-done.11.refs_1_, f32[192,512]{1,0:T(8,128)S(1)} %get-tuple-element.59.refs_2_, ...), custom_call_target="tpu_custom_call" | custom-call | tf_op jit(solution)/shard_map/pallas_call | solution.py:468
  76.8 3.6 %collective-permute-done.12.other_ref = bf16[96,8192]{1,0:T(8,128)(2,1)S(1)} collective-permute-done((bf16[96,8192]{1,0:T(8,128)(2,1)}, bf16[96,8192]{1,0:T(8,128)(2,1)S(1)}, u32[]{:S(2)}, u32[]{:S(2)}) %collective-permute-start.12) | collective-permute-done | bytes 1572896 | tf_op jit(solution)/shard_map/ppermute | solution.py:109
  81.0 1.8 collective-permute-start.14
  82.8 1.4 collective-permute-start.15
  84.3 5.5 %shard_map.113 = (bf16[1024,384]{1,0:T(8,128)(2,1)}, bf16[384,1024]{1,0:T(8,128)(2,1)}, bf16[384,128]{1,0:T(8,128)(2,1)}, bf16[576,1024]{1,0:T(8,128)(2,1)}, bf1...) custom-call(s32[4]{0:T(128)} %get-tuple-element.55.refs_0_.info_ref, ...), custom_call_target="tpu_custom_call" | custom-call | tf_op jit(solution)/shard_map/pallas_call | solution.py:573
  89.8 3.0 %collective-permute-done.13.refs_1_ = bf16[24,8192]{1,0:T(8,128)(2,1)S(1)} collective-permute-done((bf16[24,8192]{1,0:T(8,128)(2,1)S(1)}, bf16[24,8192]{1,0:T(8,128)(2,1)S(1)}, u32[]{:S(2)}, u32[]{:S(2)}) %collective-permute-start.13) | collective-permute-done | bytes 393248 | tf_op jit(solution)/shard_map/ppermute | solution.py:109
  92.7 6.9 %collective-permute-done.14.refs_2_ = bf16[24,8192]{1,0:T(8,128)(2,1)S(1)} collective-permute-done((bf16[24,8192]{1,0:T(8,128)(2,1)S(1)}, bf16[24,8192]{1,0:T(8,128)(2,1)S(1)}, u32[]{:S(2)}, u32[]{:S(2)}) %collective-permute-start.14) | collective-permute-done | bytes 393248 | tf_op jit(solution)/shard_map/ppermute | solution.py:109
  99.7 1.6 collective-permute-done.15.refs_3_
  101.3 0.9 copy-done.11
  102.2 1.5 shard_map.114
  103.8 0.9 collective-permute-start.17
  104.7 1.5 collective-permute-start.18
  106.2 1.2 collective-permute-start.19
  107.4 2.7 %shard_map.115 = (f32[384,1024]{1,0:T(8,128)S(1)}, f32[128,1024]{1,0:T(8,128)S(1)}, bf16[384,128]{1,0:T(8,128)(2,1)S(1)}, f32[8,128]{1,0:T(8,128)S(1)}) custom-call(bf16[192,1024]{1,0:T(8,128)(2,1)S(1)} %get-tuple-element.71.refs_0_, bf16[192,1024]{1,0:T(8,128)(2,1)S(1)} %collective-permute-done.16.refs_1_, bf16[384,1024]{1,0:T(8,128)(2,1)S(1)} %copy-done.22, ...), custom_call_target="tpu_custom_call" | custom-call | flops 17179869184 | bytes 4194304 | tf_op jit(solution)/shard_map/pallas_call | solution.py:86
  110.2 5.8 %collective-permute-done.17.refs_0_ = bf16[192,1024]{1,0:T(8,128)(2,1)S(1)} collective-permute-done((bf16[192,1024]{1,0:T(8,128)(2,1)}, bf16[192,1024]{1,0:T(8,128)(2,1)S(1)}, u32[]{:S(2)}, u32[]{:S(2)}) %collective-permute-start.17) | collective-permute-done | bytes 393248 | tf_op jit(solution)/shard_map/ppermute | solution.py:109
  116.0 8.5 %collective-permute-done.18.refs_0_ = bf16[192,1024]{1,0:T(8,128)(2,1)S(1)} collective-permute-done((bf16[192,1024]{1,0:T(8,128)(2,1)}, bf16[192,1024]{1,0:T(8,128)(2,1)S(1)}, u32[]{:S(2)}, u32[]{:S(2)}) %collective-permute-start.18) | collective-permute-done | bytes 393248 | tf_op jit(solution)/shard_map/ppermute | solution.py:109
  125.1 4.2 %shard_map.119 = (f32[384,1024]{1,0:T(8,128)S(1)}, f32[128,1024]{1,0:T(8,128)S(1)}, bf16[576,128]{1,0:T(8,128)(2,1)S(1)}, f32[8,128]{1,0:T(8,128)}) custom-call(bf16[192,1024]{1,0:T(8,128)(2,1)S(1)} %shard_map.116.refs_0_, bf16[192,1024]{1,0:T(8,128)(2,1)S(1)} %shard_map.117.refs_1_, bf16[192,1024]{1,0:T(8,128)(2,1)S(1)} %shard_map.118.refs_2_, ...), custom_call_target="tpu_custom_call" | custom-call | flops 17179869184 | bytes 4194304 | tf_op jit(solution)/shard_map/pallas_call | solution.py:86
  129.4 5.2 %shard_map.120 = (bf16[1024,384]{1,0:T(8,128)(2,1)}, bf16[1280,128]{1,0:T(8,128)(2,1)}, bf16[2,256,128]{2,1,0:T(8,128)(2,1)S(1)}) custom-call(s32[4]{0:T(128)S(1)} %copy-done.14, bf16[192,1024]{1,0:T(8,128)(2,1)S(1)} %collective-permute-done.20.refs_1_, bf16[192,1024]{1,0:T(8,128)(2,1)S(1)} %collective-permute-done.21.refs_2_, ...), custom_call_target="tpu_custom_call" | custom-call | flops 17179869184 | bytes 4194304 | tf_op jit(solution)/shard_map/pallas_call | solution.py:86
  134.6 10.0 %all-to-all-start = ((bf16[32,32,384]{2,1,0:T(8,128)(2,1)}), bf16[32,32,384]{2,1,0:T(8,128)(2,1)S(1)}, u32[]{:S(2)}, u32[]{:S(2)}) async-start(bf16[32,32,384]{2,1,0:T(8,128)(2,1)} %bitcast.5), calls=%async_computation | async-start | bytes 1572864 | tf_op jit(solution)/shard_map/all_to_all | solution.py:868
  144.9 1.6 collective-permute-done.23.refs_3_
  146.5 0.8 shard_map.121
  147.3 1.8 %collective-permute-start.24 = (bf16[896,128]{1,0:T(8,128)(2,1)}, bf16[896,128]{1,0:T(8,128)(2,1)S(1)}, u32[]{:S(2)}, u32[]{:S(2)}) collective-permute-start(bf16[896,128]{1,0:T(8,128)(2,1)} %get-tuple-element.89), channel_id=1, source_target_pairs={{0,2},{1,3},{2,0},{3,1},{4,6},{5,7},{6,4},{7,5},{8,10},{9,11},{10,... | collective-permute-start | bytes 688136 | tf_op jit(solution)/shard_map/ppermute | solution.py:109
  149.2 1.5 collective-permute-start.25
  150.9 9.3 %collective-permute-done.24.refs_1_.refs_2_ = bf16[896,128]{1,0:T(8,128)(2,1)S(1)} collective-permute-done((bf16[896,128]{1,0:T(8,128)(2,1)}, bf16[896,128]{1,0:T(8,128)(2,1)S(1)}, u32[]{:S(2)}, u32[]{:S(2)}) %collective-permute-start.24) | collective-permute-done | bytes 229408 | tf_op jit(solution)/shard_map/ppermute | solution.py:109
  160.2 1.3 shard_map.123
  161.6 1.6 collective-permute-start.27
  163.1 2.3 %collective-permute-start.28 = (bf16[256,128]{1,0:T(8,128)(2,1)}, bf16[256,128]{1,0:T(8,128)(2,1)S(1)}, u32[]{:S(2)}, u32[]{:S(2)}) collective-permute-start(bf16[256,128]{1,0:T(8,128)(2,1)} %get-tuple-element.97), channel_id=1, source_target_pairs={{0,16},{8,24},{16,0},{24,8},{1,17},{9,25},{17,1},{25,9},{2,18},{10... | collective-permute-start | bytes 196616 | tf_op jit(solution)/shard_map/ppermute | solution.py:811
  166.7 3.7 %shard_map.122 = (bf16[192,1024]{1,0:T(8,128)(2,1)}, f32[8,128]{1,0:T(8,128)}) custom-call(s32[4]{0:T(128)} %get-tuple-element.55.refs_0_.info_ref, f32[192,1024]{1,0:T(8,128)} %get-tuple-element.70.state_ref, bf16[1,1024,1024]{2,1,0:T(8,128)(2,1)} %w_ref.5, bf16[896,128]{1,0:T(8,128)(2,1)} %copy-done.2, bf16[896,128]{1,0:T(8,128)(2,1)} %copy-done.3, ...), custom_call_target="tpu_custom_call" | custom-call | tf_op jit(solution)/shard_map/pallas_call | solution.py:880
  170.4 0.7 copy-done.18
  172.4 0.9 copy-done.25
  173.3 2.1 %shard_map.125 = (f32[1,32,3072]{2,1,0:T(8,128)}, f32[1,32,1024]{2,1,0:T(8,128)}) custom-call(bf16[32,32,384]{2,1,0:T(8,128)(2,1)} %copy-done.25, bf16[256,128]{1,0:T(8,128)(2,1)} %copy-done.10, bf16[256,128]{1,0:T(8,128)(2,1)} %copy-done.28, bf16[256,128]{1,0:T(8,128)(2,1)} %copy-done.29, bf16[256,128]{1,0:T(8,128)(2,1)} %copy-done.30), custom_call_target="tpu_custom_call" | custom-call | tf_op jit(solution)/shard_map/pallas_call | solution.py:888
  (109 shorter events, 10.7 us)
Async XLA Ops:
  7.2 77.1 %all-gather.2.cloned.1.call-start = ((), (), s32[]{:S(2)}) async-start(), calls=%async_computation.1 | async-start | bytes 3538944 | tf_op jit(solution)/shard_map/all_gather | solution.py:862
  8.5 5.3 %collective-permute-start = (bf16[24,8192]{1,0:T(8,128)(2,1)S(1)}, bf16[24,8192]{1,0:T(8,128)(2,1)S(1)}, u32[]{:S(2)}, u32[]{:S(2)}) collective-permute-start(bf16[24,8192]{1,0:T(8,128)(2,1)S(1)} %shard_map.103.refs_0_), channel_id=1, source_target_pairs={{0,1},{1,0},{2,3},{3,2},{4,5},{5,4},{6,7},{7,6},{8,9},{9,8},{10,11... | collective-permute-start | bytes 1179656 | tf_op jit(solution)/shard_map/ppermute | solution.py:109
  9.1 12.5 %collective-permute-start.1 = (bf16[24,8192]{1,0:T(8,128)(2,1)S(1)}, bf16[24,8192]{1,0:T(8,128)(2,1)S(1)}, u32[]{:S(2)}, u32[]{:S(2)}) collective-permute-start(bf16[24,8192]{1,0:T(8,128)(2,1)S(1)} %shard_map.103.refs_0_), channel_id=1, source_target_pairs={{0,2},{1,3},{2,0},{3,1},{4,6},{5,7},{6,4},{7,5},{8,10},{9,11},{10,... | collective-permute-start | bytes 1179656 | tf_op jit(solution)/shard_map/ppermute | solution.py:109
  11.6 19.6 %collective-permute-start.2 = (bf16[24,8192]{1,0:T(8,128)(2,1)S(1)}, bf16[24,8192]{1,0:T(8,128)(2,1)S(1)}, u32[]{:S(2)}, u32[]{:S(2)}) collective-permute-start(bf16[24,8192]{1,0:T(8,128)(2,1)S(1)} %shard_map.103.refs_0_), channel_id=1, source_target_pairs={{0,4},{1,5},{2,6},{3,7},{4,0},{5,1},{6,2},{7,3},{8,12},{9,13},{10,... | collective-permute-start | bytes 1179656 | tf_op jit(solution)/shard_map/ppermute | solution.py:109
  13.1 18.8 %collective-permute-start.3 = (bf16[24,8192]{1,0:T(8,128)(2,1)S(1)}, bf16[24,8192]{1,0:T(8,128)(2,1)S(1)}, u32[]{:S(2)}, u32[]{:S(2)}) collective-permute-start(bf16[24,8192]{1,0:T(8,128)(2,1)S(1)} %shard_map.103.refs_0_), channel_id=1, source_target_pairs={{0,6},{1,7},{2,4},{3,5},{4,2},{5,3},{6,0},{7,1},{8,14},{9,15},{10,... | collective-permute-start | bytes 1179656 | tf_op jit(solution)/shard_map/ppermute | solution.py:109
  19.2 15.2 %copy-start.1 = (bf16[24,8192]{1,0:T(8,128)(2,1)S(1)}, bf16[24,8192]{1,0:T(8,128)(2,1)}, u32[]{:S(2)}) copy-start(bf16[24,8192]{1,0:T(8,128)(2,1)} %copy-done) | copy-start | bytes 1179652
  19.2 15.2 %copy-start.5 = (bf16[192,1024]{1,0:T(8,128)(2,1)S(1)}, bf16[192,1024]{1,0:T(8,128)(2,1)}, u32[]{:S(2)}) copy-start(bf16[192,1024]{1,0:T(8,128)(2,1)} %refs_9_.1) | copy-start | bytes 1179652
  22.3 10.8 %collective-permute-start.4 = (bf16[24,8192]{1,0:T(8,128)(2,1)S(1)}, bf16[24,8192]{1,0:T(8,128)(2,1)S(1)}, u32[]{:S(2)}, u32[]{:S(2)}) collective-permute-start(bf16[24,8192]{1,0:T(8,128)(2,1)S(1)} %shard_map.105.refs_1_), channel_id=1, source_target_pairs={{0,1},{1,0},{2,3},{3,2},{4,5},{5,4},{6,7},{7,6},{8,9},{9,8},{10,11... | collective-permute-start | bytes 1179656 | tf_op jit(solution)/shard_map/ppermute | solution.py:109
  31.9 1.7 collective-permute-start.5
  32.6 1.9 %collective-permute-start.6 = (bf16[24,8192]{1,0:T(8,128)(2,1)S(1)}, bf16[24,8192]{1,0:T(8,128)(2,1)S(1)}, u32[]{:S(2)}, u32[]{:S(2)}) collective-permute-start(bf16[24,8192]{1,0:T(8,128)(2,1)S(1)} %shard_map.107.refs_3_), channel_id=1, source_target_pairs={{0,1},{1,0},{2,3},{3,2},{4,5},{5,4},{6,7},{7,6},{8,9},{9,8},{10,11... | collective-permute-start | bytes 1179656 | tf_op jit(solution)/shard_map/ppermute | solution.py:109
  34.4 9.0 %copy-start.31 = (s32[8]{0:T(128)S(1)}, s32[8]{0:T(128)}, u32[]{:S(2)}) copy-start(s32[8]{0:T(128)} %constant.45.clone) | copy-start | bytes 100
  43.4 12.7 %collective-permute-start.7 = (bf16[2,192,512]{2,1,0:T(8,128)(2,1)}, bf16[2,192,512]{2,1,0:T(8,128)(2,1)S(1)}, u32[]{:S(2)}, u32[]{:S(2)}) collective-permute-start(bf16[2,192,512]{2,1,0:T(8,128)(2,1)} %get-tuple-element.56.refs_6_), channel_id=1, source_target_pairs={{0,8},{16,24},{1,9},{17,25},{2,10},{18,26},{3,11},{19,27},{4,12},{... | collective-permute-start | bytes 1179656 | tf_op jit(solution)/shard_map/ppermute | solution.py:353
  47.1 6.7 %collective-permute-start.8 = (bf16[192,512]{1,0:T(8,128)(2,1)}, bf16[192,512]{1,0:T(8,128)(2,1)S(1)}, u32[]{:S(2)}, u32[]{:S(2)}) collective-permute-start(bf16[192,512]{1,0:T(8,128)(2,1)} %get-tuple-element.54._.refs_5_), channel_id=1, source_target_pairs={{24,8},{25,9},{26,10},{27,11},{28,12},{29,13},{30,14},{31,15}} | collective-permute-start | bytes 589832 | tf_op jit(solution)/shard_map/ppermute | solution.py:354
  47.8 6.0 %collective-permute-start.9 = (bf16[192,512]{1,0:T(8,128)(2,1)}, bf16[192,512]{1,0:T(8,128)(2,1)S(1)}, u32[]{:S(2)}, u32[]{:S(2)}) collective-permute-start(bf16[192,512]{1,0:T(8,128)(2,1)} %get-tuple-element.54._.refs_5_), channel_id=1, source_target_pairs={{16,8},{17,9},{18,10},{19,11},{20,12},{21,13},{22,14},{23,15}} | collective-permute-start | bytes 589832 | tf_op jit(solution)/shard_map/ppermute | solution.py:354
  48.6 7.6 %copy-start.4 = (bf16[192,512]{1,0:T(8,128)(2,1)S(1)}, bf16[192,512]{1,0:T(8,128)(2,1)}, u32[]{:S(2)}) copy-start(bf16[192,512]{1,0:T(8,128)(2,1)} %get-tuple-element.54._.refs_5_) | copy-start | bytes 589828
  48.6 7.6 %copy-start.8 = (bf16[2,192,512]{2,1,0:T(8,128)(2,1)S(1)}, bf16[2,192,512]{2,1,0:T(8,128)(2,1)}, u32[]{:S(2)}) copy-start(bf16[2,192,512]{2,1,0:T(8,128)(2,1)} %get-tuple-element.56.refs_6_) | copy-start | bytes 1179652
  60.4 12.8 %collective-permute-start.10 = (bf16[208,640]{1,0:T(8,128)(2,1)}, bf16[208,640]{1,0:T(8,128)(2,1)S(1)}, u32[]{:S(2)}, u32[]{:S(2)}) collective-permute-start(bf16[208,640]{1,0:T(8,128)(2,1)} %get-tuple-element.57), channel_id=1, source_target_pairs={{0,8},{8,16},{16,24},{1,9},{9,17},{17,25},{2,10},{10,18},{18,26},{... | collective-permute-start | bytes 798728 | tf_op jit(solution)/shard_map/ppermute | solution.py:367
  67.1 6.2 %collective-permute-start.11 = (bf16[208,640]{1,0:T(8,128)(2,1)}, bf16[208,640]{1,0:T(8,128)(2,1)S(1)}, u32[]{:S(2)}, u32[]{:S(2)}) collective-permute-start(bf16[208,640]{1,0:T(8,128)(2,1)} %get-tuple-element.58), channel_id=1, source_target_pairs={{8,24},{9,25},{10,26},{11,27},{12,28},{13,29},{14,30},{15,31}} | collective-permute-start | bytes 798728 | tf_op jit(solution)/shard_map/ppermute | solution.py:366
  76.7 3.7 %collective-permute-start.12 = (bf16[96,8192]{1,0:T(8,128)(2,1)}, bf16[96,8192]{1,0:T(8,128)(2,1)S(1)}, u32[]{:S(2)}, u32[]{:S(2)}) collective-permute-start(bf16[96,8192]{1,0:T(8,128)(2,1)} %get-tuple-element.63), channel_id=1, source_target_pairs={{0,1},{1,0},{2,3},{3,2},{4,5},{5,4},{6,7},{7,6},{8,9},{9,8},{10,11... | collective-permute-start | bytes 4718600 | tf_op jit(solution)/shard_map/ppermute | solution.py:109
  80.7 12.0 %collective-permute-start.13 = (bf16[24,8192]{1,0:T(8,128)(2,1)S(1)}, bf16[24,8192]{1,0:T(8,128)(2,1)S(1)}, u32[]{:S(2)}, u32[]{:S(2)}) collective-permute-start(bf16[24,8192]{1,0:T(8,128)(2,1)S(1)} %get-tuple-element.65), channel_id=1, source_target_pairs={{0,2},{1,3},{2,0},{3,1},{4,6},{5,7},{6,4},{7,5},{8,10},{9,11},{10,... | collective-permute-start | bytes 1179656 | tf_op jit(solution)/shard_map/ppermute | solution.py:109
  81.0 18.6 %collective-permute-start.14 = (bf16[24,8192]{1,0:T(8,128)(2,1)S(1)}, bf16[24,8192]{1,0:T(8,128)(2,1)S(1)}, u32[]{:S(2)}, u32[]{:S(2)}) collective-permute-start(bf16[24,8192]{1,0:T(8,128)(2,1)S(1)} %get-tuple-element.66), channel_id=1, source_target_pairs={{0,4},{1,5},{2,6},{3,7},{4,0},{5,1},{6,2},{7,3},{8,12},{9,13},{10,... | collective-permute-start | bytes 1179656 | tf_op jit(solution)/shard_map/ppermute | solution.py:109
  82.8 18.5 %copy-start.6 = (bf16[192,1024]{1,0:T(8,128)(2,1)S(1)}, bf16[192,1024]{1,0:T(8,128)(2,1)}, u32[]{:S(2)}) copy-start(bf16[192,1024]{1,0:T(8,128)(2,1)} %refs_4_.1) | copy-start | bytes 1179652
  82.8 18.5 %collective-permute-start.15 = (bf16[24,8192]{1,0:T(8,128)(2,1)S(1)}, bf16[24,8192]{1,0:T(8,128)(2,1)S(1)}, u32[]{:S(2)}, u32[]{:S(2)}) collective-permute-start(bf16[24,8192]{1,0:T(8,128)(2,1)S(1)} %get-tuple-element.67), channel_id=1, source_target_pairs={{0,6},{1,7},{2,4},{3,5},{4,2},{5,3},{6,0},{7,1},{8,14},{9,15},{10,... | collective-permute-start | bytes 1179656 | tf_op jit(solution)/shard_map/ppermute | solution.py:109
  102.2 5.2 %copy-start.12 = (bf16[384,128]{1,0:T(8,128)(2,1)S(1)}, bf16[384,128]{1,0:T(8,128)(2,1)}, u32[]{:S(2)}) copy-start(bf16[384,128]{1,0:T(8,128)(2,1)} %get-tuple-element.69.refs_5_.refs_3_) | copy-start | bytes 294916
  102.2 5.2 %copy-start.21 = (bf16[1024,384]{1,0:T(8,128)(2,1)S(1)}, bf16[1024,384]{1,0:T(8,128)(2,1)}, u32[]{:S(2)}) copy-start(bf16[1024,384]{1,0:T(8,128)(2,1)} %get-tuple-element.74.refs_4_.refs_5_.refs_6_) | copy-start | bytes 2359300
  102.2 5.2 %copy-start.22 = (bf16[384,1024]{1,0:T(8,128)(2,1)S(1)}, bf16[384,1024]{1,0:T(8,128)(2,1)}, u32[]{:S(2)}) copy-start(bf16[384,1024]{1,0:T(8,128)(2,1)} %get-tuple-element.73.refs_2_) | copy-start | bytes 2359300
  103.8 3.6 %collective-permute-start.16 = (bf16[192,1024]{1,0:T(8,128)(2,1)}, bf16[192,1024]{1,0:T(8,128)(2,1)S(1)}, u32[]{:S(2)}, u32[]{:S(2)}) collective-permute-start(bf16[192,1024]{1,0:T(8,128)(2,1)} %get-tuple-element.72), channel_id=1, source_target_pairs={{0,1},{1,0},{2,3},{3,2},{4,5},{5,4},{6,7},{7,6},{8,9},{9,8},{10,11... | collective-permute-start | bytes 1179656 | tf_op jit(solution)/shard_map/ppermute | solution.py:109
  103.8 12.2 %collective-permute-start.17 = (bf16[192,1024]{1,0:T(8,128)(2,1)}, bf16[192,1024]{1,0:T(8,128)(2,1)S(1)}, u32[]{:S(2)}, u32[]{:S(2)}) collective-permute-start(bf16[192,1024]{1,0:T(8,128)(2,1)} %get-tuple-element.72), channel_id=1, source_target_pairs={{0,2},{1,3},{2,0},{3,1},{4,6},{5,7},{6,4},{7,5},{8,10},{9,11},{10,... | collective-permute-start | bytes 1179656 | tf_op jit(solution)/shard_map/ppermute | solution.py:109
  104.7 19.8 %collective-permute-start.18 = (bf16[192,1024]{1,0:T(8,128)(2,1)}, bf16[192,1024]{1,0:T(8,128)(2,1)S(1)}, u32[]{:S(2)}, u32[]{:S(2)}) collective-permute-start(bf16[192,1024]{1,0:T(8,128)(2,1)} %get-tuple-element.72), channel_id=1, source_target_pairs={{0,4},{1,5},{2,6},{3,7},{4,0},{5,1},{6,2},{7,3},{8,12},{9,13},{10,... | collective-permute-start | bytes 1179656 | tf_op jit(solution)/shard_map/ppermute | solution.py:109
  106.2 18.3 %collective-permute-start.19 = (bf16[192,1024]{1,0:T(8,128)(2,1)}, bf16[192,1024]{1,0:T(8,128)(2,1)S(1)}, u32[]{:S(2)}, u32[]{:S(2)}) collective-permute-start(bf16[192,1024]{1,0:T(8,128)(2,1)} %get-tuple-element.72), channel_id=1, source_target_pairs={{0,6},{1,7},{2,4},{3,5},{4,2},{5,3},{6,0},{7,1},{8,14},{9,15},{10,... | collective-permute-start | bytes 1179656 | tf_op jit(solution)/shard_map/ppermute | solution.py:109
  110.2 14.9 %copy-start.20 = (bf16[576,1024]{1,0:T(8,128)(2,1)S(1)}, bf16[576,1024]{1,0:T(8,128)(2,1)}, u32[]{:S(2)}) copy-start(bf16[576,1024]{1,0:T(8,128)(2,1)} %get-tuple-element.77.refs_3_) | copy-start | bytes 3538948
  110.2 14.9 %copy-start.24 = (bf16[576,128]{1,0:T(8,128)(2,1)S(1)}, bf16[576,128]{1,0:T(8,128)(2,1)}, u32[]{:S(2)}) copy-start(bf16[576,128]{1,0:T(8,128)(2,1)} %get-tuple-element.78.refs_4_) | copy-start | bytes 442372
  116.0 13.3 %collective-permute-start.20 = (bf16[192,1024]{1,0:T(8,128)(2,1)S(1)}, bf16[192,1024]{1,0:T(8,128)(2,1)S(1)}, u32[]{:S(2)}, u32[]{:S(2)}) collective-permute-start(bf16[192,1024]{1,0:T(8,128)(2,1)S(1)} %shard_map.116.refs_0_), channel_id=1, source_target_pairs={{0,1},{1,0},{2,3},{3,2},{4,5},{5,4},{6,7},{7,6},{8,9},{9,8},{10,11... | collective-permute-start | bytes 1179656 | tf_op jit(solution)/shard_map/ppermute | solution.py:109
  124.5 4.8 %collective-permute-start.21 = (bf16[192,1024]{1,0:T(8,128)(2,1)S(1)}, bf16[192,1024]{1,0:T(8,128)(2,1)S(1)}, u32[]{:S(2)}, u32[]{:S(2)}) collective-permute-start(bf16[192,1024]{1,0:T(8,128)(2,1)S(1)} %shard_map.117.refs_1_), channel_id=1, source_target_pairs={{0,1},{1,0},{2,3},{3,2},{4,5},{5,4},{6,7},{7,6},{8,9},{9,8},{10,11... | collective-permute-start | bytes 1179656 | tf_op jit(solution)/shard_map/ppermute | solution.py:109
  124.5 4.8 %collective-permute-start.22 = (bf16[192,1024]{1,0:T(8,128)(2,1)S(1)}, bf16[192,1024]{1,0:T(8,128)(2,1)S(1)}, u32[]{:S(2)}, u32[]{:S(2)}) collective-permute-start(bf16[192,1024]{1,0:T(8,128)(2,1)S(1)} %shard_map.118.refs_2_), channel_id=1, source_target_pairs={{0,1},{1,0},{2,3},{3,2},{4,5},{5,4},{6,7},{7,6},{8,9},{9,8},{10,11... | collective-permute-start | bytes 1179656 | tf_op jit(solution)/shard_map/ppermute | solution.py:109
  125.1 4.3 %copy-start.19 = (bf16[576,1024]{1,0:T(8,128)(2,1)S(1)}, bf16[576,1024]{1,0:T(8,128)(2,1)}, u32[]{:S(2)}) copy-start(bf16[576,1024]{1,0:T(8,128)(2,1)} %get-tuple-element.82.refs_4_) | copy-start | bytes 3538948
  125.1 4.3 %copy-start.23 = (bf16[576,128]{1,0:T(8,128)(2,1)S(1)}, bf16[576,128]{1,0:T(8,128)(2,1)}, u32[]{:S(2)}) copy-start(bf16[576,128]{1,0:T(8,128)(2,1)} %get-tuple-element.83.refs_5_) | copy-start | bytes 442372
  134.6 37.1 %all-to-all-start = ((bf16[32,32,384]{2,1,0:T(8,128)(2,1)}), bf16[32,32,384]{2,1,0:T(8,128)(2,1)S(1)}, u32[]{:S(2)}, u32[]{:S(2)}) async-start(bf16[32,32,384]{2,1,0:T(8,128)(2,1)} %bitcast.5), calls=%async_computation | async-start | bytes 1572864 | tf_op jit(solution)/shard_map/all_to_all | solution.py:868
  144.6 1.9 %collective-permute-start.23 = (bf16[1280,128]{1,0:T(8,128)(2,1)}, bf16[1280,128]{1,0:T(8,128)(2,1)S(1)}, u32[]{:S(2)}, u32[]{:S(2)}) collective-permute-start(bf16[1280,128]{1,0:T(8,128)(2,1)} %get-tuple-element.87), channel_id=1, source_target_pairs={{0,1},{1,0},{2,3},{3,2},{4,5},{5,4},{6,7},{7,6},{8,9},{9,8},{10,11... | collective-permute-start | bytes 983048 | tf_op jit(solution)/shard_map/ppermute | solution.py:109
  147.3 18.7 %copy-start.2 = (bf16[896,128]{1,0:T(8,128)(2,1)}, bf16[896,128]{1,0:T(8,128)(2,1)S(1)}, u32[]{:S(2)}) copy-start(bf16[896,128]{1,0:T(8,128)(2,1)S(1)} %get-tuple-element.88.refs_0_.refs_1_) | copy-start | bytes 688132
  147.3 12.9 %collective-permute-start.24 = (bf16[896,128]{1,0:T(8,128)(2,1)}, bf16[896,128]{1,0:T(8,128)(2,1)S(1)}, u32[]{:S(2)}, u32[]{:S(2)}) collective-permute-start(bf16[896,128]{1,0:T(8,128)(2,1)} %get-tuple-element.89), channel_id=1, source_target_pairs={{0,2},{1,3},{2,0},{3,1},{4,6},{5,7},{6,4},{7,5},{8,10},{9,11},{10,... | collective-permute-start | bytes 688136 | tf_op jit(solution)/shard_map/ppermute | solution.py:109
  149.2 16.9 %collective-permute-start.25 = (bf16[384,128]{1,0:T(8,128)(2,1)}, bf16[384,128]{1,0:T(8,128)(2,1)S(1)}, u32[]{:S(2)}, u32[]{:S(2)}) collective-permute-start(bf16[384,128]{1,0:T(8,128)(2,1)} %get-tuple-element.90), channel_id=1, source_target_pairs={{0,4},{1,5},{2,6},{3,7},{4,0},{5,1},{6,2},{7,3},{8,12},{9,13},{10,... | collective-permute-start | bytes 294920 | tf_op jit(solution)/shard_map/ppermute | solution.py:109
  150.6 15.4 %collective-permute-start.26 = (bf16[384,128]{1,0:T(8,128)(2,1)}, bf16[384,128]{1,0:T(8,128)(2,1)S(1)}, u32[]{:S(2)}, u32[]{:S(2)}) collective-permute-start(bf16[384,128]{1,0:T(8,128)(2,1)} %get-tuple-element.91), channel_id=1, source_target_pairs={{0,6},{1,7},{2,4},{3,5},{4,2},{5,3},{6,0},{7,1},{8,14},{9,15},{10,... | collective-permute-start | bytes 294920 | tf_op jit(solution)/shard_map/ppermute | solution.py:109
  160.2 5.8 %copy-start.3 = (bf16[896,128]{1,0:T(8,128)(2,1)}, bf16[896,128]{1,0:T(8,128)(2,1)S(1)}, u32[]{:S(2)}) copy-start(bf16[896,128]{1,0:T(8,128)(2,1)S(1)} %collective-permute-done.24.refs_1_.refs_2_) | copy-start | bytes 688132
  161.6 8.8 %copy-start.9 = (bf16[256,128]{1,0:T(8,128)(2,1)S(1)}, bf16[256,128]{1,0:T(8,128)(2,1)}, u32[]{:S(2)}) copy-start(bf16[256,128]{1,0:T(8,128)(2,1)} %get-tuple-element.94.refs_0_) | copy-start | bytes 196612
  161.6 10.1 %collective-permute-start.27 = (bf16[256,128]{1,0:T(8,128)(2,1)}, bf16[256,128]{1,0:T(8,128)(2,1)S(1)}, u32[]{:S(2)}, u32[]{:S(2)}) collective-permute-start(bf16[256,128]{1,0:T(8,128)(2,1)} %get-tuple-element.96), channel_id=1, source_target_pairs={{0,8},{8,0},{16,24},{24,16},{1,9},{9,1},{17,25},{25,17},{2,10},{10... | collective-permute-start | bytes 196616 | tf_op jit(solution)/shard_map/ppermute | solution.py:811
  163.1 8.5 %collective-permute-start.28 = (bf16[256,128]{1,0:T(8,128)(2,1)}, bf16[256,128]{1,0:T(8,128)(2,1)S(1)}, u32[]{:S(2)}, u32[]{:S(2)}) collective-permute-start(bf16[256,128]{1,0:T(8,128)(2,1)} %get-tuple-element.97), channel_id=1, source_target_pairs={{0,16},{8,24},{16,0},{24,8},{1,17},{9,25},{17,1},{25,9},{2,18},{10... | collective-permute-start | bytes 196616 | tf_op jit(solution)/shard_map/ppermute | solution.py:811
  165.4 6.3 %collective-permute-start.29 = (bf16[256,128]{1,0:T(8,128)(2,1)}, bf16[256,128]{1,0:T(8,128)(2,1)S(1)}, u32[]{:S(2)}, u32[]{:S(2)}) collective-permute-start(bf16[256,128]{1,0:T(8,128)(2,1)} %get-tuple-element.98), channel_id=1, source_target_pairs={{0,24},{8,16},{16,8},{24,0},{1,25},{9,17},{17,9},{25,1},{2,26},{10... | collective-permute-start | bytes 196616 | tf_op jit(solution)/shard_map/ppermute | solution.py:811
  (16 other events, 15.0 us)
Sparse Core Ops, SparseCore 0:
  43.5 32.6 all-gather.1

commit v4 on v3

--- a/solution.py
+++ b/solution.py
@@ -17,8 +17,9 @@
 BF16 = jnp.bfloat16
 MIB = 1 << 20
 LARGE = 60
-TOKEN = jax.ShapeDtypeStruct((8, 128), jnp.float32)
+TOKEN = pltpu.VMEM((8, 128), jnp.float32)
 LANES = 128
+EDGE_ROWS = 16
 
 
 def params(mib):
@@ -28,7 +29,7 @@
 def call(body, outs, scratch=(), mib=32):
     return pl.pallas_call(
         body,
-        out_shape=[jax.ShapeDtypeStruct(shape, dtype) for shape, dtype in outs],
+        out_shape=[out if out is TOKEN else jax.ShapeDtypeStruct(*out) for out in outs],
         scratch_shapes=list(scratch),
         compiler_params=params(mib),
     )
@@ -90,7 +91,7 @@
         + [free] * (len(held) + len(tokens)),
         out_specs=[there] * len(sent) + [here] * len(outs),
         out_shape=[pltpu.HBM(shape, dtype) for shape, dtype in sent]
-        + [jax.ShapeDtypeStruct(shape, dtype) for shape, dtype in outs],
+        + [out if out is TOKEN else jax.ShapeDtypeStruct(*out) for out in outs],
         scratch_shapes=[pltpu.VMEM(value.shape, value.dtype) for value in held]
         + [pltpu.VMEM(shape, dtype) for shape, dtype in sent]
         + list(scratch)
@@ -122,7 +123,7 @@
     pass
 
 
-def tie(value, *after):
+def tie(value, *after, mib=1):
     there = pl.BlockSpec(memory_space=pl.ANY)
     return pl.pallas_call(
         tie_body,
@@ -130,7 +131,7 @@
         out_specs=there,
         out_shape=jax.ShapeDtypeStruct(value.shape, value.dtype),
         input_output_aliases={0: 0},
-        compiler_params=params(1),
+        compiler_params=params(mib),
     )(value, *after)
 
 
@@ -200,9 +201,9 @@
     return jnp.concatenate([ref[...].astype(F32) for ref in refs], axis=0).astype(BF16)
 
 
-def project_body(count, *refs):
+def project_body(count, tp_count, info_ref, *refs):
     x_refs, refs = refs[:count], refs[count:]
-    first_ref, pass_ref, w_ref, q, kv, passed, held, sems = refs
+    first_ref, pass_ref, w_ref, q, kv, passed, held, wide, sems = refs
     kinds, rows, _ = held.shape
     depth = math.gcd(rows, 1024)
     copies = {}
@@ -214,6 +215,7 @@
             )
             copies[c, k].start()
     x = stack(x_refs)
+    count_rows = x.shape[0]
     passed.ref[...] = pass_ref[...]
     passed.send()
     for c in range(kinds + 1):
@@ -232,42 +234,50 @@
             if c < 2:
                 part = part * lax.rsqrt(jnp.mean(part * part, axis=-1, keepdims=True) + EPS)
             if c == 0:
-                q.ref[:, at] = part.astype(BF16)
+                wide[:, at] = part
             else:
-                kv.ref[c - 1, :, at] = part.astype(BF16)
+                kv.ref[(c - 1) * count_rows : c * count_rows, at] = part.astype(BF16)
         if c == 0:
+            q.ref[...] = wide[...].astype(BF16)
             q.send()
-
-
-def project(pieces, first, weights, passed):
+            last = wide[pl.ds(last_row(info_ref, count_rows, tp_count), 1), :]
+            spread = jnp.broadcast_to(last, (EDGE_ROWS, last.shape[1]))
+            kv.ref[kinds * count_rows :, :] = spread.astype(BF16)
+
+
+def project(info, pieces, first, weights, passed, tp_count):
     rows = sum(piece.shape[0] for piece in pieces)
     kinds, deep, width = weights.shape
     here, there = pl.BlockSpec(memory_space=pltpu.VMEM), pl.BlockSpec(memory_space=pltpu.HBM)
-    outs = [((rows, width), BF16), ((kinds - 1, rows, width), BF16), (passed.shape, passed.dtype)]
+    outs = [((rows, width), BF16), (((kinds - 1) * rows + EDGE_ROWS, width), BF16)]
+    outs.append((passed.shape, passed.dtype))
     count = len(pieces)
 
     def body(*refs):
-        in_refs, far, near = refs[: count + 3], refs[count + 3 : count + 6], refs[count + 6 : count + 9]
-        held, sems, out_sems = refs[count + 9 :]
+        in_refs, refs = refs[: count + 4], refs[count + 4 :]
+        far, near, (held, wide, sems, out_sems) = refs[:3], refs[3:6], refs[6:]
         outputs = [Sent(n, f, out_sems.at[i]) for i, (f, n) in enumerate(zip(far, near))]
-        project_body(count, *in_refs, *outputs, held, sems)
+        project_body(count, tp_count, *in_refs, *outputs, held, wide, sems)
         outputs[1].send()
         for output in outputs:
             output.copy.wait()
 
     return pl.pallas_call(
         body,
-        in_specs=[here] * (count + 2) + [pl.BlockSpec(memory_space=pl.ANY)],
+        in_specs=[pl.BlockSpec(memory_space=pltpu.SMEM)]
+        + [here] * (count + 2)
+        + [pl.BlockSpec(memory_space=pl.ANY)],
         out_specs=[there] * 3,
         out_shape=[pltpu.HBM(shape, dtype) for shape, dtype in outs],
         scratch_shapes=[pltpu.VMEM(shape, dtype) for shape, dtype in outs]
         + [
             pltpu.VMEM((kinds - 1, deep, width), BF16),
+            pltpu.VMEM((rows, width), F32),
             pltpu.SemaphoreType.DMA(((kinds - 1) * deep // math.gcd(deep, 1024),)),
             pltpu.SemaphoreType.DMA((3,)),
         ],
         compiler_params=params(40),
-    )(*pieces, first, passed, weights)
+    )(info, *pieces, first, passed, weights)
 
 
 def heads_of(ref_width):
@@ -289,83 +299,113 @@
     return high + pltpu.roll(dens - high, count, 1)
 
 
-def attend_body(tp_count, info_ref, kv_in_ref, q3_ref, q2_ref, mask_ref, *refs):
-    q_in, kv_here, back3, back2, top_ref, den_ref, far_top, far_den = refs
-    back3_ref, back2_ref = back3.ref, back2.ref
-    q_ref, kv_ref = q_in(), kv_here()
+ROOT = 1.0 / math.sqrt(HEAD_DIM)
+
+
+def weigh(q, k):
+    expo = jnp.exp(dot(q, k, ((1,), (1,))) * ROOT)
+    return expo, jnp.sum(expo, axis=-1, keepdims=True)
+
+
+def den_lanes(rows):
+    return -(-(rows + 1) // LANES) * LANES
+
+
+def far_body(tp_count, info_ref, kv_in_ref, q3_ref, q2_ref, kv, *refs):
+    back3, back2, token_ref, far_top, far_den = refs
+    token_ref[...] = jnp.zeros_like(token_ref)
+    kv_ref = kv()
+    rows, width = q2_ref.shape
+    heads = heads_of(width)
+    count = len(heads)
+    keys, values = slice(0, rows), slice(rows, 2 * rows)
+    last = last_row(info_ref, rows, tp_count)
+    spread = den_lanes(rows) - rows
+
+    def sums(q_ref, at_rows, top_ref):
+        size = at_rows.stop - at_rows.start
+        lane = lax.broadcasted_iota(jnp.int32, (size, LANES), 1)
+        dens = jnp.zeros((size, LANES), F32)
+        for h, at in enumerate(heads):
+            q = q_ref[at_rows, at]
+            own, own_den = weigh(q, kv_ref[keys, at])
+            other, other_den = weigh(q, kv_in_ref[keys, at])
+            top_ref[:size, at] = dot(own.astype(BF16), kv_ref[values, at]) + dot(
+                other.astype(BF16), kv_in_ref[values, at]
+            )
+            dens = jnp.where(lane == h, own_den + other_den, dens)
+        return dens
+
+    def fill(back, top, den, edge_top, edge_den):
+        back.ref[:rows, :] = top.astype(BF16)
+        back.ref[rows : rows + EDGE_ROWS, :] = edge_top.astype(BF16)
+        den = jnp.concatenate([den, jnp.broadcast_to(edge_den, (spread, LANES))], axis=0)
+        turned = split_den(den, count).T[:EDGE_ROWS].astype(BF16)
+        back.ref[rows + EDGE_ROWS :, : turned.shape[1]] = turned
+        if turned.shape[1] < width:
+            rest = jnp.zeros((EDGE_ROWS, width - turned.shape[1]), BF16)
+            back.ref[rows + EDGE_ROWS :, turned.shape[1] :] = rest
+        back.send()
+
+    everything = slice(0, rows)
+    far_den[...] = sums(q2_ref, everything, far_top.at[0])
+    den3 = sums(q3_ref, everything, far_top.at[1])
+    row = jnp.broadcast_to(far_top[0, pl.ds(last, 1), :], (EDGE_ROWS, width))
+    fill(back3, far_top[1], den3, row, far_den[pl.ds(last, 1), :])
+    edge_den = sums(kv_ref, slice(2 * rows, 2 * rows + EDGE_ROWS), far_top.at[1])
+    fill(back2, far_top[0], far_den[...], far_top[1, :EDGE_ROWS, :], edge_den[:1])
+
+
+def near_body(info_ref, kv_in_ref, mask_ref, _, q, kv, top_ref, den_ref, edge_ref):
+    q_ref, kv_ref = q(), kv()
     rows, width = q_ref.shape
-    root = 1.0 / math.sqrt(HEAD_DIM)
     allowed = mask_ref[...] > 0
     linked = jnp.where(info_ref[3] % 2 == 1, 1.0, 0.0)
-    heads = heads_of(width)
-    count = len(heads)
     lane = lax.broadcasted_iota(jnp.int32, (rows, LANES), 1)
+    edge_lane = lax.broadcasted_iota(jnp.int32, (EDGE_ROWS, LANES), 1)
     dens = jnp.zeros((rows, LANES), F32)
-    far_dens = [dens, dens]
-    for h, at in enumerate(heads):
-        q, k, v = q_ref[:, at], kv_ref[0, :, at], kv_ref[1, :, at]
-        k_in, v_in = kv_in_ref[0, :, at], kv_in_ref[1, :, at]
-        own = jnp.where(allowed, jnp.exp(dot(q, k, ((1,), (1,))) * root), 0.0)
-        other = jnp.exp(dot(q, k_in, ((1,), (1,))) * root) * linked
-        top_ref[:, at] = dot(own.astype(BF16), v) + dot(other.astype(BF16), v_in)
-        den = jnp.sum(own, axis=-1, keepdims=True) + jnp.sum(other, axis=-1, keepdims=True)
-        dens = jnp.where(lane == h, den, dens)
-        for index, far_ref in enumerate((q3_ref, q2_ref)):
-            far = far_ref[:, at]
-            own = jnp.exp(dot(far, k, ((1,), (1,))) * root)
-            other = jnp.exp(dot(far, k_in, ((1,), (1,))) * root)
-            far_top[index, :, at] = dot(own.astype(BF16), v) + dot(other.astype(BF16), v_in)
-            den = jnp.sum(own, axis=-1, keepdims=True) + jnp.sum(other, axis=-1, keepdims=True)
-            far_dens[index] = jnp.where(lane == h, den, far_dens[index])
+    edge_dens = jnp.zeros((EDGE_ROWS, LANES), F32)
+    keys, values = slice(0, rows), slice(rows, 2 * rows)
+    for h, at in enumerate(heads_of(width)):
+        k, v = kv_ref[keys, at], kv_ref[values, at]
+        k_in, v_in = kv_in_ref[keys, at], kv_in_ref[values, at]
+        q = q_ref[:, at]
+        own = jnp.where(allowed, jnp.exp(dot(q, k, ((1,), (1,))) * ROOT), 0.0)
+        own_den = jnp.sum(own, axis=-1, keepdims=True)
+        other, other_den = weigh(q, k_in)
+        top_ref[:, at] = dot(own.astype(BF16), v) + dot((other * linked).astype(BF16), v_in)
+        dens = jnp.where(lane == h, own_den + other_den * linked, dens)
+        edge, edge_den = weigh(kv_in_ref[2 * rows :, at], k_in)
+        edge_ref[:, at] = dot((edge * linked).astype(BF16), v_in)
+        edge_dens = jnp.where(edge_lane == h, edge_den * linked, edge_dens)
     den_ref[...] = dens
-    last = last_row(info_ref, rows, tp_count)
-    edge_rows = EDGE_ROWS
-
-    def fill(ref, at, top, den):
-        ref[at, :width] = top.astype(BF16)
-        ref[at, width:] = split_den(den, count).astype(BF16)
-
-    def spread(row):
-        return jnp.broadcast_to(row, (edge_rows, row.shape[1]))
-
-    far_den[...] = far_dens[1]
-    fill(back3_ref, slice(0, rows), far_top[0], far_dens[0])
-    fill(
-        back3_ref,
-        slice(rows, rows + edge_rows),
-        spread(far_top[1, pl.ds(last, 1), :]),
-        spread(far_den[pl.ds(last, 1), :]),
-    )
-    back3.send()
-    fill(back2_ref, slice(0, rows), far_top[1], far_dens[1])
-    fill(
-        back2_ref,
-        slice(rows, rows + edge_rows),
-        spread(top_ref[pl.ds(last, 1), :]),
-        spread(den_ref[pl.ds(last, 1), :]),
-    )
-
-
-EDGE_ROWS = 16
+    edge_ref[:, width:] = edge_dens
 
 
 def attend_paired(info, q, kv, mask, tp_count):
     kv_in = lax.ppermute(kv, "ctx", [(0, 1), (2, 3)])
     far = [lax.ppermute(q, "ctx", [(c, 1)]) for c in (3, 2)]
     rows, width = q.shape
-    back = ((rows + EDGE_ROWS, width + LANES), BF16)
-    back3, back2, top, den = staged(
-        functools.partial(attend_body, tp_count),
-        [kv_in, *far, mask],
+    back = ((rows + 2 * EDGE_ROWS, width), BF16)
+    back3, back2, done = staged(
+        functools.partial(far_body, tp_count),
+        [kv_in, *far],
         [back, back],
-        [((rows, width), F32), ((rows, LANES), F32)],
+        [TOKEN],
         [pltpu.VMEM((2, rows, width), F32), pltpu.VMEM((rows, LANES), F32)],
         info,
+        held=[kv],
+    )
+    back = [lax.ppermute(back3, "ctx", [(1, 3)]), lax.ppermute(back2, "ctx", [(1, 2)])]
+    top, den, edge = staged(
+        near_body,
+        [kv_in, mask, done],
+        [],
+        [((rows, width), F32), ((rows, LANES), F32), ((EDGE_ROWS, width + LANES), F32)],
+        info=info,
         held=[q, kv],
     )
-    back3 = lax.ppermute(back3, "ctx", [(1, 3)])
-    back2 = lax.ppermute(back2, "ctx", [(c, c + 1) for c in range(3)])
-    return top, den, [back2, back3]
+    return top, den, edge, back
 
 
 def attend_all_body(tp_count, info_ref, mask_ref, q_ref, k_ref, v_ref, top_ref, den_ref, edge_ref):
@@ -384,17 +424,17 @@
     count = edge_ref.shape[0]
     top = jnp.broadcast_to(top_ref[pl.ds(last, 1), :], (count, width))
     den = jnp.broadcast_to(den_ref[pl.ds(last, 1), :], (count, LANES))
-    edge_ref[:, :width] = top.astype(BF16)
-    edge_ref[:, width:] = split_den(den, len(heads)).astype(BF16)
+    edge_ref[:, :width] = top
+    edge_ref[:, width:] = den
 
 
 def attend_all(info, q, kv, mask, tp_count):
     planes = lax.axis_size("ctx")
-    keys = lax.all_gather(kv[0], "ctx", axis=0, tiled=True)
-    values = lax.all_gather(kv[1], "ctx", axis=0, tiled=True)
     rows, width = q.shape
+    keys = lax.all_gather(kv[:rows], "ctx", axis=0, tiled=True)
+    values = lax.all_gather(kv[rows : 2 * rows], "ctx", axis=0, tiled=True)
     here = pl.BlockSpec(memory_space=pltpu.VMEM)
-    outs = [((rows, width), F32), ((rows, LANES), F32), ((EDGE_ROWS, width + LANES), BF16)]
+    outs = [((rows, width), F32), ((rows, LANES), F32), ((EDGE_ROWS, width + LANES), F32)]
     top, den, edge = pl.pallas_call(
         functools.partial(attend_all_body, tp_count),
         in_specs=[pl.BlockSpec(memory_space=pltpu.SMEM)] + [here] * 4,
@@ -402,35 +442,35 @@
         out_shape=[jax.ShapeDtypeStruct(shape, dtype) for shape, dtype in outs],
         compiler_params=params(48),
     )(info, mask, q, keys, values)
-    back = jnp.concatenate([jnp.zeros((rows, width + LANES), BF16), edge], axis=0)
-    return top, den, [lax.ppermute(back, "ctx", [(c, c + 1) for c in range(planes - 1)])]
+    edge = lax.ppermute(edge, "ctx", [(c, c + 1) for c in range(planes - 1)])
+    return top, den, edge, []
 
 
 def output_body(count, tp_count, info_ref, *refs):
     back_refs = refs[:count]
-    top_ref, den_ref, w_ref, odd_out, even_ref, whole, odd_ref, out_sems = refs[count:]
+    top_ref, den_ref, edge_ref, w_ref, odd_out, even_ref, whole, odd_ref, out_sems = refs[count:]
     depth = w_ref.shape[0]
     blocks, _, step = odd_ref.shape
     rows = top_ref.shape[0]
     heads = heads_of(depth)
     edges = []
 
-    def column(ref, at, h):
-        high, low = depth + h, depth + len(heads) + h
-        return ref[at, high : high + 1].astype(F32) + ref[at, low : low + 1].astype(F32)
+    back_dens = []
+    for ref in back_refs:
+        turned = ref[rows + EDGE_ROWS :, : den_lanes(rows)].astype(F32)
+        rest = jnp.zeros((LANES - EDGE_ROWS, turned.shape[1]), F32)
+        back_dens.append(jnp.concatenate([turned, rest], axis=0).T)
 
     for h, lanes in enumerate(heads):
         top, den = top_ref[:, lanes], den_ref[:, h : h + 1]
-        edge, edge_den = 0.0, 0.0
-        for index, ref in enumerate(back_refs):
-            mine, mine_den = ref[:rows, lanes].astype(F32), column(ref, slice(0, rows), h)
-            if index == 0:
-                taken = info_ref[3] == 2
-                mine, mine_den = jnp.where(taken, mine, 0.0), jnp.where(taken, mine_den, 0.0)
-            top += mine
-            den += mine_den
-            edge += ref[rows:, lanes].astype(F32)
-            edge_den += column(ref, slice(rows, None), h)
+        edge, edge_den = edge_ref[:, lanes], edge_ref[:, depth + h : depth + h + 1]
+        for ref in back_refs:
+            top += ref[:rows, lanes].astype(F32)
+            edge += ref[rows : rows + EDGE_ROWS, lanes].astype(F32)
+        for value in back_dens:
+            both = value[:, h : h + 1] + value[:, len(heads) + h : len(heads) + h + 1]
+            den += both[:rows]
+            edge_den += both[rows : rows + EDGE_ROWS]
         whole[:, lanes] = top / den
         edges.append(jnp.where(edge_den > 0, edge / jnp.where(edge_den > 0, edge_den, 1.0), 0.0))
     edge = jnp.concatenate(edges, axis=1)[:1]
@@ -459,7 +499,7 @@
         copy.wait()
 
 
-def output_project(info, top, den, back, weights, tp_count):
+def output_project(info, top, den, edge, back, weights, tp_count):
     rows, depth = top.shape
     width = weights.shape[1]
     step = min(width, 1024)
@@ -467,7 +507,7 @@
     blocks = width // step
     odd, even = pl.pallas_call(
         functools.partial(output_body, len(back), tp_count),
-        in_specs=[pl.BlockSpec(memory_space=pltpu.SMEM)] + [here] * (3 + len(back)),
+        in_specs=[pl.BlockSpec(memory_space=pltpu.SMEM)] + [here] * (4 + len(back)),
         out_specs=[there, here],
         out_shape=[
             pltpu.HBM((rows // 2, width), BF16),
@@ -479,7 +519,7 @@
             pltpu.SemaphoreType.DMA((blocks,)),
         ],
         compiler_params=params(16),
-    )(info, *back, top, den, weights)
+    )(info, *back, top, den, edge, weights)
     return even, odd
 
 
@@ -545,7 +585,8 @@
     return scale * (grad - y * jnp.mean(grad * y, axis=-1, keepdims=True))
 
 
-def prepare_body(parts, info_ref, gb_ref, wq_ref, wk_ref, wv_ref, wo_ref, *refs):
+def prepare_body(parts, info_ref, gb_ref, wq_ref, wk_ref, wv_ref, wo_ref, token_ref, *refs):
+    token_ref[...] = jnp.zeros_like(token_ref)
     weights_ref = refs[0]
     d = LOCAL_HEAD_DIM
     rows = refs[1].shape[0] // len(parts[0])
@@ -570,7 +611,7 @@
     outs = [(width, 3 * d)]
     for part in parts:
         outs += [(len(part) * rows, width), (len(part) * rows, d)]
-    weights, *blocks = pl.pallas_call(
+    token, weights, *blocks = pl.pallas_call(
         functools.partial(prepare_body, parts),
         grid_spec=pltpu.PrefetchScalarGridSpec(
             num_scalar_prefetch=1,
@@ -582,12 +623,12 @@
                 qkv_spec(2),
                 pl.BlockSpec((1, d, width), lambda i, info: (0, info[0], 0)),
             ],
-            out_specs=[pl.BlockSpec(shape, lambda i, info: (0, 0)) for shape in outs],
+            out_specs=[pl.BlockSpec(shape, lambda i, info: (0, 0)) for shape in [TOKEN.shape, *outs]],
         ),
-        out_shape=[jax.ShapeDtypeStruct(shape, BF16) for shape in outs],
+        out_shape=[TOKEN] + [jax.ShapeDtypeStruct(shape, BF16) for shape in outs],
         compiler_params=params(LARGE),
     )(info, gb_all, local_qkv, local_qkv, local_qkv, local_out)
-    return weights, blocks[0::2], blocks[1::2]
+    return token, weights, blocks[0::2], blocks[1::2]
 
 
 def window(rows):
@@ -694,7 +735,8 @@
 def relay_body(count, ab0_ref, ab1_ref, kept_ref, there_ref, *refs):
     rows = ab0_ref.shape[0] // 2
     deep = kept_ref.shape[1]
-    *messages, own = refs
+    *messages, own, token_ref = refs
+    token_ref[...] = jnp.zeros_like(token_ref)
     for k, message in enumerate([own, *messages]):
         parts = []
         if k <= count:
@@ -725,7 +767,7 @@
             functools.partial(local_body, len(xs)),
             [*xs, gbs[index], cores[index], weights, *carry],
             [],
-            [*totals, ((len(xs) * rows, d), BF16), (TOKEN.shape, F32)],
+            [*totals, ((len(xs) * rows, d), BF16), TOKEN],
             flops=1 << 34,
             mib=20,
         )
@@ -748,14 +790,14 @@
         mib=20,
     )
     sizes = [2 * rows * (k <= count) + 2 * deep * (k < halves) for k in range(max(count + 1, halves))]
-    *messages, own = staged(
+    *messages, own, done = staged(
         functools.partial(relay_body, count),
         [ab0, ab1, kept, swap(message, 1)],
         [((size, d), BF16) for size in sizes[1:]],
-        [((sizes[0], d), BF16)],
+        [((sizes[0], d), BF16), TOKEN],
     )
     messages = [own] + [swap(value, 2 * (k + 1)) for k, value in enumerate(messages)]
-    return messages, grad_qkv
+    return messages, tie(grad_qkv, done, mib=LARGE)
 
 
 def hidden_body(heads, count, info_ref, state_ref, w_ref, *refs):
@@ -788,7 +830,7 @@
         out.send()
 
 
-def final_body(heads, parts_ref, *refs):
+def final_body(heads, parts_ref, _, *refs):
     *terms, gqkv_ref, gout_ref = refs
     gout = sum(term[...].astype(F32) for term in terms)
     gout_ref[0] = chunks_out(gout, gout_ref.shape[1])
@@ -837,16 +879,15 @@
     weights_in, head_info = preload(global_qkv, head_info, mine)
     even = [tie(swap(patch_in, bits), head_info) for bits in range(2, tp_count, 2)]
     pieces = [patch_in, *even, mine, *(swap(piece, 1) for piece in even)]
-    q, kv, gb = project(pieces, weights_in, global_qkv, cotangent)
+    q, kv, gb = project(head_info, pieces, weights_in, global_qkv, cotangent, tp_count)
 
     place = (
         (me ^ jnp.array(order, jnp.int32))[:, None] * patches
         + jnp.arange(patches, dtype=jnp.int32)[None, :]
     ).reshape(-1)
-    weights_out, head_info = preload(global_out, head_info, q)
-    if planes == 4:
+    if planes == 4 and den_lanes(shard_rows) <= q.shape[1]:
         mask = (place[None, :] <= place[:, None]).astype(F32)
-        top, den, back = attend_paired(
+        top, den, edge, back = attend_paired(
             head_info, q, kv, mask, tp_count
         )
     else:
@@ -854,14 +895,17 @@
             jnp.arange(planes, dtype=jnp.int32)[:, None] * shard_rows + place[None, :]
         ).reshape(-1)
         mask = (key_place[None, :] <= (plane * shard_rows + place)[:, None]).astype(F32)
-        top, den, back = attend_all(head_info, q, kv, mask, tp_count)
-
-    even, odd = output_project(head_info, top, den, back, weights_out, tp_count)
+        top, den, edge, back = attend_all(head_info, q, kv, mask, tp_count)
+
+    weights_out, _ = preload(global_out, head_info, den)
+    even, odd = output_project(head_info, top, den, edge, back, weights_out, tp_count)
 
     parts = [[0, 1], list(range(2, group, 2)), list(range(3, group, 2))]
     gb_all = lax.all_gather(gb, "tp", axis=0, tiled=True)
-    weights, gbs, cores = prepare(head_info, gb_all, local_qkv, local_out, byte_count, parts)
-    state, normed, normed_near = byte_state(scatter_sum(even, odd, patches), local_embeds, cores[0])
+    prepared, weights, gbs, cores = prepare(head_info, gb_all, local_qkv, local_out, byte_count, parts)
+    state, normed, normed_near = byte_state(
+        scatter_sum(even, odd, patches), local_embeds, prepared
+    )
     messages, grad_qkv = local_layer(
         normed, normed_near, head_info, parts, gbs, cores, weights, rounds, tp_count
     )
@@ -882,14 +926,13 @@
         in_specs=[pl.BlockSpec(memory_space=pltpu.SMEM)] + [here] * (3 + count),
         out_specs=[here, here],
         out_shape=[jax.ShapeDtypeStruct((byte_count, width), BF16), TOKEN],
-        compiler_params=params(LARGE),
+        compiler_params=params(16),
     )(head_info, state, local_out, *messages[: count + 1])
-    out_pieces[0] = tie(out_pieces[0], done)
     grad_qkv, grad_out = call(
         functools.partial(final_body, heads),
         [((1, share, 3 * width), F32), ((1, share, width), F32)],
-        mib=LARGE,
-    )(grad_qkv.reshape(devices, share, 3 * LOCAL_HEAD_DIM), *out_pieces)
+        mib=16,
+    )(grad_qkv.reshape(devices, share, 3 * LOCAL_HEAD_DIM), done, *out_pieces)
     return (hidden, grad_qkv, grad_out)
 
 

time: 183 us -> 180 us (0.984)
  starting transfers between devices: 43.6 us -> 37 us
  waiting for transfers between devices: 60.8 us -> 66.9 us
  local copies, waits for them, and re-layouts: 8.91 us -> 6.81 us
    ppermute x2, starting transfers between devices: 7.5 us -> 1.35 us  [the longest x1 0.68 us: attend_paired(): lax.ppermute(back3, 'ctx', [(1, 3)])]
    ppermute x1, waiting for transfers between devices: 2.33 us -> 7.75 us  [attend_paired(): kv_in = lax.ppermute(kv, 'ctx', [(0, 1), (2, 3)])]
    ppermute x2, waiting for transfers between devices: 5.29 us -> 0.01 us  [the longest x1 0.01 us: attend_paired(): lax.ppermute(back3, 'ctx', [(1, 3)])]
    ppermute x22, waiting for transfers between devices: 53.1 us -> 56.8 us  [swap(): lax.ppermute(value, 'tp', [(source, source ^ bits) for source in range(co...]
    pallas_call x7 -> x8, Pallas kernels: 19.4 us -> 21.7 us  [staged(): pl.pallas_call(kernel, in_specs=[pl.BlockSpec(memory_space=pltpu.SMEM)] *...]
    ppermute x3, waiting for transfers between devices: 0.01 us -> 2.28 us  [swap_planes(): lax.ppermute(pieces[k], 'ctx', [(c, c ^ k) for c in range(count)])]
    unnamed x64 -> x58, local copies, waits for them, and re-layouts: 8.83 us -> 6.73 us
  transfers between devices with their start and end apart: 32 -> 32, of which waited for: 14 -> 16; matrix products, arithmetic and copies ran while one was open for 0% -> 0% of each run, Pallas kernels for 19% -> 19%
where the time goes in v4:
time: 180 us
  waiting for transfers between devices  66.9 us (37%)
  Pallas kernels  53.6 us (30%)
  starting transfers between devices  37 us (21%)
  between operations  14.5 us (8%)
  local copies, waits for them, and re-layouts  6.81 us (4%)
    ppermute x22, waiting for transfers between devices, swap(): lax.ppermute(value, 'tp', [(source, source ^ bits) for source in range(co...  56.8 us
    pallas_call x8, Pallas kernels, staged(): pl.pallas_call(kernel, in_specs=[pl.BlockSpec(memory_space=pltpu.SMEM)] *...  21.7 us
    ppermute x22, starting transfers between devices, swap(): lax.ppermute(value, 'tp', [(source, source ^ bits) for source in range(co...  16.6 us
    pallas_call x1, Pallas kernels, project(): pl.pallas_call(body, in_specs=[pl.BlockSpec(memory_space=pltpu.SMEM)] + [...  9.61 us
    pallas_call x2, Pallas kernels, preload(): pl.pallas_call(functools.partial(preload_body, parts), in_specs=[scalar,...  9.45 us
    all_to_all x1, starting transfers between devices, per_device(): grad_qkv = lax.all_to_all(grad_qkv, ('ctx', 'tp'), 0, 0, tiled=True)  9.37 us
    ppermute x1, waiting for transfers between devices, attend_paired(): kv_in = lax.ppermute(kv, 'ctx', [(0, 1), (2, 3)])  7.75 us
    unnamed x58, local copies, waits for them, and re-layouts  6.73 us
  transfers between devices with their start and end apart: 32, of which 16 were waited for; matrix products, arithmetic and copies ran while one was open for 0% of the time, Pallas kernels for 19%

profile of v4, /device:TPU:0, one launch (start us, length us, event | category | flops | bytes accessed | tf_op | source)
XLA Modules:
  0.0 179.6 jit_solution(1728930361286602033)
XLA Ops:
  7.2 1.0 copy-done.10
  9.1 2.6 %collective-permute-start.2 = (bf16[24,8192]{1,0:T(8,128)(2,1)S(1)}, bf16[24,8192]{1,0:T(8,128)(2,1)S(1)}, u32[]{:S(2)}, u32[]{:S(2)}) collective-permute-start(bf16[24,8192]{1,0:T(8,128)(2,1)S(1)} %shard_map.103.refs_1_), channel_id=1, source_target_pairs={{0,4},{1,5},{2,6},{3,7},{4,0},{5,1},{6,2},{7,3},{8,12},{9,13},{10,... | collective-permute-start | bytes 1179656 | tf_op jit(solution)/shard_map/ppermute | solution.py:110
  11.7 1.4 collective-permute-start.3
  13.8 0.7 copy-done.3
  14.6 4.7 %shard_map.104 = (bf16[8192,512]{1,0:T(8,128)(2,1)S(1)}, s32[4]{0:T(128)}) custom-call(s32[4]{0:T(128)} %pad_add_fusion.info_ref, bf16[3,8192,512]{2,1,0:T(8,128)(2,1)} %refs_11_.1, bf16[24,8192]{1,0:T(8,128)(2,1)} %copy-done.3), custom_call_target="tpu_custom_call" | custom-call | bytes 8388608 | tf_op jit(solution)/shard_map/pallas_call | solution.py:156
  19.3 10.5 %collective-permute-done.2.refs_0_ = bf16[24,8192]{1,0:T(8,128)(2,1)S(1)} collective-permute-done((bf16[24,8192]{1,0:T(8,128)(2,1)S(1)}, bf16[24,8192]{1,0:T(8,128)(2,1)S(1)}, u32[]{:S(2)}, u32[]{:S(2)}) %collective-permute-start.2) | collective-permute-done | bytes 393248 | tf_op jit(solution)/shard_map/ppermute | solution.py:110
  31.1 1.1 collective-permute-done.5.refs_7_
  33.3 9.6 %shard_map.108 = (bf16[192,512]{1,0:T(8,128)(2,1)}, bf16[400,512]{1,0:T(8,128)(2,1)}, bf16[192,1024]{1,0:T(8,128)(2,1)}) custom-call(s32[4]{0:T(128)S(1)} %copy-done.13, bf16[24,8192]{1,0:T(8,128)(2,1)S(1)} %shard_map.103.refs_1_, bf16[24,8192]{1,0:T(8,128)(2,1)S(1)} %shard_map.105.refs_2_, bf16[24,8192]{1,0:T(8,128)(2,1)S(1)} %shard_map.106.refs_3_, ...), custom_call_target="tpu_custom_call" | custom-call | tf_op jit(solution)/shard_map/pallas_call | solution.py:265
  42.9 3.9 %collective-permute-start.7 = (bf16[400,512]{1,0:T(8,128)(2,1)}, bf16[400,512]{1,0:T(8,128)(2,1)S(1)}, u32[]{:S(2)}, u32[]{:S(2)}) collective-permute-start(bf16[400,512]{1,0:T(8,128)(2,1)} %get-tuple-element.57.refs_4_.refs_5_), channel_id=1, source_target_pairs={{0,8},{16,24},{1,9},{17,25},{2,10},{18,26},{3,11},{19,27},{4,12},{... | collective-permute-start | bytes 1228808 | tf_op jit(solution)/shard_map/ppermute | solution.py:386
  46.8 0.7 collective-permute-start.8
  47.5 0.7 collective-permute-start.9
  48.4 7.7 %collective-permute-done.7.refs_1_ = bf16[400,512]{1,0:T(8,128)(2,1)S(1)} collective-permute-done((bf16[400,512]{1,0:T(8,128)(2,1)}, bf16[400,512]{1,0:T(8,128)(2,1)S(1)}, u32[]{:S(2)}, u32[]{:S(2)}) %collective-permute-start.7) | collective-permute-done | bytes 409632 | tf_op jit(solution)/shard_map/ppermute | solution.py:386
  56.1 1.0 copy-done.1
  57.1 3.3 %shard_map.109 = (bf16[224,512]{1,0:T(8,128)(2,1)}, bf16[224,512]{1,0:T(8,128)(2,1)}, f32[8,128]{1,0:T(8,128)S(1)}) custom-call(s32[4]{0:T(128)S(1)} %copy-done.14, bf16[400,512]{1,0:T(8,128)(2,1)S(1)} %collective-permute-done.7.refs_1_, bf16[192,512]{1,0:T(8,128)(2,1)S(1)} %collective-permute-done.8.refs_2_, ...), custom_call_target="tpu_custom_call" | custom-call | bytes 4194304 | tf_op jit(solution)/shard_map/pallas_call | solution.py:87
  60.4 0.7 collective-permute-start.10
  61.1 0.7 collective-permute-start.11
  61.9 0.9 copy-done.11
  62.8 2.4 %shard_map.110 = (f32[192,512]{1,0:T(8,128)S(1)}, f32[192,128]{1,0:T(8,128)S(1)}, f32[16,640]{1,0:T(8,128)S(1)}) custom-call(s32[4]{0:T(128)S(1)} %copy-done.14, bf16[400,512]{1,0:T(8,128)(2,1)S(1)} %collective-permute-done.7.refs_1_, f32[192,192]{1,0:T(8,128)S(1)} %compare_convert_fusion.refs_2_, f32[8,128]{1,0:T(8,128)S(1)} %get-tuple-element.61.refs_3_, ...), custom_call_target="tpu_custom_call" | custom-call | bytes 4194304 | tf_op jit(solution)/shard_map/pallas_call | solution.py:87
  65.9 4.8 %shard_map.111 = (bf16[512,8192]{1,0:T(8,128)(2,1)S(1)}, s32[4]{0:T(128)}) custom-call(s32[4]{0:T(128)} %get-tuple-element.55.refs_1_.refs_0_.info_ref, bf16[512,8192]{1,0:T(8,128)(2,1)} %w_ref.4, f32[192,128]{1,0:T(8,128)} %copy-done.7), custom_call_target="tpu_custom_call" | custom-call | bytes 8388608 | tf_op jit(solution)/shard_map/pallas_call | solution.py:156
  70.7 3.5 %shard_map.112 = (bf16[96,8192]{1,0:T(8,128)(2,1)}, bf16[96,8192]{1,0:T(8,128)(2,1)S(1)}) custom-call(s32[4]{0:T(128)S(1)} %copy-done.15, bf16[224,512]{1,0:T(8,128)(2,1)S(1)} %collective-permute-done.10.refs_0_, bf16[224,512]{1,0:T(8,128)(2,1)S(1)} %collective-permute-done.11.refs_1_, f32[192,512]{1,0:T(8,128)S(1)} %get-tuple-element.62.refs_2_, ...), custom_call_target="tpu_custom_call" | custom-call | tf_op jit(solution)/shard_map/pallas_call | solution.py:508
  74.3 3.6 %collective-permute-done.12.other_ref = bf16[96,8192]{1,0:T(8,128)(2,1)S(1)} collective-permute-done((bf16[96,8192]{1,0:T(8,128)(2,1)}, bf16[96,8192]{1,0:T(8,128)(2,1)S(1)}, u32[]{:S(2)}, u32[]{:S(2)}) %collective-permute-start.12) | collective-permute-done | bytes 1572896 | tf_op jit(solution)/shard_map/ppermute | solution.py:110
  78.2 1.6 collective-permute-start.13
  79.8 1.6 collective-permute-start.14
  81.8 5.5 %shard_map.114 = (f32[8,128]{1,0:T(8,128)S(1)}, bf16[1024,384]{1,0:T(8,128)(2,1)}, bf16[384,1024]{1,0:T(8,128)(2,1)}, bf16[384,128]{1,0:T(8,128)(2,1)}, bf16[576...) custom-call(s32[4]{0:T(128)} %get-tuple-element.55.refs_1_.refs_0_.info_ref,, ...), custom_call_target="tpu_custom_call" | custom-call | tf_op jit(solution)/shard_map/pallas_call | solution.py:614
  87.3 2.9 %collective-permute-done.13.refs_1_ = bf16[24,8192]{1,0:T(8,128)(2,1)S(1)} collective-permute-done((bf16[24,8192]{1,0:T(8,128)(2,1)S(1)}, bf16[24,8192]{1,0:T(8,128)(2,1)S(1)}, u32[]{:S(2)}, u32[]{:S(2)}) %collective-permute-start.13) | collective-permute-done | bytes 393248 | tf_op jit(solution)/shard_map/ppermute | solution.py:110
  90.3 8.8 %collective-permute-done.14.refs_2_ = bf16[24,8192]{1,0:T(8,128)(2,1)S(1)} collective-permute-done((bf16[24,8192]{1,0:T(8,128)(2,1)S(1)}, bf16[24,8192]{1,0:T(8,128)(2,1)S(1)}, u32[]{:S(2)}, u32[]{:S(2)}) %collective-permute-start.14) | collective-permute-done | bytes 393248 | tf_op jit(solution)/shard_map/ppermute | solution.py:110
  99.1 1.6 shard_map.115
  100.7 1.7 collective-permute-start.19
  102.4 1.1 collective-permute-start.18
  103.5 0.7 collective-permute-start.17
  104.3 2.7 %shard_map.116 = (f32[384,1024]{1,0:T(8,128)S(1)}, f32[128,1024]{1,0:T(8,128)S(1)}, bf16[384,128]{1,0:T(8,128)(2,1)S(1)}, f32[8,128]{1,0:T(8,128)S(1)}) custom-call(bf16[192,1024]{1,0:T(8,128)(2,1)S(1)} %get-tuple-element.75.refs_0_, bf16[192,1024]{1,0:T(8,128)(2,1)S(1)} %collective-permute-done.16.refs_1_, bf16[384,1024]{1,0:T(8,128)(2,1)S(1)} %copy-done.21, ...), custom_call_target="tpu_custom_call" | custom-call | flops 17179869184 | bytes 4194304 | tf_op jit(solution)/shard_map/pallas_call | solution.py:87
  107.1 6.8 %collective-permute-done.19.refs_0_ = bf16[192,1024]{1,0:T(8,128)(2,1)S(1)} collective-permute-done((bf16[192,1024]{1,0:T(8,128)(2,1)}, bf16[192,1024]{1,0:T(8,128)(2,1)S(1)}, u32[]{:S(2)}, u32[]{:S(2)}) %collective-permute-start.19) | collective-permute-done | bytes 393248 | tf_op jit(solution)/shard_map/ppermute | solution.py:110
  113.9 7.9 %collective-permute-done.18.refs_0_ = bf16[192,1024]{1,0:T(8,128)(2,1)S(1)} collective-permute-done((bf16[192,1024]{1,0:T(8,128)(2,1)}, bf16[192,1024]{1,0:T(8,128)(2,1)S(1)}, u32[]{:S(2)}, u32[]{:S(2)}) %collective-permute-start.18) | collective-permute-done | bytes 393248 | tf_op jit(solution)/shard_map/ppermute | solution.py:110
  122.3 4.2 %shard_map.120 = (f32[384,1024]{1,0:T(8,128)S(1)}, f32[128,1024]{1,0:T(8,128)S(1)}, bf16[576,128]{1,0:T(8,128)(2,1)S(1)}, f32[8,128]{1,0:T(8,128)}) custom-call(bf16[192,1024]{1,0:T(8,128)(2,1)S(1)} %shard_map.117.refs_0_, bf16[192,1024]{1,0:T(8,128)(2,1)S(1)} %shard_map.118.refs_1_, bf16[192,1024]{1,0:T(8,128)(2,1)S(1)} %shard_map.119.refs_2_, ...), custom_call_target="tpu_custom_call" | custom-call | flops 17179869184 | bytes 4194304 | tf_op jit(solution)/shard_map/pallas_call | solution.py:87
  126.6 5.4 %shard_map.121 = (bf16[1024,384]{1,0:T(8,128)(2,1)}, bf16[1280,128]{1,0:T(8,128)(2,1)}, bf16[2,256,128]{2,1,0:T(8,128)(2,1)S(1)}) custom-call(s32[4]{0:T(128)S(1)} %copy-done.16, bf16[192,1024]{1,0:T(8,128)(2,1)S(1)} %collective-permute-done.20.refs_1_, bf16[192,1024]{1,0:T(8,128)(2,1)S(1)} %collective-permute-done.21.refs_2_, ...), custom_call_target="tpu_custom_call" | custom-call | flops 17179869184 | bytes 4194304 | tf_op jit(solution)/shard_map/pallas_call | solution.py:87
  132.3 1.7 collective-permute-done.23.refs_3_
  134.0 0.8 shard_map.122
  135.4 9.4 %all-to-all-start = ((bf16[32,32,384]{2,1,0:T(8,128)(2,1)}), bf16[32,32,384]{2,1,0:T(8,128)(2,1)S(1)}, u32[]{:S(2)}, u32[]{:S(2)}) async-start(bf16[32,32,384]{2,1,0:T(8,128)(2,1)} %bitcast.5), calls=%async_computation | async-start | bytes 1572864 | tf_op jit(solution)/shard_map/all_to_all | solution.py:912
  144.8 1.8 %collective-permute-start.24 = (bf16[896,128]{1,0:T(8,128)(2,1)S(1)}, bf16[896,128]{1,0:T(8,128)(2,1)S(1)}, u32[]{:S(2)}, u32[]{:S(2)}) collective-permute-start(bf16[896,128]{1,0:T(8,128)(2,1)S(1)} %copy-done.25), channel_id=1, source_target_pairs={{0,2},{1,3},{2,0},{3,1},{4,6},{5,7},{6,4},{7,5},{8,10},{9,11},{10,... | collective-permute-start | bytes 688136 | tf_op jit(solution)/shard_map/ppermute | solution.py:110
  146.6 1.5 collective-permute-start.25
  148.3 12.1 %collective-permute-done.24.refs_1_.refs_2_ = bf16[896,128]{1,0:T(8,128)(2,1)S(1)} collective-permute-done((bf16[896,128]{1,0:T(8,128)(2,1)S(1)}, bf16[896,128]{1,0:T(8,128)(2,1)S(1)}, u32[]{:S(2)}, u32[]{:S(2)}) %collective-permute-start.24) | collective-permute-done | bytes 229408 | tf_op jit(solution)/shard_map/ppermute | solution.py:110
  160.4 1.3 shard_map.125
  161.7 1.5 collective-permute-start.27
  163.2 2.3 %collective-permute-start.28 = (bf16[256,128]{1,0:T(8,128)(2,1)}, bf16[256,128]{1,0:T(8,128)(2,1)S(1)}, u32[]{:S(2)}, u32[]{:S(2)}) collective-permute-start(bf16[256,128]{1,0:T(8,128)(2,1)} %get-tuple-element.103), channel_id=1, source_target_pairs={{0,16},{8,24},{16,0},{24,8},{1,17},{9,25},{17,1},{25,9},{2,18},{10... | collective-permute-start | bytes 196616 | tf_op jit(solution)/shard_map/ppermute | solution.py:853
  166.2 1.1 copy-done.5
  167.3 2.3 %shard_map.123 = (bf16[192,1024]{1,0:T(8,128)(2,1)}, f32[8,128]{1,0:T(8,128)S(1)}) custom-call(s32[4]{0:T(128)S(1)} %copy-done.16, f32[192,1024]{1,0:T(8,128)S(1)} %copy-done.5, bf16[1,1024,1024]{2,1,0:T(8,128)(2,1)S(1)} %copy-done, bf16[896,128]{1,0:T(8,128)(2,1)S(1)} %get-tuple-element.93.refs_0_.refs_1_, ...), custom_call_target="tpu_custom_call" | custom-call | tf_op jit(solution)/shard_map/pallas_call | solution.py:924
  170.0 1.8 %collective-permute-done.29.refs_3_ = bf16[256,128]{1,0:T(8,128)(2,1)S(1)} collective-permute-done((bf16[256,128]{1,0:T(8,128)(2,1)}, bf16[256,128]{1,0:T(8,128)(2,1)S(1)}, u32[]{:S(2)}, u32[]{:S(2)}) %collective-permute-start.29) | collective-permute-done | bytes 65568 | tf_op jit(solution)/shard_map/ppermute | solution.py:853
  171.8 0.9 shard_map.126
  (104 shorter events, 8.6 us)
Async XLA Ops:
  7.2 74.6 %all-gather.2.cloned.1.call-start = ((), (), s32[]{:S(2)}) async-start(), calls=%async_computation.1 | async-start | bytes 3538944 | tf_op jit(solution)/shard_map/all_gather | solution.py:904
  8.5 5.3 %collective-permute-start = (bf16[24,8192]{1,0:T(8,128)(2,1)S(1)}, bf16[24,8192]{1,0:T(8,128)(2,1)S(1)}, u32[]{:S(2)}, u32[]{:S(2)}) collective-permute-start(bf16[24,8192]{1,0:T(8,128)(2,1)S(1)} %shard_map.103.refs_1_), channel_id=1, source_target_pairs={{0,1},{1,0},{2,3},{3,2},{4,5},{5,4},{6,7},{7,6},{8,9},{9,8},{10,11... | collective-permute-start | bytes 1179656 | tf_op jit(solution)/shard_map/ppermute | solution.py:110
  9.1 20.7 %collective-permute-start.2 = (bf16[24,8192]{1,0:T(8,128)(2,1)S(1)}, bf16[24,8192]{1,0:T(8,128)(2,1)S(1)}, u32[]{:S(2)}, u32[]{:S(2)}) collective-permute-start(bf16[24,8192]{1,0:T(8,128)(2,1)S(1)} %shard_map.103.refs_1_), channel_id=1, source_target_pairs={{0,4},{1,5},{2,6},{3,7},{4,0},{5,1},{6,2},{7,3},{8,12},{9,13},{10,... | collective-permute-start | bytes 1179656 | tf_op jit(solution)/shard_map/ppermute | solution.py:110
  11.7 18.8 %collective-permute-start.3 = (bf16[24,8192]{1,0:T(8,128)(2,1)S(1)}, bf16[24,8192]{1,0:T(8,128)(2,1)S(1)}, u32[]{:S(2)}, u32[]{:S(2)}) collective-permute-start(bf16[24,8192]{1,0:T(8,128)(2,1)S(1)} %shard_map.103.refs_1_), channel_id=1, source_target_pairs={{0,6},{1,7},{2,4},{3,5},{4,2},{5,3},{6,0},{7,1},{8,14},{9,15},{10,... | collective-permute-start | bytes 1179656 | tf_op jit(solution)/shard_map/ppermute | solution.py:110
  13.1 18.0 %collective-permute-start.1 = (bf16[24,8192]{1,0:T(8,128)(2,1)S(1)}, bf16[24,8192]{1,0:T(8,128)(2,1)S(1)}, u32[]{:S(2)}, u32[]{:S(2)}) collective-permute-start(bf16[24,8192]{1,0:T(8,128)(2,1)S(1)} %shard_map.103.refs_1_), channel_id=1, source_target_pairs={{0,2},{1,3},{2,0},{3,1},{4,6},{5,7},{6,4},{7,5},{8,10},{9,11},{10,... | collective-permute-start | bytes 1179656 | tf_op jit(solution)/shard_map/ppermute | solution.py:110
  19.2 14.1 %copy-start.4 = (bf16[24,8192]{1,0:T(8,128)(2,1)S(1)}, bf16[24,8192]{1,0:T(8,128)(2,1)}, u32[]{:S(2)}) copy-start(bf16[24,8192]{1,0:T(8,128)(2,1)} %copy-done.3) | copy-start | bytes 1179652
  19.2 14.0 %copy-start.6 = (bf16[192,1024]{1,0:T(8,128)(2,1)S(1)}, bf16[192,1024]{1,0:T(8,128)(2,1)}, u32[]{:S(2)}) copy-start(bf16[192,1024]{1,0:T(8,128)(2,1)} %refs_10_.1) | copy-start | bytes 1179652
  30.4 1.7 collective-permute-start.5
  30.4 2.3 %collective-permute-start.6 = (bf16[24,8192]{1,0:T(8,128)(2,1)S(1)}, bf16[24,8192]{1,0:T(8,128)(2,1)S(1)}, u32[]{:S(2)}, u32[]{:S(2)}) collective-permute-start(bf16[24,8192]{1,0:T(8,128)(2,1)S(1)} %shard_map.107.refs_4_), channel_id=1, source_target_pairs={{0,1},{1,0},{2,3},{3,2},{4,5},{5,4},{6,7},{7,6},{8,9},{9,8},{10,11... | collective-permute-start | bytes 1179656 | tf_op jit(solution)/shard_map/ppermute | solution.py:110
  31.1 2.2 %collective-permute-start.4 = (bf16[24,8192]{1,0:T(8,128)(2,1)S(1)}, bf16[24,8192]{1,0:T(8,128)(2,1)S(1)}, u32[]{:S(2)}, u32[]{:S(2)}) collective-permute-start(bf16[24,8192]{1,0:T(8,128)(2,1)S(1)} %shard_map.105.refs_2_), channel_id=1, source_target_pairs={{0,1},{1,0},{2,3},{3,2},{4,5},{5,4},{6,7},{7,6},{8,9},{9,8},{10,11... | collective-permute-start | bytes 1179656 | tf_op jit(solution)/shard_map/ppermute | solution.py:110
  33.3 13.5 %copy-start.28 = (s32[8]{0:T(128)S(1)}, s32[8]{0:T(128)}, u32[]{:S(2)}) copy-start(s32[8]{0:T(128)} %constant.45.clone) | copy-start | bytes 100
  33.3 22.8 %copy-start.14 = (s32[4]{0:T(128)S(1)}, s32[4]{0:T(128)}, u32[]{:S(2)}) copy-start(s32[4]{0:T(128)} %get-tuple-element.55.refs_1_.refs_0_.info_ref) | copy-start | bytes 52
  42.9 19.0 %copy-start.2 = (bf16[400,512]{1,0:T(8,128)(2,1)S(1)}, bf16[400,512]{1,0:T(8,128)(2,1)}, u32[]{:S(2)}) copy-start(bf16[400,512]{1,0:T(8,128)(2,1)} %get-tuple-element.57.refs_4_.refs_5_) | copy-start | bytes 1228804
  42.9 13.2 %collective-permute-start.7 = (bf16[400,512]{1,0:T(8,128)(2,1)}, bf16[400,512]{1,0:T(8,128)(2,1)S(1)}, u32[]{:S(2)}, u32[]{:S(2)}) collective-permute-start(bf16[400,512]{1,0:T(8,128)(2,1)} %get-tuple-element.57.refs_4_.refs_5_), channel_id=1, source_target_pairs={{0,8},{16,24},{1,9},{17,25},{2,10},{18,26},{3,11},{19,27},{4,12},{... | collective-permute-start | bytes 1228808 | tf_op jit(solution)/shard_map/ppermute | solution.py:386
  46.8 1.5 collective-permute-start.8
  47.5 0.8 collective-permute-start.9
  60.4 10.3 %collective-permute-start.10 = (bf16[224,512]{1,0:T(8,128)(2,1)}, bf16[224,512]{1,0:T(8,128)(2,1)S(1)}, u32[]{:S(2)}, u32[]{:S(2)}) collective-permute-start(bf16[224,512]{1,0:T(8,128)(2,1)} %get-tuple-element.59), channel_id=1, source_target_pairs={{8,24},{9,25},{10,26},{11,27},{12,28},{13,29},{14,30},{15,31}} | collective-permute-start | bytes 688136 | tf_op jit(solution)/shard_map/ppermute | solution.py:399
  61.1 9.6 %collective-permute-start.11 = (bf16[224,512]{1,0:T(8,128)(2,1)}, bf16[224,512]{1,0:T(8,128)(2,1)S(1)}, u32[]{:S(2)}, u32[]{:S(2)}) collective-permute-start(bf16[224,512]{1,0:T(8,128)(2,1)} %get-tuple-element.60), channel_id=1, source_target_pairs={{8,16},{9,17},{10,18},{11,19},{12,20},{13,21},{14,22},{15,23}} | collective-permute-start | bytes 688136 | tf_op jit(solution)/shard_map/ppermute | solution.py:399
  65.9 4.8 %copy-start.15 = (s32[4]{0:T(128)S(1)}, s32[4]{0:T(128)}, u32[]{:S(2)}) copy-start(s32[4]{0:T(128)} %get-tuple-element.55.refs_1_.refs_0_.info_ref) | copy-start | bytes 52
  74.2 3.7 %collective-permute-start.12 = (bf16[96,8192]{1,0:T(8,128)(2,1)}, bf16[96,8192]{1,0:T(8,128)(2,1)S(1)}, u32[]{:S(2)}, u32[]{:S(2)}) collective-permute-start(bf16[96,8192]{1,0:T(8,128)(2,1)} %get-tuple-element.67), channel_id=1, source_target_pairs={{0,1},{1,0},{2,3},{3,2},{4,5},{5,4},{6,7},{7,6},{8,9},{9,8},{10,11... | collective-permute-start | bytes 4718600 | tf_op jit(solution)/shard_map/ppermute | solution.py:110
  78.2 12.0 %collective-permute-start.13 = (bf16[24,8192]{1,0:T(8,128)(2,1)S(1)}, bf16[24,8192]{1,0:T(8,128)(2,1)S(1)}, u32[]{:S(2)}, u32[]{:S(2)}) collective-permute-start(bf16[24,8192]{1,0:T(8,128)(2,1)S(1)} %get-tuple-element.69), channel_id=1, source_target_pairs={{0,2},{1,3},{2,0},{3,1},{4,6},{5,7},{6,4},{7,5},{8,10},{9,11},{10,... | collective-permute-start | bytes 1179656 | tf_op jit(solution)/shard_map/ppermute | solution.py:110
  79.8 19.3 %collective-permute-start.14 = (bf16[24,8192]{1,0:T(8,128)(2,1)S(1)}, bf16[24,8192]{1,0:T(8,128)(2,1)S(1)}, u32[]{:S(2)}, u32[]{:S(2)}) collective-permute-start(bf16[24,8192]{1,0:T(8,128)(2,1)S(1)} %get-tuple-element.70), channel_id=1, source_target_pairs={{0,4},{1,5},{2,6},{3,7},{4,0},{5,1},{6,2},{7,3},{8,12},{9,13},{10,... | collective-permute-start | bytes 1179656 | tf_op jit(solution)/shard_map/ppermute | solution.py:110
  81.4 17.7 %copy-start.9 = (bf16[192,1024]{1,0:T(8,128)(2,1)S(1)}, bf16[192,1024]{1,0:T(8,128)(2,1)}, u32[]{:S(2)}) copy-start(bf16[192,1024]{1,0:T(8,128)(2,1)} %refs_4_.1) | copy-start | bytes 1179652
  81.4 17.7 %collective-permute-start.15 = (bf16[24,8192]{1,0:T(8,128)(2,1)S(1)}, bf16[24,8192]{1,0:T(8,128)(2,1)S(1)}, u32[]{:S(2)}, u32[]{:S(2)}) collective-permute-start(bf16[24,8192]{1,0:T(8,128)(2,1)S(1)} %get-tuple-element.71), channel_id=1, source_target_pairs={{0,6},{1,7},{2,4},{3,5},{4,2},{5,3},{6,0},{7,1},{8,14},{9,15},{10,... | collective-permute-start | bytes 1179656 | tf_op jit(solution)/shard_map/ppermute | solution.py:110
  87.3 17.0 %copy-start.20 = (bf16[1024,384]{1,0:T(8,128)(2,1)S(1)}, bf16[1024,384]{1,0:T(8,128)(2,1)}, u32[]{:S(2)}) copy-start(bf16[1024,384]{1,0:T(8,128)(2,1)} %get-tuple-element.79.refs_4_.refs_5_.refs_6_) | copy-start | bytes 2359300
  87.3 17.0 %copy-start.21 = (bf16[384,1024]{1,0:T(8,128)(2,1)S(1)}, bf16[384,1024]{1,0:T(8,128)(2,1)}, u32[]{:S(2)}) copy-start(bf16[384,1024]{1,0:T(8,128)(2,1)} %get-tuple-element.77.refs_2_) | copy-start | bytes 2359300
  87.3 17.0 %copy-start.24 = (bf16[384,128]{1,0:T(8,128)(2,1)S(1)}, bf16[384,128]{1,0:T(8,128)(2,1)}, u32[]{:S(2)}) copy-start(bf16[384,128]{1,0:T(8,128)(2,1)} %get-tuple-element.78.refs_3_) | copy-start | bytes 294916
  100.7 3.6 %collective-permute-start.16 = (bf16[192,1024]{1,0:T(8,128)(2,1)}, bf16[192,1024]{1,0:T(8,128)(2,1)S(1)}, u32[]{:S(2)}, u32[]{:S(2)}) collective-permute-start(bf16[192,1024]{1,0:T(8,128)(2,1)} %get-tuple-element.76), channel_id=1, source_target_pairs={{0,1},{1,0},{2,3},{3,2},{4,5},{5,4},{6,7},{7,6},{8,9},{9,8},{10,11... | collective-permute-start | bytes 1179656 | tf_op jit(solution)/shard_map/ppermute | solution.py:110
  100.7 13.1 %collective-permute-start.19 = (bf16[192,1024]{1,0:T(8,128)(2,1)}, bf16[192,1024]{1,0:T(8,128)(2,1)S(1)}, u32[]{:S(2)}, u32[]{:S(2)}) collective-permute-start(bf16[192,1024]{1,0:T(8,128)(2,1)} %get-tuple-element.76), channel_id=1, source_target_pairs={{0,6},{1,7},{2,4},{3,5},{4,2},{5,3},{6,0},{7,1},{8,14},{9,15},{10,... | collective-permute-start | bytes 1179656 | tf_op jit(solution)/shard_map/ppermute | solution.py:110
  102.4 19.4 %collective-permute-start.18 = (bf16[192,1024]{1,0:T(8,128)(2,1)}, bf16[192,1024]{1,0:T(8,128)(2,1)S(1)}, u32[]{:S(2)}, u32[]{:S(2)}) collective-permute-start(bf16[192,1024]{1,0:T(8,128)(2,1)} %get-tuple-element.76), channel_id=1, source_target_pairs={{0,4},{1,5},{2,6},{3,7},{4,0},{5,1},{6,2},{7,3},{8,12},{9,13},{10,... | collective-permute-start | bytes 1179656 | tf_op jit(solution)/shard_map/ppermute | solution.py:110
  103.5 18.4 %collective-permute-start.17 = (bf16[192,1024]{1,0:T(8,128)(2,1)}, bf16[192,1024]{1,0:T(8,128)(2,1)S(1)}, u32[]{:S(2)}, u32[]{:S(2)}) collective-permute-start(bf16[192,1024]{1,0:T(8,128)(2,1)} %get-tuple-element.76), channel_id=1, source_target_pairs={{0,2},{1,3},{2,0},{3,1},{4,6},{5,7},{6,4},{7,5},{8,10},{9,11},{10,... | collective-permute-start | bytes 1179656 | tf_op jit(solution)/shard_map/ppermute | solution.py:110
  107.1 15.3 %copy-start.19 = (bf16[576,1024]{1,0:T(8,128)(2,1)S(1)}, bf16[576,1024]{1,0:T(8,128)(2,1)}, u32[]{:S(2)}) copy-start(bf16[576,1024]{1,0:T(8,128)(2,1)} %get-tuple-element.82.refs_3_) | copy-start | bytes 3538948
  107.1 15.2 %copy-start.23 = (bf16[576,128]{1,0:T(8,128)(2,1)S(1)}, bf16[576,128]{1,0:T(8,128)(2,1)}, u32[]{:S(2)}) copy-start(bf16[576,128]{1,0:T(8,128)(2,1)} %get-tuple-element.83.refs_4_) | copy-start | bytes 442372
  113.9 12.7 %collective-permute-start.22 = (bf16[192,1024]{1,0:T(8,128)(2,1)S(1)}, bf16[192,1024]{1,0:T(8,128)(2,1)S(1)}, u32[]{:S(2)}, u32[]{:S(2)}) collective-permute-start(bf16[192,1024]{1,0:T(8,128)(2,1)S(1)} %shard_map.119.refs_2_), channel_id=1, source_target_pairs={{0,1},{1,0},{2,3},{3,2},{4,5},{5,4},{6,7},{7,6},{8,9},{9,8},{10,11... | collective-permute-start | bytes 1179656 | tf_op jit(solution)/shard_map/ppermute | solution.py:110
  121.8 4.8 %collective-permute-start.21 = (bf16[192,1024]{1,0:T(8,128)(2,1)S(1)}, bf16[192,1024]{1,0:T(8,128)(2,1)S(1)}, u32[]{:S(2)}, u32[]{:S(2)}) collective-permute-start(bf16[192,1024]{1,0:T(8,128)(2,1)S(1)} %shard_map.118.refs_1_), channel_id=1, source_target_pairs={{0,1},{1,0},{2,3},{3,2},{4,5},{5,4},{6,7},{7,6},{8,9},{9,8},{10,11... | collective-permute-start | bytes 1179656 | tf_op jit(solution)/shard_map/ppermute | solution.py:110
  122.0 4.7 %collective-permute-start.20 = (bf16[192,1024]{1,0:T(8,128)(2,1)S(1)}, bf16[192,1024]{1,0:T(8,128)(2,1)S(1)}, u32[]{:S(2)}, u32[]{:S(2)}) collective-permute-start(bf16[192,1024]{1,0:T(8,128)(2,1)S(1)} %shard_map.117.refs_0_), channel_id=1, source_target_pairs={{0,1},{1,0},{2,3},{3,2},{4,5},{5,4},{6,7},{7,6},{8,9},{9,8},{10,11... | collective-permute-start | bytes 1179656 | tf_op jit(solution)/shard_map/ppermute | solution.py:110
  132.1 1.9 %collective-permute-start.23 = (bf16[1280,128]{1,0:T(8,128)(2,1)}, bf16[1280,128]{1,0:T(8,128)(2,1)S(1)}, u32[]{:S(2)}, u32[]{:S(2)}) collective-permute-start(bf16[1280,128]{1,0:T(8,128)(2,1)} %get-tuple-element.92), channel_id=1, source_target_pairs={{0,1},{1,0},{2,3},{3,2},{4,5},{5,4},{6,7},{7,6},{8,9},{9,8},{10,11... | collective-permute-start | bytes 983048 | tf_op jit(solution)/shard_map/ppermute | solution.py:110
  134.0 32.2 %copy-start = (bf16[1,1024,1024]{2,1,0:T(8,128)(2,1)S(1)}, bf16[1,1024,1024]{2,1,0:T(8,128)(2,1)}, u32[]{:S(2)}) copy-start(bf16[1,1024,1024]{2,1,0:T(8,128)(2,1)} %w_ref.5) | copy-start | bytes 6291460
  135.4 9.4 %copy-start.25 = (bf16[896,128]{1,0:T(8,128)(2,1)S(1)}, bf16[896,128]{1,0:T(8,128)(2,1)}, u32[]{:S(2)}) copy-start(bf16[896,128]{1,0:T(8,128)(2,1)} %get-tuple-element.94) | copy-start | bytes 688132
  135.4 11.2 %copy-start.27 = (bf16[384,128]{1,0:T(8,128)(2,1)S(1)}, bf16[384,128]{1,0:T(8,128)(2,1)}, u32[]{:S(2)}) copy-start(bf16[384,128]{1,0:T(8,128)(2,1)} %get-tuple-element.95) | copy-start | bytes 294916
  135.4 12.7 %copy-start.26 = (bf16[384,128]{1,0:T(8,128)(2,1)S(1)}, bf16[384,128]{1,0:T(8,128)(2,1)}, u32[]{:S(2)}) copy-start(bf16[384,128]{1,0:T(8,128)(2,1)} %get-tuple-element.96) | copy-start | bytes 294916
  135.4 36.5 %all-to-all-start = ((bf16[32,32,384]{2,1,0:T(8,128)(2,1)}), bf16[32,32,384]{2,1,0:T(8,128)(2,1)S(1)}, u32[]{:S(2)}, u32[]{:S(2)}) async-start(bf16[32,32,384]{2,1,0:T(8,128)(2,1)} %bitcast.5), calls=%async_computation | async-start | bytes 1572864 | tf_op jit(solution)/shard_map/all_to_all | solution.py:912
  144.8 15.6 %collective-permute-start.24 = (bf16[896,128]{1,0:T(8,128)(2,1)S(1)}, bf16[896,128]{1,0:T(8,128)(2,1)S(1)}, u32[]{:S(2)}, u32[]{:S(2)}) collective-permute-start(bf16[896,128]{1,0:T(8,128)(2,1)S(1)} %copy-done.25), channel_id=1, source_target_pairs={{0,2},{1,3},{2,0},{3,1},{4,6},{5,7},{6,4},{7,5},{8,10},{9,11},{10,... | collective-permute-start | bytes 688136 | tf_op jit(solution)/shard_map/ppermute | solution.py:110
  146.6 19.6 %collective-permute-start.25 = (bf16[384,128]{1,0:T(8,128)(2,1)S(1)}, bf16[384,128]{1,0:T(8,128)(2,1)S(1)}, u32[]{:S(2)}, u32[]{:S(2)}) collective-permute-start(bf16[384,128]{1,0:T(8,128)(2,1)S(1)} %copy-done.27), channel_id=1, source_target_pairs={{0,4},{1,5},{2,6},{3,7},{4,0},{5,1},{6,2},{7,3},{8,12},{9,13},{10,... | collective-permute-start | bytes 294920 | tf_op jit(solution)/shard_map/ppermute | solution.py:110
  148.1 18.1 %collective-permute-start.26 = (bf16[384,128]{1,0:T(8,128)(2,1)S(1)}, bf16[384,128]{1,0:T(8,128)(2,1)S(1)}, u32[]{:S(2)}, u32[]{:S(2)}) collective-permute-start(bf16[384,128]{1,0:T(8,128)(2,1)S(1)} %copy-done.26), channel_id=1, source_target_pairs={{0,6},{1,7},{2,4},{3,5},{4,2},{5,3},{6,0},{7,1},{8,14},{9,15},{10,... | collective-permute-start | bytes 294920 | tf_op jit(solution)/shard_map/ppermute | solution.py:110
  161.7 7.9 %collective-permute-start.27 = (bf16[256,128]{1,0:T(8,128)(2,1)}, bf16[256,128]{1,0:T(8,128)(2,1)S(1)}, u32[]{:S(2)}, u32[]{:S(2)}) collective-permute-start(bf16[256,128]{1,0:T(8,128)(2,1)} %get-tuple-element.102), channel_id=1, source_target_pairs={{0,8},{8,0},{16,24},{24,16},{1,9},{9,1},{17,25},{25,17},{2,10},{10... | collective-permute-start | bytes 196616 | tf_op jit(solution)/shard_map/ppermute | solution.py:853
  163.2 6.8 %collective-permute-start.28 = (bf16[256,128]{1,0:T(8,128)(2,1)}, bf16[256,128]{1,0:T(8,128)(2,1)S(1)}, u32[]{:S(2)}, u32[]{:S(2)}) collective-permute-start(bf16[256,128]{1,0:T(8,128)(2,1)} %get-tuple-element.103), channel_id=1, source_target_pairs={{0,16},{8,24},{16,0},{24,8},{1,17},{9,25},{17,1},{25,9},{2,18},{10... | collective-permute-start | bytes 196616 | tf_op jit(solution)/shard_map/ppermute | solution.py:853
  165.6 6.3 %collective-permute-start.29 = (bf16[256,128]{1,0:T(8,128)(2,1)}, bf16[256,128]{1,0:T(8,128)(2,1)S(1)}, u32[]{:S(2)}, u32[]{:S(2)}) collective-permute-start(bf16[256,128]{1,0:T(8,128)(2,1)} %get-tuple-element.104), channel_id=1, source_target_pairs={{0,24},{8,16},{16,8},{24,0},{1,25},{9,17},{17,9},{25,1},{2,26},{10... | collective-permute-start | bytes 196616 | tf_op jit(solution)/shard_map/ppermute | solution.py:853
  (13 other events, 28.9 us)
Sparse Core Ops, SparseCore 0:
  43.1 34.9 all-gather.1

commit v5 on v4

--- a/solution.py
+++ b/solution.py
@@ -20,6 +20,7 @@
 TOKEN = pltpu.VMEM((8, 128), jnp.float32)
 LANES = 128
 EDGE_ROWS = 16
+BF16_ROWS = 16
 
 
 def params(mib):
@@ -311,49 +312,52 @@
     return -(-(rows + 1) // LANES) * LANES
 
 
-def far_body(tp_count, info_ref, kv_in_ref, q3_ref, q2_ref, kv, *refs):
-    back3, back2, token_ref, far_top, far_den = refs
-    token_ref[...] = jnp.zeros_like(token_ref)
+def far_body(tp_count, info_ref, kv_in_ref, q_ref, *refs):
+    first = len(refs) == 6
+    if first:
+        kv, back, given_ref, token_ref, top, dens_ref = refs
+        token_ref[...] = jnp.zeros_like(token_ref)
+    else:
+        given_ref, kv, back, top = refs
     kv_ref = kv()
-    rows, width = q2_ref.shape
+    rows, width = q_ref.shape
     heads = heads_of(width)
     count = len(heads)
     keys, values = slice(0, rows), slice(rows, 2 * rows)
-    last = last_row(info_ref, rows, tp_count)
-    spread = den_lanes(rows) - rows
-
-    def sums(q_ref, at_rows, top_ref):
+
+    def sums(source_ref, at_rows):
         size = at_rows.stop - at_rows.start
         lane = lax.broadcasted_iota(jnp.int32, (size, LANES), 1)
         dens = jnp.zeros((size, LANES), F32)
+        tops = []
         for h, at in enumerate(heads):
-            q = q_ref[at_rows, at]
+            q = source_ref[at_rows, at]
             own, own_den = weigh(q, kv_ref[keys, at])
             other, other_den = weigh(q, kv_in_ref[keys, at])
-            top_ref[:size, at] = dot(own.astype(BF16), kv_ref[values, at]) + dot(
-                other.astype(BF16), kv_in_ref[values, at]
+            tops.append(
+                dot(own.astype(BF16), kv_ref[values, at])
+                + dot(other.astype(BF16), kv_in_ref[values, at])
             )
             dens = jnp.where(lane == h, own_den + other_den, dens)
-        return dens
-
-    def fill(back, top, den, edge_top, edge_den):
-        back.ref[:rows, :] = top.astype(BF16)
-        back.ref[rows : rows + EDGE_ROWS, :] = edge_top.astype(BF16)
-        den = jnp.concatenate([den, jnp.broadcast_to(edge_den, (spread, LANES))], axis=0)
-        turned = split_den(den, count).T[:EDGE_ROWS].astype(BF16)
-        back.ref[rows + EDGE_ROWS :, : turned.shape[1]] = turned
-        if turned.shape[1] < width:
-            rest = jnp.zeros((EDGE_ROWS, width - turned.shape[1]), BF16)
-            back.ref[rows + EDGE_ROWS :, turned.shape[1] :] = rest
-        back.send()
-
-    everything = slice(0, rows)
-    far_den[...] = sums(q2_ref, everything, far_top.at[0])
-    den3 = sums(q3_ref, everything, far_top.at[1])
-    row = jnp.broadcast_to(far_top[0, pl.ds(last, 1), :], (EDGE_ROWS, width))
-    fill(back3, far_top[1], den3, row, far_den[pl.ds(last, 1), :])
-    edge_den = sums(kv_ref, slice(2 * rows, 2 * rows + EDGE_ROWS), far_top.at[1])
-    fill(back2, far_top[0], far_den[...], far_top[1, :EDGE_ROWS, :], edge_den[:1])
+        return jnp.concatenate(tops, axis=1), dens
+
+    top[...], dens = sums(q_ref, slice(0, rows))
+    if first:
+        dens_ref[...] = dens
+        last = last_row(info_ref, rows, tp_count)
+        given_ref[:, :width] = jnp.broadcast_to(top[pl.ds(last, 1), :], (EDGE_ROWS, width))
+        given_ref[:, width:] = jnp.broadcast_to(dens_ref[pl.ds(last, 1), :], (EDGE_ROWS, LANES))
+        edge_top, edge_den = sums(kv_ref, slice(2 * rows, 2 * rows + EDGE_ROWS))
+    else:
+        edge_top, edge_den = given_ref[:, :width], given_ref[:, width:]
+    back.ref[:rows, :] = top[...].astype(BF16)
+    back.ref[rows : rows + EDGE_ROWS, :] = edge_top.astype(BF16)
+    spread = jnp.broadcast_to(edge_den[:1], (den_lanes(rows) - rows, LANES))
+    turned = split_den(jnp.concatenate([dens, spread], axis=0), count).T[:EDGE_ROWS].astype(BF16)
+    back.ref[rows + EDGE_ROWS :, : turned.shape[1]] = turned
+    if turned.shape[1] < width:
+        rest = jnp.zeros((EDGE_ROWS, width - turned.shape[1]), BF16)
+        back.ref[rows + EDGE_ROWS :, turned.shape[1] :] = rest
 
 
 def near_body(info_ref, kv_in_ref, mask_ref, _, q, kv, top_ref, den_ref, edge_ref):
@@ -384,19 +388,24 @@
 
 def attend_paired(info, q, kv, mask, tp_count):
     kv_in = lax.ppermute(kv, "ctx", [(0, 1), (2, 3)])
-    far = [lax.ppermute(q, "ctx", [(c, 1)]) for c in (3, 2)]
+    q2, q3 = (lax.ppermute(q, "ctx", [(c, 1)]) for c in (2, 3))
     rows, width = q.shape
     back = ((rows + 2 * EDGE_ROWS, width), BF16)
-    back3, back2, done = staged(
-        functools.partial(far_body, tp_count),
-        [kv_in, *far],
-        [back, back],
-        [TOKEN],
-        [pltpu.VMEM((2, rows, width), F32), pltpu.VMEM((rows, LANES), F32)],
+    body = functools.partial(far_body, tp_count)
+    tops = pltpu.VMEM((rows, width), F32)
+    back2, given, done = staged(
+        body,
+        [kv_in, q2],
+        [back],
+        [((EDGE_ROWS, width + LANES), F32), TOKEN],
+        [tops, pltpu.VMEM((rows, LANES), F32)],
         info,
         held=[kv],
     )
-    back = [lax.ppermute(back3, "ctx", [(1, 3)]), lax.ppermute(back2, "ctx", [(1, 2)])]
+    back2 = lax.ppermute(back2, "ctx", [(1, 2)])
+    back3 = staged(body, [kv_in, q3, given], [back], scratch=[tops], info=info, held=[kv])[0]
+    back3 = lax.ppermute(back3, "ctx", [(1, 3)])
+    back = [back2, back3]
     top, den, edge = staged(
         near_body,
         [kv_in, mask, done],
@@ -693,11 +702,12 @@
 def local_grads(x_refs, gb_ref, core_ref, w_ref, carry):
     x = rows_of(x_refs)
     rows = x_refs[0].shape[0]
-    allowed = window(rows)
+    tile = rows // 2 if rows % (2 * BF16_ROWS) == 0 else rows
+    allowed = window(tile)
     qkv = dot(x, w_ref[...])
     abs_, gqs = [], []
-    for index in range(len(x_refs)):
-        at = slice(index * rows, (index + 1) * rows)
+    for start in range(0, x.shape[0], tile):
+        at = slice(start, start + tile)
         query, key, vb, weight = core_weights(qkv[at], allowed)
         abs_.append(core_forward(weight, vb))
         gqs.append(core_backward(query, key, vb, weight, core_ref[at, :]))
@@ -709,53 +719,55 @@
     return gqkv, gout, abs_
 
 
-def local_last_body(count, info_ref, *refs):
+def local_last_body(count, rounds, info_ref, *refs):
     x_refs, refs = refs[:count], refs[count:]
-    gb_ref, core_ref, w_ref, *carry, ab0_ref, gqkv_out, message, kept_ref, held = refs
+    gb_ref, core_ref, w_ref, *refs = refs
+    *carry, ab0_ref = refs[:3]
+    gqkv_out, message, *pieces = refs[3 : 4 + rounds]
+    own_ref, held = refs[4 + rounds :]
     gqkv, gout, abs_ = local_grads(x_refs, gb_ref, core_ref, w_ref, carry)
+    held[...] = gout
+    deep = own_ref.shape[0]
+    piece_rows = deep * LANES // held.shape[1]
+    for k in range(rounds):
+        at = pl.multiple_of((info_ref[2] ^ k) * piece_rows, piece_rows)
+        piece = chunks_in(held[pl.ds(at, piece_rows), :]).astype(BF16)
+        if k:
+            pieces[k - 1].ref[...] = piece
+            pieces[k - 1].send()
+        else:
+            own_ref[...] = piece
     gqkv_out.ref[...] = gqkv.T.astype(BF16)
     gqkv_out.send()
-    held[...] = gout
     rows = x_refs[0].shape[0]
     message.ref[:rows, :] = ab0_ref[rows:, :]
-    for index, ab in enumerate(abs_):
-        message.ref[(index + 1) * rows : (index + 2) * rows, :] = ab
-    deep = kept_ref.shape[1]
-    piece_rows = deep * LANES // held.shape[1]
-    for k in range(held.shape[0] // piece_rows):
-        at = pl.multiple_of((info_ref[2] ^ k) * piece_rows, piece_rows)
-        piece = chunks_in(held[pl.ds(at, piece_rows), :]).astype(BF16)
-        if k % 2:
-            start = (count + 1) * rows + k // 2 * deep
-            message.ref[start : start + deep, :] = piece
-        else:
-            kept_ref[k // 2] = piece
-
-
-def relay_body(count, ab0_ref, ab1_ref, kept_ref, there_ref, *refs):
+    message.ref[rows:, :] = jnp.concatenate(abs_, axis=0)
+
+
+def relay_body(count, rounds, planes, info_ref, *refs):
+    (ab0_ref, ab1_ref, there_ref), refs = refs[:3], refs[3:]
+    pieces, refs = refs[:rounds], refs[rounds:]
+    messages, outs, (own_ref, held) = refs[:count], refs[count : count + planes], refs[count + planes :]
     rows = ab0_ref.shape[0] // 2
-    deep = kept_ref.shape[1]
-    *messages, own, token_ref = refs
-    token_ref[...] = jnp.zeros_like(token_ref)
-    for k, message in enumerate([own, *messages]):
-        parts = []
-        if k <= count:
-            parts.append(ab0_ref[:rows, :] if k == 0 else ab1_ref[(k - 1) * rows : k * rows, :])
-            parts.append(there_ref[k * rows : (k + 1) * rows, :])
-        if k < kept_ref.shape[0]:
-            start = (count + 1) * rows + k * deep
-            parts.append(kept_ref[k])
-            parts.append(there_ref[start : start + deep, :])
-        at = 0
-        target = message if k == 0 else message.ref
-        for part in parts:
-            target[at : at + part.shape[0], :] = part
-            at += part.shape[0]
+    for k, piece in enumerate(pieces):
+        held[k] = piece[...].astype(F32)
+    for z, out in enumerate(outs):
+        total = None
+        for outer in range(rounds // planes):
+            term = held[info_ref[2] ^ ((info_ref[3] ^ z) + outer * planes)]
+            total = term if total is None else total + term
+        out.ref[...] = total.astype(BF16)
+        out.send()
+    for k in range(count + 1):
+        mine = ab0_ref[:rows, :] if k == 0 else ab1_ref[(k - 1) * rows : k * rows, :]
+        target = messages[k - 1].ref if k else own_ref
+        target[:rows, :] = mine
+        target[rows:, :] = there_ref[k * rows : (k + 1) * rows, :]
         if k:
-            message.send()
-
-
-def local_layer(normed, normed_near, info, parts, gbs, cores, weights, rounds, tp_count):
+            messages[k - 1].send()
+
+
+def local_layer(normed, normed_near, info, parts, gbs, cores, weights, rounds, planes):
     rows, width = normed.shape
     d = LOCAL_HEAD_DIM
     near = [swap(normed, bits) for bits in parts[1]]
@@ -777,27 +789,29 @@
     far = [swap(block, 1) for block in near]
     *carry, ab1, _ = step(1, near, carry)
     deep = d // rounds * width // LANES
-    halves = rounds // 2
-    length = (count + 1) * rows + halves * deep
-    grad_qkv, message, kept = staged(
-        functools.partial(local_last_body, count),
+    piece = ((deep, d), BF16)
+    grad_qkv, message, *pieces, own = staged(
+        functools.partial(local_last_body, count, rounds),
         [*far, gbs[2], cores[2], weights, *carry, ab0],
-        [((width, 3 * d), BF16), ((length, d), BF16)],
-        [((halves, deep, d), BF16)],
+        [((width, 3 * d), BF16), (((count + 1) * rows, d), BF16)] + [piece] * (rounds - 1),
+        [piece],
         [pltpu.VMEM((d, width), F32)],
         info,
         flops=1 << 34,
         mib=20,
     )
-    sizes = [2 * rows * (k <= count) + 2 * deep * (k < halves) for k in range(max(count + 1, halves))]
-    *messages, own, done = staged(
-        functools.partial(relay_body, count),
-        [ab0, ab1, kept, swap(message, 1)],
-        [((size, d), BF16) for size in sizes[1:]],
-        [((sizes[0], d), BF16), TOKEN],
-    )
-    messages = [own] + [swap(value, 2 * (k + 1)) for k, value in enumerate(messages)]
-    return messages, tie(grad_qkv, done, mib=LARGE)
+    pieces = [own] + [swap(value, k + 1) for k, value in enumerate(pieces)]
+    block = ((2 * rows, d), BF16)
+    *sent, own = staged(
+        functools.partial(relay_body, count, rounds, planes),
+        [ab0, ab1, swap(message, 1), *pieces],
+        [block] * count + [piece] * planes,
+        [block],
+        [pltpu.VMEM((rounds, deep, d), F32)],
+        info,
+    )
+    messages = [own] + [swap(value, 2 * (k + 1)) for k, value in enumerate(sent[:count])]
+    return messages, sent[count:], grad_qkv
 
 
 def hidden_body(heads, count, info_ref, state_ref, w_ref, *refs):
@@ -812,22 +826,6 @@
         weights = w_ref[0, pl.ds(pl.multiple_of(head * d, d), d), :]
         total += dot(messages[bits // 2][at : at + rows, :], weights)
     out_ref[...] = total.astype(BF16)
-
-
-def planes_body(planes, count, rounds, rows, info_ref, *refs):
-    half = rounds // 2
-    messages, outs, held = refs[:half], refs[half:-1], refs[-1]
-    deep = held.shape[1]
-    for k in range(rounds):
-        start = 2 * rows * (k // 2 <= count) + k % 2 * deep
-        held[k] = messages[k // 2][start : start + deep, :].astype(F32)
-    for z, out in enumerate(outs):
-        total = None
-        for outer in range(rounds // planes):
-            term = held[info_ref[2] ^ ((info_ref[3] ^ z) + outer * planes)]
-            total = term if total is None else total + term
-        out.ref[...] = total.astype(BF16)
-        out.send()
 
 
 def final_body(heads, parts_ref, _, *refs):
@@ -906,19 +904,11 @@
     state, normed, normed_near = byte_state(
         scatter_sum(even, odd, patches), local_embeds, prepared
     )
-    messages, grad_qkv = local_layer(
-        normed, normed_near, head_info, parts, gbs, cores, weights, rounds, tp_count
+    messages, out_pieces, grad_qkv = local_layer(
+        normed, normed_near, head_info, parts, gbs, cores, weights, rounds, planes
     )
     grad_qkv = lax.all_to_all(grad_qkv, ("ctx", "tp"), 0, 0, tiled=True)
-    flat = (share * width // LANES, LANES)
     count = group // 2 - 1
-    out_pieces = staged(
-        functools.partial(planes_body, planes, count, rounds, byte_count),
-        messages[: rounds // 2],
-        [(flat, BF16)] * planes,
-        scratch=[pltpu.VMEM((rounds,) + flat, F32)],
-        info=head_info,
-    )
     out_pieces = swap_planes(out_pieces)
     here = pl.BlockSpec(memory_space=pltpu.VMEM)
     hidden, done = pl.pallas_call(

time: 180 us -> 177 us (0.983)
  waiting for transfers between devices: 66.9 us -> 60.7 us
  starting transfers between devices: 37 us -> 42.3 us
    ppermute x22 -> x25, waiting for transfers between devices: 56.8 us -> 52.6 us  [swap(): lax.ppermute(value, 'tp', [(source, source ^ bits) for source in range(co...]
    ppermute x22 -> x25, starting transfers between devices: 16.6 us -> 18.7 us  [swap(): lax.ppermute(value, 'tp', [(source, source ^ bits) for source in range(co...]
    ppermute x3, starting transfers between devices: 4.45 us -> 6.57 us  [swap_planes(): lax.ppermute(pieces[k], 'ctx', [(c, c ^ k) for c in range(count)])]
    ppermute x3, waiting for transfers between devices: 2.28 us -> 0.27 us  [swap_planes(): lax.ppermute(pieces[k], 'ctx', [(c, c ^ k) for c in range(count)])]
    unnamed x58 -> x50, local copies, waits for them, and re-layouts: 6.73 us -> 5.21 us
  transfers between devices with their start and end apart: 32 -> 35, of which waited for: 16 -> 15; matrix products, arithmetic and copies ran while one was open for 0% -> 0% of each run, Pallas kernels for 19% -> 20%
where the time goes in v5:
time: 177 us; the launch traced here: 176 us
  waiting for transfers between devices  60.7 us (34%)
  Pallas kernels  52.7 us (30%)
  starting transfers between devices  42.3 us (24%)
  between operations  14.5 us (8%)
  local copies, waits for them, and re-layouts  5.29 us (3%)
    ppermute x25, waiting for transfers between devices, swap(): lax.ppermute(value, 'tp', [(source, source ^ bits) for source in range(co...  52.6 us
    pallas_call x8, Pallas kernels, staged(): pl.pallas_call(kernel, in_specs=[pl.BlockSpec(memory_space=pltpu.SMEM)] *...  20.8 us
    ppermute x25, starting transfers between devices, swap(): lax.ppermute(value, 'tp', [(source, source ^ bits) for source in range(co...  18.7 us
    all_to_all x1, starting transfers between devices, per_device(): grad_qkv = lax.all_to_all(grad_qkv, ('ctx', 'tp'), 0, 0, tiled=True)  10.2 us
    pallas_call x1, Pallas kernels, project(): pl.pallas_call(body, in_specs=[pl.BlockSpec(memory_space=pltpu.SMEM)] + [...  9.58 us
    pallas_call x2, Pallas kernels, preload(): pl.pallas_call(functools.partial(preload_body, parts), in_specs=[scalar,...  9.5 us
    ppermute x1, waiting for transfers between devices, attend_paired(): kv_in = lax.ppermute(kv, 'ctx', [(0, 1), (2, 3)])  7.74 us
    ppermute x3, starting transfers between devices, swap_planes(): lax.ppermute(pieces[k], 'ctx', [(c, c ^ k) for c in range(count)])  6.57 us
  transfers between devices with their start and end apart: 35, of which 15 were waited for; matrix products, arithmetic and copies ran while one was open for 0% of the time, Pallas kernels for 20%

profile of v5, /device:TPU:0, one launch (start us, length us, event | category | flops | bytes accessed | tf_op | source)
XLA Modules:
  0.0 176.2 jit_solution(17849914063137544701)
XLA Ops:
  7.2 1.0 copy-done.10
  9.1 2.6 %collective-permute-start.2 = (bf16[24,8192]{1,0:T(8,128)(2,1)S(1)}, bf16[24,8192]{1,0:T(8,128)(2,1)S(1)}, u32[]{:S(2)}, u32[]{:S(2)}) collective-permute-start(bf16[24,8192]{1,0:T(8,128)(2,1)S(1)} %shard_map.103.refs_1_), channel_id=1, source_target_pairs={{0,4},{1,5},{2,6},{3,7},{4,0},{5,1},{6,2},{7,3},{8,12},{9,13},{10,... | collective-permute-start | bytes 1179656 | tf_op jit(solution)/shard_map/ppermute | solution.py:111
  11.7 1.4 collective-permute-start.3
  13.8 0.7 copy-done.3
  14.5 4.7 %shard_map.104 = (bf16[8192,512]{1,0:T(8,128)(2,1)S(1)}, s32[4]{0:T(128)}) custom-call(s32[4]{0:T(128)} %pad_add_fusion.info_ref, bf16[3,8192,512]{2,1,0:T(8,128)(2,1)} %refs_11_.1, bf16[24,8192]{1,0:T(8,128)(2,1)} %copy-done.3), custom_call_target="tpu_custom_call" | custom-call | bytes 8388608 | tf_op jit(solution)/shard_map/pallas_call | solution.py:157
  19.2 10.6 %collective-permute-done.2.refs_0_ = bf16[24,8192]{1,0:T(8,128)(2,1)S(1)} collective-permute-done((bf16[24,8192]{1,0:T(8,128)(2,1)S(1)}, bf16[24,8192]{1,0:T(8,128)(2,1)S(1)}, u32[]{:S(2)}, u32[]{:S(2)}) %collective-permute-start.2) | collective-permute-done | bytes 393248 | tf_op jit(solution)/shard_map/ppermute | solution.py:111
  31.1 1.1 collective-permute-done.5.refs_7_
  33.3 9.6 %shard_map.108 = (bf16[192,512]{1,0:T(8,128)(2,1)}, bf16[400,512]{1,0:T(8,128)(2,1)}, bf16[192,1024]{1,0:T(8,128)(2,1)}) custom-call(s32[4]{0:T(128)S(1)} %copy-done.12, bf16[24,8192]{1,0:T(8,128)(2,1)S(1)} %shard_map.103.refs_1_, bf16[24,8192]{1,0:T(8,128)(2,1)S(1)} %shard_map.105.refs_2_, bf16[24,8192]{1,0:T(8,128)(2,1)S(1)} %shard_map.106.refs_3_, ...), custom_call_target="tpu_custom_call" | custom-call | tf_op jit(solution)/shard_map/pallas_call | solution.py:266
  42.9 3.9 %collective-permute-start.7 = (bf16[400,512]{1,0:T(8,128)(2,1)}, bf16[400,512]{1,0:T(8,128)(2,1)S(1)}, u32[]{:S(2)}, u32[]{:S(2)}) collective-permute-start(bf16[400,512]{1,0:T(8,128)(2,1)} %get-tuple-element.59.refs_3_.refs_4_.refs_5_), channel_id=1, source_target_pairs={{0,8},{16,24},{1,9},{17,25},{2,10},{18,26},{3,11},{19,27},{4,12},{... | collective-permute-start | bytes 1228808 | tf_op jit(solution)/shard_map/ppermute | solution.py:390
  46.8 0.7 collective-permute-start.8
  47.5 0.7 collective-permute-start.10
  48.3 7.7 %collective-permute-done.7.refs_1_ = bf16[400,512]{1,0:T(8,128)(2,1)S(1)} collective-permute-done((bf16[400,512]{1,0:T(8,128)(2,1)}, bf16[400,512]{1,0:T(8,128)(2,1)S(1)}, u32[]{:S(2)}, u32[]{:S(2)}) %collective-permute-start.7) | collective-permute-done | bytes 409632 | tf_op jit(solution)/shard_map/ppermute | solution.py:390
  56.1 1.0 copy-done.1
  57.1 2.9 %shard_map.109 = (bf16[224,512]{1,0:T(8,128)(2,1)}, f32[16,640]{1,0:T(8,128)S(1)}, f32[8,128]{1,0:T(8,128)S(1)}) custom-call(s32[4]{0:T(128)S(1)} %copy-done.13, bf16[400,512]{1,0:T(8,128)(2,1)S(1)} %collective-permute-done.7.refs_1_, bf16[192,512]{1,0:T(8,128)(2,1)S(1)} %collective-permute-done.8.refs_2_, bf16[400,512]{1,0:T(8,128)(2,1)S(1)} %copy-done.1), custom_call_target="tpu_custom_call" | custom-call | bytes 4194304 | tf_op jit(solution)/shard_map/pallas_call | solution.py:88
  60.0 2.3 %shard_map.110 = bf16[224,512]{1,0:T(8,128)(2,1)} custom-call(s32[4]{0:T(128)S(1)} %copy-done.13, bf16[400,512]{1,0:T(8,128)(2,1)S(1)} %collective-permute-done.7.refs_1_, bf16[192,512]{1,0:T(8,128)(2,1)S(1)} %collective-permute-done.10.refs_2_, f32[16,640]{1,0:T(8,128)S(1)} %get-tuple-element.62.refs_3_, bf16[400,512]{1,0:T(8,128)(2,1)S(1)} %copy-done.1), custom_call_target="tpu_custom_call" | custom-call | bytes 4194304 | tf_op jit(solution)/shard_map/pallas_call | solution.py:88
  62.3 0.7 collective-permute-start.11
  62.9 0.9 collective-permute-start.9
  63.9 2.2 %shard_map.111 = (f32[192,512]{1,0:T(8,128)S(1)}, f32[192,128]{1,0:T(8,128)S(1)}, f32[16,640]{1,0:T(8,128)S(1)}) custom-call(s32[4]{0:T(128)S(1)} %copy-done.13, bf16[400,512]{1,0:T(8,128)(2,1)S(1)} %collective-permute-done.7.refs_1_, f32[192,192]{1,0:T(8,128)S(1)} %compare_convert_fusion.refs_2_, f32[8,128]{1,0:T(8,128)S(1)} %get-tuple-element.63.refs_3_, ...), custom_call_target="tpu_custom_call" | custom-call | bytes 4194304 | tf_op jit(solution)/shard_map/pallas_call | solution.py:88
  66.8 4.9 %shard_map.112 = (bf16[512,8192]{1,0:T(8,128)(2,1)S(1)}, s32[4]{0:T(128)}) custom-call(s32[4]{0:T(128)} %get-tuple-element.57.refs_1_.refs_0_.info_ref, bf16[512,8192]{1,0:T(8,128)(2,1)} %w_ref.4, f32[192,128]{1,0:T(8,128)} %copy-done.7), custom_call_target="tpu_custom_call" | custom-call | bytes 8388608 | tf_op jit(solution)/shard_map/pallas_call | solution.py:157
  71.7 3.4 %shard_map.113 = (bf16[96,8192]{1,0:T(8,128)(2,1)}, bf16[96,8192]{1,0:T(8,128)(2,1)S(1)}) custom-call(s32[4]{0:T(128)S(1)} %copy-done.14, bf16[224,512]{1,0:T(8,128)(2,1)S(1)} %collective-permute-done.9.refs_0_, bf16[224,512]{1,0:T(8,128)(2,1)S(1)} %collective-permute-done.11.refs_1_, f32[192,512]{1,0:T(8,128)S(1)} %get-tuple-element.64.refs_2_, ...), custom_call_target="tpu_custom_call" | custom-call | tf_op jit(solution)/shard_map/pallas_call | solution.py:517
  75.2 3.6 %collective-permute-done.12.other_ref = bf16[96,8192]{1,0:T(8,128)(2,1)S(1)} collective-permute-done((bf16[96,8192]{1,0:T(8,128)(2,1)}, bf16[96,8192]{1,0:T(8,128)(2,1)S(1)}, u32[]{:S(2)}, u32[]{:S(2)}) %collective-permute-start.12) | collective-permute-done | bytes 1572896 | tf_op jit(solution)/shard_map/ppermute | solution.py:111
  79.2 1.6 collective-permute-start.13
  80.7 1.5 collective-permute-start.14
  82.7 5.5 %shard_map.115 = (f32[8,128]{1,0:T(8,128)S(1)}, bf16[1024,384]{1,0:T(8,128)(2,1)}, bf16[384,1024]{1,0:T(8,128)(2,1)}, bf16[384,128]{1,0:T(8,128)(2,1)}, bf16[576...) custom-call(s32[4]{0:T(128)} %get-tuple-element.57.refs_1_.refs_0_.info_ref,, ...), custom_call_target="tpu_custom_call" | custom-call | tf_op jit(solution)/shard_map/pallas_call | solution.py:623
  88.2 2.9 %collective-permute-done.13.refs_1_ = bf16[24,8192]{1,0:T(8,128)(2,1)S(1)} collective-permute-done((bf16[24,8192]{1,0:T(8,128)(2,1)S(1)}, bf16[24,8192]{1,0:T(8,128)(2,1)S(1)}, u32[]{:S(2)}, u32[]{:S(2)}) %collective-permute-start.13) | collective-permute-done | bytes 393248 | tf_op jit(solution)/shard_map/ppermute | solution.py:111
  91.2 8.8 %collective-permute-done.14.refs_2_ = bf16[24,8192]{1,0:T(8,128)(2,1)S(1)} collective-permute-done((bf16[24,8192]{1,0:T(8,128)(2,1)S(1)}, bf16[24,8192]{1,0:T(8,128)(2,1)S(1)}, u32[]{:S(2)}, u32[]{:S(2)}) %collective-permute-start.14) | collective-permute-done | bytes 393248 | tf_op jit(solution)/shard_map/ppermute | solution.py:111
  100.0 1.6 shard_map.116
  101.7 1.5 collective-permute-start.19
  103.2 1.2 collective-permute-start.18
  104.5 0.8 collective-permute-start.17
  105.3 2.4 %shard_map.117 = (f32[384,1024]{1,0:T(8,128)S(1)}, f32[128,1024]{1,0:T(8,128)S(1)}, bf16[384,128]{1,0:T(8,128)(2,1)S(1)}, f32[8,128]{1,0:T(8,128)S(1)}) custom-call(bf16[192,1024]{1,0:T(8,128)(2,1)S(1)} %get-tuple-element.77.refs_0_, bf16[192,1024]{1,0:T(8,128)(2,1)S(1)} %collective-permute-done.16.refs_1_, bf16[384,1024]{1,0:T(8,128)(2,1)S(1)} %copy-done.20, ...), custom_call_target="tpu_custom_call" | custom-call | flops 17179869184 | bytes 4194304 | tf_op jit(solution)/shard_map/pallas_call | solution.py:88
  107.7 7.1 %collective-permute-done.19.refs_0_ = bf16[192,1024]{1,0:T(8,128)(2,1)S(1)} collective-permute-done((bf16[192,1024]{1,0:T(8,128)(2,1)}, bf16[192,1024]{1,0:T(8,128)(2,1)S(1)}, u32[]{:S(2)}, u32[]{:S(2)}) %collective-permute-start.19) | collective-permute-done | bytes 393248 | tf_op jit(solution)/shard_map/ppermute | solution.py:111
  114.8 7.9 %collective-permute-done.18.refs_0_ = bf16[192,1024]{1,0:T(8,128)(2,1)S(1)} collective-permute-done((bf16[192,1024]{1,0:T(8,128)(2,1)}, bf16[192,1024]{1,0:T(8,128)(2,1)S(1)}, u32[]{:S(2)}, u32[]{:S(2)}) %collective-permute-start.18) | collective-permute-done | bytes 393248 | tf_op jit(solution)/shard_map/ppermute | solution.py:111
  123.3 3.5 %shard_map.121 = (f32[384,1024]{1,0:T(8,128)S(1)}, f32[128,1024]{1,0:T(8,128)S(1)}, bf16[576,128]{1,0:T(8,128)(2,1)S(1)}, f32[8,128]{1,0:T(8,128)}) custom-call(bf16[192,1024]{1,0:T(8,128)(2,1)S(1)} %shard_map.118.refs_0_, bf16[192,1024]{1,0:T(8,128)(2,1)S(1)} %shard_map.119.refs_1_, bf16[192,1024]{1,0:T(8,128)(2,1)S(1)} %shard_map.120.refs_2_, ...), custom_call_target="tpu_custom_call" | custom-call | flops 17179869184 | bytes 4194304 | tf_op jit(solution)/shard_map/pallas_call | solution.py:88
  126.8 4.6 %shard_map.122 = (bf16[1024,384]{1,0:T(8,128)(2,1)}, bf16[768,128]{1,0:T(8,128)(2,1)}, bf16[256,128]{1,0:T(8,128)(2,1)}, bf16[256,128]{1,0:T(8,128)(2,1)}, bf16[...) custom-call(s32[4]{0:T(128)S(1)} %copy-done.15, bf16[192,1024]{1,0:T(8,128)(2,1)S(1)} %collective-permute-done.20.refs_1_, ...), custom_call_target="tpu_custom_call" | custom-call | flops 17179869184 | bytes 4194304 | tf_op jit(solution)/shard_map/pallas_call | solution.py:88
  131.4 10.2 %all-to-all-start = ((bf16[32,32,384]{2,1,0:T(8,128)(2,1)}), bf16[32,32,384]{2,1,0:T(8,128)(2,1)S(1)}, u32[]{:S(2)}, u32[]{:S(2)}) async-start(bf16[32,32,384]{2,1,0:T(8,128)(2,1)} %bitcast.5), calls=%async_computation | async-start | bytes 1572864 | tf_op jit(solution)/shard_map/all_to_all | solution.py:910
  142.2 1.8 %collective-permute-start.25 = (bf16[256,128]{1,0:T(8,128)(2,1)}, bf16[256,128]{1,0:T(8,128)(2,1)S(1)}, u32[]{:S(2)}, u32[]{:S(2)}) collective-permute-start(bf16[256,128]{1,0:T(8,128)(2,1)} %get-tuple-element.96), channel_id=1, source_target_pairs={{0,2},{1,3},{2,0},{3,1},{4,6},{5,7},{6,4},{7,5},{8,10},{9,11},{10,... | collective-permute-start | bytes 196616 | tf_op jit(solution)/shard_map/ppermute | solution.py:111
  144.0 8.0 %collective-permute-done.25.refs_6_ = bf16[256,128]{1,0:T(8,128)(2,1)S(1)} collective-permute-done((bf16[256,128]{1,0:T(8,128)(2,1)}, bf16[256,128]{1,0:T(8,128)(2,1)S(1)}, u32[]{:S(2)}, u32[]{:S(2)}) %collective-permute-start.25) | collective-permute-done | bytes 65568 | tf_op jit(solution)/shard_map/ppermute | solution.py:111
  152.0 1.1 collective-permute-done.26.refs_7_
  153.2 1.5 shard_map.123
  154.6 0.7 collective-permute-start.27
  155.3 1.5 collective-permute-start.28
  156.8 1.4 collective-permute-start.29
  158.6 3.6 %collective-permute-start.31 = (bf16[256,128]{1,0:T(8,128)(2,1)}, bf16[256,128]{1,0:T(8,128)(2,1)S(1)}, u32[]{:S(2)}, u32[]{:S(2)}) collective-permute-start(bf16[256,128]{1,0:T(8,128)(2,1)} %get-tuple-element.107), channel_id=1, source_target_pairs={{0,16},{8,24},{16,0},{24,8},{1,17},{9,25},{17,1},{25,9},{2,18},{10... | collective-permute-start | bytes 196616 | tf_op jit(solution)/shard_map/ppermute | solution.py:851
  162.2 2.6 %collective-permute-start.32 = (bf16[256,128]{1,0:T(8,128)(2,1)}, bf16[256,128]{1,0:T(8,128)(2,1)S(1)}, u32[]{:S(2)}, u32[]{:S(2)}) collective-permute-start(bf16[256,128]{1,0:T(8,128)(2,1)} %get-tuple-element.108), channel_id=1, source_target_pairs={{0,24},{8,16},{16,8},{24,0},{1,25},{9,17},{17,9},{25,1},{2,26},{10... | collective-permute-start | bytes 196616 | tf_op jit(solution)/shard_map/ppermute | solution.py:851
  164.8 1.1 copy-done.5
  165.9 2.3 %shard_map.124 = (bf16[192,1024]{1,0:T(8,128)(2,1)}, f32[8,128]{1,0:T(8,128)S(1)}) custom-call(s32[4]{0:T(128)S(1)} %copy-done.15, f32[192,1024]{1,0:T(8,128)S(1)} %copy-done.5, bf16[1,1024,1024]{2,1,0:T(8,128)(2,1)S(1)} %copy-done, bf16[384,128]{1,0:T(8,128)(2,1)S(1)} %get-tuple-element.98.refs_0_, bf16[384,128]{1,0:T(8,128)(2,1)S(1)} %collective-permute-done.27.refs_1_, ...), custom_call_target="tpu_custom_call" | custom-call | tf_op jit(solution)/shard_map/pallas_call | solution.py:914
  168.5 0.9 shard_map.125
  (101 shorter events, 7.7 us)
Async XLA Ops:
  7.2 75.6 %all-gather.2.cloned.1.call-start = ((), (), s32[]{:S(2)}) async-start(), calls=%async_computation.1 | async-start | bytes 3538944 | tf_op jit(solution)/shard_map/all_gather | solution.py:902
  8.5 5.2 %collective-permute-start = (bf16[24,8192]{1,0:T(8,128)(2,1)S(1)}, bf16[24,8192]{1,0:T(8,128)(2,1)S(1)}, u32[]{:S(2)}, u32[]{:S(2)}) collective-permute-start(bf16[24,8192]{1,0:T(8,128)(2,1)S(1)} %shard_map.103.refs_1_), channel_id=1, source_target_pairs={{0,1},{1,0},{2,3},{3,2},{4,5},{5,4},{6,7},{7,6},{8,9},{9,8},{10,11... | collective-permute-start | bytes 1179656 | tf_op jit(solution)/shard_map/ppermute | solution.py:111
  9.1 20.7 %collective-permute-start.2 = (bf16[24,8192]{1,0:T(8,128)(2,1)S(1)}, bf16[24,8192]{1,0:T(8,128)(2,1)S(1)}, u32[]{:S(2)}, u32[]{:S(2)}) collective-permute-start(bf16[24,8192]{1,0:T(8,128)(2,1)S(1)} %shard_map.103.refs_1_), channel_id=1, source_target_pairs={{0,4},{1,5},{2,6},{3,7},{4,0},{5,1},{6,2},{7,3},{8,12},{9,13},{10,... | collective-permute-start | bytes 1179656 | tf_op jit(solution)/shard_map/ppermute | solution.py:111
  11.7 18.8 %collective-permute-start.3 = (bf16[24,8192]{1,0:T(8,128)(2,1)S(1)}, bf16[24,8192]{1,0:T(8,128)(2,1)S(1)}, u32[]{:S(2)}, u32[]{:S(2)}) collective-permute-start(bf16[24,8192]{1,0:T(8,128)(2,1)S(1)} %shard_map.103.refs_1_), channel_id=1, source_target_pairs={{0,6},{1,7},{2,4},{3,5},{4,2},{5,3},{6,0},{7,1},{8,14},{9,15},{10,... | collective-permute-start | bytes 1179656 | tf_op jit(solution)/shard_map/ppermute | solution.py:111
  13.1 18.0 %collective-permute-start.1 = (bf16[24,8192]{1,0:T(8,128)(2,1)S(1)}, bf16[24,8192]{1,0:T(8,128)(2,1)S(1)}, u32[]{:S(2)}, u32[]{:S(2)}) collective-permute-start(bf16[24,8192]{1,0:T(8,128)(2,1)S(1)} %shard_map.103.refs_1_), channel_id=1, source_target_pairs={{0,2},{1,3},{2,0},{3,1},{4,6},{5,7},{6,4},{7,5},{8,10},{9,11},{10,... | collective-permute-start | bytes 1179656 | tf_op jit(solution)/shard_map/ppermute | solution.py:111
  19.2 14.1 %copy-start.4 = (bf16[24,8192]{1,0:T(8,128)(2,1)S(1)}, bf16[24,8192]{1,0:T(8,128)(2,1)}, u32[]{:S(2)}) copy-start(bf16[24,8192]{1,0:T(8,128)(2,1)} %copy-done.3) | copy-start | bytes 1179652
  19.2 14.1 %copy-start.6 = (bf16[192,1024]{1,0:T(8,128)(2,1)S(1)}, bf16[192,1024]{1,0:T(8,128)(2,1)}, u32[]{:S(2)}) copy-start(bf16[192,1024]{1,0:T(8,128)(2,1)} %refs_10_.1) | copy-start | bytes 1179652
  30.4 1.7 collective-permute-start.5
  30.4 2.3 %collective-permute-start.6 = (bf16[24,8192]{1,0:T(8,128)(2,1)S(1)}, bf16[24,8192]{1,0:T(8,128)(2,1)S(1)}, u32[]{:S(2)}, u32[]{:S(2)}) collective-permute-start(bf16[24,8192]{1,0:T(8,128)(2,1)S(1)} %shard_map.107.refs_4_), channel_id=1, source_target_pairs={{0,1},{1,0},{2,3},{3,2},{4,5},{5,4},{6,7},{7,6},{8,9},{9,8},{10,11... | collective-permute-start | bytes 1179656 | tf_op jit(solution)/shard_map/ppermute | solution.py:111
  31.1 2.2 %collective-permute-start.4 = (bf16[24,8192]{1,0:T(8,128)(2,1)S(1)}, bf16[24,8192]{1,0:T(8,128)(2,1)S(1)}, u32[]{:S(2)}, u32[]{:S(2)}) collective-permute-start(bf16[24,8192]{1,0:T(8,128)(2,1)S(1)} %shard_map.105.refs_2_), channel_id=1, source_target_pairs={{0,1},{1,0},{2,3},{3,2},{4,5},{5,4},{6,7},{7,6},{8,9},{9,8},{10,11... | collective-permute-start | bytes 1179656 | tf_op jit(solution)/shard_map/ppermute | solution.py:111
  33.3 13.5 %copy-start.24 = (s32[8]{0:T(128)S(1)}, s32[8]{0:T(128)}, u32[]{:S(2)}) copy-start(s32[8]{0:T(128)} %constant.45.clone) | copy-start | bytes 100
  33.3 22.8 %copy-start.13 = (s32[4]{0:T(128)S(1)}, s32[4]{0:T(128)}, u32[]{:S(2)}) copy-start(s32[4]{0:T(128)} %get-tuple-element.57.refs_1_.refs_0_.info_ref) | copy-start | bytes 52
  42.9 21.0 %copy-start.2 = (bf16[400,512]{1,0:T(8,128)(2,1)S(1)}, bf16[400,512]{1,0:T(8,128)(2,1)}, u32[]{:S(2)}) copy-start(bf16[400,512]{1,0:T(8,128)(2,1)} %get-tuple-element.59.refs_3_.refs_4_.refs_5_) | copy-start | bytes 1228804
  42.9 13.2 %collective-permute-start.7 = (bf16[400,512]{1,0:T(8,128)(2,1)}, bf16[400,512]{1,0:T(8,128)(2,1)S(1)}, u32[]{:S(2)}, u32[]{:S(2)}) collective-permute-start(bf16[400,512]{1,0:T(8,128)(2,1)} %get-tuple-element.59.refs_3_.refs_4_.refs_5_), channel_id=1, source_target_pairs={{0,8},{16,24},{1,9},{17,25},{2,10},{18,26},{3,11},{19,27},{4,12},{... | collective-permute-start | bytes 1228808 | tf_op jit(solution)/shard_map/ppermute | solution.py:390
  46.8 1.5 collective-permute-start.8
  47.5 12.4 %collective-permute-start.10 = (bf16[192,512]{1,0:T(8,128)(2,1)}, bf16[192,512]{1,0:T(8,128)(2,1)S(1)}, u32[]{:S(2)}, u32[]{:S(2)}) collective-permute-start(bf16[192,512]{1,0:T(8,128)(2,1)} %get-tuple-element.60.refs_4_), channel_id=1, source_target_pairs={{24,8},{25,9},{26,10},{27,11},{28,12},{29,13},{30,14},{31,15}} | collective-permute-start | bytes 589832 | tf_op jit(solution)/shard_map/ppermute | solution.py:391
  57.1 6.8 %copy-start.11 = (bf16[192,512]{1,0:T(8,128)(2,1)S(1)}, bf16[192,512]{1,0:T(8,128)(2,1)}, u32[]{:S(2)}) copy-start(bf16[192,512]{1,0:T(8,128)(2,1)} %get-tuple-element.60.refs_4_) | copy-start | bytes 589828
  62.3 9.4 %collective-permute-start.11 = (bf16[224,512]{1,0:T(8,128)(2,1)}, bf16[224,512]{1,0:T(8,128)(2,1)S(1)}, u32[]{:S(2)}, u32[]{:S(2)}) collective-permute-start(bf16[224,512]{1,0:T(8,128)(2,1)} %shard_map.110), channel_id=1, source_target_pairs={{8,24},{9,25},{10,26},{11,27},{12,28},{13,29},{14,30},{15,31}} | collective-permute-start | bytes 688136 | tf_op jit(solution)/shard_map/ppermute | solution.py:407
  62.9 8.7 %collective-permute-start.9 = (bf16[224,512]{1,0:T(8,128)(2,1)}, bf16[224,512]{1,0:T(8,128)(2,1)S(1)}, u32[]{:S(2)}, u32[]{:S(2)}) collective-permute-start(bf16[224,512]{1,0:T(8,128)(2,1)} %get-tuple-element.61), channel_id=1, source_target_pairs={{8,16},{9,17},{10,18},{11,19},{12,20},{13,21},{14,22},{15,23}} | collective-permute-start | bytes 688136 | tf_op jit(solution)/shard_map/ppermute | solution.py:405
  75.1 3.7 %collective-permute-start.12 = (bf16[96,8192]{1,0:T(8,128)(2,1)}, bf16[96,8192]{1,0:T(8,128)(2,1)S(1)}, u32[]{:S(2)}, u32[]{:S(2)}) collective-permute-start(bf16[96,8192]{1,0:T(8,128)(2,1)} %get-tuple-element.69), channel_id=1, source_target_pairs={{0,1},{1,0},{2,3},{3,2},{4,5},{5,4},{6,7},{7,6},{8,9},{9,8},{10,11... | collective-permute-start | bytes 4718600 | tf_op jit(solution)/shard_map/ppermute | solution.py:111
  79.2 12.0 %collective-permute-start.13 = (bf16[24,8192]{1,0:T(8,128)(2,1)S(1)}, bf16[24,8192]{1,0:T(8,128)(2,1)S(1)}, u32[]{:S(2)}, u32[]{:S(2)}) collective-permute-start(bf16[24,8192]{1,0:T(8,128)(2,1)S(1)} %get-tuple-element.71), channel_id=1, source_target_pairs={{0,2},{1,3},{2,0},{3,1},{4,6},{5,7},{6,4},{7,5},{8,10},{9,11},{10,... | collective-permute-start | bytes 1179656 | tf_op jit(solution)/shard_map/ppermute | solution.py:111
  80.7 19.3 %collective-permute-start.14 = (bf16[24,8192]{1,0:T(8,128)(2,1)S(1)}, bf16[24,8192]{1,0:T(8,128)(2,1)S(1)}, u32[]{:S(2)}, u32[]{:S(2)}) collective-permute-start(bf16[24,8192]{1,0:T(8,128)(2,1)S(1)} %get-tuple-element.72), channel_id=1, source_target_pairs={{0,4},{1,5},{2,6},{3,7},{4,0},{5,1},{6,2},{7,3},{8,12},{9,13},{10,... | collective-permute-start | bytes 1179656 | tf_op jit(solution)/shard_map/ppermute | solution.py:111
  82.3 17.8 %copy-start.9 = (bf16[192,1024]{1,0:T(8,128)(2,1)S(1)}, bf16[192,1024]{1,0:T(8,128)(2,1)}, u32[]{:S(2)}) copy-start(bf16[192,1024]{1,0:T(8,128)(2,1)} %refs_4_.1) | copy-start | bytes 1179652
  82.3 17.8 %collective-permute-start.15 = (bf16[24,8192]{1,0:T(8,128)(2,1)S(1)}, bf16[24,8192]{1,0:T(8,128)(2,1)S(1)}, u32[]{:S(2)}, u32[]{:S(2)}) collective-permute-start(bf16[24,8192]{1,0:T(8,128)(2,1)S(1)} %get-tuple-element.73), channel_id=1, source_target_pairs={{0,6},{1,7},{2,4},{3,5},{4,2},{5,3},{6,0},{7,1},{8,14},{9,15},{10,... | collective-permute-start | bytes 1179656 | tf_op jit(solution)/shard_map/ppermute | solution.py:111
  88.2 17.0 %copy-start.19 = (bf16[1024,384]{1,0:T(8,128)(2,1)S(1)}, bf16[1024,384]{1,0:T(8,128)(2,1)}, u32[]{:S(2)}) copy-start(bf16[1024,384]{1,0:T(8,128)(2,1)} %get-tuple-element.81.refs_4_.refs_5_.refs_6_) | copy-start | bytes 2359300
  88.2 17.0 %copy-start.20 = (bf16[384,1024]{1,0:T(8,128)(2,1)S(1)}, bf16[384,1024]{1,0:T(8,128)(2,1)}, u32[]{:S(2)}) copy-start(bf16[384,1024]{1,0:T(8,128)(2,1)} %get-tuple-element.79.refs_2_) | copy-start | bytes 2359300
  88.2 17.0 %copy-start.23 = (bf16[384,128]{1,0:T(8,128)(2,1)S(1)}, bf16[384,128]{1,0:T(8,128)(2,1)}, u32[]{:S(2)}) copy-start(bf16[384,128]{1,0:T(8,128)(2,1)} %get-tuple-element.80.refs_3_) | copy-start | bytes 294916
  101.6 3.6 %collective-permute-start.16 = (bf16[192,1024]{1,0:T(8,128)(2,1)}, bf16[192,1024]{1,0:T(8,128)(2,1)S(1)}, u32[]{:S(2)}, u32[]{:S(2)}) collective-permute-start(bf16[192,1024]{1,0:T(8,128)(2,1)} %get-tuple-element.78), channel_id=1, source_target_pairs={{0,1},{1,0},{2,3},{3,2},{4,5},{5,4},{6,7},{7,6},{8,9},{9,8},{10,11... | collective-permute-start | bytes 1179656 | tf_op jit(solution)/shard_map/ppermute | solution.py:111
  101.7 13.1 %collective-permute-start.19 = (bf16[192,1024]{1,0:T(8,128)(2,1)}, bf16[192,1024]{1,0:T(8,128)(2,1)S(1)}, u32[]{:S(2)}, u32[]{:S(2)}) collective-permute-start(bf16[192,1024]{1,0:T(8,128)(2,1)} %get-tuple-element.78), channel_id=1, source_target_pairs={{0,6},{1,7},{2,4},{3,5},{4,2},{5,3},{6,0},{7,1},{8,14},{9,15},{10,... | collective-permute-start | bytes 1179656 | tf_op jit(solution)/shard_map/ppermute | solution.py:111
  103.2 19.5 %collective-permute-start.18 = (bf16[192,1024]{1,0:T(8,128)(2,1)}, bf16[192,1024]{1,0:T(8,128)(2,1)S(1)}, u32[]{:S(2)}, u32[]{:S(2)}) collective-permute-start(bf16[192,1024]{1,0:T(8,128)(2,1)} %get-tuple-element.78), channel_id=1, source_target_pairs={{0,4},{1,5},{2,6},{3,7},{4,0},{5,1},{6,2},{7,3},{8,12},{9,13},{10,... | collective-permute-start | bytes 1179656 | tf_op jit(solution)/shard_map/ppermute | solution.py:111
  104.5 18.4 %collective-permute-start.17 = (bf16[192,1024]{1,0:T(8,128)(2,1)}, bf16[192,1024]{1,0:T(8,128)(2,1)S(1)}, u32[]{:S(2)}, u32[]{:S(2)}) collective-permute-start(bf16[192,1024]{1,0:T(8,128)(2,1)} %get-tuple-element.78), channel_id=1, source_target_pairs={{0,2},{1,3},{2,0},{3,1},{4,6},{5,7},{6,4},{7,5},{8,10},{9,11},{10,... | collective-permute-start | bytes 1179656 | tf_op jit(solution)/shard_map/ppermute | solution.py:111
  107.6 15.6 %copy-start.18 = (bf16[576,1024]{1,0:T(8,128)(2,1)S(1)}, bf16[576,1024]{1,0:T(8,128)(2,1)}, u32[]{:S(2)}) copy-start(bf16[576,1024]{1,0:T(8,128)(2,1)} %get-tuple-element.84.refs_3_) | copy-start | bytes 3538948
  107.7 15.6 %copy-start.22 = (bf16[576,128]{1,0:T(8,128)(2,1)S(1)}, bf16[576,128]{1,0:T(8,128)(2,1)}, u32[]{:S(2)}) copy-start(bf16[576,128]{1,0:T(8,128)(2,1)} %get-tuple-element.85.refs_4_) | copy-start | bytes 442372
  114.8 12.0 %collective-permute-start.22 = (bf16[192,1024]{1,0:T(8,128)(2,1)S(1)}, bf16[192,1024]{1,0:T(8,128)(2,1)S(1)}, u32[]{:S(2)}, u32[]{:S(2)}) collective-permute-start(bf16[192,1024]{1,0:T(8,128)(2,1)S(1)} %shard_map.120.refs_2_), channel_id=1, source_target_pairs={{0,1},{1,0},{2,3},{3,2},{4,5},{5,4},{6,7},{7,6},{8,9},{9,8},{10,11... | collective-permute-start | bytes 1179656 | tf_op jit(solution)/shard_map/ppermute | solution.py:111
  122.7 4.0 %collective-permute-start.21 = (bf16[192,1024]{1,0:T(8,128)(2,1)S(1)}, bf16[192,1024]{1,0:T(8,128)(2,1)S(1)}, u32[]{:S(2)}, u32[]{:S(2)}) collective-permute-start(bf16[192,1024]{1,0:T(8,128)(2,1)S(1)} %shard_map.119.refs_1_), channel_id=1, source_target_pairs={{0,1},{1,0},{2,3},{3,2},{4,5},{5,4},{6,7},{7,6},{8,9},{9,8},{10,11... | collective-permute-start | bytes 1179656 | tf_op jit(solution)/shard_map/ppermute | solution.py:111
  122.9 3.9 %collective-permute-start.20 = (bf16[192,1024]{1,0:T(8,128)(2,1)S(1)}, bf16[192,1024]{1,0:T(8,128)(2,1)S(1)}, u32[]{:S(2)}, u32[]{:S(2)}) collective-permute-start(bf16[192,1024]{1,0:T(8,128)(2,1)S(1)} %shard_map.118.refs_0_), channel_id=1, source_target_pairs={{0,1},{1,0},{2,3},{3,2},{4,5},{5,4},{6,7},{7,6},{8,9},{9,8},{10,11... | collective-permute-start | bytes 1179656 | tf_op jit(solution)/shard_map/ppermute | solution.py:111
  131.4 33.3 %copy-start = (bf16[1,1024,1024]{2,1,0:T(8,128)(2,1)S(1)}, bf16[1,1024,1024]{2,1,0:T(8,128)(2,1)}, u32[]{:S(2)}) copy-start(bf16[1,1024,1024]{2,1,0:T(8,128)(2,1)} %w_ref.5) | copy-start | bytes 6291460
  131.4 37.0 %all-to-all-start = ((bf16[32,32,384]{2,1,0:T(8,128)(2,1)}), bf16[32,32,384]{2,1,0:T(8,128)(2,1)S(1)}, u32[]{:S(2)}, u32[]{:S(2)}) async-start(bf16[32,32,384]{2,1,0:T(8,128)(2,1)} %bitcast.5), calls=%async_computation | async-start | bytes 1572864 | tf_op jit(solution)/shard_map/all_to_all | solution.py:910
  141.7 11.5 %collective-permute-start.23 = (bf16[768,128]{1,0:T(8,128)(2,1)}, bf16[768,128]{1,0:T(8,128)(2,1)S(1)}, u32[]{:S(2)}, u32[]{:S(2)}) collective-permute-start(bf16[768,128]{1,0:T(8,128)(2,1)} %get-tuple-element.93), channel_id=1, source_target_pairs={{0,1},{1,0},{2,3},{3,2},{4,5},{5,4},{6,7},{7,6},{8,9},{9,8},{10,11... | collective-permute-start | bytes 589832 | tf_op jit(solution)/shard_map/ppermute | solution.py:111
  142.0 2.0 %collective-permute-start.24 = (bf16[256,128]{1,0:T(8,128)(2,1)}, bf16[256,128]{1,0:T(8,128)(2,1)S(1)}, u32[]{:S(2)}, u32[]{:S(2)}) collective-permute-start(bf16[256,128]{1,0:T(8,128)(2,1)} %get-tuple-element.95), channel_id=1, source_target_pairs={{0,1},{1,0},{2,3},{3,2},{4,5},{5,4},{6,7},{7,6},{8,9},{9,8},{10,11... | collective-permute-start | bytes 196616 | tf_op jit(solution)/shard_map/ppermute | solution.py:111
  142.2 9.8 %collective-permute-start.25 = (bf16[256,128]{1,0:T(8,128)(2,1)}, bf16[256,128]{1,0:T(8,128)(2,1)S(1)}, u32[]{:S(2)}, u32[]{:S(2)}) collective-permute-start(bf16[256,128]{1,0:T(8,128)(2,1)} %get-tuple-element.96), channel_id=1, source_target_pairs={{0,2},{1,3},{2,0},{3,1},{4,6},{5,7},{6,4},{7,5},{8,10},{9,11},{10,... | collective-permute-start | bytes 196616 | tf_op jit(solution)/shard_map/ppermute | solution.py:111
  144.0 9.2 %collective-permute-start.26 = (bf16[256,128]{1,0:T(8,128)(2,1)}, bf16[256,128]{1,0:T(8,128)(2,1)S(1)}, u32[]{:S(2)}, u32[]{:S(2)}) collective-permute-start(bf16[256,128]{1,0:T(8,128)(2,1)} %get-tuple-element.97), channel_id=1, source_target_pairs={{0,3},{1,2},{2,1},{3,0},{4,7},{5,6},{6,5},{7,4},{8,11},{9,10},{10,... | collective-permute-start | bytes 196616 | tf_op jit(solution)/shard_map/ppermute | solution.py:111
  154.6 7.6 %collective-permute-start.27 = (bf16[384,128]{1,0:T(8,128)(2,1)}, bf16[384,128]{1,0:T(8,128)(2,1)S(1)}, u32[]{:S(2)}, u32[]{:S(2)}) collective-permute-start(bf16[384,128]{1,0:T(8,128)(2,1)} %get-tuple-element.99), channel_id=1, source_target_pairs={{0,2},{1,3},{2,0},{3,1},{4,6},{5,7},{6,4},{7,5},{8,10},{9,11},{10,... | collective-permute-start | bytes 294920 | tf_op jit(solution)/shard_map/ppermute | solution.py:111
  155.3 9.5 %collective-permute-start.28 = (bf16[384,128]{1,0:T(8,128)(2,1)}, bf16[384,128]{1,0:T(8,128)(2,1)S(1)}, u32[]{:S(2)}, u32[]{:S(2)}) collective-permute-start(bf16[384,128]{1,0:T(8,128)(2,1)} %get-tuple-element.100), channel_id=1, source_target_pairs={{0,4},{1,5},{2,6},{3,7},{4,0},{5,1},{6,2},{7,3},{8,12},{9,13},{10,... | collective-permute-start | bytes 294920 | tf_op jit(solution)/shard_map/ppermute | solution.py:111
  156.8 7.9 %collective-permute-start.29 = (bf16[384,128]{1,0:T(8,128)(2,1)}, bf16[384,128]{1,0:T(8,128)(2,1)S(1)}, u32[]{:S(2)}, u32[]{:S(2)}) collective-permute-start(bf16[384,128]{1,0:T(8,128)(2,1)} %get-tuple-element.101), channel_id=1, source_target_pairs={{0,6},{1,7},{2,4},{3,5},{4,2},{5,3},{6,0},{7,1},{8,14},{9,15},{10,... | collective-permute-start | bytes 294920 | tf_op jit(solution)/shard_map/ppermute | solution.py:111
  158.2 10.0 %collective-permute-start.30 = (bf16[256,128]{1,0:T(8,128)(2,1)}, bf16[256,128]{1,0:T(8,128)(2,1)S(1)}, u32[]{:S(2)}, u32[]{:S(2)}) collective-permute-start(bf16[256,128]{1,0:T(8,128)(2,1)} %get-tuple-element.106), channel_id=1, source_target_pairs={{0,8},{8,0},{16,24},{24,16},{1,9},{9,1},{17,25},{25,17},{2,10},{10... | collective-permute-start | bytes 196616 | tf_op jit(solution)/shard_map/ppermute | solution.py:851
  158.6 9.6 %collective-permute-start.31 = (bf16[256,128]{1,0:T(8,128)(2,1)}, bf16[256,128]{1,0:T(8,128)(2,1)S(1)}, u32[]{:S(2)}, u32[]{:S(2)}) collective-permute-start(bf16[256,128]{1,0:T(8,128)(2,1)} %get-tuple-element.107), channel_id=1, source_target_pairs={{0,16},{8,24},{16,0},{24,8},{1,17},{9,25},{17,1},{25,9},{2,18},{10... | collective-permute-start | bytes 196616 | tf_op jit(solution)/shard_map/ppermute | solution.py:851
  162.2 6.3 %collective-permute-start.32 = (bf16[256,128]{1,0:T(8,128)(2,1)}, bf16[256,128]{1,0:T(8,128)(2,1)S(1)}, u32[]{:S(2)}, u32[]{:S(2)}) collective-permute-start(bf16[256,128]{1,0:T(8,128)(2,1)} %get-tuple-element.108), channel_id=1, source_target_pairs={{0,24},{8,16},{16,8},{24,0},{1,25},{9,17},{17,9},{25,1},{2,26},{10... | collective-permute-start | bytes 196616 | tf_op jit(solution)/shard_map/ppermute | solution.py:851
  (12 other events, 28.1 us)
Sparse Core Ops, SparseCore 0:
  43.0 35.6 all-gather.1

commit v6 on v5

--- a/solution.py
+++ b/solution.py
@@ -204,7 +204,7 @@
 
 def project_body(count, tp_count, info_ref, *refs):
     x_refs, refs = refs[:count], refs[count:]
-    first_ref, pass_ref, w_ref, q, kv, passed, held, wide, sems = refs
+    first_ref, pass_ref, w_ref, q, kv, passed, kv_ref, held, wide, sems = refs
     kinds, rows, _ = held.shape
     depth = math.gcd(rows, 1024)
     copies = {}
@@ -237,13 +237,13 @@
             if c == 0:
                 wide[:, at] = part
             else:
-                kv.ref[(c - 1) * count_rows : c * count_rows, at] = part.astype(BF16)
+                kv_ref[(c - 1) * count_rows : c * count_rows, at] = part.astype(BF16)
         if c == 0:
             q.ref[...] = wide[...].astype(BF16)
             q.send()
             last = wide[pl.ds(last_row(info_ref, count_rows, tp_count), 1), :]
             spread = jnp.broadcast_to(last, (EDGE_ROWS, last.shape[1]))
-            kv.ref[kinds * count_rows :, :] = spread.astype(BF16)
+            kv_ref[kinds * count_rows :, :] = spread.astype(BF16)
 
 
 def project(info, pieces, first, weights, passed, tp_count):
@@ -256,9 +256,10 @@
 
     def body(*refs):
         in_refs, refs = refs[: count + 4], refs[count + 4 :]
-        far, near, (held, wide, sems, out_sems) = refs[:3], refs[3:6], refs[6:]
+        far, kv_near, near, (held, wide, sems, out_sems) = refs[:3], refs[3], refs[4:7], refs[7:]
         outputs = [Sent(n, f, out_sems.at[i]) for i, (f, n) in enumerate(zip(far, near))]
-        project_body(count, tp_count, *in_refs, *outputs, held, wide, sems)
+        project_body(count, tp_count, *in_refs, *outputs, kv_near, held, wide, sems)
+        near[1][...] = kv_near[...]
         outputs[1].send()
         for output in outputs:
             output.copy.wait()
@@ -268,8 +269,9 @@
         in_specs=[pl.BlockSpec(memory_space=pltpu.SMEM)]
         + [here] * (count + 2)
         + [pl.BlockSpec(memory_space=pl.ANY)],
-        out_specs=[there] * 3,
-        out_shape=[pltpu.HBM(shape, dtype) for shape, dtype in outs],
+        out_specs=[there] * 3 + [here],
+        out_shape=[pltpu.HBM(shape, dtype) for shape, dtype in outs]
+        + [jax.ShapeDtypeStruct(*outs[1])],
         scratch_shapes=[pltpu.VMEM(shape, dtype) for shape, dtype in outs]
         + [
             pltpu.VMEM((kinds - 1, deep, width), BF16),
@@ -312,56 +314,52 @@
     return -(-(rows + 1) // LANES) * LANES
 
 
-def far_body(tp_count, info_ref, kv_in_ref, q_ref, *refs):
-    first = len(refs) == 6
-    if first:
-        kv, back, given_ref, token_ref, top, dens_ref = refs
-        token_ref[...] = jnp.zeros_like(token_ref)
-    else:
-        given_ref, kv, back, top = refs
-    kv_ref = kv()
-    rows, width = q_ref.shape
+def far_body(tp_count, info_ref, kv_ref, kv_in_ref, q3_ref, q2_ref, *refs):
+    back3, back2, token_ref, far_top, far_den = refs
+    token_ref[...] = jnp.zeros_like(token_ref)
+    rows, width = q2_ref.shape
     heads = heads_of(width)
     count = len(heads)
     keys, values = slice(0, rows), slice(rows, 2 * rows)
-
-    def sums(source_ref, at_rows):
+    last = last_row(info_ref, rows, tp_count)
+    spread = den_lanes(rows) - rows
+
+    def sums(q_ref, at_rows, top_ref):
         size = at_rows.stop - at_rows.start
         lane = lax.broadcasted_iota(jnp.int32, (size, LANES), 1)
         dens = jnp.zeros((size, LANES), F32)
-        tops = []
         for h, at in enumerate(heads):
-            q = source_ref[at_rows, at]
+            q = q_ref[at_rows, at]
             own, own_den = weigh(q, kv_ref[keys, at])
             other, other_den = weigh(q, kv_in_ref[keys, at])
-            tops.append(
-                dot(own.astype(BF16), kv_ref[values, at])
-                + dot(other.astype(BF16), kv_in_ref[values, at])
+            top_ref[:size, at] = dot(own.astype(BF16), kv_ref[values, at]) + dot(
+                other.astype(BF16), kv_in_ref[values, at]
             )
             dens = jnp.where(lane == h, own_den + other_den, dens)
-        return jnp.concatenate(tops, axis=1), dens
-
-    top[...], dens = sums(q_ref, slice(0, rows))
-    if first:
-        dens_ref[...] = dens
-        last = last_row(info_ref, rows, tp_count)
-        given_ref[:, :width] = jnp.broadcast_to(top[pl.ds(last, 1), :], (EDGE_ROWS, width))
-        given_ref[:, width:] = jnp.broadcast_to(dens_ref[pl.ds(last, 1), :], (EDGE_ROWS, LANES))
-        edge_top, edge_den = sums(kv_ref, slice(2 * rows, 2 * rows + EDGE_ROWS))
-    else:
-        edge_top, edge_den = given_ref[:, :width], given_ref[:, width:]
-    back.ref[:rows, :] = top[...].astype(BF16)
-    back.ref[rows : rows + EDGE_ROWS, :] = edge_top.astype(BF16)
-    spread = jnp.broadcast_to(edge_den[:1], (den_lanes(rows) - rows, LANES))
-    turned = split_den(jnp.concatenate([dens, spread], axis=0), count).T[:EDGE_ROWS].astype(BF16)
-    back.ref[rows + EDGE_ROWS :, : turned.shape[1]] = turned
-    if turned.shape[1] < width:
-        rest = jnp.zeros((EDGE_ROWS, width - turned.shape[1]), BF16)
-        back.ref[rows + EDGE_ROWS :, turned.shape[1] :] = rest
-
-
-def near_body(info_ref, kv_in_ref, mask_ref, _, q, kv, top_ref, den_ref, edge_ref):
-    q_ref, kv_ref = q(), kv()
+        return dens
+
+    def fill(back, top, den, edge_top, edge_den):
+        back.ref[:rows, :] = top.astype(BF16)
+        back.ref[rows : rows + EDGE_ROWS, :] = edge_top.astype(BF16)
+        den = jnp.concatenate([den, jnp.broadcast_to(edge_den, (spread, LANES))], axis=0)
+        turned = split_den(den, count).T[:EDGE_ROWS].astype(BF16)
+        back.ref[rows + EDGE_ROWS :, : turned.shape[1]] = turned
+        if turned.shape[1] < width:
+            rest = jnp.zeros((EDGE_ROWS, width - turned.shape[1]), BF16)
+            back.ref[rows + EDGE_ROWS :, turned.shape[1] :] = rest
+        back.send()
+
+    everything = slice(0, rows)
+    far_den[...] = sums(q2_ref, everything, far_top.at[0])
+    den3 = sums(q3_ref, everything, far_top.at[1])
+    row = jnp.broadcast_to(far_top[0, pl.ds(last, 1), :], (EDGE_ROWS, width))
+    fill(back3, far_top[1], den3, row, far_den[pl.ds(last, 1), :])
+    edge_den = sums(kv_ref, slice(2 * rows, 2 * rows + EDGE_ROWS), far_top.at[1])
+    fill(back2, far_top[0], far_den[...], far_top[1, :EDGE_ROWS, :], edge_den[:1])
+
+
+def near_body(info_ref, kv_ref, kv_in_ref, mask_ref, _, q, top_ref, den_ref, edge_ref):
+    q_ref = q()
     rows, width = q_ref.shape
     allowed = mask_ref[...] > 0
     linked = jnp.where(info_ref[3] % 2 == 1, 1.0, 0.0)
@@ -386,33 +384,27 @@
     edge_ref[:, width:] = edge_dens
 
 
-def attend_paired(info, q, kv, mask, tp_count):
+def attend_paired(info, q, kv, kv_near, mask, tp_count):
     kv_in = lax.ppermute(kv, "ctx", [(0, 1), (2, 3)])
-    q2, q3 = (lax.ppermute(q, "ctx", [(c, 1)]) for c in (2, 3))
+    far = [lax.ppermute(q, "ctx", [(c, 1)]) for c in (3, 2)]
     rows, width = q.shape
     back = ((rows + 2 * EDGE_ROWS, width), BF16)
-    body = functools.partial(far_body, tp_count)
-    tops = pltpu.VMEM((rows, width), F32)
-    back2, given, done = staged(
-        body,
-        [kv_in, q2],
-        [back],
-        [((EDGE_ROWS, width + LANES), F32), TOKEN],
-        [tops, pltpu.VMEM((rows, LANES), F32)],
+    back3, back2, done = staged(
+        functools.partial(far_body, tp_count),
+        [kv_near, kv_in, *far],
+        [back, back],
+        [TOKEN],
+        [pltpu.VMEM((2, rows, width), F32), pltpu.VMEM((rows, LANES), F32)],
         info,
-        held=[kv],
-    )
-    back2 = lax.ppermute(back2, "ctx", [(1, 2)])
-    back3 = staged(body, [kv_in, q3, given], [back], scratch=[tops], info=info, held=[kv])[0]
-    back3 = lax.ppermute(back3, "ctx", [(1, 3)])
-    back = [back2, back3]
+    )
+    back = [lax.ppermute(back3, "ctx", [(1, 3)]), lax.ppermute(back2, "ctx", [(1, 2)])]
     top, den, edge = staged(
         near_body,
-        [kv_in, mask, done],
+        [kv_near, kv_in, mask, done],
         [],
         [((rows, width), F32), ((rows, LANES), F32), ((EDGE_ROWS, width + LANES), F32)],
         info=info,
-        held=[q, kv],
+        held=[q],
     )
     return top, den, edge, back
 
@@ -744,10 +736,10 @@
     message.ref[rows:, :] = jnp.concatenate(abs_, axis=0)
 
 
-def relay_body(count, rounds, planes, info_ref, *refs):
+def relay_body(heads, count, rounds, planes, info_ref, state_ref, w_ref, *refs):
     (ab0_ref, ab1_ref, there_ref), refs = refs[:3], refs[3:]
     pieces, refs = refs[:rounds], refs[rounds:]
-    messages, outs, (own_ref, held) = refs[:count], refs[count : count + planes], refs[count + planes :]
+    messages, outs, (total_ref, held) = refs[:count], refs[count : count + planes], refs[count + planes :]
     rows = ab0_ref.shape[0] // 2
     for k, piece in enumerate(pieces):
         held[k] = piece[...].astype(F32)
@@ -758,16 +750,25 @@
             total = term if total is None else total + term
         out.ref[...] = total.astype(BF16)
         out.send()
-    for k in range(count + 1):
-        mine = ab0_ref[:rows, :] if k == 0 else ab1_ref[(k - 1) * rows : k * rows, :]
-        target = messages[k - 1].ref if k else own_ref
-        target[:rows, :] = mine
-        target[rows:, :] = there_ref[k * rows : (k + 1) * rows, :]
-        if k:
-            messages[k - 1].send()
-
-
-def local_layer(normed, normed_near, info, parts, gbs, cores, weights, rounds, planes):
+    for k, message in enumerate(messages):
+        message.ref[:rows, :] = ab1_ref[k * rows : (k + 1) * rows, :]
+        message.ref[rows:, :] = there_ref[(k + 1) * rows : (k + 2) * rows, :]
+        message.send()
+    total = add_heads(heads, info_ref, state_ref[...], w_ref, 0, [ab0_ref[:rows, :]])
+    total_ref[...] = add_heads(heads, info_ref, total, w_ref, 1, [there_ref[:rows, :]])
+
+
+def add_heads(heads, info_ref, total, w_ref, first, values):
+    d = LOCAL_HEAD_DIM
+    for index, value in enumerate(values):
+        head = heads(info_ref[1] ^ (first + index))
+        total += dot(value, w_ref[0, pl.ds(pl.multiple_of(head * d, d), d), :])
+    return total
+
+
+def local_layer(
+    normed, normed_near, info, parts, gbs, cores, weights, rounds, planes, heads, state, local_out
+):
     rows, width = normed.shape
     d = LOCAL_HEAD_DIM
     near = [swap(normed, bits) for bits in parts[1]]
@@ -801,31 +802,24 @@
         mib=20,
     )
     pieces = [own] + [swap(value, k + 1) for k, value in enumerate(pieces)]
-    block = ((2 * rows, d), BF16)
-    *sent, own = staged(
-        functools.partial(relay_body, count, rounds, planes),
-        [ab0, ab1, swap(message, 1), *pieces],
-        [block] * count + [piece] * planes,
-        [block],
+    *sent, total = staged(
+        functools.partial(relay_body, heads, count, rounds, planes),
+        [state, local_out, ab0, ab1, swap(message, 1), *pieces],
+        [((2 * rows, d), BF16)] * count + [piece] * planes,
+        [((rows, width), F32)],
         [pltpu.VMEM((rounds, deep, d), F32)],
         info,
     )
-    messages = [own] + [swap(value, 2 * (k + 1)) for k, value in enumerate(sent[:count])]
-    return messages, sent[count:], grad_qkv
-
-
-def hidden_body(heads, count, info_ref, state_ref, w_ref, *refs):
+    messages = [swap(value, 2 * (k + 1)) for k, value in enumerate(sent[:count])]
+    return total, messages, sent[count:], grad_qkv
+
+
+def hidden_body(heads, info_ref, total_ref, w_ref, *refs):
     *messages, out_ref, token_ref = refs
     token_ref[...] = jnp.zeros_like(token_ref)
-    rows = state_ref.shape[0]
-    d = LOCAL_HEAD_DIM
-    total = state_ref[...]
-    for bits in range(2 * count + 2):
-        at = bits % 2 * rows
-        head = heads(info_ref[1] ^ bits)
-        weights = w_ref[0, pl.ds(pl.multiple_of(head * d, d), d), :]
-        total += dot(messages[bits // 2][at : at + rows, :], weights)
-    out_ref[...] = total.astype(BF16)
+    rows = total_ref.shape[0]
+    values = [message[at : at + rows, :] for message in messages for at in (0, rows)]
+    out_ref[...] = add_heads(heads, info_ref, total_ref[...], w_ref, 2, values).astype(BF16)
 
 
 def final_body(heads, parts_ref, _, *refs):
@@ -877,7 +871,7 @@
     weights_in, head_info = preload(global_qkv, head_info, mine)
     even = [tie(swap(patch_in, bits), head_info) for bits in range(2, tp_count, 2)]
     pieces = [patch_in, *even, mine, *(swap(piece, 1) for piece in even)]
-    q, kv, gb = project(head_info, pieces, weights_in, global_qkv, cotangent, tp_count)
+    q, kv, gb, kv_near = project(head_info, pieces, weights_in, global_qkv, cotangent, tp_count)
 
     place = (
         (me ^ jnp.array(order, jnp.int32))[:, None] * patches
@@ -886,7 +880,7 @@
     if planes == 4 and den_lanes(shard_rows) <= q.shape[1]:
         mask = (place[None, :] <= place[:, None]).astype(F32)
         top, den, edge, back = attend_paired(
-            head_info, q, kv, mask, tp_count
+            head_info, q, kv, kv_near, mask, tp_count
         )
     else:
         key_place = (
@@ -904,20 +898,19 @@
     state, normed, normed_near = byte_state(
         scatter_sum(even, odd, patches), local_embeds, prepared
     )
-    messages, out_pieces, grad_qkv = local_layer(
-        normed, normed_near, head_info, parts, gbs, cores, weights, rounds, planes
+    total, messages, out_pieces, grad_qkv = local_layer(
+        normed, normed_near, head_info, parts, gbs, cores, weights, rounds, planes, head_of, state, local_out
     )
     grad_qkv = lax.all_to_all(grad_qkv, ("ctx", "tp"), 0, 0, tiled=True)
-    count = group // 2 - 1
     out_pieces = swap_planes(out_pieces)
     here = pl.BlockSpec(memory_space=pltpu.VMEM)
     hidden, done = pl.pallas_call(
-        functools.partial(hidden_body, head_of, count),
-        in_specs=[pl.BlockSpec(memory_space=pltpu.SMEM)] + [here] * (3 + count),
+        functools.partial(hidden_body, head_of),
+        in_specs=[pl.BlockSpec(memory_space=pltpu.SMEM)] + [here] * (2 + len(messages)),
         out_specs=[here, here],
         out_shape=[jax.ShapeDtypeStruct((byte_count, width), BF16), TOKEN],
         compiler_params=params(16),
-    )(head_info, state, local_out, *messages[: count + 1])
+    )(head_info, total, local_out, *messages)
     grad_qkv, grad_out = call(
         functools.partial(final_body, heads),
         [((1, share, 3 * width), F32), ((1, share, width), F32)],

time: 177 us -> 175 us (0.989)
  Pallas kernels: 52.7 us -> 50.4 us
  waiting for transfers between devices: 60.7 us -> 63 us
    ppermute x3, waiting for transfers between devices: 0.27 us -> 2.39 us  [swap_planes(): lax.ppermute(pieces[k], 'ctx', [(c, c ^ k) for c in range(count)])]
    pallas_call x8 -> x7, Pallas kernels: 20.8 us -> 18.8 us  [staged(): pl.pallas_call(kernel, in_specs=[pl.BlockSpec(memory_space=pltpu.SMEM)] *...]
    unnamed x50 -> x46, local copies, waits for them, and re-layouts: 5.21 us -> 5.17 us
  transfers between devices with their start and end apart: 35 -> 35, of which waited for: 15 -> 16; matrix products, arithmetic and copies ran while one was open for 0% -> 0% of each run, Pallas kernels for 20% -> 19%
where the time goes in v6:
time: 175 us
  waiting for transfers between devices  63 us (36%)
  Pallas kernels  50.4 us (29%)
  starting transfers between devices  40.7 us (23%)
  between operations  14.5 us (8%)
  local copies, waits for them, and re-layouts  5.25 us (3%)
    ppermute x25, waiting for transfers between devices, swap(): lax.ppermute(value, 'tp', [(source, source ^ bits) for source in range(co...  52.8 us
    pallas_call x7, Pallas kernels, staged(): pl.pallas_call(kernel, in_specs=[pl.BlockSpec(memory_space=pltpu.SMEM)] *...  18.8 us
    ppermute x25, starting transfers between devices, swap(): lax.ppermute(value, 'tp', [(source, source ^ bits) for source in range(co...  18.7 us
    pallas_call x1, Pallas kernels, project(): pl.pallas_call(body, in_specs=[pl.BlockSpec(memory_space=pltpu.SMEM)] + [...  9.63 us
    all_to_all x1, starting transfers between devices, per_device(): grad_qkv = lax.all_to_all(grad_qkv, ('ctx', 'tp'), 0, 0, tiled=True)  9.48 us
    pallas_call x2, Pallas kernels, preload(): pl.pallas_call(functools.partial(preload_body, parts), in_specs=[scalar,...  9.44 us
    ppermute x1, waiting for transfers between devices, attend_paired(): kv_in = lax.ppermute(kv, 'ctx', [(0, 1), (2, 3)])  7.75 us
    ppermute x3, starting transfers between devices, swap_planes(): lax.ppermute(pieces[k], 'ctx', [(c, c ^ k) for c in range(count)])  5.83 us
  transfers between devices with their start and end apart: 35, of which 16 were waited for; matrix products, arithmetic and copies ran while one was open for 0% of the time, Pallas kernels for 19%

profile of v6, /device:TPU:0, one launch (start us, length us, event | category | flops | bytes accessed | tf_op | source)
XLA Modules:
  0.0 174.5 jit_solution(12039789691738672533)
XLA Ops:
  7.2 1.0 copy-done.8
  9.1 2.6 %collective-permute-start.2 = (bf16[24,8192]{1,0:T(8,128)(2,1)S(1)}, bf16[24,8192]{1,0:T(8,128)(2,1)S(1)}, u32[]{:S(2)}, u32[]{:S(2)}) collective-permute-start(bf16[24,8192]{1,0:T(8,128)(2,1)S(1)} %shard_map.103.refs_1_), channel_id=1, source_target_pairs={{0,4},{1,5},{2,6},{3,7},{4,0},{5,1},{6,2},{7,3},{8,12},{9,13},{10,... | collective-permute-start | bytes 1179656 | tf_op jit(solution)/shard_map/ppermute | solution.py:111
  11.7 1.4 collective-permute-start.3
  13.8 0.7 copy-done.1
  14.5 4.7 %shard_map.104 = (bf16[8192,512]{1,0:T(8,128)(2,1)S(1)}, s32[4]{0:T(128)}) custom-call(s32[4]{0:T(128)} %pad_add_fusion.info_ref, bf16[3,8192,512]{2,1,0:T(8,128)(2,1)} %refs_11_.1, bf16[24,8192]{1,0:T(8,128)(2,1)} %copy-done.1), custom_call_target="tpu_custom_call" | custom-call | bytes 8388608 | tf_op jit(solution)/shard_map/pallas_call | solution.py:157
  19.2 10.6 %collective-permute-done.2.refs_0_ = bf16[24,8192]{1,0:T(8,128)(2,1)S(1)} collective-permute-done((bf16[24,8192]{1,0:T(8,128)(2,1)S(1)}, bf16[24,8192]{1,0:T(8,128)(2,1)S(1)}, u32[]{:S(2)}, u32[]{:S(2)}) %collective-permute-start.2) | collective-permute-done | bytes 393248 | tf_op jit(solution)/shard_map/ppermute | solution.py:111
  31.1 1.1 collective-permute-done.5.refs_7_
  33.3 9.6 %shard_map.108 = (bf16[192,512]{1,0:T(8,128)(2,1)}, bf16[400,512]{1,0:T(8,128)(2,1)}, bf16[192,1024]{1,0:T(8,128)(2,1)}, bf16[400,512]{1,0:T(8,128)(2,1)S(1)}) custom-call(s32[4]{0:T(128)S(1)} %copy-done.11, bf16[24,8192]{1,0:T(8,128)(2,1)S(1)} %shard_map.103.refs_1_, bf16[24,8192]{1,0:T(8,128)(2,1)S(1)} %shard_map.105.refs_2_, ...), custom_call_target="tpu_custom_call" | custom-call | tf_op jit(solution)/shard_map/pallas_call | solution.py:267
  43.0 3.7 %collective-permute-start.7 = (bf16[400,512]{1,0:T(8,128)(2,1)}, bf16[400,512]{1,0:T(8,128)(2,1)S(1)}, u32[]{:S(2)}, u32[]{:S(2)}) collective-permute-start(bf16[400,512]{1,0:T(8,128)(2,1)} %get-tuple-element.61), channel_id=1, source_target_pairs={{0,8},{16,24},{1,9},{17,25},{2,10},{18,26},{3,11},{19,27},{4,12},{... | collective-permute-start | bytes 1228808 | tf_op jit(solution)/shard_map/ppermute | solution.py:388
  46.8 0.7 collective-permute-start.8
  48.3 7.7 %collective-permute-done.7.refs_2_ = bf16[400,512]{1,0:T(8,128)(2,1)S(1)} collective-permute-done((bf16[400,512]{1,0:T(8,128)(2,1)}, bf16[400,512]{1,0:T(8,128)(2,1)S(1)}, u32[]{:S(2)}, u32[]{:S(2)}) %collective-permute-start.7) | collective-permute-done | bytes 409632 | tf_op jit(solution)/shard_map/ppermute | solution.py:388
  56.0 3.1 %shard_map.109 = (bf16[224,512]{1,0:T(8,128)(2,1)}, bf16[224,512]{1,0:T(8,128)(2,1)}, f32[8,128]{1,0:T(8,128)S(1)}) custom-call(s32[4]{0:T(128)S(1)} %copy-done.12, bf16[400,512]{1,0:T(8,128)(2,1)S(1)} %get-tuple-element.60.refs_1_, bf16[400,512]{1,0:T(8,128)(2,1)S(1)} %collective-permute-done.7.refs_2_, ...), custom_call_target="tpu_custom_call" | custom-call | bytes 4194304 | tf_op jit(solution)/shard_map/pallas_call | solution.py:88
  59.1 0.7 collective-permute-start.10
  59.8 0.9 collective-permute-start.11
  60.8 0.9 copy-done.9
  61.7 2.0 %shard_map.110 = (f32[192,512]{1,0:T(8,128)S(1)}, f32[192,128]{1,0:T(8,128)S(1)}, f32[16,640]{1,0:T(8,128)S(1)}) custom-call(s32[4]{0:T(128)S(1)} %copy-done.12, bf16[400,512]{1,0:T(8,128)(2,1)S(1)} %get-tuple-element.60.refs_1_, bf16[400,512]{1,0:T(8,128)(2,1)S(1)} %collective-permute-done.7.refs_2_, f32[192,192]{1,0:T(8,128)S(1)} %compare_convert_fusion.refs_3_, ...), custom_call_target="tpu_custom_call" | custom-call | bytes 4194304 | tf_op jit(solution)/shard_map/pallas_call | solution.py:88
  64.3 4.8 %shard_map.111 = (bf16[512,8192]{1,0:T(8,128)(2,1)S(1)}, s32[4]{0:T(128)}) custom-call(s32[4]{0:T(128)} %get-tuple-element.58.refs_1_.refs_0_.info_ref, bf16[512,8192]{1,0:T(8,128)(2,1)} %w_ref.4, f32[192,128]{1,0:T(8,128)} %copy-done.5), custom_call_target="tpu_custom_call" | custom-call | bytes 8388608 | tf_op jit(solution)/shard_map/pallas_call | solution.py:157
  69.2 3.5 %shard_map.112 = (bf16[96,8192]{1,0:T(8,128)(2,1)}, bf16[96,8192]{1,0:T(8,128)(2,1)S(1)}) custom-call(s32[4]{0:T(128)S(1)} %copy-done.13, bf16[224,512]{1,0:T(8,128)(2,1)S(1)} %collective-permute-done.10.refs_0_, bf16[224,512]{1,0:T(8,128)(2,1)S(1)} %collective-permute-done.11.refs_1_, f32[192,512]{1,0:T(8,128)S(1)} %get-tuple-element.66.refs_2_, ...), custom_call_target="tpu_custom_call" | custom-call | tf_op jit(solution)/shard_map/pallas_call | solution.py:509
  72.7 3.6 %collective-permute-done.12.other_ref = bf16[96,8192]{1,0:T(8,128)(2,1)S(1)} collective-permute-done((bf16[96,8192]{1,0:T(8,128)(2,1)}, bf16[96,8192]{1,0:T(8,128)(2,1)S(1)}, u32[]{:S(2)}, u32[]{:S(2)}) %collective-permute-start.12) | collective-permute-done | bytes 1572896 | tf_op jit(solution)/shard_map/ppermute | solution.py:111
  76.7 1.6 collective-permute-start.13
  78.2 1.6 collective-permute-start.14
  80.2 5.5 %shard_map.114 = (f32[8,128]{1,0:T(8,128)S(1)}, bf16[1024,384]{1,0:T(8,128)(2,1)}, bf16[384,1024]{1,0:T(8,128)(2,1)}, bf16[384,128]{1,0:T(8,128)(2,1)}, bf16[576...) custom-call(s32[4]{0:T(128)} %get-tuple-element.58.refs_1_.refs_0_.info_ref,, ...), custom_call_target="tpu_custom_call" | custom-call | tf_op jit(solution)/shard_map/pallas_call | solution.py:615
  85.7 2.9 %collective-permute-done.13.refs_1_ = bf16[24,8192]{1,0:T(8,128)(2,1)S(1)} collective-permute-done((bf16[24,8192]{1,0:T(8,128)(2,1)S(1)}, bf16[24,8192]{1,0:T(8,128)(2,1)S(1)}, u32[]{:S(2)}, u32[]{:S(2)}) %collective-permute-start.13) | collective-permute-done | bytes 393248 | tf_op jit(solution)/shard_map/ppermute | solution.py:111
  88.7 8.1 %collective-permute-done.14.refs_2_ = bf16[24,8192]{1,0:T(8,128)(2,1)S(1)} collective-permute-done((bf16[24,8192]{1,0:T(8,128)(2,1)S(1)}, bf16[24,8192]{1,0:T(8,128)(2,1)S(1)}, u32[]{:S(2)}, u32[]{:S(2)}) %collective-permute-start.14) | collective-permute-done | bytes 393248 | tf_op jit(solution)/shard_map/ppermute | solution.py:111
  96.7 0.9 collective-permute-done.15.refs_3_
  97.7 1.5 shard_map.115
  99.3 1.8 %collective-permute-start.19 = (bf16[192,1024]{1,0:T(8,128)(2,1)}, bf16[192,1024]{1,0:T(8,128)(2,1)S(1)}, u32[]{:S(2)}, u32[]{:S(2)}) collective-permute-start(bf16[192,1024]{1,0:T(8,128)(2,1)} %get-tuple-element.80), channel_id=1, source_target_pairs={{0,6},{1,7},{2,4},{3,5},{4,2},{5,3},{6,0},{7,1},{8,14},{9,15},{10,... | collective-permute-start | bytes 1179656 | tf_op jit(solution)/shard_map/ppermute | solution.py:111
  101.1 1.0 collective-permute-start.18
  102.1 0.7 collective-permute-start.17
  102.9 2.4 %shard_map.116 = (f32[384,1024]{1,0:T(8,128)S(1)}, f32[128,1024]{1,0:T(8,128)S(1)}, bf16[384,128]{1,0:T(8,128)(2,1)S(1)}, f32[8,128]{1,0:T(8,128)S(1)}) custom-call(bf16[192,1024]{1,0:T(8,128)(2,1)S(1)} %get-tuple-element.79.refs_0_, bf16[192,1024]{1,0:T(8,128)(2,1)S(1)} %collective-permute-done.16.refs_1_, bf16[384,1024]{1,0:T(8,128)(2,1)S(1)} %copy-done.18, ...), custom_call_target="tpu_custom_call" | custom-call | flops 17179869184 | bytes 4194304 | tf_op jit(solution)/shard_map/pallas_call | solution.py:88
  105.3 7.2 %collective-permute-done.19.refs_0_ = bf16[192,1024]{1,0:T(8,128)(2,1)S(1)} collective-permute-done((bf16[192,1024]{1,0:T(8,128)(2,1)}, bf16[192,1024]{1,0:T(8,128)(2,1)S(1)}, u32[]{:S(2)}, u32[]{:S(2)}) %collective-permute-start.19) | collective-permute-done | bytes 393248 | tf_op jit(solution)/shard_map/ppermute | solution.py:111
  112.4 7.9 %collective-permute-done.18.refs_0_ = bf16[192,1024]{1,0:T(8,128)(2,1)S(1)} collective-permute-done((bf16[192,1024]{1,0:T(8,128)(2,1)}, bf16[192,1024]{1,0:T(8,128)(2,1)S(1)}, u32[]{:S(2)}, u32[]{:S(2)}) %collective-permute-start.18) | collective-permute-done | bytes 393248 | tf_op jit(solution)/shard_map/ppermute | solution.py:111
  120.9 3.5 %shard_map.120 = (f32[384,1024]{1,0:T(8,128)S(1)}, f32[128,1024]{1,0:T(8,128)S(1)}, bf16[576,128]{1,0:T(8,128)(2,1)S(1)}, f32[8,128]{1,0:T(8,128)}) custom-call(bf16[192,1024]{1,0:T(8,128)(2,1)S(1)} %shard_map.117.refs_0_, bf16[192,1024]{1,0:T(8,128)(2,1)S(1)} %shard_map.118.refs_1_, bf16[192,1024]{1,0:T(8,128)(2,1)S(1)} %shard_map.119.refs_2_, ...), custom_call_target="tpu_custom_call" | custom-call | flops 17179869184 | bytes 4194304 | tf_op jit(solution)/shard_map/pallas_call | solution.py:88
  124.5 4.6 %shard_map.121 = (bf16[1024,384]{1,0:T(8,128)(2,1)}, bf16[768,128]{1,0:T(8,128)(2,1)}, bf16[256,128]{1,0:T(8,128)(2,1)}, bf16[256,128]{1,0:T(8,128)(2,1)}, bf16[...) custom-call(s32[4]{0:T(128)S(1)} %copy-done.14, bf16[192,1024]{1,0:T(8,128)(2,1)S(1)} %collective-permute-done.20.refs_1_, ...), custom_call_target="tpu_custom_call" | custom-call | flops 17179869184 | bytes 4194304 | tf_op jit(solution)/shard_map/pallas_call | solution.py:88
  129.1 9.5 %all-to-all-start = ((bf16[32,32,384]{2,1,0:T(8,128)(2,1)}), bf16[32,32,384]{2,1,0:T(8,128)(2,1)S(1)}, u32[]{:S(2)}, u32[]{:S(2)}) async-start(bf16[32,32,384]{2,1,0:T(8,128)(2,1)} %bitcast.5), calls=%async_computation | async-start | bytes 1572864 | tf_op jit(solution)/shard_map/all_to_all | solution.py:904
  139.1 1.8 %collective-permute-start.25 = (bf16[256,128]{1,0:T(8,128)(2,1)}, bf16[256,128]{1,0:T(8,128)(2,1)S(1)}, u32[]{:S(2)}, u32[]{:S(2)}) collective-permute-start(bf16[256,128]{1,0:T(8,128)(2,1)} %get-tuple-element.98), channel_id=1, source_target_pairs={{0,2},{1,3},{2,0},{3,1},{4,6},{5,7},{6,4},{7,5},{8,10},{9,11},{10,... | collective-permute-start | bytes 196616 | tf_op jit(solution)/shard_map/ppermute | solution.py:111
  140.9 8.0 %collective-permute-done.25.refs_8_ = bf16[256,128]{1,0:T(8,128)(2,1)S(1)} collective-permute-done((bf16[256,128]{1,0:T(8,128)(2,1)}, bf16[256,128]{1,0:T(8,128)(2,1)S(1)}, u32[]{:S(2)}, u32[]{:S(2)}) %collective-permute-start.25) | collective-permute-done | bytes 65568 | tf_op jit(solution)/shard_map/ppermute | solution.py:111
  148.9 1.1 collective-permute-done.26.refs_9_
  150.1 1.1 copy-done.3
  151.2 1.8 %shard_map.122 = (bf16[384,128]{1,0:T(8,128)(2,1)}, bf16[384,128]{1,0:T(8,128)(2,1)}, bf16[384,128]{1,0:T(8,128)(2,1)}, bf16[256,128]{1,0:T(8,128)(2,1)}, bf16[2...) custom-call(s32[4]{0:T(128)S(1)} %copy-done.14, ...), custom_call_target="tpu_custom_call" | custom-call | bytes 4194304 | tf_op jit(solution)/shard_map/pallas_call | solution.py:88
  153.0 0.7 collective-permute-start.27
  153.7 1.5 collective-permute-start.28
  155.2 1.3 collective-permute-start.29
  157.0 3.6 %collective-permute-start.31 = (bf16[256,128]{1,0:T(8,128)(2,1)}, bf16[256,128]{1,0:T(8,128)(2,1)S(1)}, u32[]{:S(2)}, u32[]{:S(2)}) collective-permute-start(bf16[256,128]{1,0:T(8,128)(2,1)} %get-tuple-element.109), channel_id=1, source_target_pairs={{0,16},{8,24},{16,0},{24,8},{1,17},{9,25},{17,1},{25,9},{2,18},{10... | collective-permute-start | bytes 196616 | tf_op jit(solution)/shard_map/ppermute | solution.py:845
  160.5 1.8 %collective-permute-start.32 = (bf16[256,128]{1,0:T(8,128)(2,1)}, bf16[256,128]{1,0:T(8,128)(2,1)S(1)}, u32[]{:S(2)}, u32[]{:S(2)}) collective-permute-start(bf16[256,128]{1,0:T(8,128)(2,1)} %get-tuple-element.110), channel_id=1, source_target_pairs={{0,24},{8,16},{16,8},{24,0},{1,25},{9,17},{17,9},{25,1},{2,26},{10... | collective-permute-start | bytes 196616 | tf_op jit(solution)/shard_map/ppermute | solution.py:845
  162.4 2.1 %shard_map.123 = (bf16[192,1024]{1,0:T(8,128)(2,1)}, f32[8,128]{1,0:T(8,128)S(1)}) custom-call(s32[4]{0:T(128)S(1)} %copy-done.14, f32[192,1024]{1,0:T(8,128)S(1)} %get-tuple-element.100.total_ref, bf16[1,1024,1024]{2,1,0:T(8,128)(2,1)S(1)} %copy-done, bf16[384,128]{1,0:T(8,128)(2,1)S(1)} %collective-permute-done.27.refs_0_, ...), custom_call_target="tpu_custom_call" | custom-call | tf_op jit(solution)/shard_map/pallas_call | solution.py:907
  164.4 2.4 %collective-permute-done.32.refs_3_ = bf16[256,128]{1,0:T(8,128)(2,1)S(1)} collective-permute-done((bf16[256,128]{1,0:T(8,128)(2,1)}, bf16[256,128]{1,0:T(8,128)(2,1)S(1)}, u32[]{:S(2)}, u32[]{:S(2)}) %collective-permute-start.32) | collective-permute-done | bytes 65568 | tf_op jit(solution)/shard_map/ppermute | solution.py:845
  166.8 0.9 shard_map.124
  (96 shorter events, 8.1 us)
Async XLA Ops:
  7.2 73.1 %all-gather.2.cloned.1.call-start = ((), (), s32[]{:S(2)}) async-start(), calls=%async_computation.1 | async-start | bytes 3538944 | tf_op jit(solution)/shard_map/all_gather | solution.py:896
  8.5 5.2 %collective-permute-start = (bf16[24,8192]{1,0:T(8,128)(2,1)S(1)}, bf16[24,8192]{1,0:T(8,128)(2,1)S(1)}, u32[]{:S(2)}, u32[]{:S(2)}) collective-permute-start(bf16[24,8192]{1,0:T(8,128)(2,1)S(1)} %shard_map.103.refs_1_), channel_id=1, source_target_pairs={{0,1},{1,0},{2,3},{3,2},{4,5},{5,4},{6,7},{7,6},{8,9},{9,8},{10,11... | collective-permute-start | bytes 1179656 | tf_op jit(solution)/shard_map/ppermute | solution.py:111
  9.1 20.7 %collective-permute-start.2 = (bf16[24,8192]{1,0:T(8,128)(2,1)S(1)}, bf16[24,8192]{1,0:T(8,128)(2,1)S(1)}, u32[]{:S(2)}, u32[]{:S(2)}) collective-permute-start(bf16[24,8192]{1,0:T(8,128)(2,1)S(1)} %shard_map.103.refs_1_), channel_id=1, source_target_pairs={{0,4},{1,5},{2,6},{3,7},{4,0},{5,1},{6,2},{7,3},{8,12},{9,13},{10,... | collective-permute-start | bytes 1179656 | tf_op jit(solution)/shard_map/ppermute | solution.py:111
  11.7 18.8 %collective-permute-start.3 = (bf16[24,8192]{1,0:T(8,128)(2,1)S(1)}, bf16[24,8192]{1,0:T(8,128)(2,1)S(1)}, u32[]{:S(2)}, u32[]{:S(2)}) collective-permute-start(bf16[24,8192]{1,0:T(8,128)(2,1)S(1)} %shard_map.103.refs_1_), channel_id=1, source_target_pairs={{0,6},{1,7},{2,4},{3,5},{4,2},{5,3},{6,0},{7,1},{8,14},{9,15},{10,... | collective-permute-start | bytes 1179656 | tf_op jit(solution)/shard_map/ppermute | solution.py:111
  13.1 18.0 %collective-permute-start.1 = (bf16[24,8192]{1,0:T(8,128)(2,1)S(1)}, bf16[24,8192]{1,0:T(8,128)(2,1)S(1)}, u32[]{:S(2)}, u32[]{:S(2)}) collective-permute-start(bf16[24,8192]{1,0:T(8,128)(2,1)S(1)} %shard_map.103.refs_1_), channel_id=1, source_target_pairs={{0,2},{1,3},{2,0},{3,1},{4,6},{5,7},{6,4},{7,5},{8,10},{9,11},{10,... | collective-permute-start | bytes 1179656 | tf_op jit(solution)/shard_map/ppermute | solution.py:111
  19.2 14.1 %copy-start.2 = (bf16[24,8192]{1,0:T(8,128)(2,1)S(1)}, bf16[24,8192]{1,0:T(8,128)(2,1)}, u32[]{:S(2)}) copy-start(bf16[24,8192]{1,0:T(8,128)(2,1)} %copy-done.1) | copy-start | bytes 1179652
  19.2 14.1 %copy-start.4 = (bf16[192,1024]{1,0:T(8,128)(2,1)S(1)}, bf16[192,1024]{1,0:T(8,128)(2,1)}, u32[]{:S(2)}) copy-start(bf16[192,1024]{1,0:T(8,128)(2,1)} %refs_10_.1) | copy-start | bytes 1179652
  30.5 1.7 collective-permute-start.5
  30.5 2.3 %collective-permute-start.6 = (bf16[24,8192]{1,0:T(8,128)(2,1)S(1)}, bf16[24,8192]{1,0:T(8,128)(2,1)S(1)}, u32[]{:S(2)}, u32[]{:S(2)}) collective-permute-start(bf16[24,8192]{1,0:T(8,128)(2,1)S(1)} %shard_map.107.refs_4_), channel_id=1, source_target_pairs={{0,1},{1,0},{2,3},{3,2},{4,5},{5,4},{6,7},{7,6},{8,9},{9,8},{10,11... | collective-permute-start | bytes 1179656 | tf_op jit(solution)/shard_map/ppermute | solution.py:111
  31.1 2.2 %collective-permute-start.4 = (bf16[24,8192]{1,0:T(8,128)(2,1)S(1)}, bf16[24,8192]{1,0:T(8,128)(2,1)S(1)}, u32[]{:S(2)}, u32[]{:S(2)}) collective-permute-start(bf16[24,8192]{1,0:T(8,128)(2,1)S(1)} %shard_map.105.refs_2_), channel_id=1, source_target_pairs={{0,1},{1,0},{2,3},{3,2},{4,5},{5,4},{6,7},{7,6},{8,9},{9,8},{10,11... | collective-permute-start | bytes 1179656 | tf_op jit(solution)/shard_map/ppermute | solution.py:111
  33.3 13.4 %copy-start.22 = (s32[8]{0:T(128)S(1)}, s32[8]{0:T(128)}, u32[]{:S(2)}) copy-start(s32[8]{0:T(128)} %constant.45.clone) | copy-start | bytes 100
  33.3 22.7 %copy-start.12 = (s32[4]{0:T(128)S(1)}, s32[4]{0:T(128)}, u32[]{:S(2)}) copy-start(s32[4]{0:T(128)} %get-tuple-element.58.refs_1_.refs_0_.info_ref) | copy-start | bytes 52
  43.0 13.1 %collective-permute-start.7 = (bf16[400,512]{1,0:T(8,128)(2,1)}, bf16[400,512]{1,0:T(8,128)(2,1)S(1)}, u32[]{:S(2)}, u32[]{:S(2)}) collective-permute-start(bf16[400,512]{1,0:T(8,128)(2,1)} %get-tuple-element.61), channel_id=1, source_target_pairs={{0,8},{16,24},{1,9},{17,25},{2,10},{18,26},{3,11},{19,27},{4,12},{... | collective-permute-start | bytes 1228808 | tf_op jit(solution)/shard_map/ppermute | solution.py:388
  46.8 1.5 collective-permute-start.8
  47.4 0.8 collective-permute-start.9
  59.1 10.0 %collective-permute-start.10 = (bf16[224,512]{1,0:T(8,128)(2,1)}, bf16[224,512]{1,0:T(8,128)(2,1)S(1)}, u32[]{:S(2)}, u32[]{:S(2)}) collective-permute-start(bf16[224,512]{1,0:T(8,128)(2,1)} %get-tuple-element.63), channel_id=1, source_target_pairs={{8,24},{9,25},{10,26},{11,27},{12,28},{13,29},{14,30},{15,31}} | collective-permute-start | bytes 688136 | tf_op jit(solution)/shard_map/ppermute | solution.py:400
  59.8 9.3 %collective-permute-start.11 = (bf16[224,512]{1,0:T(8,128)(2,1)}, bf16[224,512]{1,0:T(8,128)(2,1)S(1)}, u32[]{:S(2)}, u32[]{:S(2)}) collective-permute-start(bf16[224,512]{1,0:T(8,128)(2,1)} %get-tuple-element.64), channel_id=1, source_target_pairs={{8,16},{9,17},{10,18},{11,19},{12,20},{13,21},{14,22},{15,23}} | collective-permute-start | bytes 688136 | tf_op jit(solution)/shard_map/ppermute | solution.py:400
  64.3 4.8 %copy-start.13 = (s32[4]{0:T(128)S(1)}, s32[4]{0:T(128)}, u32[]{:S(2)}) copy-start(s32[4]{0:T(128)} %get-tuple-element.58.refs_1_.refs_0_.info_ref) | copy-start | bytes 52
  72.6 3.7 %collective-permute-start.12 = (bf16[96,8192]{1,0:T(8,128)(2,1)}, bf16[96,8192]{1,0:T(8,128)(2,1)S(1)}, u32[]{:S(2)}, u32[]{:S(2)}) collective-permute-start(bf16[96,8192]{1,0:T(8,128)(2,1)} %get-tuple-element.71), channel_id=1, source_target_pairs={{0,1},{1,0},{2,3},{3,2},{4,5},{5,4},{6,7},{7,6},{8,9},{9,8},{10,11... | collective-permute-start | bytes 4718600 | tf_op jit(solution)/shard_map/ppermute | solution.py:111
  76.7 12.0 %collective-permute-start.13 = (bf16[24,8192]{1,0:T(8,128)(2,1)S(1)}, bf16[24,8192]{1,0:T(8,128)(2,1)S(1)}, u32[]{:S(2)}, u32[]{:S(2)}) collective-permute-start(bf16[24,8192]{1,0:T(8,128)(2,1)S(1)} %get-tuple-element.73), channel_id=1, source_target_pairs={{0,2},{1,3},{2,0},{3,1},{4,6},{5,7},{6,4},{7,5},{8,10},{9,11},{10,... | collective-permute-start | bytes 1179656 | tf_op jit(solution)/shard_map/ppermute | solution.py:111
  78.2 18.5 %collective-permute-start.14 = (bf16[24,8192]{1,0:T(8,128)(2,1)S(1)}, bf16[24,8192]{1,0:T(8,128)(2,1)S(1)}, u32[]{:S(2)}, u32[]{:S(2)}) collective-permute-start(bf16[24,8192]{1,0:T(8,128)(2,1)S(1)} %get-tuple-element.74), channel_id=1, source_target_pairs={{0,4},{1,5},{2,6},{3,7},{4,0},{5,1},{6,2},{7,3},{8,12},{9,13},{10,... | collective-permute-start | bytes 1179656 | tf_op jit(solution)/shard_map/ppermute | solution.py:111
  79.8 17.9 %copy-start.7 = (bf16[192,1024]{1,0:T(8,128)(2,1)S(1)}, bf16[192,1024]{1,0:T(8,128)(2,1)}, u32[]{:S(2)}) copy-start(bf16[192,1024]{1,0:T(8,128)(2,1)} %refs_4_.1) | copy-start | bytes 1179652
  79.8 17.9 %collective-permute-start.15 = (bf16[24,8192]{1,0:T(8,128)(2,1)S(1)}, bf16[24,8192]{1,0:T(8,128)(2,1)S(1)}, u32[]{:S(2)}, u32[]{:S(2)}) collective-permute-start(bf16[24,8192]{1,0:T(8,128)(2,1)S(1)} %get-tuple-element.75), channel_id=1, source_target_pairs={{0,6},{1,7},{2,4},{3,5},{4,2},{5,3},{6,0},{7,1},{8,14},{9,15},{10,... | collective-permute-start | bytes 1179656 | tf_op jit(solution)/shard_map/ppermute | solution.py:111
  85.7 17.1 %copy-start.17 = (bf16[1024,384]{1,0:T(8,128)(2,1)S(1)}, bf16[1024,384]{1,0:T(8,128)(2,1)}, u32[]{:S(2)}) copy-start(bf16[1024,384]{1,0:T(8,128)(2,1)} %get-tuple-element.83.refs_4_.refs_5_.refs_6_) | copy-start | bytes 2359300
  85.7 17.1 %copy-start.18 = (bf16[384,1024]{1,0:T(8,128)(2,1)S(1)}, bf16[384,1024]{1,0:T(8,128)(2,1)}, u32[]{:S(2)}) copy-start(bf16[384,1024]{1,0:T(8,128)(2,1)} %get-tuple-element.81.refs_2_) | copy-start | bytes 2359300
  85.7 17.1 %copy-start.21 = (bf16[384,128]{1,0:T(8,128)(2,1)S(1)}, bf16[384,128]{1,0:T(8,128)(2,1)}, u32[]{:S(2)}) copy-start(bf16[384,128]{1,0:T(8,128)(2,1)} %get-tuple-element.82.refs_3_) | copy-start | bytes 294916
  99.2 3.6 %collective-permute-start.16 = (bf16[192,1024]{1,0:T(8,128)(2,1)}, bf16[192,1024]{1,0:T(8,128)(2,1)S(1)}, u32[]{:S(2)}, u32[]{:S(2)}) collective-permute-start(bf16[192,1024]{1,0:T(8,128)(2,1)} %get-tuple-element.80), channel_id=1, source_target_pairs={{0,1},{1,0},{2,3},{3,2},{4,5},{5,4},{6,7},{7,6},{8,9},{9,8},{10,11... | collective-permute-start | bytes 1179656 | tf_op jit(solution)/shard_map/ppermute | solution.py:111
  99.3 13.1 %collective-permute-start.19 = (bf16[192,1024]{1,0:T(8,128)(2,1)}, bf16[192,1024]{1,0:T(8,128)(2,1)S(1)}, u32[]{:S(2)}, u32[]{:S(2)}) collective-permute-start(bf16[192,1024]{1,0:T(8,128)(2,1)} %get-tuple-element.80), channel_id=1, source_target_pairs={{0,6},{1,7},{2,4},{3,5},{4,2},{5,3},{6,0},{7,1},{8,14},{9,15},{10,... | collective-permute-start | bytes 1179656 | tf_op jit(solution)/shard_map/ppermute | solution.py:111
  101.1 19.3 %collective-permute-start.18 = (bf16[192,1024]{1,0:T(8,128)(2,1)}, bf16[192,1024]{1,0:T(8,128)(2,1)S(1)}, u32[]{:S(2)}, u32[]{:S(2)}) collective-permute-start(bf16[192,1024]{1,0:T(8,128)(2,1)} %get-tuple-element.80), channel_id=1, source_target_pairs={{0,4},{1,5},{2,6},{3,7},{4,0},{5,1},{6,2},{7,3},{8,12},{9,13},{10,... | collective-permute-start | bytes 1179656 | tf_op jit(solution)/shard_map/ppermute | solution.py:111
  102.1 18.4 %collective-permute-start.17 = (bf16[192,1024]{1,0:T(8,128)(2,1)}, bf16[192,1024]{1,0:T(8,128)(2,1)S(1)}, u32[]{:S(2)}, u32[]{:S(2)}) collective-permute-start(bf16[192,1024]{1,0:T(8,128)(2,1)} %get-tuple-element.80), channel_id=1, source_target_pairs={{0,2},{1,3},{2,0},{3,1},{4,6},{5,7},{6,4},{7,5},{8,10},{9,11},{10,... | collective-permute-start | bytes 1179656 | tf_op jit(solution)/shard_map/ppermute | solution.py:111
  105.2 15.6 %copy-start.16 = (bf16[576,1024]{1,0:T(8,128)(2,1)S(1)}, bf16[576,1024]{1,0:T(8,128)(2,1)}, u32[]{:S(2)}) copy-start(bf16[576,1024]{1,0:T(8,128)(2,1)} %get-tuple-element.86.refs_3_) | copy-start | bytes 3538948
  105.3 15.6 %copy-start.20 = (bf16[576,128]{1,0:T(8,128)(2,1)S(1)}, bf16[576,128]{1,0:T(8,128)(2,1)}, u32[]{:S(2)}) copy-start(bf16[576,128]{1,0:T(8,128)(2,1)} %get-tuple-element.87.refs_4_) | copy-start | bytes 442372
  112.4 12.0 %collective-permute-start.22 = (bf16[192,1024]{1,0:T(8,128)(2,1)S(1)}, bf16[192,1024]{1,0:T(8,128)(2,1)S(1)}, u32[]{:S(2)}, u32[]{:S(2)}) collective-permute-start(bf16[192,1024]{1,0:T(8,128)(2,1)S(1)} %shard_map.119.refs_2_), channel_id=1, source_target_pairs={{0,1},{1,0},{2,3},{3,2},{4,5},{5,4},{6,7},{7,6},{8,9},{9,8},{10,11... | collective-permute-start | bytes 1179656 | tf_op jit(solution)/shard_map/ppermute | solution.py:111
  120.4 4.0 %collective-permute-start.21 = (bf16[192,1024]{1,0:T(8,128)(2,1)S(1)}, bf16[192,1024]{1,0:T(8,128)(2,1)S(1)}, u32[]{:S(2)}, u32[]{:S(2)}) collective-permute-start(bf16[192,1024]{1,0:T(8,128)(2,1)S(1)} %shard_map.118.refs_1_), channel_id=1, source_target_pairs={{0,1},{1,0},{2,3},{3,2},{4,5},{5,4},{6,7},{7,6},{8,9},{9,8},{10,11... | collective-permute-start | bytes 1179656 | tf_op jit(solution)/shard_map/ppermute | solution.py:111
  120.5 3.9 %collective-permute-start.20 = (bf16[192,1024]{1,0:T(8,128)(2,1)S(1)}, bf16[192,1024]{1,0:T(8,128)(2,1)S(1)}, u32[]{:S(2)}, u32[]{:S(2)}) collective-permute-start(bf16[192,1024]{1,0:T(8,128)(2,1)S(1)} %shard_map.117.refs_0_), channel_id=1, source_target_pairs={{0,1},{1,0},{2,3},{3,2},{4,5},{5,4},{6,7},{7,6},{8,9},{9,8},{10,11... | collective-permute-start | bytes 1179656 | tf_op jit(solution)/shard_map/ppermute | solution.py:111
  124.5 25.6 %copy-start = (bf16[1,1024,1024]{2,1,0:T(8,128)(2,1)S(1)}, bf16[1,1024,1024]{2,1,0:T(8,128)(2,1)}, u32[]{:S(2)}) copy-start(bf16[1,1024,1024]{2,1,0:T(8,128)(2,1)} %w_ref.5) | copy-start | bytes 6291460
  129.1 37.8 %all-to-all-start = ((bf16[32,32,384]{2,1,0:T(8,128)(2,1)}), bf16[32,32,384]{2,1,0:T(8,128)(2,1)S(1)}, u32[]{:S(2)}, u32[]{:S(2)}) async-start(bf16[32,32,384]{2,1,0:T(8,128)(2,1)} %bitcast.5), calls=%async_computation | async-start | bytes 1572864 | tf_op jit(solution)/shard_map/all_to_all | solution.py:904
  138.5 11.5 %collective-permute-start.23 = (bf16[768,128]{1,0:T(8,128)(2,1)}, bf16[768,128]{1,0:T(8,128)(2,1)S(1)}, u32[]{:S(2)}, u32[]{:S(2)}) collective-permute-start(bf16[768,128]{1,0:T(8,128)(2,1)} %get-tuple-element.95), channel_id=1, source_target_pairs={{0,1},{1,0},{2,3},{3,2},{4,5},{5,4},{6,7},{7,6},{8,9},{9,8},{10,11... | collective-permute-start | bytes 589832 | tf_op jit(solution)/shard_map/ppermute | solution.py:111
  138.9 2.0 %collective-permute-start.24 = (bf16[256,128]{1,0:T(8,128)(2,1)}, bf16[256,128]{1,0:T(8,128)(2,1)S(1)}, u32[]{:S(2)}, u32[]{:S(2)}) collective-permute-start(bf16[256,128]{1,0:T(8,128)(2,1)} %get-tuple-element.97), channel_id=1, source_target_pairs={{0,1},{1,0},{2,3},{3,2},{4,5},{5,4},{6,7},{7,6},{8,9},{9,8},{10,11... | collective-permute-start | bytes 196616 | tf_op jit(solution)/shard_map/ppermute | solution.py:111
  139.1 9.8 %collective-permute-start.25 = (bf16[256,128]{1,0:T(8,128)(2,1)}, bf16[256,128]{1,0:T(8,128)(2,1)S(1)}, u32[]{:S(2)}, u32[]{:S(2)}) collective-permute-start(bf16[256,128]{1,0:T(8,128)(2,1)} %get-tuple-element.98), channel_id=1, source_target_pairs={{0,2},{1,3},{2,0},{3,1},{4,6},{5,7},{6,4},{7,5},{8,10},{9,11},{10,... | collective-permute-start | bytes 196616 | tf_op jit(solution)/shard_map/ppermute | solution.py:111
  140.9 9.2 %collective-permute-start.26 = (bf16[256,128]{1,0:T(8,128)(2,1)}, bf16[256,128]{1,0:T(8,128)(2,1)S(1)}, u32[]{:S(2)}, u32[]{:S(2)}) collective-permute-start(bf16[256,128]{1,0:T(8,128)(2,1)} %get-tuple-element.99), channel_id=1, source_target_pairs={{0,3},{1,2},{2,1},{3,0},{4,7},{5,6},{6,5},{7,4},{8,11},{9,10},{10,... | collective-permute-start | bytes 196616 | tf_op jit(solution)/shard_map/ppermute | solution.py:111
  153.0 13.9 %copy-start.10 = (bf16[256,128]{1,0:T(8,128)(2,1)S(1)}, bf16[256,128]{1,0:T(8,128)(2,1)}, u32[]{:S(2)}) copy-start(bf16[256,128]{1,0:T(8,128)(2,1)} %get-tuple-element.107.refs_0_) | copy-start | bytes 196612
  153.0 7.6 %collective-permute-start.27 = (bf16[384,128]{1,0:T(8,128)(2,1)}, bf16[384,128]{1,0:T(8,128)(2,1)S(1)}, u32[]{:S(2)}, u32[]{:S(2)}) collective-permute-start(bf16[384,128]{1,0:T(8,128)(2,1)} %get-tuple-element.101), channel_id=1, source_target_pairs={{0,2},{1,3},{2,0},{3,1},{4,6},{5,7},{6,4},{7,5},{8,10},{9,11},{10,... | collective-permute-start | bytes 294920 | tf_op jit(solution)/shard_map/ppermute | solution.py:111
  153.7 8.7 %collective-permute-start.28 = (bf16[384,128]{1,0:T(8,128)(2,1)}, bf16[384,128]{1,0:T(8,128)(2,1)S(1)}, u32[]{:S(2)}, u32[]{:S(2)}) collective-permute-start(bf16[384,128]{1,0:T(8,128)(2,1)} %get-tuple-element.102), channel_id=1, source_target_pairs={{0,4},{1,5},{2,6},{3,7},{4,0},{5,1},{6,2},{7,3},{8,12},{9,13},{10,... | collective-permute-start | bytes 294920 | tf_op jit(solution)/shard_map/ppermute | solution.py:111
  155.2 7.2 %collective-permute-start.29 = (bf16[384,128]{1,0:T(8,128)(2,1)}, bf16[384,128]{1,0:T(8,128)(2,1)S(1)}, u32[]{:S(2)}, u32[]{:S(2)}) collective-permute-start(bf16[384,128]{1,0:T(8,128)(2,1)} %get-tuple-element.103), channel_id=1, source_target_pairs={{0,6},{1,7},{2,4},{3,5},{4,2},{5,3},{6,0},{7,1},{8,14},{9,15},{10,... | collective-permute-start | bytes 294920 | tf_op jit(solution)/shard_map/ppermute | solution.py:111
  156.5 7.9 %collective-permute-start.30 = (bf16[256,128]{1,0:T(8,128)(2,1)}, bf16[256,128]{1,0:T(8,128)(2,1)S(1)}, u32[]{:S(2)}, u32[]{:S(2)}) collective-permute-start(bf16[256,128]{1,0:T(8,128)(2,1)} %get-tuple-element.108), channel_id=1, source_target_pairs={{0,8},{8,0},{16,24},{24,16},{1,9},{9,1},{17,25},{25,17},{2,10},{10... | collective-permute-start | bytes 196616 | tf_op jit(solution)/shard_map/ppermute | solution.py:845
  157.0 7.5 %collective-permute-start.31 = (bf16[256,128]{1,0:T(8,128)(2,1)}, bf16[256,128]{1,0:T(8,128)(2,1)S(1)}, u32[]{:S(2)}, u32[]{:S(2)}) collective-permute-start(bf16[256,128]{1,0:T(8,128)(2,1)} %get-tuple-element.109), channel_id=1, source_target_pairs={{0,16},{8,24},{16,0},{24,8},{1,17},{9,25},{17,1},{25,9},{2,18},{10... | collective-permute-start | bytes 196616 | tf_op jit(solution)/shard_map/ppermute | solution.py:845
  160.5 6.3 %collective-permute-start.32 = (bf16[256,128]{1,0:T(8,128)(2,1)}, bf16[256,128]{1,0:T(8,128)(2,1)S(1)}, u32[]{:S(2)}, u32[]{:S(2)}) collective-permute-start(bf16[256,128]{1,0:T(8,128)(2,1)} %get-tuple-element.110), channel_id=1, source_target_pairs={{0,24},{8,16},{16,8},{24,0},{1,25},{9,17},{17,9},{25,1},{2,26},{10... | collective-permute-start | bytes 196616 | tf_op jit(solution)/shard_map/ppermute | solution.py:845
  (10 other events, 20.6 us)
Sparse Core Ops, SparseCore 0:
  43.1 33.8 all-gather.1

commit v7 on v6

--- a/solution.py
+++ b/solution.py
@@ -397,7 +397,7 @@
         [pltpu.VMEM((2, rows, width), F32), pltpu.VMEM((rows, LANES), F32)],
         info,
     )
-    back = [lax.ppermute(back3, "ctx", [(1, 3)]), lax.ppermute(back2, "ctx", [(1, 2)])]
+    back = [lax.ppermute(back2, "ctx", [(1, 2)]), lax.ppermute(back3, "ctx", [(1, 3)])]
     top, den, edge = staged(
         near_body,
         [kv_near, kv_in, mask, done],
@@ -538,7 +538,7 @@
     pieces = call(pair_sum_body, [(block, F32)] + [(block, BF16)] * (blocks - 1))(
         even, swap(odd, 1)
     )
-    return [pieces[0]] + [swap(piece, 2 * (index + 1)) for index, piece in enumerate(pieces[1:])]
+    return [pieces[0]] + [swap(pieces[k], 2 * k) for k in range(blocks - 1, 0, -1)]
 
 
 def state_body(count, *refs):
@@ -736,11 +736,19 @@
     message.ref[rows:, :] = jnp.concatenate(abs_, axis=0)
 
 
-def relay_body(heads, count, rounds, planes, info_ref, state_ref, w_ref, *refs):
-    (ab0_ref, ab1_ref, there_ref), refs = refs[:3], refs[3:]
-    pieces, refs = refs[:rounds], refs[rounds:]
-    messages, outs, (total_ref, held) = refs[:count], refs[count : count + planes], refs[count + planes :]
+def relay_body(*refs):
+    ab0_ref, ab1_ref, there_ref, *messages, own_ref = refs
     rows = ab0_ref.shape[0] // 2
+    for k, message in enumerate(messages):
+        message.ref[:rows, :] = ab1_ref[k * rows : (k + 1) * rows, :]
+        message.ref[rows:, :] = there_ref[(k + 1) * rows : (k + 2) * rows, :]
+        message.send()
+    own_ref[:rows, :] = ab0_ref[:rows, :]
+    own_ref[rows:, :] = there_ref[:rows, :]
+
+
+def planes_body(rounds, planes, info_ref, *refs):
+    pieces, outs, held = refs[:rounds], refs[rounds:-1], refs[-1]
     for k, piece in enumerate(pieces):
         held[k] = piece[...].astype(F32)
     for z, out in enumerate(outs):
@@ -750,25 +758,9 @@
             total = term if total is None else total + term
         out.ref[...] = total.astype(BF16)
         out.send()
-    for k, message in enumerate(messages):
-        message.ref[:rows, :] = ab1_ref[k * rows : (k + 1) * rows, :]
-        message.ref[rows:, :] = there_ref[(k + 1) * rows : (k + 2) * rows, :]
-        message.send()
-    total = add_heads(heads, info_ref, state_ref[...], w_ref, 0, [ab0_ref[:rows, :]])
-    total_ref[...] = add_heads(heads, info_ref, total, w_ref, 1, [there_ref[:rows, :]])
-
-
-def add_heads(heads, info_ref, total, w_ref, first, values):
-    d = LOCAL_HEAD_DIM
-    for index, value in enumerate(values):
-        head = heads(info_ref[1] ^ (first + index))
-        total += dot(value, w_ref[0, pl.ds(pl.multiple_of(head * d, d), d), :])
-    return total
-
-
-def local_layer(
-    normed, normed_near, info, parts, gbs, cores, weights, rounds, planes, heads, state, local_out
-):
+
+
+def local_layer(normed, normed_near, info, parts, gbs, cores, weights, rounds, planes):
     rows, width = normed.shape
     d = LOCAL_HEAD_DIM
     near = [swap(normed, bits) for bits in parts[1]]
@@ -802,24 +794,33 @@
         mib=20,
     )
     pieces = [own] + [swap(value, k + 1) for k, value in enumerate(pieces)]
-    *sent, total = staged(
-        functools.partial(relay_body, heads, count, rounds, planes),
-        [state, local_out, ab0, ab1, swap(message, 1), *pieces],
-        [((2 * rows, d), BF16)] * count + [piece] * planes,
-        [((rows, width), F32)],
-        [pltpu.VMEM((rounds, deep, d), F32)],
-        info,
-    )
-    messages = [swap(value, 2 * (k + 1)) for k, value in enumerate(sent[:count])]
-    return total, messages, sent[count:], grad_qkv
-
-
-def hidden_body(heads, info_ref, total_ref, w_ref, *refs):
+    block = ((2 * rows, d), BF16)
+    *sent, own = staged(
+        relay_body, [ab0, ab1, swap(message, 1)], [block] * count, [block]
+    )
+    messages = [own] + [swap(value, 2 * (k + 1)) for k, value in enumerate(sent)]
+    pieces = staged(
+        functools.partial(planes_body, rounds, planes),
+        pieces,
+        [piece] * planes,
+        scratch=[pltpu.VMEM((rounds, deep, d), F32)],
+        info=info,
+    )
+    return messages, pieces, grad_qkv
+
+
+def hidden_body(heads, info_ref, state_ref, w_ref, *refs):
     *messages, out_ref, token_ref = refs
     token_ref[...] = jnp.zeros_like(token_ref)
-    rows = total_ref.shape[0]
-    values = [message[at : at + rows, :] for message in messages for at in (0, rows)]
-    out_ref[...] = add_heads(heads, info_ref, total_ref[...], w_ref, 2, values).astype(BF16)
+    rows = state_ref.shape[0]
+    d = LOCAL_HEAD_DIM
+    total = state_ref[...]
+    for bits in range(2 * len(messages)):
+        at = bits % 2 * rows
+        head = heads(info_ref[1] ^ bits)
+        weights = w_ref[0, pl.ds(pl.multiple_of(head * d, d), d), :]
+        total += dot(messages[bits // 2][at : at + rows, :], weights)
+    out_ref[...] = total.astype(BF16)
 
 
 def final_body(heads, parts_ref, _, *refs):
@@ -898,8 +899,8 @@
     state, normed, normed_near = byte_state(
         scatter_sum(even, odd, patches), local_embeds, prepared
     )
-    total, messages, out_pieces, grad_qkv = local_layer(
-        normed, normed_near, head_info, parts, gbs, cores, weights, rounds, planes, head_of, state, local_out
+    messages, out_pieces, grad_qkv = local_layer(
+        normed, normed_near, head_info, parts, gbs, cores, weights, rounds, planes
     )
     grad_qkv = lax.all_to_all(grad_qkv, ("ctx", "tp"), 0, 0, tiled=True)
     out_pieces = swap_planes(out_pieces)
@@ -910,7 +911,7 @@
         out_specs=[here, here],
         out_shape=[jax.ShapeDtypeStruct((byte_count, width), BF16), TOKEN],
         compiler_params=params(16),
-    )(head_info, total, local_out, *messages)
+    )(head_info, state, local_out, *messages)
     grad_qkv, grad_out = call(
         functools.partial(final_body, heads),
         [((1, share, 3 * width), F32), ((1, share, width), F32)],

time: 175 us -> 174 us (level)
    pallas_call x7 -> x8, Pallas kernels: 18.8 us -> 19.1 us  [staged(): pl.pallas_call(kernel, in_specs=[pl.BlockSpec(memory_space=pltpu.SMEM)] *...]
  transfers between devices with their start and end apart: 35 -> 35, of which waited for: 16 -> 17; matrix products, arithmetic and copies ran while one was open for 0% -> 1% of each run, Pallas kernels for 19% -> 20%
where the time goes in v7:
time: 174 us; the launch traced here: 173 us
  waiting for transfers between devices  61.7 us (35%)
  Pallas kernels  51 us (29%)
  starting transfers between devices  40.1 us (23%)
  between operations  14.5 us (8%)
  local copies, waits for them, and re-layouts  5.24 us (3%)
    ppermute x25, waiting for transfers between devices, swap(): lax.ppermute(value, 'tp', [(source, source ^ bits) for source in range(co...  51.2 us
    pallas_call x8, Pallas kernels, staged(): pl.pallas_call(kernel, in_specs=[pl.BlockSpec(memory_space=pltpu.SMEM)] *...  19.1 us
    ppermute x25, starting transfers between devices, swap(): lax.ppermute(value, 'tp', [(source, source ^ bits) for source in range(co...  18.8 us
    all_to_all x1, starting transfers between devices, per_device(): grad_qkv = lax.all_to_all(grad_qkv, ('ctx', 'tp'), 0, 0, tiled=True)  10.2 us
    pallas_call x1, Pallas kernels, project(): pl.pallas_call(body, in_specs=[pl.BlockSpec(memory_space=pltpu.SMEM)] + [...  9.61 us
    pallas_call x2, Pallas kernels, preload(): pl.pallas_call(functools.partial(preload_body, parts), in_specs=[scalar,...  9.44 us
    ppermute x1, waiting for transfers between devices, attend_paired(): kv_in = lax.ppermute(kv, 'ctx', [(0, 1), (2, 3)])  7.76 us
    pallas_call x1, Pallas kernels, prepare(): pl.pallas_call(functools.partial(prepare_body, parts), grid_spec=pltpu.Pr...  5.49 us
  transfers between devices with their start and end apart: 35, of which 17 were waited for; matrix products, arithmetic and copies ran while one was open for 1% of the time, Pallas kernels for 20%

profile of v7, /device:TPU:0, one launch (start us, length us, event | category | flops | bytes accessed | tf_op | source)
XLA Modules:
  0.0 173.3 jit_solution(14755048067135734507)
XLA Ops:
  7.2 1.0 copy-done.8
  9.1 2.6 %collective-permute-start.2 = (bf16[24,8192]{1,0:T(8,128)(2,1)S(1)}, bf16[24,8192]{1,0:T(8,128)(2,1)S(1)}, u32[]{:S(2)}, u32[]{:S(2)}) collective-permute-start(bf16[24,8192]{1,0:T(8,128)(2,1)S(1)} %shard_map.103.refs_1_), channel_id=1, source_target_pairs={{0,4},{1,5},{2,6},{3,7},{4,0},{5,1},{6,2},{7,3},{8,12},{9,13},{10,... | collective-permute-start | bytes 1179656 | tf_op jit(solution)/shard_map/ppermute | solution.py:111
  11.7 1.4 collective-permute-start.3
  13.9 0.7 copy-done.1
  14.6 4.7 %shard_map.104 = (bf16[8192,512]{1,0:T(8,128)(2,1)S(1)}, s32[4]{0:T(128)}) custom-call(s32[4]{0:T(128)} %pad_add_fusion.info_ref, bf16[3,8192,512]{2,1,0:T(8,128)(2,1)} %refs_11_.1, bf16[24,8192]{1,0:T(8,128)(2,1)} %copy-done.1), custom_call_target="tpu_custom_call" | custom-call | bytes 8388608 | tf_op jit(solution)/shard_map/pallas_call | solution.py:157
  19.3 10.5 %collective-permute-done.2.refs_0_ = bf16[24,8192]{1,0:T(8,128)(2,1)S(1)} collective-permute-done((bf16[24,8192]{1,0:T(8,128)(2,1)S(1)}, bf16[24,8192]{1,0:T(8,128)(2,1)S(1)}, u32[]{:S(2)}, u32[]{:S(2)}) %collective-permute-start.2) | collective-permute-done | bytes 393248 | tf_op jit(solution)/shard_map/ppermute | solution.py:111
  31.1 1.1 collective-permute-done.5.refs_7_
  33.3 9.6 %shard_map.108 = (bf16[192,512]{1,0:T(8,128)(2,1)}, bf16[400,512]{1,0:T(8,128)(2,1)}, bf16[192,1024]{1,0:T(8,128)(2,1)}, bf16[400,512]{1,0:T(8,128)(2,1)S(1)}) custom-call(s32[4]{0:T(128)S(1)} %copy-done.11, bf16[24,8192]{1,0:T(8,128)(2,1)S(1)} %shard_map.103.refs_1_, bf16[24,8192]{1,0:T(8,128)(2,1)S(1)} %shard_map.105.refs_2_, ...), custom_call_target="tpu_custom_call" | custom-call | tf_op jit(solution)/shard_map/pallas_call | solution.py:267
  43.0 3.7 %collective-permute-start.7 = (bf16[400,512]{1,0:T(8,128)(2,1)}, bf16[400,512]{1,0:T(8,128)(2,1)S(1)}, u32[]{:S(2)}, u32[]{:S(2)}) collective-permute-start(bf16[400,512]{1,0:T(8,128)(2,1)} %get-tuple-element.61), channel_id=1, source_target_pairs={{0,8},{16,24},{1,9},{17,25},{2,10},{18,26},{3,11},{19,27},{4,12},{... | collective-permute-start | bytes 1228808 | tf_op jit(solution)/shard_map/ppermute | solution.py:388
  46.7 0.7 collective-permute-start.8
  48.3 7.8 %collective-permute-done.7.refs_2_ = bf16[400,512]{1,0:T(8,128)(2,1)S(1)} collective-permute-done((bf16[400,512]{1,0:T(8,128)(2,1)}, bf16[400,512]{1,0:T(8,128)(2,1)S(1)}, u32[]{:S(2)}, u32[]{:S(2)}) %collective-permute-start.7) | collective-permute-done | bytes 409632 | tf_op jit(solution)/shard_map/ppermute | solution.py:388
  56.0 3.1 %shard_map.109 = (bf16[224,512]{1,0:T(8,128)(2,1)}, bf16[224,512]{1,0:T(8,128)(2,1)}, f32[8,128]{1,0:T(8,128)S(1)}) custom-call(s32[4]{0:T(128)S(1)} %copy-done.12, bf16[400,512]{1,0:T(8,128)(2,1)S(1)} %get-tuple-element.60.refs_1_, bf16[400,512]{1,0:T(8,128)(2,1)S(1)} %collective-permute-done.7.refs_2_, ...), custom_call_target="tpu_custom_call" | custom-call | bytes 4194304 | tf_op jit(solution)/shard_map/pallas_call | solution.py:88
  59.1 0.7 collective-permute-start.10
  59.8 0.9 collective-permute-start.11
  60.8 0.9 copy-done.9
  61.7 2.0 %shard_map.110 = (f32[192,512]{1,0:T(8,128)S(1)}, f32[192,128]{1,0:T(8,128)S(1)}, f32[16,640]{1,0:T(8,128)S(1)}) custom-call(s32[4]{0:T(128)S(1)} %copy-done.12, bf16[400,512]{1,0:T(8,128)(2,1)S(1)} %get-tuple-element.60.refs_1_, bf16[400,512]{1,0:T(8,128)(2,1)S(1)} %collective-permute-done.7.refs_2_, f32[192,192]{1,0:T(8,128)S(1)} %compare_convert_fusion.refs_3_, ...), custom_call_target="tpu_custom_call" | custom-call | bytes 4194304 | tf_op jit(solution)/shard_map/pallas_call | solution.py:88
  64.3 4.8 %shard_map.111 = (bf16[512,8192]{1,0:T(8,128)(2,1)S(1)}, s32[4]{0:T(128)}) custom-call(s32[4]{0:T(128)} %get-tuple-element.58.refs_1_.refs_0_.info_ref, bf16[512,8192]{1,0:T(8,128)(2,1)} %w_ref.4, f32[192,128]{1,0:T(8,128)} %copy-done.5), custom_call_target="tpu_custom_call" | custom-call | bytes 8388608 | tf_op jit(solution)/shard_map/pallas_call | solution.py:157
  69.2 3.5 %shard_map.112 = (bf16[96,8192]{1,0:T(8,128)(2,1)}, bf16[96,8192]{1,0:T(8,128)(2,1)S(1)}) custom-call(s32[4]{0:T(128)S(1)} %copy-done.13, bf16[224,512]{1,0:T(8,128)(2,1)S(1)} %collective-permute-done.10.refs_0_, bf16[224,512]{1,0:T(8,128)(2,1)S(1)} %collective-permute-done.11.refs_1_, f32[192,512]{1,0:T(8,128)S(1)} %get-tuple-element.66.refs_2_, ...), custom_call_target="tpu_custom_call" | custom-call | tf_op jit(solution)/shard_map/pallas_call | solution.py:509
  72.7 3.6 %collective-permute-done.12.other_ref = bf16[96,8192]{1,0:T(8,128)(2,1)S(1)} collective-permute-done((bf16[96,8192]{1,0:T(8,128)(2,1)}, bf16[96,8192]{1,0:T(8,128)(2,1)S(1)}, u32[]{:S(2)}, u32[]{:S(2)}) %collective-permute-start.12) | collective-permute-done | bytes 1572896 | tf_op jit(solution)/shard_map/ppermute | solution.py:111
  76.6 2.5 %collective-permute-start.13 = (bf16[24,8192]{1,0:T(8,128)(2,1)S(1)}, bf16[24,8192]{1,0:T(8,128)(2,1)S(1)}, u32[]{:S(2)}, u32[]{:S(2)}) collective-permute-start(bf16[24,8192]{1,0:T(8,128)(2,1)S(1)} %get-tuple-element.73), channel_id=1, source_target_pairs={{0,6},{1,7},{2,4},{3,5},{4,2},{5,3},{6,0},{7,1},{8,14},{9,15},{10,... | collective-permute-start | bytes 1179656 | tf_op jit(solution)/shard_map/ppermute | solution.py:111
  80.2 5.5 %shard_map.114 = (f32[8,128]{1,0:T(8,128)S(1)}, bf16[1024,384]{1,0:T(8,128)(2,1)}, bf16[384,1024]{1,0:T(8,128)(2,1)}, bf16[384,128]{1,0:T(8,128)(2,1)}, bf16[576...) custom-call(s32[4]{0:T(128)} %get-tuple-element.58.refs_1_.refs_0_.info_ref,, ...), custom_call_target="tpu_custom_call" | custom-call | tf_op jit(solution)/shard_map/pallas_call | solution.py:615
  85.7 3.9 %collective-permute-done.13.refs_1_ = bf16[24,8192]{1,0:T(8,128)(2,1)S(1)} collective-permute-done((bf16[24,8192]{1,0:T(8,128)(2,1)S(1)}, bf16[24,8192]{1,0:T(8,128)(2,1)S(1)}, u32[]{:S(2)}, u32[]{:S(2)}) %collective-permute-start.13) | collective-permute-done | bytes 393248 | tf_op jit(solution)/shard_map/ppermute | solution.py:111
  89.6 7.6 %collective-permute-done.14.refs_2_ = bf16[24,8192]{1,0:T(8,128)(2,1)S(1)} collective-permute-done((bf16[24,8192]{1,0:T(8,128)(2,1)S(1)}, bf16[24,8192]{1,0:T(8,128)(2,1)S(1)}, u32[]{:S(2)}, u32[]{:S(2)}) %collective-permute-start.14) | collective-permute-done | bytes 393248 | tf_op jit(solution)/shard_map/ppermute | solution.py:111
  97.5 1.5 shard_map.115
  99.1 1.6 collective-permute-start.19
  100.7 1.4 collective-permute-start.18
  102.7 2.4 %shard_map.116 = (f32[384,1024]{1,0:T(8,128)S(1)}, f32[128,1024]{1,0:T(8,128)S(1)}, bf16[384,128]{1,0:T(8,128)(2,1)S(1)}, f32[8,128]{1,0:T(8,128)S(1)}) custom-call(bf16[192,1024]{1,0:T(8,128)(2,1)S(1)} %get-tuple-element.79.refs_0_, bf16[192,1024]{1,0:T(8,128)(2,1)S(1)} %collective-permute-done.16.refs_1_, bf16[384,1024]{1,0:T(8,128)(2,1)S(1)} %copy-done.18, ...), custom_call_target="tpu_custom_call" | custom-call | flops 17179869184 | bytes 4194304 | tf_op jit(solution)/shard_map/pallas_call | solution.py:88
  105.1 7.2 %collective-permute-done.19.refs_0_ = bf16[192,1024]{1,0:T(8,128)(2,1)S(1)} collective-permute-done((bf16[192,1024]{1,0:T(8,128)(2,1)}, bf16[192,1024]{1,0:T(8,128)(2,1)S(1)}, u32[]{:S(2)}, u32[]{:S(2)}) %collective-permute-start.19) | collective-permute-done | bytes 393248 | tf_op jit(solution)/shard_map/ppermute | solution.py:111
  112.2 7.9 %collective-permute-done.18.refs_0_ = bf16[192,1024]{1,0:T(8,128)(2,1)S(1)} collective-permute-done((bf16[192,1024]{1,0:T(8,128)(2,1)}, bf16[192,1024]{1,0:T(8,128)(2,1)S(1)}, u32[]{:S(2)}, u32[]{:S(2)}) %collective-permute-start.18) | collective-permute-done | bytes 393248 | tf_op jit(solution)/shard_map/ppermute | solution.py:111
  120.7 3.5 %shard_map.120 = (f32[384,1024]{1,0:T(8,128)S(1)}, f32[128,1024]{1,0:T(8,128)S(1)}, bf16[576,128]{1,0:T(8,128)(2,1)S(1)}, f32[8,128]{1,0:T(8,128)}) custom-call(bf16[192,1024]{1,0:T(8,128)(2,1)S(1)} %shard_map.117.refs_0_, bf16[192,1024]{1,0:T(8,128)(2,1)S(1)} %shard_map.118.refs_1_, bf16[192,1024]{1,0:T(8,128)(2,1)S(1)} %shard_map.119.refs_2_, ...), custom_call_target="tpu_custom_call" | custom-call | flops 17179869184 | bytes 4194304 | tf_op jit(solution)/shard_map/pallas_call | solution.py:88
  124.2 4.6 %shard_map.121 = (bf16[1024,384]{1,0:T(8,128)(2,1)}, bf16[768,128]{1,0:T(8,128)(2,1)}, bf16[256,128]{1,0:T(8,128)(2,1)}, bf16[256,128]{1,0:T(8,128)(2,1)}, bf16[...) custom-call(s32[4]{0:T(128)S(1)} %copy-done.14, bf16[192,1024]{1,0:T(8,128)(2,1)S(1)} %collective-permute-done.20.refs_1_, ...), custom_call_target="tpu_custom_call" | custom-call | flops 17179869184 | bytes 4194304 | tf_op jit(solution)/shard_map/pallas_call | solution.py:88
  128.9 10.2 %all-to-all-start = ((bf16[32,32,384]{2,1,0:T(8,128)(2,1)}), bf16[32,32,384]{2,1,0:T(8,128)(2,1)S(1)}, u32[]{:S(2)}, u32[]{:S(2)}) async-start(bf16[32,32,384]{2,1,0:T(8,128)(2,1)} %bitcast.5), calls=%async_computation | async-start | bytes 1572864 | tf_op jit(solution)/shard_map/all_to_all | solution.py:905
  139.6 1.1 collective-permute-done.23.refs_2_
  140.8 0.7 shard_map.122
  141.5 1.8 %collective-permute-start.24 = (bf16[384,128]{1,0:T(8,128)(2,1)}, bf16[384,128]{1,0:T(8,128)(2,1)S(1)}, u32[]{:S(2)}, u32[]{:S(2)}) collective-permute-start(bf16[384,128]{1,0:T(8,128)(2,1)} %get-tuple-element.97), channel_id=1, source_target_pairs={{0,2},{1,3},{2,0},{3,1},{4,6},{5,7},{6,4},{7,5},{8,10},{9,11},{10,... | collective-permute-start | bytes 294920 | tf_op jit(solution)/shard_map/ppermute | solution.py:111
  143.6 1.0 collective-permute-start.29
  144.6 1.5 collective-permute-start.25
  146.0 0.8 collective-permute-start.26
  146.9 5.8 %collective-permute-done.28.refs_3_ = bf16[256,128]{1,0:T(8,128)(2,1)S(1)} collective-permute-done((bf16[256,128]{1,0:T(8,128)(2,1)}, bf16[256,128]{1,0:T(8,128)(2,1)S(1)}, u32[]{:S(2)}, u32[]{:S(2)}) %collective-permute-start.28) | collective-permute-done | bytes 65568 | tf_op jit(solution)/shard_map/ppermute | solution.py:111
  152.6 1.0 collective-permute-done.29.refs_4_
  153.6 1.3 shard_map.124
  155.0 1.2 collective-permute-start.30
  156.1 3.1 %collective-permute-start.31 = (bf16[256,128]{1,0:T(8,128)(2,1)}, bf16[256,128]{1,0:T(8,128)(2,1)S(1)}, u32[]{:S(2)}, u32[]{:S(2)}) collective-permute-start(bf16[256,128]{1,0:T(8,128)(2,1)} %get-tuple-element.109), channel_id=1, source_target_pairs={{0,16},{8,24},{16,0},{24,8},{1,17},{9,25},{17,1},{25,9},{2,18},{10... | collective-permute-start | bytes 196616 | tf_op jit(solution)/shard_map/ppermute | solution.py:846
  159.4 1.1 copy-done.3
  160.6 2.3 %shard_map.123 = (bf16[192,1024]{1,0:T(8,128)(2,1)}, f32[8,128]{1,0:T(8,128)S(1)}) custom-call(s32[4]{0:T(128)S(1)} %copy-done.14, f32[192,1024]{1,0:T(8,128)S(1)} %copy-done.3, bf16[1,1024,1024]{2,1,0:T(8,128)(2,1)S(1)} %copy-done, bf16[384,128]{1,0:T(8,128)(2,1)S(1)} %get-tuple-element.96.refs_0_, bf16[384,128]{1,0:T(8,128)(2,1)S(1)} %collective-permute-done.24.refs_1_, ...), custom_call_target="tpu_custom_call" | custom-call | tf_op jit(solution)/shard_map/pallas_call | solution.py:908
  162.8 0.9 collective-permute-done.31.refs_2_
  163.8 1.8 %collective-permute-done.32.refs_3_ = bf16[256,128]{1,0:T(8,128)(2,1)S(1)} collective-permute-done((bf16[256,128]{1,0:T(8,128)(2,1)}, bf16[256,128]{1,0:T(8,128)(2,1)S(1)}, u32[]{:S(2)}, u32[]{:S(2)}) %collective-permute-start.32) | collective-permute-done | bytes 65568 | tf_op jit(solution)/shard_map/ppermute | solution.py:846
  165.6 0.9 shard_map.125
  (97 shorter events, 9.6 us)
Async XLA Ops:
  7.2 73.0 %all-gather.2.cloned.1.call-start = ((), (), s32[]{:S(2)}) async-start(), calls=%async_computation.1 | async-start | bytes 3538944 | tf_op jit(solution)/shard_map/all_gather | solution.py:897
  8.5 5.3 %collective-permute-start = (bf16[24,8192]{1,0:T(8,128)(2,1)S(1)}, bf16[24,8192]{1,0:T(8,128)(2,1)S(1)}, u32[]{:S(2)}, u32[]{:S(2)}) collective-permute-start(bf16[24,8192]{1,0:T(8,128)(2,1)S(1)} %shard_map.103.refs_1_), channel_id=1, source_target_pairs={{0,1},{1,0},{2,3},{3,2},{4,5},{5,4},{6,7},{7,6},{8,9},{9,8},{10,11... | collective-permute-start | bytes 1179656 | tf_op jit(solution)/shard_map/ppermute | solution.py:111
  9.1 20.7 %collective-permute-start.2 = (bf16[24,8192]{1,0:T(8,128)(2,1)S(1)}, bf16[24,8192]{1,0:T(8,128)(2,1)S(1)}, u32[]{:S(2)}, u32[]{:S(2)}) collective-permute-start(bf16[24,8192]{1,0:T(8,128)(2,1)S(1)} %shard_map.103.refs_1_), channel_id=1, source_target_pairs={{0,4},{1,5},{2,6},{3,7},{4,0},{5,1},{6,2},{7,3},{8,12},{9,13},{10,... | collective-permute-start | bytes 1179656 | tf_op jit(solution)/shard_map/ppermute | solution.py:111
  11.7 18.8 %collective-permute-start.3 = (bf16[24,8192]{1,0:T(8,128)(2,1)S(1)}, bf16[24,8192]{1,0:T(8,128)(2,1)S(1)}, u32[]{:S(2)}, u32[]{:S(2)}) collective-permute-start(bf16[24,8192]{1,0:T(8,128)(2,1)S(1)} %shard_map.103.refs_1_), channel_id=1, source_target_pairs={{0,6},{1,7},{2,4},{3,5},{4,2},{5,3},{6,0},{7,1},{8,14},{9,15},{10,... | collective-permute-start | bytes 1179656 | tf_op jit(solution)/shard_map/ppermute | solution.py:111
  13.1 18.0 %collective-permute-start.1 = (bf16[24,8192]{1,0:T(8,128)(2,1)S(1)}, bf16[24,8192]{1,0:T(8,128)(2,1)S(1)}, u32[]{:S(2)}, u32[]{:S(2)}) collective-permute-start(bf16[24,8192]{1,0:T(8,128)(2,1)S(1)} %shard_map.103.refs_1_), channel_id=1, source_target_pairs={{0,2},{1,3},{2,0},{3,1},{4,6},{5,7},{6,4},{7,5},{8,10},{9,11},{10,... | collective-permute-start | bytes 1179656 | tf_op jit(solution)/shard_map/ppermute | solution.py:111
  19.3 14.0 %copy-start.2 = (bf16[24,8192]{1,0:T(8,128)(2,1)S(1)}, bf16[24,8192]{1,0:T(8,128)(2,1)}, u32[]{:S(2)}) copy-start(bf16[24,8192]{1,0:T(8,128)(2,1)} %copy-done.1) | copy-start | bytes 1179652
  19.3 14.0 %copy-start.4 = (bf16[192,1024]{1,0:T(8,128)(2,1)S(1)}, bf16[192,1024]{1,0:T(8,128)(2,1)}, u32[]{:S(2)}) copy-start(bf16[192,1024]{1,0:T(8,128)(2,1)} %refs_10_.1) | copy-start | bytes 1179652
  30.5 1.7 collective-permute-start.5
  30.5 2.3 %collective-permute-start.6 = (bf16[24,8192]{1,0:T(8,128)(2,1)S(1)}, bf16[24,8192]{1,0:T(8,128)(2,1)S(1)}, u32[]{:S(2)}, u32[]{:S(2)}) collective-permute-start(bf16[24,8192]{1,0:T(8,128)(2,1)S(1)} %shard_map.107.refs_4_), channel_id=1, source_target_pairs={{0,1},{1,0},{2,3},{3,2},{4,5},{5,4},{6,7},{7,6},{8,9},{9,8},{10,11... | collective-permute-start | bytes 1179656 | tf_op jit(solution)/shard_map/ppermute | solution.py:111
  31.1 2.2 %collective-permute-start.4 = (bf16[24,8192]{1,0:T(8,128)(2,1)S(1)}, bf16[24,8192]{1,0:T(8,128)(2,1)S(1)}, u32[]{:S(2)}, u32[]{:S(2)}) collective-permute-start(bf16[24,8192]{1,0:T(8,128)(2,1)S(1)} %shard_map.105.refs_2_), channel_id=1, source_target_pairs={{0,1},{1,0},{2,3},{3,2},{4,5},{5,4},{6,7},{7,6},{8,9},{9,8},{10,11... | collective-permute-start | bytes 1179656 | tf_op jit(solution)/shard_map/ppermute | solution.py:111
  33.3 13.4 %copy-start.22 = (s32[8]{0:T(128)S(1)}, s32[8]{0:T(128)}, u32[]{:S(2)}) copy-start(s32[8]{0:T(128)} %constant.45.clone) | copy-start | bytes 100
  33.3 22.7 %copy-start.12 = (s32[4]{0:T(128)S(1)}, s32[4]{0:T(128)}, u32[]{:S(2)}) copy-start(s32[4]{0:T(128)} %get-tuple-element.58.refs_1_.refs_0_.info_ref) | copy-start | bytes 52
  43.0 13.1 %collective-permute-start.7 = (bf16[400,512]{1,0:T(8,128)(2,1)}, bf16[400,512]{1,0:T(8,128)(2,1)S(1)}, u32[]{:S(2)}, u32[]{:S(2)}) collective-permute-start(bf16[400,512]{1,0:T(8,128)(2,1)} %get-tuple-element.61), channel_id=1, source_target_pairs={{0,8},{16,24},{1,9},{17,25},{2,10},{18,26},{3,11},{19,27},{4,12},{... | collective-permute-start | bytes 1228808 | tf_op jit(solution)/shard_map/ppermute | solution.py:388
  46.7 1.5 collective-permute-start.8
  47.4 0.8 collective-permute-start.9
  59.1 10.0 %collective-permute-start.10 = (bf16[224,512]{1,0:T(8,128)(2,1)}, bf16[224,512]{1,0:T(8,128)(2,1)S(1)}, u32[]{:S(2)}, u32[]{:S(2)}) collective-permute-start(bf16[224,512]{1,0:T(8,128)(2,1)} %get-tuple-element.63), channel_id=1, source_target_pairs={{8,16},{9,17},{10,18},{11,19},{12,20},{13,21},{14,22},{15,23}} | collective-permute-start | bytes 688136 | tf_op jit(solution)/shard_map/ppermute | solution.py:400
  59.8 9.3 %collective-permute-start.11 = (bf16[224,512]{1,0:T(8,128)(2,1)}, bf16[224,512]{1,0:T(8,128)(2,1)S(1)}, u32[]{:S(2)}, u32[]{:S(2)}) collective-permute-start(bf16[224,512]{1,0:T(8,128)(2,1)} %get-tuple-element.64), channel_id=1, source_target_pairs={{8,24},{9,25},{10,26},{11,27},{12,28},{13,29},{14,30},{15,31}} | collective-permute-start | bytes 688136 | tf_op jit(solution)/shard_map/ppermute | solution.py:400
  64.3 4.8 %copy-start.13 = (s32[4]{0:T(128)S(1)}, s32[4]{0:T(128)}, u32[]{:S(2)}) copy-start(s32[4]{0:T(128)} %get-tuple-element.58.refs_1_.refs_0_.info_ref) | copy-start | bytes 52
  72.6 3.7 %collective-permute-start.12 = (bf16[96,8192]{1,0:T(8,128)(2,1)}, bf16[96,8192]{1,0:T(8,128)(2,1)S(1)}, u32[]{:S(2)}, u32[]{:S(2)}) collective-permute-start(bf16[96,8192]{1,0:T(8,128)(2,1)} %get-tuple-element.71), channel_id=1, source_target_pairs={{0,1},{1,0},{2,3},{3,2},{4,5},{5,4},{6,7},{7,6},{8,9},{9,8},{10,11... | collective-permute-start | bytes 4718600 | tf_op jit(solution)/shard_map/ppermute | solution.py:111
  76.6 13.0 %collective-permute-start.13 = (bf16[24,8192]{1,0:T(8,128)(2,1)S(1)}, bf16[24,8192]{1,0:T(8,128)(2,1)S(1)}, u32[]{:S(2)}, u32[]{:S(2)}) collective-permute-start(bf16[24,8192]{1,0:T(8,128)(2,1)S(1)} %get-tuple-element.73), channel_id=1, source_target_pairs={{0,6},{1,7},{2,4},{3,5},{4,2},{5,3},{6,0},{7,1},{8,14},{9,15},{10,... | collective-permute-start | bytes 1179656 | tf_op jit(solution)/shard_map/ppermute | solution.py:111
  79.2 18.0 %collective-permute-start.14 = (bf16[24,8192]{1,0:T(8,128)(2,1)S(1)}, bf16[24,8192]{1,0:T(8,128)(2,1)S(1)}, u32[]{:S(2)}, u32[]{:S(2)}) collective-permute-start(bf16[24,8192]{1,0:T(8,128)(2,1)S(1)} %get-tuple-element.74), channel_id=1, source_target_pairs={{0,4},{1,5},{2,6},{3,7},{4,0},{5,1},{6,2},{7,3},{8,12},{9,13},{10,... | collective-permute-start | bytes 1179656 | tf_op jit(solution)/shard_map/ppermute | solution.py:111
  79.8 17.7 %copy-start.7 = (bf16[192,1024]{1,0:T(8,128)(2,1)S(1)}, bf16[192,1024]{1,0:T(8,128)(2,1)}, u32[]{:S(2)}) copy-start(bf16[192,1024]{1,0:T(8,128)(2,1)} %refs_4_.1) | copy-start | bytes 1179652
  79.8 17.7 %collective-permute-start.15 = (bf16[24,8192]{1,0:T(8,128)(2,1)S(1)}, bf16[24,8192]{1,0:T(8,128)(2,1)S(1)}, u32[]{:S(2)}, u32[]{:S(2)}) collective-permute-start(bf16[24,8192]{1,0:T(8,128)(2,1)S(1)} %get-tuple-element.75), channel_id=1, source_target_pairs={{0,2},{1,3},{2,0},{3,1},{4,6},{5,7},{6,4},{7,5},{8,10},{9,11},{10,... | collective-permute-start | bytes 1179656 | tf_op jit(solution)/shard_map/ppermute | solution.py:111
  85.7 17.0 %copy-start.17 = (bf16[1024,384]{1,0:T(8,128)(2,1)S(1)}, bf16[1024,384]{1,0:T(8,128)(2,1)}, u32[]{:S(2)}) copy-start(bf16[1024,384]{1,0:T(8,128)(2,1)} %get-tuple-element.83.refs_4_.refs_5_.refs_6_) | copy-start | bytes 2359300
  85.7 17.0 %copy-start.18 = (bf16[384,1024]{1,0:T(8,128)(2,1)S(1)}, bf16[384,1024]{1,0:T(8,128)(2,1)}, u32[]{:S(2)}) copy-start(bf16[384,1024]{1,0:T(8,128)(2,1)} %get-tuple-element.81.refs_2_) | copy-start | bytes 2359300
  85.7 17.0 %copy-start.21 = (bf16[384,128]{1,0:T(8,128)(2,1)S(1)}, bf16[384,128]{1,0:T(8,128)(2,1)}, u32[]{:S(2)}) copy-start(bf16[384,128]{1,0:T(8,128)(2,1)} %get-tuple-element.82.refs_3_) | copy-start | bytes 294916
  99.0 3.6 %collective-permute-start.16 = (bf16[192,1024]{1,0:T(8,128)(2,1)}, bf16[192,1024]{1,0:T(8,128)(2,1)S(1)}, u32[]{:S(2)}, u32[]{:S(2)}) collective-permute-start(bf16[192,1024]{1,0:T(8,128)(2,1)} %get-tuple-element.80), channel_id=1, source_target_pairs={{0,1},{1,0},{2,3},{3,2},{4,5},{5,4},{6,7},{7,6},{8,9},{9,8},{10,11... | collective-permute-start | bytes 1179656 | tf_op jit(solution)/shard_map/ppermute | solution.py:111
  99.1 13.1 %collective-permute-start.19 = (bf16[192,1024]{1,0:T(8,128)(2,1)}, bf16[192,1024]{1,0:T(8,128)(2,1)S(1)}, u32[]{:S(2)}, u32[]{:S(2)}) collective-permute-start(bf16[192,1024]{1,0:T(8,128)(2,1)} %get-tuple-element.80), channel_id=1, source_target_pairs={{0,6},{1,7},{2,4},{3,5},{4,2},{5,3},{6,0},{7,1},{8,14},{9,15},{10,... | collective-permute-start | bytes 1179656 | tf_op jit(solution)/shard_map/ppermute | solution.py:111
  100.7 19.5 %collective-permute-start.18 = (bf16[192,1024]{1,0:T(8,128)(2,1)}, bf16[192,1024]{1,0:T(8,128)(2,1)S(1)}, u32[]{:S(2)}, u32[]{:S(2)}) collective-permute-start(bf16[192,1024]{1,0:T(8,128)(2,1)} %get-tuple-element.80), channel_id=1, source_target_pairs={{0,4},{1,5},{2,6},{3,7},{4,0},{5,1},{6,2},{7,3},{8,12},{9,13},{10,... | collective-permute-start | bytes 1179656 | tf_op jit(solution)/shard_map/ppermute | solution.py:111
  102.1 18.1 %collective-permute-start.17 = (bf16[192,1024]{1,0:T(8,128)(2,1)}, bf16[192,1024]{1,0:T(8,128)(2,1)S(1)}, u32[]{:S(2)}, u32[]{:S(2)}) collective-permute-start(bf16[192,1024]{1,0:T(8,128)(2,1)} %get-tuple-element.80), channel_id=1, source_target_pairs={{0,2},{1,3},{2,0},{3,1},{4,6},{5,7},{6,4},{7,5},{8,10},{9,11},{10,... | collective-permute-start | bytes 1179656 | tf_op jit(solution)/shard_map/ppermute | solution.py:111
  105.1 15.6 %copy-start.16 = (bf16[576,1024]{1,0:T(8,128)(2,1)S(1)}, bf16[576,1024]{1,0:T(8,128)(2,1)}, u32[]{:S(2)}) copy-start(bf16[576,1024]{1,0:T(8,128)(2,1)} %get-tuple-element.86.refs_3_) | copy-start | bytes 3538948
  105.1 15.6 %copy-start.20 = (bf16[576,128]{1,0:T(8,128)(2,1)S(1)}, bf16[576,128]{1,0:T(8,128)(2,1)}, u32[]{:S(2)}) copy-start(bf16[576,128]{1,0:T(8,128)(2,1)} %get-tuple-element.87.refs_4_) | copy-start | bytes 442372
  112.2 11.9 %collective-permute-start.22 = (bf16[192,1024]{1,0:T(8,128)(2,1)S(1)}, bf16[192,1024]{1,0:T(8,128)(2,1)S(1)}, u32[]{:S(2)}, u32[]{:S(2)}) collective-permute-start(bf16[192,1024]{1,0:T(8,128)(2,1)S(1)} %shard_map.119.refs_2_), channel_id=1, source_target_pairs={{0,1},{1,0},{2,3},{3,2},{4,5},{5,4},{6,7},{7,6},{8,9},{9,8},{10,11... | collective-permute-start | bytes 1179656 | tf_op jit(solution)/shard_map/ppermute | solution.py:111
  120.2 4.0 %collective-permute-start.21 = (bf16[192,1024]{1,0:T(8,128)(2,1)S(1)}, bf16[192,1024]{1,0:T(8,128)(2,1)S(1)}, u32[]{:S(2)}, u32[]{:S(2)}) collective-permute-start(bf16[192,1024]{1,0:T(8,128)(2,1)S(1)} %shard_map.118.refs_1_), channel_id=1, source_target_pairs={{0,1},{1,0},{2,3},{3,2},{4,5},{5,4},{6,7},{7,6},{8,9},{9,8},{10,11... | collective-permute-start | bytes 1179656 | tf_op jit(solution)/shard_map/ppermute | solution.py:111
  120.2 4.0 %collective-permute-start.20 = (bf16[192,1024]{1,0:T(8,128)(2,1)S(1)}, bf16[192,1024]{1,0:T(8,128)(2,1)S(1)}, u32[]{:S(2)}, u32[]{:S(2)}) collective-permute-start(bf16[192,1024]{1,0:T(8,128)(2,1)S(1)} %shard_map.117.refs_0_), channel_id=1, source_target_pairs={{0,1},{1,0},{2,3},{3,2},{4,5},{5,4},{6,7},{7,6},{8,9},{9,8},{10,11... | collective-permute-start | bytes 1179656 | tf_op jit(solution)/shard_map/ppermute | solution.py:111
  128.9 30.6 %copy-start = (bf16[1,1024,1024]{2,1,0:T(8,128)(2,1)S(1)}, bf16[1,1024,1024]{2,1,0:T(8,128)(2,1)}, u32[]{:S(2)}) copy-start(bf16[1,1024,1024]{2,1,0:T(8,128)(2,1)} %w_ref.5) | copy-start | bytes 6291460
  128.9 36.7 %all-to-all-start = ((bf16[32,32,384]{2,1,0:T(8,128)(2,1)}), bf16[32,32,384]{2,1,0:T(8,128)(2,1)S(1)}, u32[]{:S(2)}, u32[]{:S(2)}) async-start(bf16[32,32,384]{2,1,0:T(8,128)(2,1)} %bitcast.5), calls=%async_computation | async-start | bytes 1572864 | tf_op jit(solution)/shard_map/all_to_all | solution.py:905
  139.0 1.7 collective-permute-start.23
  139.4 6.7 %collective-permute-start.27 = (bf16[256,128]{1,0:T(8,128)(2,1)}, bf16[256,128]{1,0:T(8,128)(2,1)S(1)}, u32[]{:S(2)}, u32[]{:S(2)}) collective-permute-start(bf16[256,128]{1,0:T(8,128)(2,1)} %get-tuple-element.104), channel_id=1, source_target_pairs={{0,1},{1,0},{2,3},{3,2},{4,5},{5,4},{6,7},{7,6},{8,9},{9,8},{10,11... | collective-permute-start | bytes 196616 | tf_op jit(solution)/shard_map/ppermute | solution.py:111
  141.5 17.7 %collective-permute-start.24 = (bf16[384,128]{1,0:T(8,128)(2,1)}, bf16[384,128]{1,0:T(8,128)(2,1)S(1)}, u32[]{:S(2)}, u32[]{:S(2)}) collective-permute-start(bf16[384,128]{1,0:T(8,128)(2,1)} %get-tuple-element.97), channel_id=1, source_target_pairs={{0,2},{1,3},{2,0},{3,1},{4,6},{5,7},{6,4},{7,5},{8,10},{9,11},{10,... | collective-permute-start | bytes 294920 | tf_op jit(solution)/shard_map/ppermute | solution.py:111
  143.3 9.3 %collective-permute-start.28 = (bf16[256,128]{1,0:T(8,128)(2,1)}, bf16[256,128]{1,0:T(8,128)(2,1)S(1)}, u32[]{:S(2)}, u32[]{:S(2)}) collective-permute-start(bf16[256,128]{1,0:T(8,128)(2,1)} %get-tuple-element.105), channel_id=1, source_target_pairs={{0,2},{1,3},{2,0},{3,1},{4,6},{5,7},{6,4},{7,5},{8,10},{9,11},{10,... | collective-permute-start | bytes 196616 | tf_op jit(solution)/shard_map/ppermute | solution.py:111
  143.6 10.0 %collective-permute-start.29 = (bf16[256,128]{1,0:T(8,128)(2,1)}, bf16[256,128]{1,0:T(8,128)(2,1)S(1)}, u32[]{:S(2)}, u32[]{:S(2)}) collective-permute-start(bf16[256,128]{1,0:T(8,128)(2,1)} %get-tuple-element.106), channel_id=1, source_target_pairs={{0,3},{1,2},{2,1},{3,0},{4,7},{5,6},{6,5},{7,4},{8,11},{9,10},{10,... | collective-permute-start | bytes 196616 | tf_op jit(solution)/shard_map/ppermute | solution.py:111
  144.6 14.8 %collective-permute-start.25 = (bf16[384,128]{1,0:T(8,128)(2,1)}, bf16[384,128]{1,0:T(8,128)(2,1)S(1)}, u32[]{:S(2)}, u32[]{:S(2)}) collective-permute-start(bf16[384,128]{1,0:T(8,128)(2,1)} %get-tuple-element.98), channel_id=1, source_target_pairs={{0,4},{1,5},{2,6},{3,7},{4,0},{5,1},{6,2},{7,3},{8,12},{9,13},{10,... | collective-permute-start | bytes 294920 | tf_op jit(solution)/shard_map/ppermute | solution.py:111
  146.0 13.4 %collective-permute-start.26 = (bf16[384,128]{1,0:T(8,128)(2,1)}, bf16[384,128]{1,0:T(8,128)(2,1)S(1)}, u32[]{:S(2)}, u32[]{:S(2)}) collective-permute-start(bf16[384,128]{1,0:T(8,128)(2,1)} %get-tuple-element.99), channel_id=1, source_target_pairs={{0,6},{1,7},{2,4},{3,5},{4,2},{5,3},{6,0},{7,1},{8,14},{9,15},{10,... | collective-permute-start | bytes 294920 | tf_op jit(solution)/shard_map/ppermute | solution.py:111
  155.0 7.9 %collective-permute-start.30 = (bf16[256,128]{1,0:T(8,128)(2,1)}, bf16[256,128]{1,0:T(8,128)(2,1)S(1)}, u32[]{:S(2)}, u32[]{:S(2)}) collective-permute-start(bf16[256,128]{1,0:T(8,128)(2,1)} %get-tuple-element.108), channel_id=1, source_target_pairs={{0,8},{8,0},{16,24},{24,16},{1,9},{9,1},{17,25},{25,17},{2,10},{10... | collective-permute-start | bytes 196616 | tf_op jit(solution)/shard_map/ppermute | solution.py:846
  156.1 7.6 %collective-permute-start.31 = (bf16[256,128]{1,0:T(8,128)(2,1)}, bf16[256,128]{1,0:T(8,128)(2,1)S(1)}, u32[]{:S(2)}, u32[]{:S(2)}) collective-permute-start(bf16[256,128]{1,0:T(8,128)(2,1)} %get-tuple-element.109), channel_id=1, source_target_pairs={{0,16},{8,24},{16,0},{24,8},{1,17},{9,25},{17,1},{25,9},{2,18},{10... | collective-permute-start | bytes 196616 | tf_op jit(solution)/shard_map/ppermute | solution.py:846
  159.2 6.3 %collective-permute-start.32 = (bf16[256,128]{1,0:T(8,128)(2,1)}, bf16[256,128]{1,0:T(8,128)(2,1)S(1)}, u32[]{:S(2)}, u32[]{:S(2)}) collective-permute-start(bf16[256,128]{1,0:T(8,128)(2,1)} %get-tuple-element.110), channel_id=1, source_target_pairs={{0,24},{8,16},{16,8},{24,0},{1,25},{9,17},{17,9},{25,1},{2,26},{10... | collective-permute-start | bytes 196616 | tf_op jit(solution)/shard_map/ppermute | solution.py:846
  160.6 5.0 %copy-start.10 = (bf16[256,128]{1,0:T(8,128)(2,1)S(1)}, bf16[256,128]{1,0:T(8,128)(2,1)}, u32[]{:S(2)}) copy-start(bf16[256,128]{1,0:T(8,128)(2,1)} %get-tuple-element.107.refs_0_) | copy-start | bytes 196612
  (10 other events, 20.5 us)
Sparse Core Ops, SparseCore 0:
  43.1 33.8 all-gather.1

commit v8 on v7

--- a/solution.py
+++ b/solution.py
@@ -20,6 +20,7 @@
 TOKEN = pltpu.VMEM((8, 128), jnp.float32)
 LANES = 128
 EDGE_ROWS = 16
+DEN_ROWS = 8
 BF16_ROWS = 16
 
 
@@ -321,41 +322,30 @@
     heads = heads_of(width)
     count = len(heads)
     keys, values = slice(0, rows), slice(rows, 2 * rows)
-    last = last_row(info_ref, rows, tp_count)
-    spread = den_lanes(rows) - rows
-
-    def sums(q_ref, at_rows, top_ref):
-        size = at_rows.stop - at_rows.start
-        lane = lax.broadcasted_iota(jnp.int32, (size, LANES), 1)
-        dens = jnp.zeros((size, LANES), F32)
-        for h, at in enumerate(heads):
-            q = q_ref[at_rows, at]
-            own, own_den = weigh(q, kv_ref[keys, at])
-            other, other_den = weigh(q, kv_in_ref[keys, at])
-            top_ref[:size, at] = dot(own.astype(BF16), kv_ref[values, at]) + dot(
-                other.astype(BF16), kv_in_ref[values, at]
-            )
-            dens = jnp.where(lane == h, own_den + other_den, dens)
-        return dens
-
-    def fill(back, top, den, edge_top, edge_den):
-        back.ref[:rows, :] = top.astype(BF16)
-        back.ref[rows : rows + EDGE_ROWS, :] = edge_top.astype(BF16)
-        den = jnp.concatenate([den, jnp.broadcast_to(edge_den, (spread, LANES))], axis=0)
-        turned = split_den(den, count).T[:EDGE_ROWS].astype(BF16)
-        back.ref[rows + EDGE_ROWS :, : turned.shape[1]] = turned
-        if turned.shape[1] < width:
-            rest = jnp.zeros((EDGE_ROWS, width - turned.shape[1]), BF16)
-            back.ref[rows + EDGE_ROWS :, turned.shape[1] :] = rest
+    queries = jnp.concatenate([q3_ref[...], q2_ref[...], kv_ref[2 * rows :, :]], axis=0)
+    lane = lax.broadcasted_iota(jnp.int32, far_den.shape, 1)
+    dens = jnp.zeros(far_den.shape, F32)
+    for h, at in enumerate(heads):
+        k = jnp.concatenate([kv_ref[keys, at], kv_in_ref[keys, at]], axis=0)
+        v = jnp.concatenate([kv_ref[values, at], kv_in_ref[values, at]], axis=0)
+        expo, den = weigh(queries[:, at], k)
+        far_top[:, at] = dot(expo.astype(BF16), v)
+        dens = jnp.where(lane == h, den, dens)
+    far_den[...] = dens
+
+    def fill(back, start, edge_row):
+        back.ref[:rows, :] = far_top[start : start + rows, :].astype(BF16)
+        edge_den = jnp.broadcast_to(far_den[pl.ds(edge_row, 1), :], (den_lanes(rows) - rows, LANES))
+        den = jnp.concatenate([far_den[start : start + rows, :], edge_den], axis=0)
+        turned = split_den(den, count).T[:DEN_ROWS]
+        rest = jnp.zeros((DEN_ROWS, width - turned.shape[1]), F32)
+        edge = jnp.broadcast_to(far_top[pl.ds(edge_row, 1), :], (EDGE_ROWS - DEN_ROWS, width))
+        tail = jnp.concatenate([jnp.concatenate([turned, rest], axis=1), edge], axis=0)
+        back.ref[rows:, :] = tail.astype(BF16)
         back.send()
 
-    everything = slice(0, rows)
-    far_den[...] = sums(q2_ref, everything, far_top.at[0])
-    den3 = sums(q3_ref, everything, far_top.at[1])
-    row = jnp.broadcast_to(far_top[0, pl.ds(last, 1), :], (EDGE_ROWS, width))
-    fill(back3, far_top[1], den3, row, far_den[pl.ds(last, 1), :])
-    edge_den = sums(kv_ref, slice(2 * rows, 2 * rows + EDGE_ROWS), far_top.at[1])
-    fill(back2, far_top[0], far_den[...], far_top[1, :EDGE_ROWS, :], edge_den[:1])
+    fill(back2, rows, 2 * rows)
+    fill(back3, 0, rows + last_row(info_ref, rows, tp_count))
 
 
 def near_body(info_ref, kv_ref, kv_in_ref, mask_ref, _, q, top_ref, den_ref, edge_ref):
@@ -388,13 +378,14 @@
     kv_in = lax.ppermute(kv, "ctx", [(0, 1), (2, 3)])
     far = [lax.ppermute(q, "ctx", [(c, 1)]) for c in (3, 2)]
     rows, width = q.shape
-    back = ((rows + 2 * EDGE_ROWS, width), BF16)
+    back = ((rows + EDGE_ROWS, width), BF16)
+    total = 2 * rows + EDGE_ROWS
     back3, back2, done = staged(
         functools.partial(far_body, tp_count),
         [kv_near, kv_in, *far],
         [back, back],
         [TOKEN],
-        [pltpu.VMEM((2, rows, width), F32), pltpu.VMEM((rows, LANES), F32)],
+        [pltpu.VMEM((total, width), F32), pltpu.VMEM((total, LANES), F32)],
         info,
     )
     back = [lax.ppermute(back2, "ctx", [(1, 2)]), lax.ppermute(back3, "ctx", [(1, 3)])]
@@ -456,22 +447,23 @@
     heads = heads_of(depth)
     edges = []
 
+    tails = [ref[rows:, :].astype(F32) for ref in back_refs]
     back_dens = []
-    for ref in back_refs:
-        turned = ref[rows + EDGE_ROWS :, : den_lanes(rows)].astype(F32)
-        rest = jnp.zeros((LANES - EDGE_ROWS, turned.shape[1]), F32)
+    for tail in tails:
+        turned = tail[:DEN_ROWS, : den_lanes(rows)]
+        rest = jnp.zeros((LANES - DEN_ROWS, turned.shape[1]), F32)
         back_dens.append(jnp.concatenate([turned, rest], axis=0).T)
 
+    some = EDGE_ROWS - DEN_ROWS
     for h, lanes in enumerate(heads):
         top, den = top_ref[:, lanes], den_ref[:, h : h + 1]
-        edge, edge_den = edge_ref[:, lanes], edge_ref[:, depth + h : depth + h + 1]
-        for ref in back_refs:
+        edge, edge_den = edge_ref[:some, lanes], edge_ref[:some, depth + h : depth + h + 1]
+        for ref, tail, value in zip(back_refs, tails, back_dens):
+            both = value[:, h : h + 1] + value[:, len(heads) + h : len(heads) + h + 1]
             top += ref[:rows, lanes].astype(F32)
-            edge += ref[rows : rows + EDGE_ROWS, lanes].astype(F32)
-        for value in back_dens:
-            both = value[:, h : h + 1] + value[:, len(heads) + h : len(heads) + h + 1]
+            edge += tail[DEN_ROWS:, lanes]
             den += both[:rows]
-            edge_den += both[rows : rows + EDGE_ROWS]
+            edge_den += both[rows : rows + some]
         whole[:, lanes] = top / den
         edges.append(jnp.where(edge_den > 0, edge / jnp.where(edge_den > 0, edge_den, 1.0), 0.0))
     edge = jnp.concatenate(edges, axis=1)[:1]
@@ -878,7 +870,8 @@
         (me ^ jnp.array(order, jnp.int32))[:, None] * patches
         + jnp.arange(patches, dtype=jnp.int32)[None, :]
     ).reshape(-1)
-    if planes == 4 and den_lanes(shard_rows) <= q.shape[1]:
+    fits = den_lanes(shard_rows) < q.shape[1] and 2 * q.shape[1] // HEAD_DIM <= DEN_ROWS
+    if planes == 4 and fits:
         mask = (place[None, :] <= place[:, None]).astype(F32)
         top, den, edge, back = attend_paired(
             head_info, q, kv, kv_near, mask, tp_count

time: 174 us -> 173 us (level)
  no operation moved by 1% of the time
where the time goes in v8:
time: 173 us; the launch traced here: 172 us
  waiting for transfers between devices  61.6 us (36%)
  Pallas kernels  50.6 us (29%)
  starting transfers between devices  39.5 us (23%)
  between operations  14.5 us (8%)
  local copies, waits for them, and re-layouts  5.24 us (3%)
    ppermute x25, waiting for transfers between devices, swap(): lax.ppermute(value, 'tp', [(source, source ^ bits) for source in range(co...  51.1 us
    ppermute x25, starting transfers between devices, swap(): lax.ppermute(value, 'tp', [(source, source ^ bits) for source in range(co...  18.8 us
    pallas_call x8, Pallas kernels, staged(): pl.pallas_call(kernel, in_specs=[pl.BlockSpec(memory_space=pltpu.SMEM)] *...  18.7 us
    pallas_call x1, Pallas kernels, project(): pl.pallas_call(body, in_specs=[pl.BlockSpec(memory_space=pltpu.SMEM)] + [...  9.61 us
    all_to_all x1, starting transfers between devices, per_device(): grad_qkv = lax.all_to_all(grad_qkv, ('ctx', 'tp'), 0, 0, tiled=True)  9.51 us
    pallas_call x2, Pallas kernels, preload(): pl.pallas_call(functools.partial(preload_body, parts), in_specs=[scalar,...  9.44 us
    ppermute x1, waiting for transfers between devices, attend_paired(): kv_in = lax.ppermute(kv, 'ctx', [(0, 1), (2, 3)])  7.76 us
    pallas_call x1, Pallas kernels, prepare(): pl.pallas_call(functools.partial(prepare_body, parts), grid_spec=pltpu.Pr...  5.5 us
  transfers between devices with their start and end apart: 35, of which 17 were waited for; matrix products, arithmetic and copies ran while one was open for 1% of the time, Pallas kernels for 20%

profile of v8, /device:TPU:0, one launch (start us, length us, event | category | flops | bytes accessed | tf_op | source)
XLA Modules:
  0.0 172.2 jit_solution(18432632080990867765)
XLA Ops:
  7.2 1.0 copy-done.8
  9.1 2.6 %collective-permute-start.2 = (bf16[24,8192]{1,0:T(8,128)(2,1)S(1)}, bf16[24,8192]{1,0:T(8,128)(2,1)S(1)}, u32[]{:S(2)}, u32[]{:S(2)}) collective-permute-start(bf16[24,8192]{1,0:T(8,128)(2,1)S(1)} %shard_map.103.refs_1_), channel_id=1, source_target_pairs={{0,4},{1,5},{2,6},{3,7},{4,0},{5,1},{6,2},{7,3},{8,12},{9,13},{10,... | collective-permute-start | bytes 1179656 | tf_op jit(solution)/shard_map/ppermute | solution.py:112
  11.7 1.4 collective-permute-start.3
  13.9 0.7 copy-done.1
  14.6 4.7 %shard_map.104 = (bf16[8192,512]{1,0:T(8,128)(2,1)S(1)}, s32[4]{0:T(128)}) custom-call(s32[4]{0:T(128)} %pad_add_fusion.info_ref, bf16[3,8192,512]{2,1,0:T(8,128)(2,1)} %refs_11_.1, bf16[24,8192]{1,0:T(8,128)(2,1)} %copy-done.1), custom_call_target="tpu_custom_call" | custom-call | bytes 8388608 | tf_op jit(solution)/shard_map/pallas_call | solution.py:158
  19.3 10.5 %collective-permute-done.2.refs_0_ = bf16[24,8192]{1,0:T(8,128)(2,1)S(1)} collective-permute-done((bf16[24,8192]{1,0:T(8,128)(2,1)S(1)}, bf16[24,8192]{1,0:T(8,128)(2,1)S(1)}, u32[]{:S(2)}, u32[]{:S(2)}) %collective-permute-start.2) | collective-permute-done | bytes 393248 | tf_op jit(solution)/shard_map/ppermute | solution.py:112
  31.1 1.1 collective-permute-done.5.refs_7_
  33.3 9.6 %shard_map.108 = (bf16[192,512]{1,0:T(8,128)(2,1)}, bf16[400,512]{1,0:T(8,128)(2,1)}, bf16[192,1024]{1,0:T(8,128)(2,1)}, bf16[400,512]{1,0:T(8,128)(2,1)S(1)}) custom-call(s32[4]{0:T(128)S(1)} %copy-done.11, bf16[24,8192]{1,0:T(8,128)(2,1)S(1)} %shard_map.103.refs_1_, bf16[24,8192]{1,0:T(8,128)(2,1)S(1)} %shard_map.105.refs_2_, ...), custom_call_target="tpu_custom_call" | custom-call | tf_op jit(solution)/shard_map/pallas_call | solution.py:268
  43.0 3.7 %collective-permute-start.7 = (bf16[400,512]{1,0:T(8,128)(2,1)}, bf16[400,512]{1,0:T(8,128)(2,1)S(1)}, u32[]{:S(2)}, u32[]{:S(2)}) collective-permute-start(bf16[400,512]{1,0:T(8,128)(2,1)} %get-tuple-element.61), channel_id=1, source_target_pairs={{0,8},{16,24},{1,9},{17,25},{2,10},{18,26},{3,11},{19,27},{4,12},{... | collective-permute-start | bytes 1228808 | tf_op jit(solution)/shard_map/ppermute | solution.py:378
  46.7 0.7 collective-permute-start.8
  48.3 7.8 %collective-permute-done.7.refs_2_ = bf16[400,512]{1,0:T(8,128)(2,1)S(1)} collective-permute-done((bf16[400,512]{1,0:T(8,128)(2,1)}, bf16[400,512]{1,0:T(8,128)(2,1)S(1)}, u32[]{:S(2)}, u32[]{:S(2)}) %collective-permute-start.7) | collective-permute-done | bytes 409632 | tf_op jit(solution)/shard_map/ppermute | solution.py:378
  56.0 2.7 %shard_map.109 = (bf16[208,512]{1,0:T(8,128)(2,1)}, bf16[208,512]{1,0:T(8,128)(2,1)}, f32[8,128]{1,0:T(8,128)S(1)}) custom-call(s32[4]{0:T(128)S(1)} %copy-done.12, bf16[400,512]{1,0:T(8,128)(2,1)S(1)} %get-tuple-element.60.refs_1_, bf16[400,512]{1,0:T(8,128)(2,1)S(1)} %collective-permute-done.7.refs_2_, ...), custom_call_target="tpu_custom_call" | custom-call | bytes 4194304 | tf_op jit(solution)/shard_map/pallas_call | solution.py:89
  58.7 0.7 collective-permute-start.10
  59.4 0.9 collective-permute-start.11
  60.3 0.9 copy-done.9
  61.3 2.0 %shard_map.110 = (f32[192,512]{1,0:T(8,128)S(1)}, f32[192,128]{1,0:T(8,128)S(1)}, f32[16,640]{1,0:T(8,128)S(1)}) custom-call(s32[4]{0:T(128)S(1)} %copy-done.12, bf16[400,512]{1,0:T(8,128)(2,1)S(1)} %get-tuple-element.60.refs_1_, bf16[400,512]{1,0:T(8,128)(2,1)S(1)} %collective-permute-done.7.refs_2_, f32[192,192]{1,0:T(8,128)S(1)} %compare_convert_fusion.refs_3_, ...), custom_call_target="tpu_custom_call" | custom-call | bytes 4194304 | tf_op jit(solution)/shard_map/pallas_call | solution.py:89
  63.9 4.8 %shard_map.111 = (bf16[512,8192]{1,0:T(8,128)(2,1)S(1)}, s32[4]{0:T(128)}) custom-call(s32[4]{0:T(128)} %get-tuple-element.58.refs_1_.refs_0_.info_ref, bf16[512,8192]{1,0:T(8,128)(2,1)} %w_ref.4, f32[192,128]{1,0:T(8,128)} %copy-done.5), custom_call_target="tpu_custom_call" | custom-call | bytes 8388608 | tf_op jit(solution)/shard_map/pallas_call | solution.py:158
  68.7 3.5 %shard_map.112 = (bf16[96,8192]{1,0:T(8,128)(2,1)}, bf16[96,8192]{1,0:T(8,128)(2,1)S(1)}) custom-call(s32[4]{0:T(128)S(1)} %copy-done.13, bf16[208,512]{1,0:T(8,128)(2,1)S(1)} %collective-permute-done.10.refs_0_, bf16[208,512]{1,0:T(8,128)(2,1)S(1)} %collective-permute-done.11.refs_1_, f32[192,512]{1,0:T(8,128)S(1)} %get-tuple-element.66.refs_2_, ...), custom_call_target="tpu_custom_call" | custom-call | tf_op jit(solution)/shard_map/pallas_call | solution.py:501
  72.3 3.6 %collective-permute-done.12.other_ref = bf16[96,8192]{1,0:T(8,128)(2,1)S(1)} collective-permute-done((bf16[96,8192]{1,0:T(8,128)(2,1)}, bf16[96,8192]{1,0:T(8,128)(2,1)S(1)}, u32[]{:S(2)}, u32[]{:S(2)}) %collective-permute-start.12) | collective-permute-done | bytes 1572896 | tf_op jit(solution)/shard_map/ppermute | solution.py:112
  76.3 2.6 %collective-permute-start.13 = (bf16[24,8192]{1,0:T(8,128)(2,1)S(1)}, bf16[24,8192]{1,0:T(8,128)(2,1)S(1)}, u32[]{:S(2)}, u32[]{:S(2)}) collective-permute-start(bf16[24,8192]{1,0:T(8,128)(2,1)S(1)} %get-tuple-element.73), channel_id=1, source_target_pairs={{0,6},{1,7},{2,4},{3,5},{4,2},{5,3},{6,0},{7,1},{8,14},{9,15},{10,... | collective-permute-start | bytes 1179656 | tf_op jit(solution)/shard_map/ppermute | solution.py:112
  79.9 5.5 %shard_map.114 = (f32[8,128]{1,0:T(8,128)S(1)}, bf16[1024,384]{1,0:T(8,128)(2,1)}, bf16[384,1024]{1,0:T(8,128)(2,1)}, bf16[384,128]{1,0:T(8,128)(2,1)}, bf16[576...) custom-call(s32[4]{0:T(128)} %get-tuple-element.58.refs_1_.refs_0_.info_ref,, ...), custom_call_target="tpu_custom_call" | custom-call | tf_op jit(solution)/shard_map/pallas_call | solution.py:607
  85.4 3.9 %collective-permute-done.13.refs_1_ = bf16[24,8192]{1,0:T(8,128)(2,1)S(1)} collective-permute-done((bf16[24,8192]{1,0:T(8,128)(2,1)S(1)}, bf16[24,8192]{1,0:T(8,128)(2,1)S(1)}, u32[]{:S(2)}, u32[]{:S(2)}) %collective-permute-start.13) | collective-permute-done | bytes 393248 | tf_op jit(solution)/shard_map/ppermute | solution.py:112
  89.3 7.6 %collective-permute-done.14.refs_2_ = bf16[24,8192]{1,0:T(8,128)(2,1)S(1)} collective-permute-done((bf16[24,8192]{1,0:T(8,128)(2,1)S(1)}, bf16[24,8192]{1,0:T(8,128)(2,1)S(1)}, u32[]{:S(2)}, u32[]{:S(2)}) %collective-permute-start.14) | collective-permute-done | bytes 393248 | tf_op jit(solution)/shard_map/ppermute | solution.py:112
  97.1 1.5 shard_map.115
  98.7 1.6 collective-permute-start.19
  100.3 1.4 collective-permute-start.18
  102.3 2.4 %shard_map.116 = (f32[384,1024]{1,0:T(8,128)S(1)}, f32[128,1024]{1,0:T(8,128)S(1)}, bf16[384,128]{1,0:T(8,128)(2,1)S(1)}, f32[8,128]{1,0:T(8,128)S(1)}) custom-call(bf16[192,1024]{1,0:T(8,128)(2,1)S(1)} %get-tuple-element.79.refs_0_, bf16[192,1024]{1,0:T(8,128)(2,1)S(1)} %collective-permute-done.16.refs_1_, bf16[384,1024]{1,0:T(8,128)(2,1)S(1)} %copy-done.18, ...), custom_call_target="tpu_custom_call" | custom-call | flops 17179869184 | bytes 4194304 | tf_op jit(solution)/shard_map/pallas_call | solution.py:89
  104.7 7.2 %collective-permute-done.19.refs_0_ = bf16[192,1024]{1,0:T(8,128)(2,1)S(1)} collective-permute-done((bf16[192,1024]{1,0:T(8,128)(2,1)}, bf16[192,1024]{1,0:T(8,128)(2,1)S(1)}, u32[]{:S(2)}, u32[]{:S(2)}) %collective-permute-start.19) | collective-permute-done | bytes 393248 | tf_op jit(solution)/shard_map/ppermute | solution.py:112
  111.8 7.9 %collective-permute-done.18.refs_0_ = bf16[192,1024]{1,0:T(8,128)(2,1)S(1)} collective-permute-done((bf16[192,1024]{1,0:T(8,128)(2,1)}, bf16[192,1024]{1,0:T(8,128)(2,1)S(1)}, u32[]{:S(2)}, u32[]{:S(2)}) %collective-permute-start.18) | collective-permute-done | bytes 393248 | tf_op jit(solution)/shard_map/ppermute | solution.py:112
  120.3 3.5 %shard_map.120 = (f32[384,1024]{1,0:T(8,128)S(1)}, f32[128,1024]{1,0:T(8,128)S(1)}, bf16[576,128]{1,0:T(8,128)(2,1)S(1)}, f32[8,128]{1,0:T(8,128)}) custom-call(bf16[192,1024]{1,0:T(8,128)(2,1)S(1)} %shard_map.117.refs_0_, bf16[192,1024]{1,0:T(8,128)(2,1)S(1)} %shard_map.118.refs_1_, bf16[192,1024]{1,0:T(8,128)(2,1)S(1)} %shard_map.119.refs_2_, ...), custom_call_target="tpu_custom_call" | custom-call | flops 17179869184 | bytes 4194304 | tf_op jit(solution)/shard_map/pallas_call | solution.py:89
  123.8 4.6 %shard_map.121 = (bf16[1024,384]{1,0:T(8,128)(2,1)}, bf16[768,128]{1,0:T(8,128)(2,1)}, bf16[256,128]{1,0:T(8,128)(2,1)}, bf16[256,128]{1,0:T(8,128)(2,1)}, bf16[...) custom-call(s32[4]{0:T(128)S(1)} %copy-done.14, bf16[192,1024]{1,0:T(8,128)(2,1)S(1)} %collective-permute-done.20.refs_1_, ...), custom_call_target="tpu_custom_call" | custom-call | flops 17179869184 | bytes 4194304 | tf_op jit(solution)/shard_map/pallas_call | solution.py:89
  128.5 9.5 %all-to-all-start = ((bf16[32,32,384]{2,1,0:T(8,128)(2,1)}), bf16[32,32,384]{2,1,0:T(8,128)(2,1)S(1)}, u32[]{:S(2)}, u32[]{:S(2)}) async-start(bf16[32,32,384]{2,1,0:T(8,128)(2,1)} %bitcast.5), calls=%async_computation | async-start | bytes 1572864 | tf_op jit(solution)/shard_map/all_to_all | solution.py:898
  138.6 1.1 collective-permute-done.23.refs_2_
  139.7 0.7 shard_map.122
  140.4 1.8 %collective-permute-start.24 = (bf16[384,128]{1,0:T(8,128)(2,1)}, bf16[384,128]{1,0:T(8,128)(2,1)S(1)}, u32[]{:S(2)}, u32[]{:S(2)}) collective-permute-start(bf16[384,128]{1,0:T(8,128)(2,1)} %get-tuple-element.97), channel_id=1, source_target_pairs={{0,2},{1,3},{2,0},{3,1},{4,6},{5,7},{6,4},{7,5},{8,10},{9,11},{10,... | collective-permute-start | bytes 294920 | tf_op jit(solution)/shard_map/ppermute | solution.py:112
  142.5 1.0 collective-permute-start.29
  143.5 1.5 collective-permute-start.25
  145.0 0.8 collective-permute-start.26
  145.8 5.8 %collective-permute-done.28.refs_3_ = bf16[256,128]{1,0:T(8,128)(2,1)S(1)} collective-permute-done((bf16[256,128]{1,0:T(8,128)(2,1)}, bf16[256,128]{1,0:T(8,128)(2,1)S(1)}, u32[]{:S(2)}, u32[]{:S(2)}) %collective-permute-start.28) | collective-permute-done | bytes 65568 | tf_op jit(solution)/shard_map/ppermute | solution.py:112
  151.6 1.0 collective-permute-done.29.refs_4_
  152.5 1.3 shard_map.124
  153.9 1.2 collective-permute-start.30
  155.1 3.1 %collective-permute-start.31 = (bf16[256,128]{1,0:T(8,128)(2,1)}, bf16[256,128]{1,0:T(8,128)(2,1)S(1)}, u32[]{:S(2)}, u32[]{:S(2)}) collective-permute-start(bf16[256,128]{1,0:T(8,128)(2,1)} %get-tuple-element.109), channel_id=1, source_target_pairs={{0,16},{8,24},{16,0},{24,8},{1,17},{9,25},{17,1},{25,9},{2,18},{10... | collective-permute-start | bytes 196616 | tf_op jit(solution)/shard_map/ppermute | solution.py:838
  158.4 1.1 copy-done.3
  159.5 2.3 %shard_map.123 = (bf16[192,1024]{1,0:T(8,128)(2,1)}, f32[8,128]{1,0:T(8,128)S(1)}) custom-call(s32[4]{0:T(128)S(1)} %copy-done.14, f32[192,1024]{1,0:T(8,128)S(1)} %copy-done.3, bf16[1,1024,1024]{2,1,0:T(8,128)(2,1)S(1)} %copy-done, bf16[384,128]{1,0:T(8,128)(2,1)S(1)} %get-tuple-element.96.refs_0_, bf16[384,128]{1,0:T(8,128)(2,1)S(1)} %collective-permute-done.24.refs_1_, ...), custom_call_target="tpu_custom_call" | custom-call | tf_op jit(solution)/shard_map/pallas_call | solution.py:901
  161.8 0.9 collective-permute-done.31.refs_2_
  162.7 1.8 %collective-permute-done.32.refs_3_ = bf16[256,128]{1,0:T(8,128)(2,1)S(1)} collective-permute-done((bf16[256,128]{1,0:T(8,128)(2,1)}, bf16[256,128]{1,0:T(8,128)(2,1)S(1)}, u32[]{:S(2)}, u32[]{:S(2)}) %collective-permute-start.32) | collective-permute-done | bytes 65568 | tf_op jit(solution)/shard_map/ppermute | solution.py:838
  164.5 0.9 shard_map.125
  (97 shorter events, 9.5 us)
Async XLA Ops:
  7.2 72.7 %all-gather.2.cloned.1.call-start = ((), (), s32[]{:S(2)}) async-start(), calls=%async_computation.1 | async-start | bytes 3538944 | tf_op jit(solution)/shard_map/all_gather | solution.py:890
  8.5 5.3 %collective-permute-start = (bf16[24,8192]{1,0:T(8,128)(2,1)S(1)}, bf16[24,8192]{1,0:T(8,128)(2,1)S(1)}, u32[]{:S(2)}, u32[]{:S(2)}) collective-permute-start(bf16[24,8192]{1,0:T(8,128)(2,1)S(1)} %shard_map.103.refs_1_), channel_id=1, source_target_pairs={{0,1},{1,0},{2,3},{3,2},{4,5},{5,4},{6,7},{7,6},{8,9},{9,8},{10,11... | collective-permute-start | bytes 1179656 | tf_op jit(solution)/shard_map/ppermute | solution.py:112
  9.1 20.7 %collective-permute-start.2 = (bf16[24,8192]{1,0:T(8,128)(2,1)S(1)}, bf16[24,8192]{1,0:T(8,128)(2,1)S(1)}, u32[]{:S(2)}, u32[]{:S(2)}) collective-permute-start(bf16[24,8192]{1,0:T(8,128)(2,1)S(1)} %shard_map.103.refs_1_), channel_id=1, source_target_pairs={{0,4},{1,5},{2,6},{3,7},{4,0},{5,1},{6,2},{7,3},{8,12},{9,13},{10,... | collective-permute-start | bytes 1179656 | tf_op jit(solution)/shard_map/ppermute | solution.py:112
  11.7 18.8 %collective-permute-start.3 = (bf16[24,8192]{1,0:T(8,128)(2,1)S(1)}, bf16[24,8192]{1,0:T(8,128)(2,1)S(1)}, u32[]{:S(2)}, u32[]{:S(2)}) collective-permute-start(bf16[24,8192]{1,0:T(8,128)(2,1)S(1)} %shard_map.103.refs_1_), channel_id=1, source_target_pairs={{0,6},{1,7},{2,4},{3,5},{4,2},{5,3},{6,0},{7,1},{8,14},{9,15},{10,... | collective-permute-start | bytes 1179656 | tf_op jit(solution)/shard_map/ppermute | solution.py:112
  13.1 18.0 %collective-permute-start.1 = (bf16[24,8192]{1,0:T(8,128)(2,1)S(1)}, bf16[24,8192]{1,0:T(8,128)(2,1)S(1)}, u32[]{:S(2)}, u32[]{:S(2)}) collective-permute-start(bf16[24,8192]{1,0:T(8,128)(2,1)S(1)} %shard_map.103.refs_1_), channel_id=1, source_target_pairs={{0,2},{1,3},{2,0},{3,1},{4,6},{5,7},{6,4},{7,5},{8,10},{9,11},{10,... | collective-permute-start | bytes 1179656 | tf_op jit(solution)/shard_map/ppermute | solution.py:112
  19.3 14.0 %copy-start.2 = (bf16[24,8192]{1,0:T(8,128)(2,1)S(1)}, bf16[24,8192]{1,0:T(8,128)(2,1)}, u32[]{:S(2)}) copy-start(bf16[24,8192]{1,0:T(8,128)(2,1)} %copy-done.1) | copy-start | bytes 1179652
  19.3 14.0 %copy-start.4 = (bf16[192,1024]{1,0:T(8,128)(2,1)S(1)}, bf16[192,1024]{1,0:T(8,128)(2,1)}, u32[]{:S(2)}) copy-start(bf16[192,1024]{1,0:T(8,128)(2,1)} %refs_10_.1) | copy-start | bytes 1179652
  30.5 1.7 %collective-permute-start.5 = (bf16[24,8192]{1,0:T(8,128)(2,1)S(1)}, bf16[24,8192]{1,0:T(8,128)(2,1)S(1)}, u32[]{:S(2)}, u32[]{:S(2)}) collective-permute-start(bf16[24,8192]{1,0:T(8,128)(2,1)S(1)} %shard_map.106.refs_3_), channel_id=1, source_target_pairs={{0,1},{1,0},{2,3},{3,2},{4,5},{5,4},{6,7},{7,6},{8,9},{9,8},{10,11... | collective-permute-start | bytes 1179656 | tf_op jit(solution)/shard_map/ppermute | solution.py:112
  30.5 2.3 %collective-permute-start.6 = (bf16[24,8192]{1,0:T(8,128)(2,1)S(1)}, bf16[24,8192]{1,0:T(8,128)(2,1)S(1)}, u32[]{:S(2)}, u32[]{:S(2)}) collective-permute-start(bf16[24,8192]{1,0:T(8,128)(2,1)S(1)} %shard_map.107.refs_4_), channel_id=1, source_target_pairs={{0,1},{1,0},{2,3},{3,2},{4,5},{5,4},{6,7},{7,6},{8,9},{9,8},{10,11... | collective-permute-start | bytes 1179656 | tf_op jit(solution)/shard_map/ppermute | solution.py:112
  31.1 2.2 %collective-permute-start.4 = (bf16[24,8192]{1,0:T(8,128)(2,1)S(1)}, bf16[24,8192]{1,0:T(8,128)(2,1)S(1)}, u32[]{:S(2)}, u32[]{:S(2)}) collective-permute-start(bf16[24,8192]{1,0:T(8,128)(2,1)S(1)} %shard_map.105.refs_2_), channel_id=1, source_target_pairs={{0,1},{1,0},{2,3},{3,2},{4,5},{5,4},{6,7},{7,6},{8,9},{9,8},{10,11... | collective-permute-start | bytes 1179656 | tf_op jit(solution)/shard_map/ppermute | solution.py:112
  33.3 13.4 %copy-start.22 = (s32[8]{0:T(128)S(1)}, s32[8]{0:T(128)}, u32[]{:S(2)}) copy-start(s32[8]{0:T(128)} %constant.45.clone) | copy-start | bytes 100
  33.3 22.7 %copy-start.12 = (s32[4]{0:T(128)S(1)}, s32[4]{0:T(128)}, u32[]{:S(2)}) copy-start(s32[4]{0:T(128)} %get-tuple-element.58.refs_1_.refs_0_.info_ref) | copy-start | bytes 52
  43.0 13.1 %collective-permute-start.7 = (bf16[400,512]{1,0:T(8,128)(2,1)}, bf16[400,512]{1,0:T(8,128)(2,1)S(1)}, u32[]{:S(2)}, u32[]{:S(2)}) collective-permute-start(bf16[400,512]{1,0:T(8,128)(2,1)} %get-tuple-element.61), channel_id=1, source_target_pairs={{0,8},{16,24},{1,9},{17,25},{2,10},{18,26},{3,11},{19,27},{4,12},{... | collective-permute-start | bytes 1228808 | tf_op jit(solution)/shard_map/ppermute | solution.py:378
  46.7 1.5 collective-permute-start.8
  47.4 0.8 collective-permute-start.9
  58.7 10.0 %collective-permute-start.10 = (bf16[208,512]{1,0:T(8,128)(2,1)}, bf16[208,512]{1,0:T(8,128)(2,1)S(1)}, u32[]{:S(2)}, u32[]{:S(2)}) collective-permute-start(bf16[208,512]{1,0:T(8,128)(2,1)} %get-tuple-element.63), channel_id=1, source_target_pairs={{8,16},{9,17},{10,18},{11,19},{12,20},{13,21},{14,22},{15,23}} | collective-permute-start | bytes 638984 | tf_op jit(solution)/shard_map/ppermute | solution.py:391
  59.4 9.3 %collective-permute-start.11 = (bf16[208,512]{1,0:T(8,128)(2,1)}, bf16[208,512]{1,0:T(8,128)(2,1)S(1)}, u32[]{:S(2)}, u32[]{:S(2)}) collective-permute-start(bf16[208,512]{1,0:T(8,128)(2,1)} %get-tuple-element.64), channel_id=1, source_target_pairs={{8,24},{9,25},{10,26},{11,27},{12,28},{13,29},{14,30},{15,31}} | collective-permute-start | bytes 638984 | tf_op jit(solution)/shard_map/ppermute | solution.py:391
  63.9 4.8 %copy-start.13 = (s32[4]{0:T(128)S(1)}, s32[4]{0:T(128)}, u32[]{:S(2)}) copy-start(s32[4]{0:T(128)} %get-tuple-element.58.refs_1_.refs_0_.info_ref) | copy-start | bytes 52
  72.3 3.7 %collective-permute-start.12 = (bf16[96,8192]{1,0:T(8,128)(2,1)}, bf16[96,8192]{1,0:T(8,128)(2,1)S(1)}, u32[]{:S(2)}, u32[]{:S(2)}) collective-permute-start(bf16[96,8192]{1,0:T(8,128)(2,1)} %get-tuple-element.71), channel_id=1, source_target_pairs={{0,1},{1,0},{2,3},{3,2},{4,5},{5,4},{6,7},{7,6},{8,9},{9,8},{10,11... | collective-permute-start | bytes 4718600 | tf_op jit(solution)/shard_map/ppermute | solution.py:112
  76.3 13.0 %collective-permute-start.13 = (bf16[24,8192]{1,0:T(8,128)(2,1)S(1)}, bf16[24,8192]{1,0:T(8,128)(2,1)S(1)}, u32[]{:S(2)}, u32[]{:S(2)}) collective-permute-start(bf16[24,8192]{1,0:T(8,128)(2,1)S(1)} %get-tuple-element.73), channel_id=1, source_target_pairs={{0,6},{1,7},{2,4},{3,5},{4,2},{5,3},{6,0},{7,1},{8,14},{9,15},{10,... | collective-permute-start | bytes 1179656 | tf_op jit(solution)/shard_map/ppermute | solution.py:112
  78.9 18.0 %collective-permute-start.14 = (bf16[24,8192]{1,0:T(8,128)(2,1)S(1)}, bf16[24,8192]{1,0:T(8,128)(2,1)S(1)}, u32[]{:S(2)}, u32[]{:S(2)}) collective-permute-start(bf16[24,8192]{1,0:T(8,128)(2,1)S(1)} %get-tuple-element.74), channel_id=1, source_target_pairs={{0,4},{1,5},{2,6},{3,7},{4,0},{5,1},{6,2},{7,3},{8,12},{9,13},{10,... | collective-permute-start | bytes 1179656 | tf_op jit(solution)/shard_map/ppermute | solution.py:112
  79.4 17.6 %copy-start.7 = (bf16[192,1024]{1,0:T(8,128)(2,1)S(1)}, bf16[192,1024]{1,0:T(8,128)(2,1)}, u32[]{:S(2)}) copy-start(bf16[192,1024]{1,0:T(8,128)(2,1)} %refs_4_.1) | copy-start | bytes 1179652
  79.4 17.6 %collective-permute-start.15 = (bf16[24,8192]{1,0:T(8,128)(2,1)S(1)}, bf16[24,8192]{1,0:T(8,128)(2,1)S(1)}, u32[]{:S(2)}, u32[]{:S(2)}) collective-permute-start(bf16[24,8192]{1,0:T(8,128)(2,1)S(1)} %get-tuple-element.75), channel_id=1, source_target_pairs={{0,2},{1,3},{2,0},{3,1},{4,6},{5,7},{6,4},{7,5},{8,10},{9,11},{10,... | collective-permute-start | bytes 1179656 | tf_op jit(solution)/shard_map/ppermute | solution.py:112
  85.4 16.9 %copy-start.17 = (bf16[1024,384]{1,0:T(8,128)(2,1)S(1)}, bf16[1024,384]{1,0:T(8,128)(2,1)}, u32[]{:S(2)}) copy-start(bf16[1024,384]{1,0:T(8,128)(2,1)} %get-tuple-element.83.refs_4_.refs_5_.refs_6_) | copy-start | bytes 2359300
  85.4 16.9 %copy-start.18 = (bf16[384,1024]{1,0:T(8,128)(2,1)S(1)}, bf16[384,1024]{1,0:T(8,128)(2,1)}, u32[]{:S(2)}) copy-start(bf16[384,1024]{1,0:T(8,128)(2,1)} %get-tuple-element.81.refs_2_) | copy-start | bytes 2359300
  85.4 16.9 %copy-start.21 = (bf16[384,128]{1,0:T(8,128)(2,1)S(1)}, bf16[384,128]{1,0:T(8,128)(2,1)}, u32[]{:S(2)}) copy-start(bf16[384,128]{1,0:T(8,128)(2,1)} %get-tuple-element.82.refs_3_) | copy-start | bytes 294916
  98.6 3.6 %collective-permute-start.16 = (bf16[192,1024]{1,0:T(8,128)(2,1)}, bf16[192,1024]{1,0:T(8,128)(2,1)S(1)}, u32[]{:S(2)}, u32[]{:S(2)}) collective-permute-start(bf16[192,1024]{1,0:T(8,128)(2,1)} %get-tuple-element.80), channel_id=1, source_target_pairs={{0,1},{1,0},{2,3},{3,2},{4,5},{5,4},{6,7},{7,6},{8,9},{9,8},{10,11... | collective-permute-start | bytes 1179656 | tf_op jit(solution)/shard_map/ppermute | solution.py:112
  98.7 13.1 %collective-permute-start.19 = (bf16[192,1024]{1,0:T(8,128)(2,1)}, bf16[192,1024]{1,0:T(8,128)(2,1)S(1)}, u32[]{:S(2)}, u32[]{:S(2)}) collective-permute-start(bf16[192,1024]{1,0:T(8,128)(2,1)} %get-tuple-element.80), channel_id=1, source_target_pairs={{0,6},{1,7},{2,4},{3,5},{4,2},{5,3},{6,0},{7,1},{8,14},{9,15},{10,... | collective-permute-start | bytes 1179656 | tf_op jit(solution)/shard_map/ppermute | solution.py:112
  100.3 19.5 %collective-permute-start.18 = (bf16[192,1024]{1,0:T(8,128)(2,1)}, bf16[192,1024]{1,0:T(8,128)(2,1)S(1)}, u32[]{:S(2)}, u32[]{:S(2)}) collective-permute-start(bf16[192,1024]{1,0:T(8,128)(2,1)} %get-tuple-element.80), channel_id=1, source_target_pairs={{0,4},{1,5},{2,6},{3,7},{4,0},{5,1},{6,2},{7,3},{8,12},{9,13},{10,... | collective-permute-start | bytes 1179656 | tf_op jit(solution)/shard_map/ppermute | solution.py:112
  101.7 18.1 %collective-permute-start.17 = (bf16[192,1024]{1,0:T(8,128)(2,1)}, bf16[192,1024]{1,0:T(8,128)(2,1)S(1)}, u32[]{:S(2)}, u32[]{:S(2)}) collective-permute-start(bf16[192,1024]{1,0:T(8,128)(2,1)} %get-tuple-element.80), channel_id=1, source_target_pairs={{0,2},{1,3},{2,0},{3,1},{4,6},{5,7},{6,4},{7,5},{8,10},{9,11},{10,... | collective-permute-start | bytes 1179656 | tf_op jit(solution)/shard_map/ppermute | solution.py:112
  104.6 15.6 %copy-start.16 = (bf16[576,1024]{1,0:T(8,128)(2,1)S(1)}, bf16[576,1024]{1,0:T(8,128)(2,1)}, u32[]{:S(2)}) copy-start(bf16[576,1024]{1,0:T(8,128)(2,1)} %get-tuple-element.86.refs_3_) | copy-start | bytes 3538948
  104.7 15.6 %copy-start.20 = (bf16[576,128]{1,0:T(8,128)(2,1)S(1)}, bf16[576,128]{1,0:T(8,128)(2,1)}, u32[]{:S(2)}) copy-start(bf16[576,128]{1,0:T(8,128)(2,1)} %get-tuple-element.87.refs_4_) | copy-start | bytes 442372
  111.8 12.0 %collective-permute-start.22 = (bf16[192,1024]{1,0:T(8,128)(2,1)S(1)}, bf16[192,1024]{1,0:T(8,128)(2,1)S(1)}, u32[]{:S(2)}, u32[]{:S(2)}) collective-permute-start(bf16[192,1024]{1,0:T(8,128)(2,1)S(1)} %shard_map.119.refs_2_), channel_id=1, source_target_pairs={{0,1},{1,0},{2,3},{3,2},{4,5},{5,4},{6,7},{7,6},{8,9},{9,8},{10,11... | collective-permute-start | bytes 1179656 | tf_op jit(solution)/shard_map/ppermute | solution.py:112
  119.8 4.0 %collective-permute-start.21 = (bf16[192,1024]{1,0:T(8,128)(2,1)S(1)}, bf16[192,1024]{1,0:T(8,128)(2,1)S(1)}, u32[]{:S(2)}, u32[]{:S(2)}) collective-permute-start(bf16[192,1024]{1,0:T(8,128)(2,1)S(1)} %shard_map.118.refs_1_), channel_id=1, source_target_pairs={{0,1},{1,0},{2,3},{3,2},{4,5},{5,4},{6,7},{7,6},{8,9},{9,8},{10,11... | collective-permute-start | bytes 1179656 | tf_op jit(solution)/shard_map/ppermute | solution.py:112
  119.8 4.0 %collective-permute-start.20 = (bf16[192,1024]{1,0:T(8,128)(2,1)S(1)}, bf16[192,1024]{1,0:T(8,128)(2,1)S(1)}, u32[]{:S(2)}, u32[]{:S(2)}) collective-permute-start(bf16[192,1024]{1,0:T(8,128)(2,1)S(1)} %shard_map.117.refs_0_), channel_id=1, source_target_pairs={{0,1},{1,0},{2,3},{3,2},{4,5},{5,4},{6,7},{7,6},{8,9},{9,8},{10,11... | collective-permute-start | bytes 1179656 | tf_op jit(solution)/shard_map/ppermute | solution.py:112
  128.4 29.9 %copy-start = (bf16[1,1024,1024]{2,1,0:T(8,128)(2,1)S(1)}, bf16[1,1024,1024]{2,1,0:T(8,128)(2,1)}, u32[]{:S(2)}) copy-start(bf16[1,1024,1024]{2,1,0:T(8,128)(2,1)} %w_ref.5) | copy-start | bytes 6291460
  128.5 36.0 %all-to-all-start = ((bf16[32,32,384]{2,1,0:T(8,128)(2,1)}), bf16[32,32,384]{2,1,0:T(8,128)(2,1)S(1)}, u32[]{:S(2)}, u32[]{:S(2)}) async-start(bf16[32,32,384]{2,1,0:T(8,128)(2,1)} %bitcast.5), calls=%async_computation | async-start | bytes 1572864 | tf_op jit(solution)/shard_map/all_to_all | solution.py:898
  138.0 1.7 collective-permute-start.23
  138.3 6.7 %collective-permute-start.27 = (bf16[256,128]{1,0:T(8,128)(2,1)}, bf16[256,128]{1,0:T(8,128)(2,1)S(1)}, u32[]{:S(2)}, u32[]{:S(2)}) collective-permute-start(bf16[256,128]{1,0:T(8,128)(2,1)} %get-tuple-element.104), channel_id=1, source_target_pairs={{0,1},{1,0},{2,3},{3,2},{4,5},{5,4},{6,7},{7,6},{8,9},{9,8},{10,11... | collective-permute-start | bytes 196616 | tf_op jit(solution)/shard_map/ppermute | solution.py:112
  140.4 17.7 %collective-permute-start.24 = (bf16[384,128]{1,0:T(8,128)(2,1)}, bf16[384,128]{1,0:T(8,128)(2,1)S(1)}, u32[]{:S(2)}, u32[]{:S(2)}) collective-permute-start(bf16[384,128]{1,0:T(8,128)(2,1)} %get-tuple-element.97), channel_id=1, source_target_pairs={{0,2},{1,3},{2,0},{3,1},{4,6},{5,7},{6,4},{7,5},{8,10},{9,11},{10,... | collective-permute-start | bytes 294920 | tf_op jit(solution)/shard_map/ppermute | solution.py:112
  142.3 9.3 %collective-permute-start.28 = (bf16[256,128]{1,0:T(8,128)(2,1)}, bf16[256,128]{1,0:T(8,128)(2,1)S(1)}, u32[]{:S(2)}, u32[]{:S(2)}) collective-permute-start(bf16[256,128]{1,0:T(8,128)(2,1)} %get-tuple-element.105), channel_id=1, source_target_pairs={{0,2},{1,3},{2,0},{3,1},{4,6},{5,7},{6,4},{7,5},{8,10},{9,11},{10,... | collective-permute-start | bytes 196616 | tf_op jit(solution)/shard_map/ppermute | solution.py:112
  142.5 10.0 %collective-permute-start.29 = (bf16[256,128]{1,0:T(8,128)(2,1)}, bf16[256,128]{1,0:T(8,128)(2,1)S(1)}, u32[]{:S(2)}, u32[]{:S(2)}) collective-permute-start(bf16[256,128]{1,0:T(8,128)(2,1)} %get-tuple-element.106), channel_id=1, source_target_pairs={{0,3},{1,2},{2,1},{3,0},{4,7},{5,6},{6,5},{7,4},{8,11},{9,10},{10,... | collective-permute-start | bytes 196616 | tf_op jit(solution)/shard_map/ppermute | solution.py:112
  143.5 14.8 %collective-permute-start.25 = (bf16[384,128]{1,0:T(8,128)(2,1)}, bf16[384,128]{1,0:T(8,128)(2,1)S(1)}, u32[]{:S(2)}, u32[]{:S(2)}) collective-permute-start(bf16[384,128]{1,0:T(8,128)(2,1)} %get-tuple-element.98), channel_id=1, source_target_pairs={{0,4},{1,5},{2,6},{3,7},{4,0},{5,1},{6,2},{7,3},{8,12},{9,13},{10,... | collective-permute-start | bytes 294920 | tf_op jit(solution)/shard_map/ppermute | solution.py:112
  145.0 13.4 %collective-permute-start.26 = (bf16[384,128]{1,0:T(8,128)(2,1)}, bf16[384,128]{1,0:T(8,128)(2,1)S(1)}, u32[]{:S(2)}, u32[]{:S(2)}) collective-permute-start(bf16[384,128]{1,0:T(8,128)(2,1)} %get-tuple-element.99), channel_id=1, source_target_pairs={{0,6},{1,7},{2,4},{3,5},{4,2},{5,3},{6,0},{7,1},{8,14},{9,15},{10,... | collective-permute-start | bytes 294920 | tf_op jit(solution)/shard_map/ppermute | solution.py:112
  153.9 7.9 %collective-permute-start.30 = (bf16[256,128]{1,0:T(8,128)(2,1)}, bf16[256,128]{1,0:T(8,128)(2,1)S(1)}, u32[]{:S(2)}, u32[]{:S(2)}) collective-permute-start(bf16[256,128]{1,0:T(8,128)(2,1)} %get-tuple-element.108), channel_id=1, source_target_pairs={{0,8},{8,0},{16,24},{24,16},{1,9},{9,1},{17,25},{25,17},{2,10},{10... | collective-permute-start | bytes 196616 | tf_op jit(solution)/shard_map/ppermute | solution.py:838
  155.1 7.6 %collective-permute-start.31 = (bf16[256,128]{1,0:T(8,128)(2,1)}, bf16[256,128]{1,0:T(8,128)(2,1)S(1)}, u32[]{:S(2)}, u32[]{:S(2)}) collective-permute-start(bf16[256,128]{1,0:T(8,128)(2,1)} %get-tuple-element.109), channel_id=1, source_target_pairs={{0,16},{8,24},{16,0},{24,8},{1,17},{9,25},{17,1},{25,9},{2,18},{10... | collective-permute-start | bytes 196616 | tf_op jit(solution)/shard_map/ppermute | solution.py:838
  158.1 6.3 %collective-permute-start.32 = (bf16[256,128]{1,0:T(8,128)(2,1)}, bf16[256,128]{1,0:T(8,128)(2,1)S(1)}, u32[]{:S(2)}, u32[]{:S(2)}) collective-permute-start(bf16[256,128]{1,0:T(8,128)(2,1)} %get-tuple-element.110), channel_id=1, source_target_pairs={{0,24},{8,16},{16,8},{24,0},{1,25},{9,17},{17,9},{25,1},{2,26},{10... | collective-permute-start | bytes 196616 | tf_op jit(solution)/shard_map/ppermute | solution.py:838
  159.5 5.0 %copy-start.10 = (bf16[256,128]{1,0:T(8,128)(2,1)S(1)}, bf16[256,128]{1,0:T(8,128)(2,1)}, u32[]{:S(2)}) copy-start(bf16[256,128]{1,0:T(8,128)(2,1)} %get-tuple-element.107.refs_0_) | copy-start | bytes 196612
  (10 other events, 20.5 us)
Sparse Core Ops, SparseCore 0:
  43.1 33.7 all-gather.1

commit v9 on v8

--- a/solution.py
+++ b/solution.py
@@ -205,7 +205,7 @@
 
 def project_body(count, tp_count, info_ref, *refs):
     x_refs, refs = refs[:count], refs[count:]
-    first_ref, pass_ref, w_ref, q, kv, passed, kv_ref, held, wide, sems = refs
+    first_ref, pass_ref, w_ref, q, kv, passed, kv_ref, q_ref, held, wide, sems = refs
     kinds, rows, _ = held.shape
     depth = math.gcd(rows, 1024)
     copies = {}
@@ -240,7 +240,8 @@
             else:
                 kv_ref[(c - 1) * count_rows : c * count_rows, at] = part.astype(BF16)
         if c == 0:
-            q.ref[...] = wide[...].astype(BF16)
+            q_ref[...] = wide[...].astype(BF16)
+            q.ref[...] = q_ref[...]
             q.send()
             last = wide[pl.ds(last_row(info_ref, count_rows, tp_count), 1), :]
             spread = jnp.broadcast_to(last, (EDGE_ROWS, last.shape[1]))
@@ -257,10 +258,10 @@
 
     def body(*refs):
         in_refs, refs = refs[: count + 4], refs[count + 4 :]
-        far, kv_near, near, (held, wide, sems, out_sems) = refs[:3], refs[3], refs[4:7], refs[7:]
+        far, kept, near, (held, wide, sems, out_sems) = refs[:3], refs[3:5], refs[5:8], refs[8:]
         outputs = [Sent(n, f, out_sems.at[i]) for i, (f, n) in enumerate(zip(far, near))]
-        project_body(count, tp_count, *in_refs, *outputs, kv_near, held, wide, sems)
-        near[1][...] = kv_near[...]
+        project_body(count, tp_count, *in_refs, *outputs, *kept, held, wide, sems)
+        near[1][...] = kept[0][...]
         outputs[1].send()
         for output in outputs:
             output.copy.wait()
@@ -270,9 +271,9 @@
         in_specs=[pl.BlockSpec(memory_space=pltpu.SMEM)]
         + [here] * (count + 2)
         + [pl.BlockSpec(memory_space=pl.ANY)],
-        out_specs=[there] * 3 + [here],
+        out_specs=[there] * 3 + [here] * 2,
         out_shape=[pltpu.HBM(shape, dtype) for shape, dtype in outs]
-        + [jax.ShapeDtypeStruct(*outs[1])],
+        + [jax.ShapeDtypeStruct(*outs[1]), jax.ShapeDtypeStruct(*outs[0])],
         scratch_shapes=[pltpu.VMEM(shape, dtype) for shape, dtype in outs]
         + [
             pltpu.VMEM((kinds - 1, deep, width), BF16),
@@ -348,8 +349,7 @@
     fill(back3, 0, rows + last_row(info_ref, rows, tp_count))
 
 
-def near_body(info_ref, kv_ref, kv_in_ref, mask_ref, _, q, top_ref, den_ref, edge_ref):
-    q_ref = q()
+def near_body(info_ref, q_ref, kv_ref, kv_in_ref, mask_ref, _, top_ref, den_ref, edge_ref):
     rows, width = q_ref.shape
     allowed = mask_ref[...] > 0
     linked = jnp.where(info_ref[3] % 2 == 1, 1.0, 0.0)
@@ -374,7 +374,7 @@
     edge_ref[:, width:] = edge_dens
 
 
-def attend_paired(info, q, kv, kv_near, mask, tp_count):
+def attend_paired(info, q, kv, q_near, kv_near, mask, tp_count):
     kv_in = lax.ppermute(kv, "ctx", [(0, 1), (2, 3)])
     far = [lax.ppermute(q, "ctx", [(c, 1)]) for c in (3, 2)]
     rows, width = q.shape
@@ -388,14 +388,13 @@
         [pltpu.VMEM((total, width), F32), pltpu.VMEM((total, LANES), F32)],
         info,
     )
-    back = [lax.ppermute(back2, "ctx", [(1, 2)]), lax.ppermute(back3, "ctx", [(1, 3)])]
+    back = [lax.ppermute(back3, "ctx", [(1, 3)]), lax.ppermute(back2, "ctx", [(1, 2)])]
     top, den, edge = staged(
         near_body,
-        [kv_near, kv_in, mask, done],
+        [q_near, kv_near, kv_in, mask, done],
         [],
         [((rows, width), F32), ((rows, LANES), F32), ((EDGE_ROWS, width + LANES), F32)],
         info=info,
-        held=[q],
     )
     return top, den, edge, back
 
@@ -790,7 +789,8 @@
     *sent, own = staged(
         relay_body, [ab0, ab1, swap(message, 1)], [block] * count, [block]
     )
-    messages = [own] + [swap(value, 2 * (k + 1)) for k, value in enumerate(sent)]
+    messages = [swap(sent[k], 2 * (k + 1)) for k in range(count - 1, -1, -1)]
+    messages = [own] + messages[::-1]
     pieces = staged(
         functools.partial(planes_body, rounds, planes),
         pieces,
@@ -864,7 +864,7 @@
     weights_in, head_info = preload(global_qkv, head_info, mine)
     even = [tie(swap(patch_in, bits), head_info) for bits in range(2, tp_count, 2)]
     pieces = [patch_in, *even, mine, *(swap(piece, 1) for piece in even)]
-    q, kv, gb, kv_near = project(head_info, pieces, weights_in, global_qkv, cotangent, tp_count)
+    q, kv, gb, kv_near, q_near = project(head_info, pieces, weights_in, global_qkv, cotangent, tp_count)
 
     place = (
         (me ^ jnp.array(order, jnp.int32))[:, None] * patches
@@ -874,7 +874,7 @@
     if planes == 4 and fits:
         mask = (place[None, :] <= place[:, None]).astype(F32)
         top, den, edge, back = attend_paired(
-            head_info, q, kv, kv_near, mask, tp_count
+            head_info, q, kv, q_near, kv_near, mask, tp_count
         )
     else:
         key_place = (

time: 173 us -> 172 us (level)
    unnamed x46 -> x44, local copies, waits for them, and re-layouts: 5.15 us -> 4.24 us
  transfers between devices with their start and end apart: 35 -> 35, of which waited for: 17 -> 17; matrix products, arithmetic and copies ran while one was open for 1% -> 0% of each run, Pallas kernels for 20% -> 20%
where the time goes in v9:
time: 172 us
  waiting for transfers between devices  61.9 us (36%)
  Pallas kernels  50.8 us (30%)
  starting transfers between devices  39.4 us (23%)
  between operations  14.5 us (8%)
  local copies, waits for them, and re-layouts  4.32 us (3%)
    ppermute x25, waiting for transfers between devices, swap(): lax.ppermute(value, 'tp', [(source, source ^ bits) for source in range(co...  51.4 us
    ppermute x25, starting transfers between devices, swap(): lax.ppermute(value, 'tp', [(source, source ^ bits) for source in range(co...  18.8 us
    pallas_call x8, Pallas kernels, staged(): pl.pallas_call(kernel, in_specs=[pl.BlockSpec(memory_space=pltpu.SMEM)] *...  18.5 us
    pallas_call x2, Pallas kernels, preload(): pl.pallas_call(functools.partial(preload_body, parts), in_specs=[scalar,...  9.95 us
    pallas_call x1, Pallas kernels, project(): pl.pallas_call(body, in_specs=[pl.BlockSpec(memory_space=pltpu.SMEM)] + [...  9.6 us
    all_to_all x1, starting transfers between devices, per_device(): grad_qkv = lax.all_to_all(grad_qkv, ('ctx', 'tp'), 0, 0, tiled=True)  9.44 us
    ppermute x1, waiting for transfers between devices, attend_paired(): kv_in = lax.ppermute(kv, 'ctx', [(0, 1), (2, 3)])  7.76 us
    pallas_call x1, Pallas kernels, prepare(): pl.pallas_call(functools.partial(prepare_body, parts), grid_spec=pltpu.Pr...  5.48 us
  transfers between devices with their start and end apart: 35, of which 17 were waited for; matrix products, arithmetic and copies ran while one was open for 0% of the time, Pallas kernels for 20%

profile of v9, /device:TPU:0, one launch (start us, length us, event | category | flops | bytes accessed | tf_op | source)
XLA Modules:
  0.0 171.6 jit_solution(1280222906384623232)
XLA Ops:
  7.2 1.0 copy-done.8
  9.1 2.6 %collective-permute-start.2 = (bf16[24,8192]{1,0:T(8,128)(2,1)S(1)}, bf16[24,8192]{1,0:T(8,128)(2,1)S(1)}, u32[]{:S(2)}, u32[]{:S(2)}) collective-permute-start(bf16[24,8192]{1,0:T(8,128)(2,1)S(1)} %shard_map.103.refs_1_), channel_id=1, source_target_pairs={{0,4},{1,5},{2,6},{3,7},{4,0},{5,1},{6,2},{7,3},{8,12},{9,13},{10,... | collective-permute-start | bytes 1179656 | tf_op jit(solution)/shard_map/ppermute | solution.py:112
  11.7 1.4 collective-permute-start.3
  13.8 0.7 copy-done.1
  14.5 4.7 %shard_map.104 = (bf16[8192,512]{1,0:T(8,128)(2,1)S(1)}, s32[4]{0:T(128)}) custom-call(s32[4]{0:T(128)} %pad_add_fusion.info_ref, bf16[3,8192,512]{2,1,0:T(8,128)(2,1)} %refs_11_.1, bf16[24,8192]{1,0:T(8,128)(2,1)} %copy-done.1), custom_call_target="tpu_custom_call" | custom-call | bytes 8388608 | tf_op jit(solution)/shard_map/pallas_call | solution.py:158
  19.2 10.6 %collective-permute-done.2.refs_0_ = bf16[24,8192]{1,0:T(8,128)(2,1)S(1)} collective-permute-done((bf16[24,8192]{1,0:T(8,128)(2,1)S(1)}, bf16[24,8192]{1,0:T(8,128)(2,1)S(1)}, u32[]{:S(2)}, u32[]{:S(2)}) %collective-permute-start.2) | collective-permute-done | bytes 393248 | tf_op jit(solution)/shard_map/ppermute | solution.py:112
  31.1 1.1 collective-permute-done.5.refs_7_
  33.3 9.6 %shard_map.108 = (bf16[192,512]{1,0:T(8,128)(2,1)}, bf16[400,512]{1,0:T(8,128)(2,1)}, bf16[192,1024]{1,0:T(8,128)(2,1)}, bf16[400,512]{1,0:T(8,128)(2,1)S(1)}, bf16[192,512]{1,0:T(8,128)(2,1)S(1)}) custom-call(s32[4]{0:T(128)S(1)} %copy-done.10, bf16[24,8192]{1,0:T(8,128)(2,1)S(1)} %shard_map.103.refs_1_, bf16[24,8192]{1,0:T(8,128)(2,1)S(1)} %shard_map.105.refs_2_, ...), custom_call_target="tpu_custom_call" | custom-call | tf_op jit(solution)/shard_map/pallas_call | solution.py:269
  42.9 3.7 %collective-permute-start.7 = (bf16[400,512]{1,0:T(8,128)(2,1)}, bf16[400,512]{1,0:T(8,128)(2,1)S(1)}, u32[]{:S(2)}, u32[]{:S(2)}) collective-permute-start(bf16[400,512]{1,0:T(8,128)(2,1)} %get-tuple-element.62), channel_id=1, source_target_pairs={{0,8},{16,24},{1,9},{17,25},{2,10},{18,26},{3,11},{19,27},{4,12},{... | collective-permute-start | bytes 1228808 | tf_op jit(solution)/shard_map/ppermute | solution.py:378
  46.7 0.7 collective-permute-start.8
  48.2 7.8 %collective-permute-done.7.refs_2_.refs_3_ = bf16[400,512]{1,0:T(8,128)(2,1)S(1)} collective-permute-done((bf16[400,512]{1,0:T(8,128)(2,1)}, bf16[400,512]{1,0:T(8,128)(2,1)S(1)}, u32[]{:S(2)}, u32[]{:S(2)}) %collective-permute-start.7) | collective-permute-done | bytes 409632 | tf_op jit(solution)/shard_map/ppermute | solution.py:378
  56.0 2.7 %shard_map.109 = (bf16[208,512]{1,0:T(8,128)(2,1)}, bf16[208,512]{1,0:T(8,128)(2,1)}, f32[8,128]{1,0:T(8,128)S(1)}) custom-call(s32[4]{0:T(128)S(1)} %copy-done.11, bf16[400,512]{1,0:T(8,128)(2,1)S(1)} %get-tuple-element.61.refs_1_.refs_2_, bf16[400,512]{1,0:T(8,128)(2,1)S(1)} %collective-permute-done.7.refs_2_.refs_3_, ...), custom_call_target="tpu_custom_call" | custom-call | bytes 4194304 | tf_op jit(solution)/shard_map/pallas_call | solution.py:89
  58.7 0.7 collective-permute-start.10
  59.4 0.9 collective-permute-start.11
  60.3 1.7 %shard_map.110 = (f32[192,512]{1,0:T(8,128)S(1)}, f32[192,128]{1,0:T(8,128)S(1)}, f32[16,640]{1,0:T(8,128)S(1)}) custom-call(s32[4]{0:T(128)S(1)} %copy-done.11, bf16[192,512]{1,0:T(8,128)(2,1)S(1)} %get-tuple-element.66.refs_1_, bf16[400,512]{1,0:T(8,128)(2,1)S(1)} %get-tuple-element.61.refs_1_.refs_2_, ...), custom_call_target="tpu_custom_call" | custom-call | bytes 4194304 | tf_op jit(solution)/shard_map/pallas_call | solution.py:89
  62.7 5.3 %shard_map.111 = (bf16[512,8192]{1,0:T(8,128)(2,1)S(1)}, s32[4]{0:T(128)}) custom-call(s32[4]{0:T(128)} %get-tuple-element.59.refs_1_.refs_0_.info_ref, bf16[512,8192]{1,0:T(8,128)(2,1)} %w_ref.4, f32[192,128]{1,0:T(8,128)} %copy-done.5), custom_call_target="tpu_custom_call" | custom-call | bytes 8388608 | tf_op jit(solution)/shard_map/pallas_call | solution.py:158
  68.1 3.5 %shard_map.112 = (bf16[96,8192]{1,0:T(8,128)(2,1)}, bf16[96,8192]{1,0:T(8,128)(2,1)S(1)}) custom-call(s32[4]{0:T(128)S(1)} %copy-done.12, bf16[208,512]{1,0:T(8,128)(2,1)S(1)} %collective-permute-done.10.refs_0_, bf16[208,512]{1,0:T(8,128)(2,1)S(1)} %collective-permute-done.11.refs_1_, f32[192,512]{1,0:T(8,128)S(1)} %get-tuple-element.68.refs_2_, ...), custom_call_target="tpu_custom_call" | custom-call | tf_op jit(solution)/shard_map/pallas_call | solution.py:500
  71.7 3.9 %collective-permute-done.12.other_ref = bf16[96,8192]{1,0:T(8,128)(2,1)S(1)} collective-permute-done((bf16[96,8192]{1,0:T(8,128)(2,1)}, bf16[96,8192]{1,0:T(8,128)(2,1)S(1)}, u32[]{:S(2)}, u32[]{:S(2)}) %collective-permute-start.12) | collective-permute-done | bytes 1572896 | tf_op jit(solution)/shard_map/ppermute | solution.py:112
  75.9 2.2 %collective-permute-start.13 = (bf16[24,8192]{1,0:T(8,128)(2,1)S(1)}, bf16[24,8192]{1,0:T(8,128)(2,1)S(1)}, u32[]{:S(2)}, u32[]{:S(2)}) collective-permute-start(bf16[24,8192]{1,0:T(8,128)(2,1)S(1)} %get-tuple-element.75), channel_id=1, source_target_pairs={{0,6},{1,7},{2,4},{3,5},{4,2},{5,3},{6,0},{7,1},{8,14},{9,15},{10,... | collective-permute-start | bytes 1179656 | tf_op jit(solution)/shard_map/ppermute | solution.py:112
  78.1 0.8 collective-permute-start.14
  79.5 5.5 %shard_map.114 = (f32[8,128]{1,0:T(8,128)S(1)}, bf16[1024,384]{1,0:T(8,128)(2,1)}, bf16[384,1024]{1,0:T(8,128)(2,1)}, bf16[384,128]{1,0:T(8,128)(2,1)}, bf16[576...) custom-call(s32[4]{0:T(128)} %get-tuple-element.59.refs_1_.refs_0_.info_ref,, ...), custom_call_target="tpu_custom_call" | custom-call | tf_op jit(solution)/shard_map/pallas_call | solution.py:606
  85.0 3.9 %collective-permute-done.13.refs_1_ = bf16[24,8192]{1,0:T(8,128)(2,1)S(1)} collective-permute-done((bf16[24,8192]{1,0:T(8,128)(2,1)S(1)}, bf16[24,8192]{1,0:T(8,128)(2,1)S(1)}, u32[]{:S(2)}, u32[]{:S(2)}) %collective-permute-start.13) | collective-permute-done | bytes 393248 | tf_op jit(solution)/shard_map/ppermute | solution.py:112
  88.9 7.6 %collective-permute-done.14.refs_2_ = bf16[24,8192]{1,0:T(8,128)(2,1)S(1)} collective-permute-done((bf16[24,8192]{1,0:T(8,128)(2,1)S(1)}, bf16[24,8192]{1,0:T(8,128)(2,1)S(1)}, u32[]{:S(2)}, u32[]{:S(2)}) %collective-permute-start.14) | collective-permute-done | bytes 393248 | tf_op jit(solution)/shard_map/ppermute | solution.py:112
  96.6 1.5 shard_map.115
  98.2 1.7 collective-permute-start.19
  99.9 1.2 collective-permute-start.18
  101.8 2.4 %shard_map.116 = (f32[384,1024]{1,0:T(8,128)S(1)}, f32[128,1024]{1,0:T(8,128)S(1)}, bf16[384,128]{1,0:T(8,128)(2,1)S(1)}, f32[8,128]{1,0:T(8,128)S(1)}) custom-call(bf16[192,1024]{1,0:T(8,128)(2,1)S(1)} %get-tuple-element.81.refs_0_, bf16[192,1024]{1,0:T(8,128)(2,1)S(1)} %collective-permute-done.16.refs_1_, bf16[384,1024]{1,0:T(8,128)(2,1)S(1)} %copy-done.17, ...), custom_call_target="tpu_custom_call" | custom-call | flops 17179869184 | bytes 4194304 | tf_op jit(solution)/shard_map/pallas_call | solution.py:89
  104.2 7.2 %collective-permute-done.19.refs_0_ = bf16[192,1024]{1,0:T(8,128)(2,1)S(1)} collective-permute-done((bf16[192,1024]{1,0:T(8,128)(2,1)}, bf16[192,1024]{1,0:T(8,128)(2,1)S(1)}, u32[]{:S(2)}, u32[]{:S(2)}) %collective-permute-start.19) | collective-permute-done | bytes 393248 | tf_op jit(solution)/shard_map/ppermute | solution.py:112
  111.3 7.9 %collective-permute-done.18.refs_0_ = bf16[192,1024]{1,0:T(8,128)(2,1)S(1)} collective-permute-done((bf16[192,1024]{1,0:T(8,128)(2,1)}, bf16[192,1024]{1,0:T(8,128)(2,1)S(1)}, u32[]{:S(2)}, u32[]{:S(2)}) %collective-permute-start.18) | collective-permute-done | bytes 393248 | tf_op jit(solution)/shard_map/ppermute | solution.py:112
  119.8 3.5 %shard_map.120 = (f32[384,1024]{1,0:T(8,128)S(1)}, f32[128,1024]{1,0:T(8,128)S(1)}, bf16[576,128]{1,0:T(8,128)(2,1)S(1)}, f32[8,128]{1,0:T(8,128)}) custom-call(bf16[192,1024]{1,0:T(8,128)(2,1)S(1)} %shard_map.117.refs_0_, bf16[192,1024]{1,0:T(8,128)(2,1)S(1)} %shard_map.118.refs_1_, bf16[192,1024]{1,0:T(8,128)(2,1)S(1)} %shard_map.119.refs_2_, ...), custom_call_target="tpu_custom_call" | custom-call | flops 17179869184 | bytes 4194304 | tf_op jit(solution)/shard_map/pallas_call | solution.py:89
  123.3 4.6 %shard_map.121 = (bf16[1024,384]{1,0:T(8,128)(2,1)}, bf16[768,128]{1,0:T(8,128)(2,1)}, bf16[256,128]{1,0:T(8,128)(2,1)}, bf16[256,128]{1,0:T(8,128)(2,1)}, bf16[...) custom-call(s32[4]{0:T(128)S(1)} %copy-done.13, bf16[192,1024]{1,0:T(8,128)(2,1)S(1)} %collective-permute-done.20.refs_1_, ...), custom_call_target="tpu_custom_call" | custom-call | flops 17179869184 | bytes 4194304 | tf_op jit(solution)/shard_map/pallas_call | solution.py:89
  128.0 9.4 %all-to-all-start = ((bf16[32,32,384]{2,1,0:T(8,128)(2,1)}), bf16[32,32,384]{2,1,0:T(8,128)(2,1)S(1)}, u32[]{:S(2)}, u32[]{:S(2)}) async-start(bf16[32,32,384]{2,1,0:T(8,128)(2,1)} %bitcast.5), calls=%async_computation | async-start | bytes 1572864 | tf_op jit(solution)/shard_map/all_to_all | solution.py:898
  138.0 1.1 collective-permute-done.23.refs_2_
  139.1 0.7 shard_map.122
  139.9 1.8 %collective-permute-start.24 = (bf16[384,128]{1,0:T(8,128)(2,1)}, bf16[384,128]{1,0:T(8,128)(2,1)S(1)}, u32[]{:S(2)}, u32[]{:S(2)}) collective-permute-start(bf16[384,128]{1,0:T(8,128)(2,1)} %get-tuple-element.99), channel_id=1, source_target_pairs={{0,2},{1,3},{2,0},{3,1},{4,6},{5,7},{6,4},{7,5},{8,10},{9,11},{10,... | collective-permute-start | bytes 294920 | tf_op jit(solution)/shard_map/ppermute | solution.py:112
  142.0 1.0 collective-permute-start.29
  142.9 1.5 collective-permute-start.25
  144.4 0.8 collective-permute-start.26
  145.2 5.8 %collective-permute-done.28.refs_3_ = bf16[256,128]{1,0:T(8,128)(2,1)S(1)} collective-permute-done((bf16[256,128]{1,0:T(8,128)(2,1)}, bf16[256,128]{1,0:T(8,128)(2,1)S(1)}, u32[]{:S(2)}, u32[]{:S(2)}) %collective-permute-start.28) | collective-permute-done | bytes 65568 | tf_op jit(solution)/shard_map/ppermute | solution.py:112
  151.0 1.0 collective-permute-done.29.refs_4_
  152.0 1.3 shard_map.124
  153.3 1.2 collective-permute-start.30
  154.5 3.1 %collective-permute-start.31 = (bf16[256,128]{1,0:T(8,128)(2,1)}, bf16[256,128]{1,0:T(8,128)(2,1)S(1)}, u32[]{:S(2)}, u32[]{:S(2)}) collective-permute-start(bf16[256,128]{1,0:T(8,128)(2,1)} %get-tuple-element.111), channel_id=1, source_target_pairs={{0,16},{8,24},{16,0},{24,8},{1,17},{9,25},{17,1},{25,9},{2,18},{10... | collective-permute-start | bytes 196616 | tf_op jit(solution)/shard_map/ppermute | solution.py:838
  157.8 1.1 copy-done.3
  158.9 2.3 %shard_map.123 = (bf16[192,1024]{1,0:T(8,128)(2,1)}, f32[8,128]{1,0:T(8,128)S(1)}) custom-call(s32[4]{0:T(128)S(1)} %copy-done.13, f32[192,1024]{1,0:T(8,128)S(1)} %copy-done.3, bf16[1,1024,1024]{2,1,0:T(8,128)(2,1)S(1)} %copy-done, bf16[384,128]{1,0:T(8,128)(2,1)S(1)} %get-tuple-element.98.refs_0_, bf16[384,128]{1,0:T(8,128)(2,1)S(1)} %collective-permute-done.24.refs_1_, ...), custom_call_target="tpu_custom_call" | custom-call | tf_op jit(solution)/shard_map/pallas_call | solution.py:901
  161.2 0.9 collective-permute-done.31.refs_2_
  162.1 1.8 %collective-permute-done.32.refs_3_ = bf16[256,128]{1,0:T(8,128)(2,1)S(1)} collective-permute-done((bf16[256,128]{1,0:T(8,128)(2,1)}, bf16[256,128]{1,0:T(8,128)(2,1)S(1)}, u32[]{:S(2)}, u32[]{:S(2)}) %collective-permute-start.32) | collective-permute-done | bytes 65568 | tf_op jit(solution)/shard_map/ppermute | solution.py:838
  163.9 0.9 shard_map.125
  (95 shorter events, 9.0 us)
Async XLA Ops:
  7.2 72.3 %all-gather.2.cloned.1.call-start = ((), (), s32[]{:S(2)}) async-start(), calls=%async_computation.1 | async-start | bytes 3538944 | tf_op jit(solution)/shard_map/all_gather | solution.py:890
  8.5 5.2 %collective-permute-start = (bf16[24,8192]{1,0:T(8,128)(2,1)S(1)}, bf16[24,8192]{1,0:T(8,128)(2,1)S(1)}, u32[]{:S(2)}, u32[]{:S(2)}) collective-permute-start(bf16[24,8192]{1,0:T(8,128)(2,1)S(1)} %shard_map.103.refs_1_), channel_id=1, source_target_pairs={{0,1},{1,0},{2,3},{3,2},{4,5},{5,4},{6,7},{7,6},{8,9},{9,8},{10,11... | collective-permute-start | bytes 1179656 | tf_op jit(solution)/shard_map/ppermute | solution.py:112
  9.1 20.7 %collective-permute-start.2 = (bf16[24,8192]{1,0:T(8,128)(2,1)S(1)}, bf16[24,8192]{1,0:T(8,128)(2,1)S(1)}, u32[]{:S(2)}, u32[]{:S(2)}) collective-permute-start(bf16[24,8192]{1,0:T(8,128)(2,1)S(1)} %shard_map.103.refs_1_), channel_id=1, source_target_pairs={{0,4},{1,5},{2,6},{3,7},{4,0},{5,1},{6,2},{7,3},{8,12},{9,13},{10,... | collective-permute-start | bytes 1179656 | tf_op jit(solution)/shard_map/ppermute | solution.py:112
  11.7 18.8 %collective-permute-start.3 = (bf16[24,8192]{1,0:T(8,128)(2,1)S(1)}, bf16[24,8192]{1,0:T(8,128)(2,1)S(1)}, u32[]{:S(2)}, u32[]{:S(2)}) collective-permute-start(bf16[24,8192]{1,0:T(8,128)(2,1)S(1)} %shard_map.103.refs_1_), channel_id=1, source_target_pairs={{0,6},{1,7},{2,4},{3,5},{4,2},{5,3},{6,0},{7,1},{8,14},{9,15},{10,... | collective-permute-start | bytes 1179656 | tf_op jit(solution)/shard_map/ppermute | solution.py:112
  13.1 18.0 %collective-permute-start.1 = (bf16[24,8192]{1,0:T(8,128)(2,1)S(1)}, bf16[24,8192]{1,0:T(8,128)(2,1)S(1)}, u32[]{:S(2)}, u32[]{:S(2)}) collective-permute-start(bf16[24,8192]{1,0:T(8,128)(2,1)S(1)} %shard_map.103.refs_1_), channel_id=1, source_target_pairs={{0,2},{1,3},{2,0},{3,1},{4,6},{5,7},{6,4},{7,5},{8,10},{9,11},{10,... | collective-permute-start | bytes 1179656 | tf_op jit(solution)/shard_map/ppermute | solution.py:112
  19.2 14.1 %copy-start.2 = (bf16[24,8192]{1,0:T(8,128)(2,1)S(1)}, bf16[24,8192]{1,0:T(8,128)(2,1)}, u32[]{:S(2)}) copy-start(bf16[24,8192]{1,0:T(8,128)(2,1)} %copy-done.1) | copy-start | bytes 1179652
  19.2 14.1 %copy-start.4 = (bf16[192,1024]{1,0:T(8,128)(2,1)S(1)}, bf16[192,1024]{1,0:T(8,128)(2,1)}, u32[]{:S(2)}) copy-start(bf16[192,1024]{1,0:T(8,128)(2,1)} %refs_10_.1) | copy-start | bytes 1179652
  30.5 1.7 %collective-permute-start.5 = (bf16[24,8192]{1,0:T(8,128)(2,1)S(1)}, bf16[24,8192]{1,0:T(8,128)(2,1)S(1)}, u32[]{:S(2)}, u32[]{:S(2)}) collective-permute-start(bf16[24,8192]{1,0:T(8,128)(2,1)S(1)} %shard_map.106.refs_3_), channel_id=1, source_target_pairs={{0,1},{1,0},{2,3},{3,2},{4,5},{5,4},{6,7},{7,6},{8,9},{9,8},{10,11... | collective-permute-start | bytes 1179656 | tf_op jit(solution)/shard_map/ppermute | solution.py:112
  30.5 2.3 %collective-permute-start.6 = (bf16[24,8192]{1,0:T(8,128)(2,1)S(1)}, bf16[24,8192]{1,0:T(8,128)(2,1)S(1)}, u32[]{:S(2)}, u32[]{:S(2)}) collective-permute-start(bf16[24,8192]{1,0:T(8,128)(2,1)S(1)} %shard_map.107.refs_4_), channel_id=1, source_target_pairs={{0,1},{1,0},{2,3},{3,2},{4,5},{5,4},{6,7},{7,6},{8,9},{9,8},{10,11... | collective-permute-start | bytes 1179656 | tf_op jit(solution)/shard_map/ppermute | solution.py:112
  31.1 2.2 %collective-permute-start.4 = (bf16[24,8192]{1,0:T(8,128)(2,1)S(1)}, bf16[24,8192]{1,0:T(8,128)(2,1)S(1)}, u32[]{:S(2)}, u32[]{:S(2)}) collective-permute-start(bf16[24,8192]{1,0:T(8,128)(2,1)S(1)} %shard_map.105.refs_2_), channel_id=1, source_target_pairs={{0,1},{1,0},{2,3},{3,2},{4,5},{5,4},{6,7},{7,6},{8,9},{9,8},{10,11... | collective-permute-start | bytes 1179656 | tf_op jit(solution)/shard_map/ppermute | solution.py:112
  33.3 13.4 %copy-start.21 = (s32[8]{0:T(128)S(1)}, s32[8]{0:T(128)}, u32[]{:S(2)}) copy-start(s32[8]{0:T(128)} %constant.45.clone) | copy-start | bytes 100
  33.3 22.7 %copy-start.11 = (s32[4]{0:T(128)S(1)}, s32[4]{0:T(128)}, u32[]{:S(2)}) copy-start(s32[4]{0:T(128)} %get-tuple-element.59.refs_1_.refs_0_.info_ref) | copy-start | bytes 52
  42.9 13.1 %collective-permute-start.7 = (bf16[400,512]{1,0:T(8,128)(2,1)}, bf16[400,512]{1,0:T(8,128)(2,1)S(1)}, u32[]{:S(2)}, u32[]{:S(2)}) collective-permute-start(bf16[400,512]{1,0:T(8,128)(2,1)} %get-tuple-element.62), channel_id=1, source_target_pairs={{0,8},{16,24},{1,9},{17,25},{2,10},{18,26},{3,11},{19,27},{4,12},{... | collective-permute-start | bytes 1228808 | tf_op jit(solution)/shard_map/ppermute | solution.py:378
  46.7 1.5 collective-permute-start.8
  47.4 0.8 collective-permute-start.9
  58.7 9.3 %collective-permute-start.10 = (bf16[208,512]{1,0:T(8,128)(2,1)}, bf16[208,512]{1,0:T(8,128)(2,1)S(1)}, u32[]{:S(2)}, u32[]{:S(2)}) collective-permute-start(bf16[208,512]{1,0:T(8,128)(2,1)} %get-tuple-element.64), channel_id=1, source_target_pairs={{8,24},{9,25},{10,26},{11,27},{12,28},{13,29},{14,30},{15,31}} | collective-permute-start | bytes 638984 | tf_op jit(solution)/shard_map/ppermute | solution.py:391
  59.4 8.7 %collective-permute-start.11 = (bf16[208,512]{1,0:T(8,128)(2,1)}, bf16[208,512]{1,0:T(8,128)(2,1)S(1)}, u32[]{:S(2)}, u32[]{:S(2)}) collective-permute-start(bf16[208,512]{1,0:T(8,128)(2,1)} %get-tuple-element.65), channel_id=1, source_target_pairs={{8,16},{9,17},{10,18},{11,19},{12,20},{13,21},{14,22},{15,23}} | collective-permute-start | bytes 638984 | tf_op jit(solution)/shard_map/ppermute | solution.py:391
  62.7 5.3 %copy-start.6 = (f32[192,128]{1,0:T(8,128)S(1)}, f32[192,128]{1,0:T(8,128)}, u32[]{:S(2)}) copy-start(f32[192,128]{1,0:T(8,128)} %copy-done.5) | copy-start | bytes 294916
  62.7 5.3 %copy-start.12 = (s32[4]{0:T(128)S(1)}, s32[4]{0:T(128)}, u32[]{:S(2)}) copy-start(s32[4]{0:T(128)} %get-tuple-element.59.refs_1_.refs_0_.info_ref) | copy-start | bytes 52
  71.6 4.0 %collective-permute-start.12 = (bf16[96,8192]{1,0:T(8,128)(2,1)}, bf16[96,8192]{1,0:T(8,128)(2,1)S(1)}, u32[]{:S(2)}, u32[]{:S(2)}) collective-permute-start(bf16[96,8192]{1,0:T(8,128)(2,1)} %get-tuple-element.73), channel_id=1, source_target_pairs={{0,1},{1,0},{2,3},{3,2},{4,5},{5,4},{6,7},{7,6},{8,9},{9,8},{10,11... | collective-permute-start | bytes 4718600 | tf_op jit(solution)/shard_map/ppermute | solution.py:112
  75.9 13.0 %collective-permute-start.13 = (bf16[24,8192]{1,0:T(8,128)(2,1)S(1)}, bf16[24,8192]{1,0:T(8,128)(2,1)S(1)}, u32[]{:S(2)}, u32[]{:S(2)}) collective-permute-start(bf16[24,8192]{1,0:T(8,128)(2,1)S(1)} %get-tuple-element.75), channel_id=1, source_target_pairs={{0,6},{1,7},{2,4},{3,5},{4,2},{5,3},{6,0},{7,1},{8,14},{9,15},{10,... | collective-permute-start | bytes 1179656 | tf_op jit(solution)/shard_map/ppermute | solution.py:112
  78.1 18.3 %collective-permute-start.14 = (bf16[24,8192]{1,0:T(8,128)(2,1)S(1)}, bf16[24,8192]{1,0:T(8,128)(2,1)S(1)}, u32[]{:S(2)}, u32[]{:S(2)}) collective-permute-start(bf16[24,8192]{1,0:T(8,128)(2,1)S(1)} %get-tuple-element.76), channel_id=1, source_target_pairs={{0,4},{1,5},{2,6},{3,7},{4,0},{5,1},{6,2},{7,3},{8,12},{9,13},{10,... | collective-permute-start | bytes 1179656 | tf_op jit(solution)/shard_map/ppermute | solution.py:112
  78.9 17.6 %copy-start.7 = (bf16[192,1024]{1,0:T(8,128)(2,1)S(1)}, bf16[192,1024]{1,0:T(8,128)(2,1)}, u32[]{:S(2)}) copy-start(bf16[192,1024]{1,0:T(8,128)(2,1)} %refs_4_.1) | copy-start | bytes 1179652
  78.9 17.6 %collective-permute-start.15 = (bf16[24,8192]{1,0:T(8,128)(2,1)S(1)}, bf16[24,8192]{1,0:T(8,128)(2,1)S(1)}, u32[]{:S(2)}, u32[]{:S(2)}) collective-permute-start(bf16[24,8192]{1,0:T(8,128)(2,1)S(1)} %get-tuple-element.77), channel_id=1, source_target_pairs={{0,2},{1,3},{2,0},{3,1},{4,6},{5,7},{6,4},{7,5},{8,10},{9,11},{10,... | collective-permute-start | bytes 1179656 | tf_op jit(solution)/shard_map/ppermute | solution.py:112
  84.9 16.8 %copy-start.16 = (bf16[1024,384]{1,0:T(8,128)(2,1)S(1)}, bf16[1024,384]{1,0:T(8,128)(2,1)}, u32[]{:S(2)}) copy-start(bf16[1024,384]{1,0:T(8,128)(2,1)} %get-tuple-element.85.refs_4_.refs_5_.refs_6_) | copy-start | bytes 2359300
  85.0 16.8 %copy-start.17 = (bf16[384,1024]{1,0:T(8,128)(2,1)S(1)}, bf16[384,1024]{1,0:T(8,128)(2,1)}, u32[]{:S(2)}) copy-start(bf16[384,1024]{1,0:T(8,128)(2,1)} %get-tuple-element.83.refs_2_) | copy-start | bytes 2359300
  85.0 16.8 %copy-start.20 = (bf16[384,128]{1,0:T(8,128)(2,1)S(1)}, bf16[384,128]{1,0:T(8,128)(2,1)}, u32[]{:S(2)}) copy-start(bf16[384,128]{1,0:T(8,128)(2,1)} %get-tuple-element.84.refs_3_) | copy-start | bytes 294916
  98.1 3.6 %collective-permute-start.16 = (bf16[192,1024]{1,0:T(8,128)(2,1)}, bf16[192,1024]{1,0:T(8,128)(2,1)S(1)}, u32[]{:S(2)}, u32[]{:S(2)}) collective-permute-start(bf16[192,1024]{1,0:T(8,128)(2,1)} %get-tuple-element.82), channel_id=1, source_target_pairs={{0,1},{1,0},{2,3},{3,2},{4,5},{5,4},{6,7},{7,6},{8,9},{9,8},{10,11... | collective-permute-start | bytes 1179656 | tf_op jit(solution)/shard_map/ppermute | solution.py:112
  98.2 13.1 %collective-permute-start.19 = (bf16[192,1024]{1,0:T(8,128)(2,1)}, bf16[192,1024]{1,0:T(8,128)(2,1)S(1)}, u32[]{:S(2)}, u32[]{:S(2)}) collective-permute-start(bf16[192,1024]{1,0:T(8,128)(2,1)} %get-tuple-element.82), channel_id=1, source_target_pairs={{0,6},{1,7},{2,4},{3,5},{4,2},{5,3},{6,0},{7,1},{8,14},{9,15},{10,... | collective-permute-start | bytes 1179656 | tf_op jit(solution)/shard_map/ppermute | solution.py:112
  99.9 19.4 %collective-permute-start.18 = (bf16[192,1024]{1,0:T(8,128)(2,1)}, bf16[192,1024]{1,0:T(8,128)(2,1)S(1)}, u32[]{:S(2)}, u32[]{:S(2)}) collective-permute-start(bf16[192,1024]{1,0:T(8,128)(2,1)} %get-tuple-element.82), channel_id=1, source_target_pairs={{0,4},{1,5},{2,6},{3,7},{4,0},{5,1},{6,2},{7,3},{8,12},{9,13},{10,... | collective-permute-start | bytes 1179656 | tf_op jit(solution)/shard_map/ppermute | solution.py:112
  101.1 18.2 %collective-permute-start.17 = (bf16[192,1024]{1,0:T(8,128)(2,1)}, bf16[192,1024]{1,0:T(8,128)(2,1)S(1)}, u32[]{:S(2)}, u32[]{:S(2)}) collective-permute-start(bf16[192,1024]{1,0:T(8,128)(2,1)} %get-tuple-element.82), channel_id=1, source_target_pairs={{0,2},{1,3},{2,0},{3,1},{4,6},{5,7},{6,4},{7,5},{8,10},{9,11},{10,... | collective-permute-start | bytes 1179656 | tf_op jit(solution)/shard_map/ppermute | solution.py:112
  104.2 15.6 %copy-start.15 = (bf16[576,1024]{1,0:T(8,128)(2,1)S(1)}, bf16[576,1024]{1,0:T(8,128)(2,1)}, u32[]{:S(2)}) copy-start(bf16[576,1024]{1,0:T(8,128)(2,1)} %get-tuple-element.88.refs_3_) | copy-start | bytes 3538948
  104.2 15.6 %copy-start.19 = (bf16[576,128]{1,0:T(8,128)(2,1)S(1)}, bf16[576,128]{1,0:T(8,128)(2,1)}, u32[]{:S(2)}) copy-start(bf16[576,128]{1,0:T(8,128)(2,1)} %get-tuple-element.89.refs_4_) | copy-start | bytes 442372
  111.3 11.9 %collective-permute-start.22 = (bf16[192,1024]{1,0:T(8,128)(2,1)S(1)}, bf16[192,1024]{1,0:T(8,128)(2,1)S(1)}, u32[]{:S(2)}, u32[]{:S(2)}) collective-permute-start(bf16[192,1024]{1,0:T(8,128)(2,1)S(1)} %shard_map.119.refs_2_), channel_id=1, source_target_pairs={{0,1},{1,0},{2,3},{3,2},{4,5},{5,4},{6,7},{7,6},{8,9},{9,8},{10,11... | collective-permute-start | bytes 1179656 | tf_op jit(solution)/shard_map/ppermute | solution.py:112
  119.3 4.0 %collective-permute-start.21 = (bf16[192,1024]{1,0:T(8,128)(2,1)S(1)}, bf16[192,1024]{1,0:T(8,128)(2,1)S(1)}, u32[]{:S(2)}, u32[]{:S(2)}) collective-permute-start(bf16[192,1024]{1,0:T(8,128)(2,1)S(1)} %shard_map.118.refs_1_), channel_id=1, source_target_pairs={{0,1},{1,0},{2,3},{3,2},{4,5},{5,4},{6,7},{7,6},{8,9},{9,8},{10,11... | collective-permute-start | bytes 1179656 | tf_op jit(solution)/shard_map/ppermute | solution.py:112
  119.3 4.0 %collective-permute-start.20 = (bf16[192,1024]{1,0:T(8,128)(2,1)S(1)}, bf16[192,1024]{1,0:T(8,128)(2,1)S(1)}, u32[]{:S(2)}, u32[]{:S(2)}) collective-permute-start(bf16[192,1024]{1,0:T(8,128)(2,1)S(1)} %shard_map.117.refs_0_), channel_id=1, source_target_pairs={{0,1},{1,0},{2,3},{3,2},{4,5},{5,4},{6,7},{7,6},{8,9},{9,8},{10,11... | collective-permute-start | bytes 1179656 | tf_op jit(solution)/shard_map/ppermute | solution.py:112
  127.9 29.8 %copy-start = (bf16[1,1024,1024]{2,1,0:T(8,128)(2,1)S(1)}, bf16[1,1024,1024]{2,1,0:T(8,128)(2,1)}, u32[]{:S(2)}) copy-start(bf16[1,1024,1024]{2,1,0:T(8,128)(2,1)} %w_ref.5) | copy-start | bytes 6291460
  128.0 35.9 %all-to-all-start = ((bf16[32,32,384]{2,1,0:T(8,128)(2,1)}), bf16[32,32,384]{2,1,0:T(8,128)(2,1)S(1)}, u32[]{:S(2)}, u32[]{:S(2)}) async-start(bf16[32,32,384]{2,1,0:T(8,128)(2,1)} %bitcast.5), calls=%async_computation | async-start | bytes 1572864 | tf_op jit(solution)/shard_map/all_to_all | solution.py:898
  137.4 1.7 %collective-permute-start.23 = (bf16[768,128]{1,0:T(8,128)(2,1)}, bf16[768,128]{1,0:T(8,128)(2,1)S(1)}, u32[]{:S(2)}, u32[]{:S(2)}) collective-permute-start(bf16[768,128]{1,0:T(8,128)(2,1)} %get-tuple-element.97), channel_id=1, source_target_pairs={{0,1},{1,0},{2,3},{3,2},{4,5},{5,4},{6,7},{7,6},{8,9},{9,8},{10,11... | collective-permute-start | bytes 589832 | tf_op jit(solution)/shard_map/ppermute | solution.py:112
  137.7 6.7 %collective-permute-start.27 = (bf16[256,128]{1,0:T(8,128)(2,1)}, bf16[256,128]{1,0:T(8,128)(2,1)S(1)}, u32[]{:S(2)}, u32[]{:S(2)}) collective-permute-start(bf16[256,128]{1,0:T(8,128)(2,1)} %get-tuple-element.106), channel_id=1, source_target_pairs={{0,1},{1,0},{2,3},{3,2},{4,5},{5,4},{6,7},{7,6},{8,9},{9,8},{10,11... | collective-permute-start | bytes 196616 | tf_op jit(solution)/shard_map/ppermute | solution.py:112
  139.9 17.7 %collective-permute-start.24 = (bf16[384,128]{1,0:T(8,128)(2,1)}, bf16[384,128]{1,0:T(8,128)(2,1)S(1)}, u32[]{:S(2)}, u32[]{:S(2)}) collective-permute-start(bf16[384,128]{1,0:T(8,128)(2,1)} %get-tuple-element.99), channel_id=1, source_target_pairs={{0,2},{1,3},{2,0},{3,1},{4,6},{5,7},{6,4},{7,5},{8,10},{9,11},{10,... | collective-permute-start | bytes 294920 | tf_op jit(solution)/shard_map/ppermute | solution.py:112
  141.7 9.3 %collective-permute-start.28 = (bf16[256,128]{1,0:T(8,128)(2,1)}, bf16[256,128]{1,0:T(8,128)(2,1)S(1)}, u32[]{:S(2)}, u32[]{:S(2)}) collective-permute-start(bf16[256,128]{1,0:T(8,128)(2,1)} %get-tuple-element.107), channel_id=1, source_target_pairs={{0,2},{1,3},{2,0},{3,1},{4,6},{5,7},{6,4},{7,5},{8,10},{9,11},{10,... | collective-permute-start | bytes 196616 | tf_op jit(solution)/shard_map/ppermute | solution.py:112
  142.0 10.0 %collective-permute-start.29 = (bf16[256,128]{1,0:T(8,128)(2,1)}, bf16[256,128]{1,0:T(8,128)(2,1)S(1)}, u32[]{:S(2)}, u32[]{:S(2)}) collective-permute-start(bf16[256,128]{1,0:T(8,128)(2,1)} %get-tuple-element.108), channel_id=1, source_target_pairs={{0,3},{1,2},{2,1},{3,0},{4,7},{5,6},{6,5},{7,4},{8,11},{9,10},{10,... | collective-permute-start | bytes 196616 | tf_op jit(solution)/shard_map/ppermute | solution.py:112
  142.9 14.8 %collective-permute-start.25 = (bf16[384,128]{1,0:T(8,128)(2,1)}, bf16[384,128]{1,0:T(8,128)(2,1)S(1)}, u32[]{:S(2)}, u32[]{:S(2)}) collective-permute-start(bf16[384,128]{1,0:T(8,128)(2,1)} %get-tuple-element.100), channel_id=1, source_target_pairs={{0,4},{1,5},{2,6},{3,7},{4,0},{5,1},{6,2},{7,3},{8,12},{9,13},{10,... | collective-permute-start | bytes 294920 | tf_op jit(solution)/shard_map/ppermute | solution.py:112
  144.4 13.4 %collective-permute-start.26 = (bf16[384,128]{1,0:T(8,128)(2,1)}, bf16[384,128]{1,0:T(8,128)(2,1)S(1)}, u32[]{:S(2)}, u32[]{:S(2)}) collective-permute-start(bf16[384,128]{1,0:T(8,128)(2,1)} %get-tuple-element.101), channel_id=1, source_target_pairs={{0,6},{1,7},{2,4},{3,5},{4,2},{5,3},{6,0},{7,1},{8,14},{9,15},{10,... | collective-permute-start | bytes 294920 | tf_op jit(solution)/shard_map/ppermute | solution.py:112
  153.3 7.9 %collective-permute-start.30 = (bf16[256,128]{1,0:T(8,128)(2,1)}, bf16[256,128]{1,0:T(8,128)(2,1)S(1)}, u32[]{:S(2)}, u32[]{:S(2)}) collective-permute-start(bf16[256,128]{1,0:T(8,128)(2,1)} %get-tuple-element.110), channel_id=1, source_target_pairs={{0,8},{8,0},{16,24},{24,16},{1,9},{9,1},{17,25},{25,17},{2,10},{10... | collective-permute-start | bytes 196616 | tf_op jit(solution)/shard_map/ppermute | solution.py:838
  154.5 7.6 %collective-permute-start.31 = (bf16[256,128]{1,0:T(8,128)(2,1)}, bf16[256,128]{1,0:T(8,128)(2,1)S(1)}, u32[]{:S(2)}, u32[]{:S(2)}) collective-permute-start(bf16[256,128]{1,0:T(8,128)(2,1)} %get-tuple-element.111), channel_id=1, source_target_pairs={{0,16},{8,24},{16,0},{24,8},{1,17},{9,25},{17,1},{25,9},{2,18},{10... | collective-permute-start | bytes 196616 | tf_op jit(solution)/shard_map/ppermute | solution.py:838
  157.6 6.3 %collective-permute-start.32 = (bf16[256,128]{1,0:T(8,128)(2,1)}, bf16[256,128]{1,0:T(8,128)(2,1)S(1)}, u32[]{:S(2)}, u32[]{:S(2)}) collective-permute-start(bf16[256,128]{1,0:T(8,128)(2,1)} %get-tuple-element.112), channel_id=1, source_target_pairs={{0,24},{8,16},{16,8},{24,0},{1,25},{9,17},{17,9},{25,1},{2,26},{10... | collective-permute-start | bytes 196616 | tf_op jit(solution)/shard_map/ppermute | solution.py:838
  (9 other events, 19.8 us)
Sparse Core Ops, SparseCore 0:
  43.1 33.7 all-gather.1
